TPU v7x, 32 devices: a whole 2x2x4 slice. The times are simulated.
32 devices in a mesh: dp: 8 (over z, core), tp: 4 (over y, x).
Axes of the slice: x: 2, y: 2, z: 4, core: 2. Of those that a mesh axis runs over, the one named last changes fastest.
Arguments:
- tokens: bfloat16 [8192, 2048], P('dp'), may hold values from -6 to 6
- cotangent: bfloat16 [8192, 2048], P('dp'), may hold values from -6 to 6
- span_order: int32 [16], replicated, may hold values from 0 to 15, as said below
- w_query: bfloat16 [2048, 2048], P('dp', 'tp'), may hold values from -0.125 to 0.125
- w_keyval: bfloat16 [2048, 1024], P('dp', 'tp'), may hold values from -0.125 to 0.125
- w_output: bfloat16 [2048, 2048], P('tp', 'dp'), may hold values from -2 to 2
- w_gateup: bfloat16 [2, 2048, 8192], P(None, 'dp', 'tp'), may hold values from -0.125 to 0.125
- w_down: bfloat16 [8192, 2048], P('tp', 'dp'), may hold values from -0.0625 to 0.0625
- norm_gains: bfloat16 [2, 2048], P(None, 'dp'), may hold values from 0.5 to 1.5
- mean_query: float32 [2048, 2048], P('dp', 'tp'), may hold values from -28 to 28
- square_query: float32 [2048, 2048], P('dp', 'tp'), may hold values from 81.92 to 327.68
- mean_keyval: float32 [2048, 1024], P('dp', 'tp'), may hold values from -28 to 28
- square_keyval: float32 [2048, 1024], P('dp', 'tp'), may hold values from 409.6 to 13107.2
- mean_output: float32 [2048, 2048], P('tp', 'dp'), may hold values from -28 to 28
- square_output: float32 [2048, 2048], P('tp', 'dp'), may hold values from 81.92 to 327.68
- mean_gateup: float32 [2, 2048, 8192], P(None, 'dp', 'tp'), may hold values from -28 to 28
- square_gateup: float32 [2, 2048, 8192], P(None, 'dp', 'tp'), may hold values from 81.92 to 327.68
- mean_down: float32 [8192, 2048], P('tp', 'dp'), may hold values from -28 to 28
- square_down: float32 [8192, 2048], P('tp', 'dp'), may hold values from 81.92 to 327.68
- mean_gains: float32 [2, 2048], P(None, 'dp'), may hold values from -28 to 28
- square_gains: float32 [2, 2048], P(None, 'dp'), may hold values from 81.92 to 327.68
Outputs:
- block_output: bfloat16 [8192, 2048], P('dp')
- grad_tokens: float32 [8192, 2048], P('dp')
- grad_query: float32 [2048, 2048], P('dp', 'tp')
- moment_query: float32 [2048, 2048], P('dp', 'tp')
- spread_query: float32 [2048, 2048], P('dp', 'tp')
- update_query: float32 [2048, 2048], P('dp', 'tp')
- grad_keyval: float32 [2048, 1024], P('dp', 'tp')
- moment_keyval: float32 [2048, 1024], P('dp', 'tp')
- spread_keyval: float32 [2048, 1024], P('dp', 'tp')
- update_keyval: float32 [2048, 1024], P('dp', 'tp')
- grad_output: float32 [2048, 2048], P('tp', 'dp')
- moment_output: float32 [2048, 2048], P('tp', 'dp')
- spread_output: float32 [2048, 2048], P('tp', 'dp')
- update_output: float32 [2048, 2048], P('tp', 'dp')
- grad_gateup: float32 [2, 2048, 8192], P(None, 'dp', 'tp')
- moment_gateup: float32 [2, 2048, 8192], P(None, 'dp', 'tp')
- spread_gateup: float32 [2, 2048, 8192], P(None, 'dp', 'tp')
- update_gateup: float32 [2, 2048, 8192], P(None, 'dp', 'tp')
- grad_down: float32 [8192, 2048], P('tp', 'dp')
- moment_down: float32 [8192, 2048], P('tp', 'dp')
- spread_down: float32 [8192, 2048], P('tp', 'dp')
- update_down: float32 [8192, 2048], P('tp', 'dp')
- grad_gains: float32 [2, 2048], P(None, 'dp')
- moment_gains: float32 [2, 2048], P(None, 'dp')
- spread_gains: float32 [2, 2048], P(None, 'dp')
- update_gains: float32 [2, 2048], P(None, 'dp')
Inputs may be any that keep to these rules, and one draw needn't show every extreme that they name: `span_order`: every span number occurs once; entries 2 i and 2 i + 1 are the spans held by index i of dp in every sequence, and they sum to 15.
All inputs are finite; a program needn't handle non-finite values.
Results may differ from a plain program's by a relative error of at most 0.024.
Values may be sent and summed in bfloat16 or wider, within the bound.
A program may use at most 384 MiB of HBM per device.

v0:
```python
import jax
import jax.numpy as jnp
from jax import lax
from jax.sharding import PartitionSpec as P

HD = 64
CH = 64
SEQS = 4
MICRO = 2
STEP = 5


norm_eps = 1e-05
rope_base = 500000.0
beta_one = 0.9
beta_two = 0.95
learn_rate = 0.01
weight_decay = 0.1
adam_eps = 1e-08
masked_score = -1e30


def tables(positions):
    half_size = HD // 2
    frequencies = rope_base ** (-(jnp.arange(half_size, dtype=jnp.float32) * 2.0 / HD))
    angles = positions.astype(jnp.float32)[:, None] * frequencies[None, :]
    cosine_table = jnp.concatenate([jnp.cos(angles), jnp.cos(angles)], axis=-1)[:, None, :]
    sine_table = jnp.concatenate([jnp.sin(angles), jnp.sin(angles)], axis=-1)[:, None, :]
    return (cosine_table, sine_table)


def rotate(values, positions):
    half_size = HD // 2
    cosine_table, sine_table = tables(positions)
    turned = jnp.concatenate([-values[..., half_size:], values[..., :half_size]], axis=-1)
    return values * cosine_table + turned * sine_table


def rotate_back(grads_in, positions):
    half_size = HD // 2
    cosine_table, sine_table = tables(positions)
    scaled = grads_in * sine_table
    turned = jnp.concatenate([scaled[..., half_size:], -scaled[..., :half_size]], axis=-1)
    return grads_in * cosine_table + turned


def scores_of(query_low, key_heads, causal):
    scores = jnp.einsum(
        "sqkgd,stkd->skgqt", query_low, key_heads, preferred_element_type=jnp.float32
    ) * HD ** (-0.5)
    return jnp.where(causal, scores, masked_score)


def norm_back(d_normed, normed, scale):
    return scale * (d_normed - normed * jnp.mean(d_normed * normed, axis=-1, keepdims=True))


def adam_update(gradient, old_mean, square, weight, decay_factor):
    moment = beta_one * old_mean + (1.0 - beta_one) * gradient
    spread = beta_two * square + (1.0 - beta_two) * gradient * gradient
    change = -learn_rate * (
        moment / (1.0 - beta_one**STEP) / (jnp.sqrt(spread / (1.0 - beta_two**STEP)) + adam_eps)
        + decay_factor * weight
    )
    return (moment, spread, change)


def per_device(
    tokens,
    cotangent,
    span_order,
    w_query,
    w_keyval,
    w_output,
    w_gateup,
    w_down,
    norm_gains,
    mean_query,
    square_query,
    mean_keyval,
    square_keyval,
    mean_output,
    square_output,
    mean_gateup,
    square_gateup,
    mean_down,
    square_down,
    mean_gains,
    square_gains,
):
    rows_batch = SEQS * 2 * CH
    seq_length = span_order.shape[0] * CH
    device = lax.axis_index("dp")
    own_spans = lax.dynamic_slice_in_dim(span_order, device * 2, 2)
    offsets = jnp.arange(CH, dtype=jnp.int32)
    own_pos = (own_spans[:, None] * CH + offsets[None, :]).reshape(-1)
    all_pos = (span_order[:, None] * CH + offsets[None, :]).reshape(-1)
    causal = (all_pos[None, :] <= own_pos[:, None])[None, None, None]
    row_pos = jnp.tile(own_pos, SEQS)
    heads_local = w_query.shape[1] // HD
    kv_local = w_keyval.shape[1] // (2 * HD)
    group_size = heads_local // kv_local
    block_outs = []
    input_grads = []
    totals = None
    for microbatch in range(MICRO):
        gathered = (
            lax.all_gather(w_query, "dp", axis=0, tiled=True),
            lax.all_gather(w_keyval, "dp", axis=0, tiled=True),
            lax.all_gather(w_output, "dp", axis=1, tiled=True),
            lax.all_gather(w_gateup, "dp", axis=1, tiled=True),
            lax.all_gather(w_down, "dp", axis=1, tiled=True),
            lax.all_gather(norm_gains, "dp", axis=1, tiled=True),
        )
        full_query, full_keyval, full_output, full_gateup, full_down, full_gains = gathered
        row_start = microbatch * rows_batch
        block_in = tokens[row_start : row_start + rows_batch].astype(jnp.float32)
        seed_low = cotangent[row_start : row_start + rows_batch]
        gain_one = full_gains[0].astype(jnp.float32)
        gain_two = full_gains[1].astype(jnp.float32)
        scale_one = lax.rsqrt(jnp.mean(block_in * block_in, axis=-1, keepdims=True) + norm_eps)
        normed_one = block_in * scale_one
        attn_in = (normed_one * gain_one).astype(jnp.bfloat16)
        queries = jnp.dot(attn_in, full_query, preferred_element_type=jnp.float32).reshape(
            rows_batch, heads_local, HD
        )
        keyvals = jnp.dot(attn_in, full_keyval, preferred_element_type=jnp.float32).reshape(
            rows_batch, kv_local, 2, HD
        )
        query_low = (
            rotate(queries, row_pos)
            .astype(jnp.bfloat16)
            .reshape(SEQS, 2 * CH, kv_local, group_size, HD)
        )
        key_low = rotate(keyvals[:, :, 0], row_pos).astype(jnp.bfloat16)
        value_low = keyvals[:, :, 1].astype(jnp.bfloat16)
        packed = jnp.stack([key_low, value_low], axis=2).reshape(SEQS, 2 * CH, kv_local * 2 * HD)
        seq_keys = lax.all_gather(packed, "dp", axis=1, tiled=True).reshape(
            SEQS, seq_length, kv_local, 2, HD
        )
        key_heads = seq_keys[:, :, :, 0]
        value_heads = seq_keys[:, :, :, 1]
        scores = scores_of(query_low, key_heads, causal)
        row_max = jnp.max(scores, axis=-1, keepdims=True)
        exponent = jnp.exp(scores - row_max)
        row_total = jnp.sum(exponent, axis=-1, keepdims=True)
        log_total = row_max + jnp.log(row_total)
        attention = (exponent / row_total).astype(jnp.bfloat16)
        attended = jnp.einsum(
            "skgqt,stkd->sqkgd", attention, value_heads, preferred_element_type=jnp.float32
        )
        attended = attended.reshape(rows_batch, heads_local * HD).astype(jnp.bfloat16)
        attn_out = lax.psum(
            jnp.dot(attended, full_output, preferred_element_type=jnp.float32), "tp"
        )
        middle = block_in + attn_out
        scale_two = lax.rsqrt(jnp.mean(middle * middle, axis=-1, keepdims=True) + norm_eps)
        normed_two = middle * scale_two
        mlp_input = (normed_two * gain_two).astype(jnp.bfloat16)
        gate_proj = jnp.dot(mlp_input, full_gateup[0], preferred_element_type=jnp.float32)
        up_proj = jnp.dot(mlp_input, full_gateup[1], preferred_element_type=jnp.float32)
        sigmoid_gate = jax.nn.sigmoid(gate_proj)
        silu_gate = gate_proj * sigmoid_gate
        hidden = (silu_gate * up_proj).astype(jnp.bfloat16)
        mlp_out = lax.psum(jnp.dot(hidden, full_down, preferred_element_type=jnp.float32), "tp")
        block_outs.append((middle + mlp_out).astype(jnp.bfloat16))
        backward_set = (
            lax.all_gather(w_query, "dp", axis=0, tiled=True),
            lax.all_gather(w_keyval, "dp", axis=0, tiled=True),
            lax.all_gather(w_output, "dp", axis=1, tiled=True),
            lax.all_gather(w_gateup, "dp", axis=1, tiled=True),
            lax.all_gather(w_down, "dp", axis=1, tiled=True),
            lax.all_gather(norm_gains, "dp", axis=1, tiled=True),
        )
        back_query, back_keyval, back_output, back_gateup, back_down, back_gains = backward_set
        back_one = back_gains[0].astype(jnp.float32)
        back_two = back_gains[1].astype(jnp.float32)
        seed_full = seed_low.astype(jnp.float32)
        batch_down = jnp.einsum("rf,rd->fd", hidden, seed_low, preferred_element_type=jnp.float32)
        d_hidden = jnp.einsum("rd,fd->rf", seed_low, back_down, preferred_element_type=jnp.float32)
        d_gate = (
            d_hidden * up_proj * sigmoid_gate * (1.0 + gate_proj * (1.0 - sigmoid_gate))
        ).astype(jnp.bfloat16)
        d_up = (d_hidden * silu_gate).astype(jnp.bfloat16)
        batch_gateup = jnp.stack(
            [
                jnp.einsum("rd,rf->df", mlp_input, d_gate, preferred_element_type=jnp.float32),
                jnp.einsum("rd,rf->df", mlp_input, d_up, preferred_element_type=jnp.float32),
            ]
        )
        d_mixed_part = jnp.einsum(
            "rf,df->rd", d_gate, back_gateup[0], preferred_element_type=jnp.float32
        ) + jnp.einsum("rf,df->rd", d_up, back_gateup[1], preferred_element_type=jnp.float32)
        d_mixed = lax.psum(d_mixed_part, "tp")
        gain_grad_two = jnp.sum(d_mixed * normed_two, axis=0)
        d_middle = seed_full + norm_back(d_mixed * back_two, normed_two, scale_two)
        d_mid_low = d_middle.astype(jnp.bfloat16)
        batch_output = jnp.einsum(
            "rh,rd->hd", attended, d_mid_low, preferred_element_type=jnp.float32
        )
        d_attend = jnp.einsum(
            "rd,hd->rh", d_mid_low, back_output, preferred_element_type=jnp.float32
        )
        d_attend = d_attend.astype(jnp.bfloat16).reshape(SEQS, 2 * CH, kv_local, group_size, HD)
        scores_again = scores_of(query_low, key_heads, causal)
        attention_full = jnp.exp(scores_again - log_total)
        attention_again = attention_full.astype(jnp.bfloat16)
        d_attention = jnp.einsum(
            "sqkgd,stkd->skgqt", d_attend, value_heads, preferred_element_type=jnp.float32
        )
        d_scores = attention_full * (
            d_attention - jnp.sum(d_attention * attention_full, axis=-1, keepdims=True)
        )
        d_scores_low = d_scores.astype(jnp.bfloat16) * HD ** (-0.5)
        d_query = jnp.einsum(
            "skgqt,stkd->sqkgd", d_scores_low, key_heads, preferred_element_type=jnp.float32
        )
        d_query = d_query.reshape(rows_batch, heads_local, HD)
        d_keys = jnp.einsum(
            "skgqt,sqkgd->stkd", d_scores_low, query_low, preferred_element_type=jnp.float32
        )
        d_values = jnp.einsum(
            "skgqt,sqkgd->stkd", attention_again, d_attend, preferred_element_type=jnp.float32
        )
        d_packed = jnp.stack([d_keys, d_values], axis=3).reshape(
            SEQS, seq_length, kv_local * 2 * HD
        )
        own_grad = lax.psum_scatter(d_packed, "dp", scatter_dimension=1, tiled=True).reshape(
            rows_batch, kv_local, 2, HD
        )
        d_key_low = rotate_back(own_grad[:, :, 0], row_pos).astype(jnp.bfloat16)
        d_value_low = own_grad[:, :, 1].astype(jnp.bfloat16)
        d_keyval_low = jnp.stack([d_key_low, d_value_low], axis=2).reshape(
            rows_batch, kv_local * 2 * HD
        )
        d_query_low = (
            rotate_back(d_query, row_pos).astype(jnp.bfloat16).reshape(rows_batch, heads_local * HD)
        )
        batch_query = jnp.einsum(
            "rd,rh->dh", attn_in, d_query_low, preferred_element_type=jnp.float32
        )
        batch_keyval = jnp.einsum(
            "rd,rh->dh", attn_in, d_keyval_low, preferred_element_type=jnp.float32
        )
        d_act_part = jnp.einsum(
            "rh,dh->rd", d_query_low, back_query, preferred_element_type=jnp.float32
        ) + jnp.einsum("rh,dh->rd", d_keyval_low, back_keyval, preferred_element_type=jnp.float32)
        d_act = lax.psum(d_act_part, "tp")
        gain_grad_one = jnp.sum(d_act * normed_one, axis=0)
        input_grads.append(d_middle + norm_back(d_act * back_one, normed_one, scale_one))
        batch_grads = (
            batch_query,
            batch_keyval,
            batch_output,
            batch_gateup,
            batch_down,
            jnp.stack([gain_grad_one, gain_grad_two]),
        )
        if totals is None:
            totals = batch_grads
        else:
            totals = jax.tree.map(jnp.add, totals, batch_grads)
    sum_query, sum_keyval, sum_output, sum_gateup, sum_down, sum_gains = totals
    owned_grads = (
        lax.psum_scatter(sum_query, "dp", scatter_dimension=0, tiled=True),
        lax.psum_scatter(sum_keyval, "dp", scatter_dimension=0, tiled=True),
        lax.psum_scatter(sum_output, "dp", scatter_dimension=1, tiled=True),
        lax.psum_scatter(sum_gateup, "dp", scatter_dimension=1, tiled=True),
        lax.psum_scatter(sum_down, "dp", scatter_dimension=1, tiled=True),
        lax.psum_scatter(sum_gains, "dp", scatter_dimension=1, tiled=True),
    )
    grad_query, grad_keyval, grad_output, grad_gateup, grad_down, grad_gains = owned_grads
    moment_query, spread_query, update_query = adam_update(
        grad_query, mean_query, square_query, w_query.astype(jnp.float32), weight_decay
    )
    moment_keyval, spread_keyval, update_keyval = adam_update(
        grad_keyval, mean_keyval, square_keyval, w_keyval.astype(jnp.float32), weight_decay
    )
    moment_output, spread_output, update_output = adam_update(
        grad_output, mean_output, square_output, w_output.astype(jnp.float32), weight_decay
    )
    moment_gateup, spread_gateup, update_gateup = adam_update(
        grad_gateup, mean_gateup, square_gateup, w_gateup.astype(jnp.float32), weight_decay
    )
    moment_down, spread_down, update_down = adam_update(
        grad_down, mean_down, square_down, w_down.astype(jnp.float32), weight_decay
    )
    moment_gains, spread_gains, update_gains = adam_update(
        grad_gains, mean_gains, square_gains, norm_gains.astype(jnp.float32), 0.0
    )
    block_output = jnp.concatenate(block_outs, axis=0)
    grad_tokens = jnp.concatenate(input_grads, axis=0)
    return (
        block_output,
        grad_tokens,
        grad_query,
        moment_query,
        spread_query,
        update_query,
        grad_keyval,
        moment_keyval,
        spread_keyval,
        update_keyval,
        grad_output,
        moment_output,
        spread_output,
        update_output,
        grad_gateup,
        moment_gateup,
        spread_gateup,
        update_gateup,
        grad_down,
        moment_down,
        spread_down,
        update_down,
        grad_gains,
        moment_gains,
        spread_gains,
        update_gains,
    )


def solution(mesh):
    placed = (
        P("dp", None),
        P("dp", None),
        P(),
        P("dp", "tp"),
        P("dp", "tp"),
        P("tp", "dp"),
        P(None, "dp", "tp"),
        P("tp", "dp"),
        P(None, "dp"),
        P("dp", "tp"),
        P("dp", "tp"),
        P("dp", "tp"),
        P("dp", "tp"),
        P("tp", "dp"),
        P("tp", "dp"),
        P(None, "dp", "tp"),
        P(None, "dp", "tp"),
        P("tp", "dp"),
        P("tp", "dp"),
        P(None, "dp"),
        P(None, "dp"),
    )
    return jax.shard_map(
        per_device,
        mesh=mesh,
        in_specs=placed,
        out_specs=(
            P("dp", None),
            P("dp", None),
            P("dp", "tp"),
            P("dp", "tp"),
            P("dp", "tp"),
            P("dp", "tp"),
            P("dp", "tp"),
            P("dp", "tp"),
            P("dp", "tp"),
            P("dp", "tp"),
            P("tp", "dp"),
            P("tp", "dp"),
            P("tp", "dp"),
            P("tp", "dp"),
            P(None, "dp", "tp"),
            P(None, "dp", "tp"),
            P(None, "dp", "tp"),
            P(None, "dp", "tp"),
            P("tp", "dp"),
            P("tp", "dp"),
            P("tp", "dp"),
            P("tp", "dp"),
            P(None, "dp"),
            P(None, "dp"),
            P(None, "dp"),
            P(None, "dp"),
        ),
        check_vma=False,
    )
```

profile of v0, /device:TPU:0, one launch (start us, length us, event | category | flops | bytes accessed | tf_op | source)
XLA Modules:
  0.0 2038.3 jit_solution(13825435659515710545)
XLA Ops:
  8.8 13.7 all_gather.16
  27.0 7.5 all-gather.8.cloned.1.call-done
  42.5 22.4 %all-gather.12.cloned.1.call-done = bf16[2048,512]{1,0:T(8,128)(2,1)} async-done(((bf16[256,512]{1,0:T(8,128)(2,1)}), bf16[2048,512]{1,0:T(8,128)(2,1)}) %all-gather.12.cloned.1.call-update) | async-done | bytes 2097168 | tf_op jit(solution)/shard_map/all_gather | solution.py:108
  85.8 11.6 all-gather.20.cloned.1.call-done
  99.6 7.7 fusion.171
  107.3 8.4 fusion.7
  115.7 7.5 fusion.96
  131.6 7.4 fusion.172
  138.9 8.3 fusion.6
  147.2 7.9 fusion.95
  170.6 170.3 %all-reduce.11.cloned.1.call-done = (f32[512,2048]{1,0:T(8,128)}, f32[512,2048]{1,0:T(8,128)}) async-done(((f32[512,2048]{1,0:T(8,128)}, f32[512,2048]{1,0:T(8,128)}), (f32[512,2048]{1,0:T(8,128)}, f32[512,2048]{1,0:T(8,128)})) %all-reduce.11.cloned.1.call-update) | async-done | bytes 8388624 | tf_op jit(solution)/shard_map/psum | solution.py:153
  351.6 142.8 %all-gather.16.cloned.1.call-done = bf16[2,2048,2048]{2,1,0:T(8,128)(2,1)} async-done(((bf16[2,256,2048]{2,1,0:T(8,128)(2,1)}), bf16[2,2048,2048]{2,1,0:T(8,128)(2,1)}) %all-gather.16.cloned.1.call-update) | async-done | bytes 16777232 | tf_op jit(solution)/shard_map/all_gather | solution.py:111
  494.4 9.5 fusion.38
  522.8 54.0 %all-gather.18.cloned.1.call-done = bf16[2048,2048]{1,0:T(8,128)(2,1)} async-done(((bf16[2048,256]{1,0:T(8,128)(2,1)}), bf16[2048,2048]{1,0:T(8,128)(2,1)}) %all-gather.18.cloned.1.call-update) | async-done | bytes 8388624 | tf_op jit(solution)/shard_map/all_gather | solution.py:112
  576.8 14.5 multiply_convert_fusion
  591.3 10.3 fusion.36
  601.6 12.7 multiply_convert_fusion.2
  614.3 10.7 fusion.37
  625.0 10.2 fusion.66
  635.3 8.4 fusion.65
  643.8 170.9 %all-reduce.9.cloned.1.call-done = (f32[512,2048]{1,0:T(8,128)}, f32[512,2048]{1,0:T(8,128)}) async-done(((f32[512,2048]{1,0:T(8,128)}, f32[512,2048]{1,0:T(8,128)}), (f32[512,2048]{1,0:T(8,128)}, f32[512,2048]{1,0:T(8,128)})) %all-reduce.9.cloned.1.call-update) | async-done | bytes 8388624 | tf_op jit(solution)/shard_map/psum | solution.py:194
  814.7 8.0 multiply_reduce_fusion.1
  837.0 9.4 fusion.110
  846.4 9.8 fusion.74
  856.2 23.7 %fusion.68 = f32[4,1024,2,1,64]{1,4,2,0,3:T(8,128)} fusion(f32[4,2,1024,128,4]{3,2,4,1,0:T(8,128)} %fusion.110, f32[4,2,4,128,1024]{3,4,2,1,0:T(8,128)} %get-tuple-element.119, f32[4,2,4,128]{3,2,1,0:T(4,128)S(1)} %bitcast.404, bf16[4,128,2,4,64]{1,0,4,3,2:T(4,128)(2,1)S(1)} %copy-done.51), kind=kOutput, calls=%fused_computation.127 | convolution fusion | flops 578819072 | bytes 36192256 | tf_op jit(solution)/shard_map/skgqt,sqkgd->stkd/dot_general | solution.py:219
  890.3 9.5 fusion.111
  899.8 27.2 %fusion.71 = f32[4,1024,2,1,64]{1,4,2,0,3:T(8,128)S(1)} fusion(f32[4,2,1024,128,4]{3,2,4,1,0:T(8,128)} %fusion.111, f32[4,2,4,128,1024]{3,4,2,1,0:T(8,128)} %get-tuple-element.117, f32[4,2,4,128]{3,2,1,0:T(4,128)S(1)} %bitcast.406, bf16[4,128,2,4,64]{1,0,4,3,2:T(4,128)(2,1)S(1)} %copy-done.49), kind=kOutput, calls=%fused_computation.128 | convolution fusion | flops 578819072 | bytes 36192256 | tf_op jit(solution)/shard_map/skgqt,sqkgd->stkd/dot_general | solution.py:219
  927.0 7.3 fusion.77
  938.8 9.5 fusion.174
  948.4 9.6 fusion.173
  957.9 27.8 %fusion.87 = f32[4,128,2,4,64]{1,4,3,2,0:T(8,128)} fusion(f32[4,2,1024,128,4]{3,2,4,1,0:T(8,128)} %fusion.110, f32[4,2,4,128,1024]{3,4,2,1,0:T(8,128)} %get-tuple-element.119, f32[4,2,4,128]{3,2,1,0:T(4,128)S(1)} %bitcast.405, bf16[4,1024,2,2,64]{1,4,3,2,0:T(8,128)(2,1)S(1)} %bitcast.367), kind=kOutput, calls=%fused_computation.140 | convolution fusion | flops 578819072 | bytes 69238784 | tf_op jit(solution)/shard_map/skgqt,stkd->sqkgd/dot_general | solution.py:215
  989.2 28.2 %fusion.90 = f32[4,128,2,4,64]{1,4,3,2,0:T(8,128)} fusion(f32[4,2,1024,128,4]{3,2,4,1,0:T(8,128)} %fusion.111, f32[4,2,4,128,1024]{3,4,2,1,0:T(8,128)} %get-tuple-element.117, f32[4,2,4,128]{3,2,1,0:T(4,128)S(1)} %bitcast.408, bf16[4,1024,2,2,64]{1,4,3,2,0:T(8,128)(2,1)S(1)} %bitcast.363), kind=kOutput, calls=%fused_computation.141 | convolution fusion | flops 578819072 | bytes 69238784 | tf_op jit(solution)/shard_map/skgqt,stkd->sqkgd/dot_general | solution.py:215
  1060.6 13.1 fusion.83
  1073.7 11.8 convolution_add_fusion
  1087.4 10.2 convolution_bitcast_fusion.2
  1097.6 8.4 convolution_bitcast_fusion.3
  1106.0 8.5 convolution_bitcast_fusion
  1114.5 8.5 convolution_bitcast_fusion.1
  1123.0 227.1 %all-reduce.7.cloned.1.call-done = (f32[512,2048]{1,0:T(8,128)}, f32[512,2048]{1,0:T(8,128)}, f32[512,2048]{1,0:T(8,128)}, f32[512,2048]{1,0:T(8,128)}) async-done(((f32[512,2048]{1,0:T(8,128)}, f32[512,2048]{1,0:T(8,128)}, f32[512,2048]{1,0:T(8,128)}, f32[512,2048]{1,0:T(8,128)}), (f32[512,2048]{1,0:T(8,128)}, f32[512,2048]{1,0:T(8,128)}, f32[512,2048]{1,0:T(8,128)}, ...) | async-done | bytes 16777232 | tf_op jit(solution)/shard_map/psum | solution.py:165
  1357.6 33.9 %maximum_add_fusion = f32[2,2048,2048]{2,1,0:T(8,128)} fusion(f32[1,2048,2048]{2,1,0:T(8,128)} %convolution_bitcast_fusion.2, f32[1,2048,2048]{2,1,0:T(8,128)} %convolution_bitcast_fusion.3, f32[1,2048,2048]{2,1,0:T(8,128)} %convolution_bitcast_fusion, f32[1,2048,2048]{2,1,0:T(8,128)} %convolution_bitcast_fusion.1), kind=kLoop, calls=%fused_computation.2 | loop fusion | flops 25165824 | bytes 100663296 | tf_op jit(solution)/shard_map/add | solution.py:262
  1391.6 12.5 reduce-scatter.15.cloned.1.call-done
  1406.6 48.6 %reduce-scatter.19.cloned.1.call-done = f32[512,256]{1,0:T(8,128)} async-done(((f32[512,2048]{1,0:T(8,128)}), f32[512,256]{1,0:T(8,128)}) %reduce-scatter.19.cloned.1.call-update) | async-done | bytes 524304 | tf_op jit(solution)/shard_map/reduce_scatter | solution.py:267
  1457.6 34.3 %reduce-scatter.17.cloned.1.call-done = f32[256,256]{1,0:T(8,128)} async-done(((f32[2048,256]{1,0:T(8,128)}), f32[256,256]{1,0:T(8,128)}) %reduce-scatter.17.cloned.1.call-update) | async-done | bytes 262160 | tf_op jit(solution)/shard_map/reduce_scatter | solution.py:266
  1510.5 6.8 pad_maximum_fusion
  1517.3 144.6 %reduce-scatter.23.cloned.1.call-done = f32[2048,256]{1,0:T(8,128)} async-done(((f32[2048,2048]{1,0:T(8,128)}), f32[2048,256]{1,0:T(8,128)}) %reduce-scatter.23.cloned.1.call-update) | async-done | bytes 2097168 | tf_op jit(solution)/shard_map/reduce_scatter | solution.py:269
  1668.4 26.9 %reduce-scatter.25.cloned.1.call-done = f32[256,2]{1,0:T(8,128)} async-done(((f32[2048,2]{1,0:T(8,128)}), f32[256,2]{1,0:T(8,128)}) %reduce-scatter.25.cloned.1.call-update) | async-done | bytes 2064
  1696.9 325.3 %reduce-scatter.21.cloned.1.call-done = f32[2,256,2048]{2,1,0:T(8,128)} async-done(((f32[2,2048,2048]{2,1,0:T(8,128)}), f32[2,256,2048]{2,1,0:T(8,128)}) %reduce-scatter.21.cloned.1.call-update) | async-done | bytes 4194320 | tf_op jit(solution)/shard_map/reduce_scatter | solution.py:268
  2022.2 8.8 add_multiply_fusion
  (338 shorter events, 206.6 us)
Async XLA Ops:
  7.2 27.3 %all-gather.8.cloned.1.call-start = ((), (), s32[]{:S(2)}) async-start(), calls=%async_computation.8 | async-start | bytes 1179648 | tf_op jit(solution)/shard_map/all_gather | solution.py:109
  7.9 56.9 %all-gather.12.cloned.1.call-start = ((), (), s32[]{:S(2)}) async-start(), calls=%async_computation.10 | async-start | bytes 2359296 | tf_op jit(solution)/shard_map/all_gather | solution.py:108
  8.7 88.7 %all-gather.20.cloned.1.call-start = ((), (), s32[]{:S(2)}) async-start(), calls=%async_computation.14 | async-start | bytes 2359296 | tf_op jit(solution)/shard_map/all_gather | solution.py:138
  23.7 15.3 copy-start.40
  23.7 15.3 copy-start.46
  27.0 37.9 %copy-start.72 = (f32[512]{0:T(512)}, f32[512]{0:T(512)S(1)}, u32[]{:S(2)}) copy-start(f32[512]{0:T(512)S(1)} %get-tuple-element.121) | copy-start | bytes 6148
  27.0 47.9 %copy-start.64 = (f32[1,2048]{1,0:T(1,128)}, f32[1,2048]{1,0:T(1,128)S(1)}, u32[]{:S(2)}) copy-start(f32[1,2048]{1,0:T(1,128)S(1)} %get-tuple-element.111) | copy-start | bytes 24580
  40.0 89.4 %all-gather.10.cloned.1.call-start = ((), (), s32[]{:S(2)}) async-start(), calls=%async_computation.9 | async-start | bytes 2359296 | tf_op jit(solution)/shard_map/all_gather | solution.py:138
  40.9 119.8 %all-gather.14.cloned.1.call-start = ((), (), s32[]{:S(2)}) async-start(), calls=%async_computation.11 | async-start | bytes 2359296 | tf_op jit(solution)/shard_map/all_gather | solution.py:110
  41.5 299.4 %all-reduce.11.cloned.1.call-start = ((), (), s32[]{:S(2)}) async-start(), calls=%async_computation.25 | async-start | bytes 16777216 | tf_op jit(solution)/shard_map/psum | solution.py:153
  85.8 21.5 %copy-start.48 = (bf16[4,128,2,4,64]{1,0,4,3,2:T(4,128)(2,1)}, bf16[4,128,2,4,64]{1,0,4,3,2:T(4,128)(2,1)S(1)}, u32[]{:S(2)}) copy-start(bf16[4,128,2,4,64]{1,0,4,3,2:T(4,128)(2,1)S(1)} %get-tuple-element.93) | copy-start | bytes 1572868
  85.8 45.8 %copy-start.50 = (bf16[4,128,2,4,64]{1,0,4,3,2:T(4,128)(2,1)}, bf16[4,128,2,4,64]{1,0,4,3,2:T(4,128)(2,1)S(1)}, u32[]{:S(2)}) copy-start(bf16[4,128,2,4,64]{1,0,4,3,2:T(4,128)(2,1)S(1)} %get-tuple-element.92) | copy-start | bytes 1572868
  99.6 16.1 copy-start.24
  123.7 37.0 %copy-start.30 = (bf16[4,128,2,4,64]{1,0,4,3,2:T(4,128)(2,1)}, bf16[4,128,2,4,64]{1,0,4,3,2:T(4,128)(2,1)S(1)}, u32[]{:S(2)}) copy-start(bf16[4,128,2,4,64]{1,0,4,3,2:T(4,128)(2,1)S(1)} %copy.168) | copy-start | bytes 1572868
  131.5 15.7 copy-start.26
  155.6 13.5 copy-start.28
  169.1 325.3 %all-gather.16.cloned.1.call-start = ((), (), s32[]{:S(2)}) async-start(), calls=%async_computation.12 | async-start | bytes 18874368 | tf_op jit(solution)/shard_map/all_gather | solution.py:111
  169.8 407.0 %all-gather.18.cloned.1.call-start = ((), (), s32[]{:S(2)}) async-start(), calls=%async_computation.13 | async-start | bytes 9437184 | tf_op jit(solution)/shard_map/all_gather | solution.py:112
  170.6 644.1 %all-reduce.9.cloned.1.call-start = ((), (), s32[]{:S(2)}) async-start(), calls=%async_computation.24 | async-start | bytes 16777216 | tf_op jit(solution)/shard_map/psum | solution.py:194
  351.6 152.3 %copy-start.42 = (bf16[512,2048]{1,0:T(8,128)(2,1)}, bf16[512,2048]{1,0:T(8,128)(2,1)S(1)}, u32[]{:S(2)}) copy-start(bf16[512,2048]{1,0:T(8,128)(2,1)S(1)} %get-tuple-element.109) | copy-start | bytes 6291460
  614.3 21.0 %slice-start = ((s8[16777216]{0:T(1024)(128)(4,1)}), s8[4194304]{0:T(1024)(128)(4,1)S(1)}, s32[]{:S(2)}) async-start(s8[16777216]{0:T(1024)(128)(4,1)} %bitcast.413), calls=%async_computation.26 | async-start | bytes 8388608
  614.3 21.0 %slice-start.1 = ((s8[16777216]{0:T(1024)(128)(4,1)}), s8[4194304]{0:T(1024)(128)(4,1)S(1)}, s32[]{:S(2)}) async-start(s8[16777216]{0:T(1024)(128)(4,1)} %bitcast.413), calls=%async_computation.27 | async-start | bytes 8388608
  643.7 380.9 %reduce-scatter.11.cloned.1.call-start = ((), (), s32[]{:S(2)}) async-start(), calls=%async_computation.15 | async-start | bytes 4718592 | tf_op jit(solution)/shard_map/reduce_scatter | solution.py:228
  884.8 141.4 %reduce-scatter.13.cloned.1.call-start = ((), (), s32[]{:S(2)}) async-start(), calls=%async_computation.16 | async-start | bytes 4718592 | tf_op jit(solution)/shard_map/reduce_scatter | solution.py:228
  937.3 412.8 %all-reduce.7.cloned.1.call-start = ((), (), s32[]{:S(2)}) async-start(), calls=%async_computation.23 | async-start | bytes 33554432 | tf_op jit(solution)/shard_map/psum | solution.py:165
  1039.2 364.9 %reduce-scatter.15.cloned.1.call-start = ((), (), s32[]{:S(2)}) async-start(), calls=%async_computation.17 | async-start | bytes 4718592 | tf_op jit(solution)/shard_map/reduce_scatter | solution.py:265
  1047.2 408.0 %reduce-scatter.19.cloned.1.call-start = ((), (), s32[]{:S(2)}) async-start(), calls=%async_computation.19 | async-start | bytes 4718592 | tf_op jit(solution)/shard_map/reduce_scatter | solution.py:267
  1055.2 436.8 %reduce-scatter.17.cloned.1.call-start = ((), (), s32[]{:S(2)}) async-start(), calls=%async_computation.18 | async-start | bytes 2359296 | tf_op jit(solution)/shard_map/reduce_scatter | solution.py:266
  1060.5 13.2 copy-start.39
  1060.5 601.3 %reduce-scatter.23.cloned.1.call-start = ((), (), s32[]{:S(2)}) async-start(), calls=%async_computation.21 | async-start | bytes 18874368 | tf_op jit(solution)/shard_map/reduce_scatter | solution.py:269
  1060.6 13.1 copy-start.18
  1085.5 609.7 %reduce-scatter.25.cloned.1.call-start = ((), (), s32[]{:S(2)}) async-start(), calls=%async_computation.22 | async-start | bytes 1179648
  1357.3 664.8 %reduce-scatter.21.cloned.1.call-start = ((), (), s32[]{:S(2)}) async-start(), calls=%async_computation.20 | async-start | bytes 37748736 | tf_op jit(solution)/shard_map/reduce_scatter | solution.py:268
  1391.5 12.6 copy-start.53
  1391.5 12.6 copy-start.55
  1391.5 12.6 copy-start.56
  1391.5 63.6 %copy-start.54 = (bf16[512,256]{1,0:T(8,128)(2,1)S(1)}, bf16[512,256]{1,0:T(8,128)(2,1)}, u32[]{:S(2)}) copy-start(bf16[512,256]{1,0:T(8,128)(2,1)} %param.26) | copy-start | bytes 786436
  1391.5 63.6 %copy-start.57 = (f32[512,256]{1,0:T(8,128)S(1)}, f32[512,256]{1,0:T(8,128)}, u32[]{:S(2)}) copy-start(f32[512,256]{1,0:T(8,128)} %param.35) | copy-start | bytes 1572868
  1391.6 63.6 %copy-start.58 = (f32[512,256]{1,0:T(8,128)S(1)}, f32[512,256]{1,0:T(8,128)}, u32[]{:S(2)}) copy-start(f32[512,256]{1,0:T(8,128)} %param.34) | copy-start | bytes 1572868
  1391.6 100.3 %copy-start.59 = (bf16[256,256]{1,0:T(8,128)(2,1)S(1)}, bf16[256,256]{1,0:T(8,128)(2,1)}, u32[]{:S(2)}) copy-start(bf16[256,256]{1,0:T(8,128)(2,1)} %param.25) | copy-start | bytes 393220
  1391.6 100.3 %copy-start.60 = (f32[256,256]{1,0:T(8,128)S(1)}, f32[256,256]{1,0:T(8,128)}, u32[]{:S(2)}) copy-start(f32[256,256]{1,0:T(8,128)} %param.33) | copy-start | bytes 786436
  1391.6 100.3 %copy-start.61 = (f32[256,256]{1,0:T(8,128)S(1)}, f32[256,256]{1,0:T(8,128)}, u32[]{:S(2)}) copy-start(f32[256,256]{1,0:T(8,128)} %param.32) | copy-start | bytes 786436
  1510.5 151.4 %copy-start.35 = (bf16[2048,256]{1,0:T(8,128)(2,1)S(1)}, bf16[2048,256]{1,0:T(8,128)(2,1)}, u32[]{:S(2)}) copy-start(bf16[2048,256]{1,0:T(8,128)(2,1)} %param.28) | copy-start | bytes 3145732
  1517.3 179.0 %copy-start.75 = (bf16[2,256]{1,0:T(2,128)(2,1)S(1)}, bf16[2,256]{1,0:T(2,128)(2,1)}, u32[]{:S(2)}) copy-start(bf16[2,256]{1,0:T(2,128)(2,1)} %param.29) | copy-start | bytes 3076
  1517.3 179.0 %copy-start.76 = (f32[2,256]{1,0:T(2,128)S(1)}, f32[2,256]{1,0:T(2,128)}, u32[]{:S(2)}) copy-start(f32[2,256]{1,0:T(2,128)} %param.41) | copy-start | bytes 6148
  1517.3 179.0 %copy-start.77 = (f32[2,256]{1,0:T(2,128)S(1)}, f32[2,256]{1,0:T(2,128)}, u32[]{:S(2)}) copy-start(f32[2,256]{1,0:T(2,128)} %param.40) | copy-start | bytes 6148
  1517.3 504.9 %copy-start.23 = (bf16[2,256,2048]{2,1,0:T(8,128)(2,1)S(1)}, bf16[2,256,2048]{2,1,0:T(8,128)(2,1)}, u32[]{:S(2)}) copy-start(bf16[2,256,2048]{2,1,0:T(8,128)(2,1)} %param.27) | copy-start | bytes 6291460
  1696.3 334.7 %copy-start.74 = (f32[2,256]{1,0:T(2,128)}, f32[2,256]{1,0:T(2,128)S(1)}, u32[]{:S(2)}) copy-start(f32[2,256]{1,0:T(2,128)S(1)} %copy.214) | copy-start | bytes 6148
  (60 other events, 348.2 us)
Sparse Core Ops, SparseCore 0:
  9.6 24.7 all-gather.7
  36.1 28.7 all-gather.11
  67.0 30.3 all-gather.19
  99.4 29.8 all-gather.9
  130.8 29.8 all-gather.13
  169.2 171.6 all-reduce.10
  342.6 151.7 all-gather.15
  496.1 80.6 all-gather.17
  643.8 170.7 all-reduce.8
  884.9 50.6 reduce-scatter.10
  938.0 50.0 reduce-scatter.12
  1039.3 310.7 all-reduce.6
  1353.1 51.0 reduce-scatter.14
  1407.0 48.1 reduce-scatter.18
  1458.0 33.9 reduce-scatter.16
  1494.8 166.9 reduce-scatter.22
  1664.7 30.5 reduce-scatter.24
  1698.2 323.9 reduce-scatter.20
where the time goes:
time: 2050 us; the launch traced here: 2040 us
  waiting for transfers between devices  1410 us (69%)
  matrix products  399 us (19%)
  other arithmetic  135 us (7%)
  local copies, waits for them, and re-layouts  60.7 us (3%)
    reduce_scatter x1, waiting for transfers between devices, per_device(): lax.psum_scatter(sum_gateup, 'dp', scatter_dimension=1, tiled=True)  325 us
    psum x1, waiting for transfers between devices, per_device(): lax.psum(jnp.dot(hidden, full_down, preferred_element_type=jnp.float32),...  227 us
    psum x1, waiting for transfers between devices, per_device(): d_mixed = lax.psum(d_mixed_part, 'tp')  171 us
    psum x1, waiting for transfers between devices, per_device(): lax.psum(jnp.dot(attended, full_output, preferred_element_type=jnp.float3...  170 us
    reduce_scatter x1, waiting for transfers between devices, per_device(): lax.psum_scatter(sum_down, 'dp', scatter_dimension=1, tiled=True)  145 us
    all_gather x1, waiting for transfers between devices, per_device(): lax.all_gather(w_gateup, 'dp', axis=1, tiled=True)  143 us
    dot_general x2, matrix products, per_device(): jnp.einsum('skgqt,stkd->sqkgd', d_scores_low, key_heads, preferred_elemen...  56 us
    all_gather x1, waiting for transfers between devices, per_device(): lax.all_gather(w_down, 'dp', axis=1, tiled=True)  54 us
  transfers between devices with their start and end apart: 18, of which 16 were waited for; matrix products, arithmetic and copies ran while one was open for 20% of the time, Pallas kernels for 0%

commit v1 on v0

v1 whole, which is shorter than its diff:
```python
import functools

import jax
import jax.numpy as jnp
from jax import lax
from jax.experimental import pallas as pl
from jax.experimental.pallas import tpu as pltpu
from jax.sharding import PartitionSpec as P

HD = 64
CH = 64
SEQS = 4
MICRO = 2
STEP = 5
CHUNKS = 2

norm_eps = 1e-05
rope_base = 500000.0
beta_one = 0.9
beta_two = 0.95
learn_rate = 0.01
weight_decay = 0.1
adam_eps = 1e-08
masked_score = -1e30

F32 = jnp.float32
BF16 = jnp.bfloat16
VMEM_LIMIT = 60 * 1024 * 1024


def lane_tables(positions, kinds):
    half_size = HD // 2
    frequencies = rope_base ** (-(jnp.arange(half_size, dtype=F32) * 2.0 / HD))
    angles = positions.astype(F32)[:, None] * frequencies[None, :]
    cos_half, sin_half = jnp.cos(angles), jnp.sin(angles)
    cos_head = jnp.concatenate([cos_half, cos_half], axis=-1)
    sin_head = jnp.concatenate([-sin_half, sin_half], axis=-1)
    ones, zeros = jnp.ones_like(cos_head), jnp.zeros_like(cos_head)
    cos_all, sin_all = [], []
    for kind in kinds:
        cos_all.append(cos_head if kind else ones)
        sin_all.append(sin_head if kind else zeros)
    return jnp.concatenate(cos_all, axis=-1), jnp.concatenate(sin_all, axis=-1)


def half_turn(values):
    width = values.shape[-1]
    axis = values.ndim - 1
    lane = lax.broadcasted_iota(jnp.int32, values.shape, axis)
    ahead = pltpu.roll(values, width - HD // 2, axis)
    behind = pltpu.roll(values, HD // 2, axis)
    return jnp.where(lane % HD < HD // 2, ahead, behind)


def mean_square_scale(values):
    return lax.rsqrt(jnp.mean(values * values, axis=-1, keepdims=True) + norm_eps)


def project_kernel(x_ref, gain_ref, w_ref, cos_ref, sin_ref, a_ref, qkv_ref):
    x = x_ref[...].astype(F32)
    a = (x * mean_square_scale(x) * gain_ref[...].astype(F32)).astype(BF16)
    a_ref[...] = a
    t = jnp.dot(a, w_ref[...], preferred_element_type=F32)
    qkv_ref[...] = (t * cos_ref[...] + half_turn(t) * sin_ref[...]).astype(BF16)


def project(x, gain, weight, cos_t, sin_t):
    rows, depth = x.shape
    width = weight.shape[1]
    block = cos_t.shape[0]
    return pl.pallas_call(
        project_kernel,
        grid=(rows // block,),
        in_specs=[
            pl.BlockSpec((block, depth), lambda i: (i, 0)),
            pl.BlockSpec((1, depth), lambda i: (0, 0)),
            pl.BlockSpec((depth, width), lambda i: (0, 0)),
            pl.BlockSpec((block, width), lambda i: (0, 0)),
            pl.BlockSpec((block, width), lambda i: (0, 0)),
        ],
        out_specs=[
            pl.BlockSpec((block, depth), lambda i: (i, 0)),
            pl.BlockSpec((block, width), lambda i: (i, 0)),
        ],
        out_shape=[
            jax.ShapeDtypeStruct((rows, depth), BF16),
            jax.ShapeDtypeStruct((rows, width), BF16),
        ],
        compiler_params=pltpu.CompilerParams(vmem_limit_bytes=VMEM_LIMIT),
        cost_estimate=pl.CostEstimate(
            flops=2 * rows * depth * width, bytes_accessed=4 * rows * depth, transcendentals=0
        ),
        name="project",
    )(x, gain, weight, cos_t, sin_t)


def stack_heads(block, group, upper):
    lane = lax.broadcasted_iota(jnp.int32, (block.shape[0], 2 * HD), 1)
    keep = (lane >= HD) if upper else (lane < HD)
    parts = []
    for head in range(group):
        pair = block[:, (head // 2) * 2 * HD : (head // 2 + 1) * 2 * HD].astype(F32)
        if (head % 2 == 1) != upper:
            pair = pltpu.roll(pair, HD, 1)
        parts.append(jnp.where(keep, pair, 0.0).astype(BF16))
    return jnp.concatenate(parts, axis=0)


def unstack_heads(stacked, group, upper):
    rows = stacked.shape[0] // group
    lane = lax.broadcasted_iota(jnp.int32, (rows, 2 * HD), 1)
    pairs = []
    for pair in range(group // 2):
        even = stacked[(2 * pair) * rows : (2 * pair + 1) * rows]
        odd = stacked[(2 * pair + 1) * rows : (2 * pair + 2) * rows]
        if upper:
            even = pltpu.roll(even, HD, 1)
        else:
            odd = pltpu.roll(odd, HD, 1)
        pairs.append(jnp.where(lane < HD, even, odd))
    return jnp.concatenate(pairs, axis=1)


def scores_and_probs(q_pad, keys, qpos, kpos, group):
    scores = (
        lax.dot_general(q_pad, keys, (((1,), (1,)), ((), ())), preferred_element_type=F32)
        * HD ** (-0.5)
    )
    rows = qpos.shape[0]
    blocked = kpos > qpos
    masked = [
        jnp.where(blocked, masked_score, scores[h * rows : (h + 1) * rows]) for h in range(group)
    ]
    scores = jnp.concatenate(masked, axis=0)
    exponent = jnp.exp(scores - jnp.max(scores, axis=-1, keepdims=True))
    return exponent * (1.0 / jnp.sum(exponent, axis=-1, keepdims=True))


def attend_kernel(group, qpos_ref, kpos_ref, q_ref, kv_ref, o_ref):
    keyvals = kv_ref[...].reshape(-1, 2 * HD)
    q_pad = stack_heads(q_ref[...].reshape(-1, group * HD), group, False)
    probs = scores_and_probs(q_pad, keyvals, qpos_ref[...], kpos_ref[...], group)
    out = jnp.dot(probs.astype(BF16), keyvals, preferred_element_type=F32)
    o_ref[...] = unstack_heads(out, group, True).astype(BF16).reshape(o_ref.shape)


def attend_back_kernel(
    group, qpos_ref, kpos_ref, cos_ref, sin_ref, q_ref, do_ref, kv_ref, dq_ref, dkv_ref
):
    keyvals = kv_ref[...].reshape(-1, 2 * HD)
    q_pad = stack_heads(q_ref[...].reshape(-1, group * HD), group, False)
    do_pad = stack_heads(do_ref[...].reshape(-1, group * HD), group, True)
    probs = scores_and_probs(q_pad, keyvals, qpos_ref[...], kpos_ref[...], group)
    d_probs = lax.dot_general(
        do_pad, keyvals, (((1,), (1,)), ((), ())), preferred_element_type=F32
    )
    d_scores = probs * (d_probs - jnp.sum(d_probs * probs, axis=-1, keepdims=True))
    ds_low = d_scores.astype(BF16) * HD ** (-0.5)
    dq = jnp.dot(ds_low, keyvals, preferred_element_type=F32)
    dq = unstack_heads(dq, group, False)
    dq = dq * cos_ref[...] + half_turn(dq * sin_ref[...])
    dq_ref[...] = dq.astype(BF16).reshape(dq_ref.shape)
    contract = (((0,), (0,)), ((), ()))
    d_keyvals = lax.dot_general(
        ds_low, q_pad, contract, preferred_element_type=F32
    ) + lax.dot_general(probs.astype(BF16), do_pad, contract, preferred_element_type=F32)
    dkv_ref[...] = d_keyvals.astype(BF16).reshape(dkv_ref.shape)


def attention_specs(qkv_heads, n_dp, span_rows, group):
    q_spec = pl.BlockSpec((1, 1, span_rows, group * HD), lambda m, s, h: (m, s, 0, h))
    kv_spec = pl.BlockSpec(
        (n_dp, 1, 1, span_rows, 2 * HD), lambda m, s, h: (0, m, s, 0, h)
    )
    pos_q = pl.BlockSpec((span_rows, 1), lambda m, s, h: (0, 0))
    pos_k = pl.BlockSpec((1, n_dp * span_rows), lambda m, s, h: (0, 0))
    return q_spec, kv_spec, pos_q, pos_k


def attend(qpos, kpos, q, kv, group):
    micro, seqs, span_rows, width = q.shape
    n_dp, heads = kv.shape[0], width // (group * HD)
    q_spec, kv_spec, pos_q, pos_k = attention_specs(heads, n_dp, span_rows, group)
    return pl.pallas_call(
        functools.partial(attend_kernel, group),
        grid=(micro, seqs, heads),
        in_specs=[pos_q, pos_k, q_spec, kv_spec],
        out_specs=q_spec,
        out_shape=jax.ShapeDtypeStruct(q.shape, BF16),
        compiler_params=pltpu.CompilerParams(vmem_limit_bytes=VMEM_LIMIT),
        cost_estimate=pl.CostEstimate(
            flops=16 * micro * seqs * span_rows * width * n_dp * span_rows,
            bytes_accessed=4 * q.size + 2 * kv.size,
            transcendentals=0,
        ),
        name="attend",
    )(qpos, kpos, q, kv)


def attend_back(qpos, kpos, cos_q, sin_q, q, d_out, kv, group):
    micro, seqs, span_rows, width = q.shape
    n_dp, heads = kv.shape[0], width // (group * HD)
    q_spec, kv_spec, pos_q, pos_k = attention_specs(heads, n_dp, span_rows, group)
    table = pl.BlockSpec((span_rows, group * HD), lambda m, s, h: (0, 0))
    return pl.pallas_call(
        functools.partial(attend_back_kernel, group),
        grid=(micro, seqs, heads),
        in_specs=[pos_q, pos_k, table, table, q_spec, q_spec, kv_spec],
        out_specs=[q_spec, kv_spec],
        out_shape=[
            jax.ShapeDtypeStruct(q.shape, BF16),
            jax.ShapeDtypeStruct(kv.shape, BF16),
        ],
        compiler_params=pltpu.CompilerParams(vmem_limit_bytes=VMEM_LIMIT),
        cost_estimate=pl.CostEstimate(
            flops=40 * micro * seqs * span_rows * width * n_dp * span_rows,
            bytes_accessed=6 * q.size + 4 * kv.size,
            transcendentals=0,
        ),
        name="attend_back",
    )(qpos, kpos, cos_q, sin_q, q, d_out, kv)


def norm_back(d_normed, normed, scale):
    return scale * (d_normed - normed * jnp.mean(d_normed * normed, axis=-1, keepdims=True))


def adam_update(gradient, old_mean, square, weight, decay_factor):
    moment = beta_one * old_mean + (1.0 - beta_one) * gradient
    spread = beta_two * square + (1.0 - beta_two) * gradient * gradient
    change = -learn_rate * (
        moment / (1.0 - beta_one**STEP) / (jnp.sqrt(spread / (1.0 - beta_two**STEP)) + adam_eps)
        + decay_factor * weight
    )
    return (moment, spread, change)


def dot(left, right):
    return jnp.dot(left, right, preferred_element_type=F32)


def dot_nt(left, right):
    return lax.dot_general(left, right, (((1,), (1,)), ((), ())), preferred_element_type=F32)


def dot_tn(left, right):
    return lax.dot_general(left, right, (((0,), (0,)), ((), ())), preferred_element_type=F32)


def per_device(
    n_dp,
    n_tp,
    tokens,
    cotangent,
    span_order,
    w_query,
    w_keyval,
    w_output,
    w_gateup,
    w_down,
    norm_gains,
    mean_query,
    square_query,
    mean_keyval,
    square_keyval,
    mean_output,
    square_output,
    mean_gateup,
    square_gateup,
    mean_down,
    square_down,
    mean_gains,
    square_gains,
):
    depth = tokens.shape[1]
    span_rows = 2 * CH
    block_rows = SEQS * span_rows // n_tp
    parts = span_rows // min(span_rows, block_rows)
    q_width = w_query.shape[1]
    kv_width = w_keyval.shape[1]
    hidden_width = w_down.shape[0]
    own_depth = w_query.shape[0]
    group = q_width // HD // (kv_width // (2 * HD))
    device = lax.axis_index("dp")
    rank = lax.axis_index("tp")

    def swap(value, k):
        return lax.ppermute(value, "tp", [(i, i ^ k) for i in range(n_tp)])

    def reorder(value):
        return jnp.concatenate(
            [lax.dynamic_slice_in_dim(value, rank ^ k, 1, axis=1) for k in range(n_tp)], axis=1
        )

    def gather_rows(own):
        return jnp.stack([own] + [swap(own, k) for k in range(1, n_tp)], axis=1)

    def exchange(blocks):
        return [blocks[0]] + [swap(blocks[k], k) for k in range(1, n_tp)]

    def scatter_sum(partial):
        got = exchange([partial[:, k].astype(BF16) for k in range(n_tp)])
        total = partial[:, 0].astype(F32)
        for k in range(1, n_tp):
            total = total + got[k].astype(F32)
        return total

    qkv_full = lax.all_gather(
        jnp.concatenate([w_query, w_keyval], axis=1), "dp", axis=0, tiled=True
    )
    gains_full = lax.all_gather(norm_gains, "dp", axis=1, tiled=True)
    out_t_full = lax.all_gather(w_output.T, "dp", axis=0, tiled=True)

    offsets = jnp.arange(CH, dtype=jnp.int32)
    all_pos = (span_order[:, None] * CH + offsets[None, :]).reshape(n_dp, parts, -1)
    all_pos = jnp.stack([all_pos[:, (rank % parts) ^ p] for p in range(parts)], axis=1)
    own_pos = lax.dynamic_slice_in_dim(all_pos, device, 1).reshape(-1)
    all_pos = all_pos.reshape(-1)
    qpos, kpos = own_pos[:, None], all_pos[None, :]
    kv_kinds = [True, False] * (kv_width // (2 * HD))
    cos_t, sin_t = lane_tables(own_pos, [True] * (q_width // HD) + kv_kinds)

    x = reorder(tokens.reshape(MICRO, n_tp, block_rows, depth))
    seed = reorder(cotangent.reshape(MICRO, n_tp, block_rows, depth))
    rows = MICRO * SEQS * span_rows
    gain_one, gain_two = gains_full[0:1], gains_full[1:2]
    attn_in, qkv = project(x.reshape(rows, depth), gain_one, qkv_full, cos_t, sin_t)
    qkv = qkv.reshape(MICRO, SEQS, span_rows, q_width + kv_width)
    q, kv = qkv[..., :q_width], qkv[..., q_width:]
    kv_all = lax.all_gather(kv, "dp", axis=0, tiled=False)

    chunk = hidden_width // CHUNKS
    w_down_t = w_down.T
    mlp_full = []
    for c in range(CHUNKS):
        cols = slice(c * chunk, (c + 1) * chunk)
        shard = jnp.concatenate(
            [w_gateup[0][:, cols], w_gateup[1][:, cols], w_down_t[:, cols]], axis=1
        )
        mlp_full.append(lax.all_gather(shard, "dp", axis=0, tiled=True))

    attended = attend(qpos, kpos, q, kv_all, group)
    by_block = (MICRO, n_tp, block_rows, -1)

    out_t_all = [out_t_full] + [swap(out_t_full, k) for k in range(1, n_tp)]
    attended_blocks = attended.reshape(by_block)
    heads_in = exchange([attended_blocks[:, k] for k in range(n_tp)])
    own_rows = MICRO * block_rows
    x_own = x[:, 0].reshape(own_rows, depth).astype(F32)
    seed_own = seed[:, 0].reshape(own_rows, depth).astype(F32)
    middle = x_own
    for k in range(n_tp):
        middle = middle + dot_nt(heads_in[k].reshape(own_rows, q_width), out_t_all[k])
    scale_two = mean_square_scale(middle)
    normed_two = middle * scale_two
    u_own = (normed_two * gain_two.astype(F32)).astype(BF16)
    u = gather_rows(u_own.reshape(MICRO, block_rows, depth)).reshape(rows, depth)
    g = seed.reshape(rows, depth)

    y_part = None
    du_part = None
    mlp_grads = []
    for c in range(CHUNKS):
        weights = mlp_full[c]
        gate_proj = dot(u, weights[:, :chunk])
        up_proj = dot(u, weights[:, chunk : 2 * chunk])
        d_hidden = dot(g, weights[:, 2 * chunk :])
        sigmoid_gate = jax.nn.sigmoid(gate_proj)
        silu_gate = gate_proj * sigmoid_gate
        hidden = (silu_gate * up_proj).astype(BF16)
        d_gate = (
            d_hidden * up_proj * sigmoid_gate * (1.0 + gate_proj * (1.0 - sigmoid_gate))
        ).astype(BF16)
        d_up = (d_hidden * silu_gate).astype(BF16)
        d_both = jnp.concatenate([d_gate, d_up], axis=1)
        du_term = dot_nt(d_both, weights[:, : 2 * chunk])
        y_term = dot_nt(hidden, weights[:, 2 * chunk :])
        du_part = du_term if du_part is None else du_part + du_term
        y_part = y_term if y_part is None else y_part + y_term
        grads = jnp.concatenate(
            [dot_tn(u, d_both).astype(BF16), dot_tn(g, hidden).astype(BF16)], axis=1
        )
        mlp_grads.append(lax.psum_scatter(grads, "dp", scatter_dimension=0, tiled=True))

    d_mixed = scatter_sum(du_part.reshape(by_block)).reshape(own_rows, depth)
    gain_grad_two = jnp.sum(d_mixed * normed_two, axis=0)
    d_middle = seed_own + norm_back(d_mixed * gain_two.astype(F32), normed_two, scale_two)
    d_mid_low = d_middle.astype(BF16)
    do_rows = [
        dot(d_mid_low, out_t_all[k]).astype(BF16).reshape(MICRO, block_rows, q_width)
        for k in range(n_tp)
    ]
    d_attend = jnp.stack(exchange(do_rows), axis=1).reshape(q.shape)
    cos_q, sin_q = cos_t[:, : group * HD], sin_t[:, : group * HD]
    d_query_low, d_kv_part = attend_back(qpos, kpos, cos_q, sin_q, q, d_attend, kv_all, group)
    own_grad = lax.psum_scatter(d_kv_part, "dp", scatter_dimension=0, tiled=False).astype(F32)

    block_own = middle + scatter_sum(y_part.reshape(by_block)).reshape(own_rows, depth)
    out_rows = gather_rows(block_own.astype(BF16).reshape(MICRO, block_rows, depth))
    block_output = reorder(out_rows).reshape(rows, depth)
    d_mid_rows = gather_rows(d_mid_low.reshape(MICRO, block_rows, depth)).reshape(rows, depth)
    out_grad_t = dot_tn(d_mid_rows, attended.reshape(rows, q_width)).astype(BF16)

    cos_k, sin_k = cos_t[:, q_width:], sin_t[:, q_width:]
    scaled = own_grad * sin_k
    lane = jnp.arange(kv_width)
    turned = jnp.where(
        lane % HD < HD // 2,
        jnp.roll(scaled, -(HD // 2), axis=-1),
        jnp.roll(scaled, HD // 2, axis=-1),
    )
    d_kv_low = (own_grad * cos_k + turned).astype(BF16)
    d_qkv = jnp.concatenate([d_query_low, d_kv_low], axis=-1)
    qkv_all = [qkv_full] + [swap(qkv_full, k) for k in range(1, n_tp)]
    d_blocks = d_qkv.reshape(by_block)
    d_heads = exchange([d_blocks[:, k] for k in range(n_tp)])
    d_act = None
    for k in range(n_tp):
        term = dot_nt(d_heads[k].reshape(own_rows, q_width + kv_width), qkv_all[k])
        d_act = term if d_act is None else d_act + term
    scale_one = mean_square_scale(x_own)
    normed_one = x_own * scale_one
    gain_grad_one = jnp.sum(d_act * normed_one, axis=0)
    tokens_own = d_middle + norm_back(d_act * gain_one.astype(F32), normed_one, scale_one)
    tokens_rows = gather_rows(tokens_own.astype(BF16).reshape(MICRO, block_rows, depth))
    grad_tokens = reorder(tokens_rows).reshape(rows, depth).astype(F32)

    qkv_grad = dot_tn(attn_in, d_qkv.reshape(rows, q_width + kv_width)).astype(BF16)
    gain_cols = jnp.stack([gain_grad_one, gain_grad_two], axis=1)
    gain_cols = jnp.pad(gain_cols, ((0, 0), (0, 126))).astype(BF16)
    attn_grads = lax.psum_scatter(
        jnp.concatenate([qkv_grad, out_grad_t, gain_cols], axis=1),
        "dp",
        scatter_dimension=0,
        tiled=True,
    )
    gain_part = attn_grads[:, 2 * q_width + kv_width :]
    gain_sum = gain_part.astype(F32)
    for k in range(1, n_tp):
        gain_sum = gain_sum + swap(gain_part, k).astype(F32)

    grad_query = attn_grads[:, :q_width].astype(F32)
    grad_keyval = attn_grads[:, q_width : q_width + kv_width].astype(F32)
    grad_output = attn_grads[:, q_width + kv_width : 2 * q_width + kv_width].astype(F32).T
    grad_gains = gain_sum[:, :2].T
    grad_gateup = jnp.stack(
        [
            jnp.concatenate([part[:, i * chunk : (i + 1) * chunk] for part in mlp_grads], axis=1)
            for i in range(2)
        ]
    ).astype(F32)
    grad_down = jnp.concatenate([part[:, 2 * chunk :] for part in mlp_grads], axis=1).astype(F32).T

    def with_update(gradient, old_mean, square, weight, decay):
        return (gradient,) + adam_update(gradient, old_mean, square, weight.astype(F32), decay)

    return (
        (block_output, grad_tokens)
        + with_update(grad_query, mean_query, square_query, w_query, weight_decay)
        + with_update(grad_keyval, mean_keyval, square_keyval, w_keyval, weight_decay)
        + with_update(grad_output, mean_output, square_output, w_output, weight_decay)
        + with_update(grad_gateup, mean_gateup, square_gateup, w_gateup, weight_decay)
        + with_update(grad_down, mean_down, square_down, w_down, weight_decay)
        + with_update(grad_gains, mean_gains, square_gains, norm_gains, 0.0)
    )


def solution(mesh):
    rows_first = P("dp", "tp")
    cols_last = P("tp", "dp")
    stacked = P(None, "dp", "tp")
    gains = P(None, "dp")
    token_rows = P("dp", None)
    placed = (
        (token_rows, token_rows, P())
        + (rows_first, rows_first, cols_last, stacked, cols_last, gains)
        + (rows_first,) * 4
        + (cols_last,) * 2
        + (stacked,) * 2
        + (cols_last,) * 2
        + (gains,) * 2
    )
    results = (
        (token_rows, token_rows)
        + (rows_first,) * 8
        + (cols_last,) * 4
        + (stacked,) * 4
        + (cols_last,) * 4
        + (gains,) * 4
    )
    return jax.shard_map(
        functools.partial(per_device, mesh.shape["dp"], mesh.shape["tp"]),
        mesh=mesh,
        in_specs=placed,
        out_specs=results,
        check_vma=False,
    )
```

time: 2050 us -> 1140 us (0.56)
  waiting for transfers between devices: 1410 us -> 633 us
  matrix products: 399 us -> 176 us
  Pallas kernels: 0 us -> 77.4 us
  other arithmetic: 135 us -> 91.3 us
  starting transfers between devices: 1.75 us -> 40.2 us
  local copies, waits for them, and re-layouts: 60.7 us -> 86.6 us
    psum x3 -> x0, waiting for transfers between devices: 568 us -> none  [the longest x1 227 us: per_device(): lax.psum(jnp.dot(hidden, full_down, preferred_element_type=jnp.float32),...]
    reduce_scatter x7 -> x4, waiting for transfers between devices: 565 us -> 69.6 us  [the longest x2 69.5 us: per_device(): lax.psum_scatter(grads, 'dp', scatter_dimension=0, tiled=True)]
    ppermute x0 -> x36, waiting for transfers between devices: none -> 394 us  [swap(): return lax.ppermute(value, 'tp', [(i, i ^ k) for i in range(n_tp)])]
    dot_general x48 -> x28, matrix products: 399 us -> 176 us  [the longest x10 69.5 us: dot(): return jnp.dot(left, right, preferred_element_type=F32)]
    all_gather x7 -> x5, waiting for transfers between devices: 249 us -> 169 us  [the longest x2 102 us: per_device(): mlp_full.append(lax.all_gather(shard, 'dp', axis=0, tiled=True))]
    pallas_call x0 -> x3, Pallas kernels: none -> 77.4 us  [the longest x1 37.2 us: attend_back(): pl.pallas_call(functools.partial(attend_back_kernel, group), grid=(micro,...]
    ppermute x0 -> x36, starting transfers between devices: none -> 39.1 us  [swap(): return lax.ppermute(value, 'tp', [(i, i ^ k) for i in range(n_tp)])]
    add x8 -> x3, other arithmetic: 42.7 us -> 3.85 us  [the longest x2 3.78 us: scatter_sum(): total = total + got[k].astype(F32)]
  transfers between devices with their start and end apart: 18 -> 45, of which waited for: 16 -> 25; matrix products, arithmetic and copies ran while one was open for 20% -> 19% of each run, Pallas kernels for 0% -> 4%
where the time goes in v1:
time: 1140 us; the launch traced here: 1130 us
  waiting for transfers between devices  633 us (56%)
  matrix products  176 us (15%)
  other arithmetic  91.3 us (8%)
  local copies, waits for them, and re-layouts  86.6 us (8%)
  Pallas kernels  77.4 us (7%)
  starting transfers between devices  40.2 us (4%)
  between operations  15.3 us (1%)
  blocking collectives  13.5 us (1%)
    ppermute x36, waiting for transfers between devices, swap(): return lax.ppermute(value, 'tp', [(i, i ^ k) for i in range(n_tp)])  394 us
    all_gather x2, waiting for transfers between devices, per_device(): mlp_full.append(lax.all_gather(shard, 'dp', axis=0, tiled=True))  102 us
    reduce_scatter x2, waiting for transfers between devices, per_device(): lax.psum_scatter(grads, 'dp', scatter_dimension=0, tiled=True)  69.5 us
    dot_general x10, matrix products, dot(): return jnp.dot(left, right, preferred_element_type=F32)  69.5 us
    dot_general x12, matrix products, dot_nt(): lax.dot_general(left, right, (((1,), (1,)), ((), ())), preferred_element_...  60.6 us
    unnamed x147, local copies, waits for them, and re-layouts  53.2 us
    dot_general x6, matrix products, dot_tn(): lax.dot_general(left, right, (((0,), (0,)), ((), ())), preferred_element_...  45.8 us
    all_gather x1, waiting for transfers between devices, per_device(): kv_all = lax.all_gather(kv, 'dp', axis=0, tiled=False)  39.4 us
  transfers between devices with their start and end apart: 45, of which 25 were waited for; matrix products, arithmetic and copies ran while one was open for 19% of the time, Pallas kernels for 4%

profile of v1, /device:TPU:0, one launch (start us, length us, event | category | flops | bytes accessed | tf_op | source)
XLA Modules:
  0.0 1133.2 jit_solution(12694923401797213507)
XLA Ops:
  13.4 13.5 %all_gather.21 = bf16[2,2048]{1,0:T(2,128)(2,1)S(1)} all-gather(bf16[2,256]{1,0:T(2,128)(2,1)S(1)} %copy-done.50), channel_id=1, replica_groups=mesh['dp'=8,'tp'=4] {'dp'}, dimensions={1}, use_global_device_ids=true | all-gather | bytes 9216 | tf_op jit(solution)/shard_map/all_gather | solution.py:311
  34.6 16.7 %all-gather.7.cloned.1.call-done.w_ref = bf16[2048,768]{1,0:T(8,128)(2,1)} async-done(((bf16[256,768]{1,0:T(8,128)(2,1)}), bf16[2048,768]{1,0:T(8,128)(2,1)}) %all-gather.7.cloned.1.call-update) | async-done | bytes 3145744 | tf_op jit(solution)/shard_map/all_gather | solution.py:308
  51.3 11.0 project.1
  73.1 10.9 all-gather.9.cloned.1.call-done
  91.3 39.4 %all-gather.15.cloned.1.call-done = bf16[16,4,128,256]{3,2,1,0:T(8,128)(2,1)} async-done(((bf16[2,4,128,256]{3,2,1,0:T(8,128)(2,1)}), bf16[16,4,128,256]{3,2,1,0:T(8,128)(2,1)}) %all-gather.15.cloned.1.call-update) | async-done | bytes 4194320 | tf_op jit(solution)/shard_map/all_gather | solution.py:330
  130.7 29.2 %attend.1 = bf16[2,4,128,512]{3,2,1,0:T(8,128)(2,1)} custom-call(s32[128,1]{1,0:T(8,128)} %copy.124.qpos_ref, s32[1,1024]{1,0:T(1,128)} %add.287.kpos_ref, bf16[2,4,128,512]{3,2,1,0:T(8,128)(2,1)} %slice.227.q_ref, bf16[8,2,4,128,256]{4,3,2,1,0:T(8,128)(2,1)} %bitcast.260), custom_call_target="tpu_custom_call" | custom-call | flops 8589934592 | bytes 6291456 | tf_op jit(solution)/shard_map/attend/pallas_call | solution.py:184
  164.9 13.3 %collective-permute-done.3 = bf16[2048,512]{0,1:T(8,128)(2,1)} collective-permute-done((bf16[2048,512]{0,1:T(8,128)(2,1)}, bf16[2048,512]{0,1:T(8,128)(2,1)}, u32[]{:S(2)}, u32[]{:S(2)}) %collective-permute-start.3) | collective-permute-done | bytes 2097184 | tf_op jit(solution)/shard_map/ppermute | solution.py:288
  178.2 10.0 collective-permute-done.2
  202.2 19.7 %collective-permute-done.6 = bf16[2,128,2048]{2,1,0:T(8,128)(2,1)S(1)} collective-permute-done((bf16[2,128,2048]{2,1,0:T(8,128)(2,1)S(1)}, bf16[2,128,2048]{2,1,0:T(8,128)(2,1)S(1)}, u32[]{:S(2)}, u32[]{:S(2)}) %collective-permute-start.6) | collective-permute-done | bytes 1048608 | tf_op jit(solution)/shard_map/ppermute | solution.py:288
  221.9 21.1 %collective-permute-done.8 = bf16[2,128,2048]{2,1,0:T(8,128)(2,1)S(1)} collective-permute-done((bf16[2,128,2048]{2,1,0:T(8,128)(2,1)S(1)}, bf16[2,128,2048]{2,1,0:T(8,128)(2,1)S(1)}, u32[]{:S(2)}, u32[]{:S(2)}) %collective-permute-start.8) | collective-permute-done | bytes 1048608 | tf_op jit(solution)/shard_map/ppermute | solution.py:288
  250.3 10.1 fusion.12
  260.4 8.6 fusion.29
  269.0 97.0 %all-gather.13.cloned.1.call-done = bf16[2048,3072]{0,1:T(8,128)(2,1)} async-done(((bf16[256,3072]{0,1:T(8,128)(2,1)}), bf16[2048,3072]{0,1:T(8,128)(2,1)}) %all-gather.13.cloned.1.call-update) | async-done | bytes 12582928 | tf_op jit(solution)/shard_map/all_gather | solution.py:340
  366.0 10.1 fusion.8
  376.1 8.5 fusion.26
  384.6 10.3 multiply_convert_fusion.3
  394.9 11.8 %multiply_convert_fusion.1 = (bf16[1024,1024]{0,1:T(8,128)(2,1)S(1)}, bf16[1024,1024]{0,1:T(8,128)(2,1)S(1)}, bf16[1024,1024]{0,1:T(8,128)(2,1)}) fusion(f32[1024,1024]{0,1:T(8,128)} %fusion.26, f32[1024,1024]{0,1:T(8,128)} %fusion.8, bf16[1024,2048]{1,0:T(8,128)(2,1)S(1)} %bitcast.219, bf16[2048,3072]{0,1:T(8,128)(2,1)} %all-gather.13.cloned.1.call-done), kind=kOutput, calls=%fused_computation.41 | convolution fusion | flops 4310695936 | bytes 23068672 | tf_op jit(solution)/shard_map/dot_general | solution.py:239
  406.8 15.1 %fusion = f32[1024,2048]{1,0:T(8,128)} fusion(bf16[2048,3072]{0,1:T(8,128)(2,1)} %all-gather.13.cloned.1.call-done, bf16[1024,1024]{0,1:T(8,128)(2,1)S(1)} %get-tuple-element.143, bf16[1024,1024]{0,1:T(8,128)(2,1)S(1)} %get-tuple-element.142), kind=kOutput, calls=%fused_computation.2 | convolution fusion | flops 8598323200 | bytes 20971520 | tf_op jit(solution)/shard_map/dot_general | solution.py:243
  421.9 13.5 %fusion.4 = f32[1024,2048]{1,0:T(8,128)S(1)} fusion(f32[1024,2048]{1,0:T(8,128)} %fusion, bf16[2048,3072]{0,1:T(8,128)(2,1)} %all-gather.11.cloned.1.call-done, bf16[1024,1024]{0,1:T(8,128)(2,1)} %get-tuple-element.140, bf16[1024,1024]{0,1:T(8,128)(2,1)S(1)} %get-tuple-element.139), kind=kOutput, calls=%fused_computation.10 | convolution fusion | flops 8600420352 | bytes 29360128 | tf_op jit(solution)/shard_map/dot_general | solution.py:243
  445.7 21.2 %collective-permute-done.15 = bf16[2,128,2048]{2,1,0:T(8,128)(2,1)} collective-permute-done((bf16[2,128,2048]{2,1,0:T(8,128)(2,1)}, bf16[2,128,2048]{2,1,0:T(8,128)(2,1)}, u32[]{:S(2)}, u32[]{:S(2)}) %collective-permute-start.15) | collective-permute-done | bytes 1048608 | tf_op jit(solution)/shard_map/ppermute | solution.py:288
  466.9 23.0 %collective-permute-done.16 = bf16[2,128,2048]{2,1,0:T(8,128)(2,1)} collective-permute-done((bf16[2,128,2048]{2,1,0:T(8,128)(2,1)}, bf16[2,128,2048]{2,1,0:T(8,128)(2,1)}, u32[]{:S(2)}, u32[]{:S(2)}) %collective-permute-start.16) | collective-permute-done | bytes 1048608 | tf_op jit(solution)/shard_map/ppermute | solution.py:288
  509.3 5.8 collective-permute-done.19
  516.2 37.2 %attend_back.1 = (bf16[2,4,128,512]{3,2,1,0:T(8,128)(2,1)}, bf16[8,2,4,128,256]{4,3,2,1,0:T(8,128)(2,1)}) custom-call(s32[128,1]{1,0:T(8,128)} %copy.124.qpos_ref, s32[1,1024]{1,0:T(1,128)} %add.287.kpos_ref, f32[128,256]{1,0:T(8,128)} %concatenate.88.cos_ref, f32[128,256]{1,0:T(8,128)} %concatenate.89.sin_ref, bf16[2,4,128,512]{3,2,1,0:T(8,128)(2,1)} %slice.227.q_ref, ...), custom_call_target="tpu_custom_call" | custom-call | flops 21474836480 | bytes 11534336 | tf_op jit(solution)/shard_map/attend_back/pallas_call | solution.py:205
  559.9 20.2 %collective-permute-done.30 = bf16[2,128,2048]{2,1,0:T(8,128)(2,1)} collective-permute-done((bf16[2,128,2048]{2,1,0:T(8,128)(2,1)}, bf16[2,128,2048]{2,1,0:T(8,128)(2,1)}, u32[]{:S(2)}, u32[]{:S(2)}) %collective-permute-start.30) | collective-permute-done | bytes 1048608 | tf_op jit(solution)/shard_map/ppermute | solution.py:288
  581.0 19.6 %collective-permute-done.31 = bf16[2,128,2048]{2,1,0:T(8,128)(2,1)} collective-permute-done((bf16[2,128,2048]{2,1,0:T(8,128)(2,1)}, bf16[2,128,2048]{2,1,0:T(8,128)(2,1)}, u32[]{:S(2)}, u32[]{:S(2)}) %collective-permute-start.31) | collective-permute-done | bytes 1048608 | tf_op jit(solution)/shard_map/ppermute | solution.py:288
  602.9 6.2 bitcast_convert_fusion
  622.6 47.4 %collective-permute-done.22 = bf16[2048,768]{1,0:T(8,128)(2,1)S(1)} collective-permute-done((bf16[2048,768]{1,0:T(8,128)(2,1)}, bf16[2048,768]{1,0:T(8,128)(2,1)S(1)}, u32[]{:S(2)}, u32[]{:S(2)}) %collective-permute-start.22) | collective-permute-done | bytes 3145760 | tf_op jit(solution)/shard_map/ppermute | solution.py:288
  670.8 74.8 %collective-permute-done.21 = bf16[2,128,768]{2,1,0:T(8,128)(2,1)S(1)} collective-permute-done((bf16[2,128,768]{2,1,0:T(8,128)(2,1)S(1)}, bf16[2,128,768]{2,1,0:T(8,128)(2,1)S(1)}, u32[]{:S(2)}, u32[]{:S(2)}) %collective-permute-start.21) | collective-permute-done | bytes 393248 | tf_op jit(solution)/shard_map/ppermute | solution.py:288
  756.7 6.0 pad_maximum_fusion.2
  763.2 7.5 convolution_convert_fusion.3
  770.7 9.7 convolution_convert_fusion.1
  780.5 14.8 %pad_maximum_fusion = bf16[2048,3072]{0,1:T(8,128)(2,1)} fusion(bf16[2048,1024]{0,1:T(8,128)(2,1)S(1)} %convolution_convert_fusion.3, bf16[2048,2048]{0,1:T(8,128)(2,1)S(1)} %convolution_convert_fusion.1), kind=kLoop, calls=%fused_computation | loop fusion | flops 25165824 | bytes 25165824 | tf_op jit(solution)/shard_map/concatenate | solution.py:380
  795.4 7.5 convolution_convert_fusion.2
  803.0 9.9 convolution_convert_fusion
  812.9 14.8 %pad_maximum_fusion.1 = bf16[2048,3072]{0,1:T(8,128)(2,1)} fusion(bf16[2048,1024]{0,1:T(8,128)(2,1)S(1)} %convolution_convert_fusion.2, bf16[2048,2048]{0,1:T(8,128)(2,1)S(1)} %convolution_convert_fusion), kind=kLoop, calls=%fused_computation.1 | loop fusion | flops 25165824 | bytes 25165824 | tf_op jit(solution)/shard_map/concatenate | solution.py:380
  827.7 7.3 fusion.31
  835.0 6.8 convolution_add_fusion
  845.9 40.7 %collective-permute-done.10 = bf16[2,128,2048]{2,1,0:T(8,128)(2,1)S(1)} collective-permute-done((bf16[2,128,2048]{2,1,0:T(8,128)(2,1)S(1)}, bf16[2,128,2048]{2,1,0:T(8,128)(2,1)S(1)}, u32[]{:S(2)}, u32[]{:S(2)}) %collective-permute-start.10) | collective-permute-done | bytes 1048608 | tf_op jit(solution)/shard_map/ppermute | solution.py:288
  895.6 22.1 %collective-permute-done.12 = bf16[2,128,2048]{2,1,0:T(8,128)(2,1)} collective-permute-done((bf16[2,128,2048]{2,1,0:T(8,128)(2,1)}, bf16[2,128,2048]{2,1,0:T(8,128)(2,1)}, u32[]{:S(2)}, u32[]{:S(2)}) %collective-permute-start.12) | collective-permute-done | bytes 1048608 | tf_op jit(solution)/shard_map/ppermute | solution.py:288
  919.8 5.4 copy.147
  925.2 5.5 copy.148
  932.3 7.8 collective-permute-done.13
  942.6 19.9 %collective-permute-done.27 = bf16[2,128,2048]{2,1,0:T(8,128)(2,1)S(1)} collective-permute-done((bf16[2,128,2048]{2,1,0:T(8,128)(2,1)}, bf16[2,128,2048]{2,1,0:T(8,128)(2,1)S(1)}, u32[]{:S(2)}, u32[]{:S(2)}) %collective-permute-start.27) | collective-permute-done | bytes 1048608 | tf_op jit(solution)/shard_map/ppermute | solution.py:288
  962.5 19.4 %collective-permute-done.28 = bf16[2,128,2048]{2,1,0:T(8,128)(2,1)} collective-permute-done((bf16[2,128,2048]{2,1,0:T(8,128)(2,1)}, bf16[2,128,2048]{2,1,0:T(8,128)(2,1)}, u32[]{:S(2)}, u32[]{:S(2)}) %collective-permute-start.28) | collective-permute-done | bytes 1048608 | tf_op jit(solution)/shard_map/ppermute | solution.py:288
  1015.3 69.5 %reduce-scatter.11.cloned.1.call-done = bf16[256,3072]{0,1:T(8,128)(2,1)} async-done(((bf16[2048,3072]{0,1:T(8,128)(2,1)}), bf16[256,3072]{0,1:T(8,128)(2,1)}) %reduce-scatter.11.cloned.1.call-update) | async-done | bytes 1572880 | tf_op jit(solution)/shard_map/reduce_scatter | solution.py:383
  1092.8 6.5 add_multiply_fusion
  1115.3 5.5 copy.158
  1120.8 5.6 add_multiply_fusion.1
  (313 shorter events, 200.3 us)
Async XLA Ops:
  7.2 44.1 %all-gather.7.cloned.1.call-start = ((), (), s32[]{:S(2)}) async-start(), calls=%async_computation.4 | async-start | bytes 3538944 | tf_op jit(solution)/shard_map/all_gather | solution.py:308
  9.1 74.9 %all-gather.9.cloned.1.call-start = ((), (), s32[]{:S(2)}) async-start(), calls=%async_computation.5 | async-start | bytes 2359296 | tf_op jit(solution)/shard_map/all_gather | solution.py:312
  9.8 120.8 %all-gather.15.cloned.1.call-start = ((), (), s32[]{:S(2)}) async-start(), calls=%async_computation.12 | async-start | bytes 4718592 | tf_op jit(solution)/shard_map/all_gather | solution.py:330
  34.6 459.1 %copy-start.42 = (f32[1,2048]{1,0:T(1,128)}, f32[1,2048]{1,0:T(1,128)S(1)}, u32[]{:S(2)}) copy-start(f32[1,2048]{1,0:T(1,128)S(1)} %get-tuple-element.195) | copy-start | bytes 24580
  64.2 186.1 %all-gather.11.cloned.1.call-start = ((), (), s32[]{:S(2)}) async-start(), calls=%async_computation.6 | async-start | bytes 14155776 | tf_op jit(solution)/shard_map/all_gather | solution.py:340
  70.5 295.5 %all-gather.13.cloned.1.call-start = ((), (), s32[]{:S(2)}) async-start(), calls=%async_computation.7 | async-start | bytes 14155776 | tf_op jit(solution)/shard_map/all_gather | solution.py:340
  72.9 536.3 %reduce-scatter.5.cloned.1.call-start = ((), (), s32[]{:S(2)}) async-start(), calls=%async_computation.8 | async-start | bytes 4718592 | tf_op jit(solution)/shard_map/reduce_scatter | solution.py:396
  84.0 94.1 %collective-permute-start.3 = (bf16[2048,512]{0,1:T(8,128)(2,1)}, bf16[2048,512]{0,1:T(8,128)(2,1)}, u32[]{:S(2)}, u32[]{:S(2)}) collective-permute-start(bf16[2048,512]{0,1:T(8,128)(2,1)} %all-gather.9.cloned.1.call-done), channel_id=1, source_target_pairs={{0,2},{1,3},{2,0},{3,1},{4,6},{5,7},{6,4},{7,5},{8,10},{9,11},{10,... | collective-permute-start | bytes 6291464 | tf_op jit(solution)/shard_map/ppermute | solution.py:288
  84.0 106.5 %collective-permute-start.5 = (bf16[2048,512]{0,1:T(8,128)(2,1)}, bf16[2048,512]{0,1:T(8,128)(2,1)}, u32[]{:S(2)}, u32[]{:S(2)}) collective-permute-start(bf16[2048,512]{0,1:T(8,128)(2,1)} %all-gather.9.cloned.1.call-done), channel_id=1, source_target_pairs={{0,3},{1,2},{2,1},{3,0},{4,7},{5,6},{6,5},{7,4},{8,11},{9,10},{10,... | collective-permute-start | bytes 6291464 | tf_op jit(solution)/shard_map/ppermute | solution.py:288
  85.3 107.5 %collective-permute-start.1 = (bf16[2048,512]{0,1:T(8,128)(2,1)}, bf16[2048,512]{0,1:T(8,128)(2,1)}, u32[]{:S(2)}, u32[]{:S(2)}) collective-permute-start(bf16[2048,512]{0,1:T(8,128)(2,1)} %all-gather.9.cloned.1.call-done), channel_id=1, source_target_pairs={{0,1},{1,0},{2,3},{3,2},{4,5},{5,4},{6,7},{7,6},{8,9},{9,8},{10,11... | collective-permute-start | bytes 6291464 | tf_op jit(solution)/shard_map/ppermute | solution.py:288
  161.2 27.0 %collective-permute-start.2 = (bf16[2,128,512]{2,1,0:T(8,128)(2,1)S(1)}, bf16[2,128,512]{2,1,0:T(8,128)(2,1)S(1)}, u32[]{:S(2)}, u32[]{:S(2)}) collective-permute-start(bf16[2,128,512]{2,1,0:T(8,128)(2,1)S(1)} %get-tuple-element.192), channel_id=1, source_target_pairs={{0,2},{1,3},{2,0},{3,1},{4,6},{5,7},{6,4},{7,5},{8,10},{9,11},{10,... | collective-permute-start | bytes 786440 | tf_op jit(solution)/shard_map/ppermute | solution.py:288
  162.7 27.8 %collective-permute-start.4 = (bf16[2,128,512]{2,1,0:T(8,128)(2,1)S(1)}, bf16[2,128,512]{2,1,0:T(8,128)(2,1)S(1)}, u32[]{:S(2)}, u32[]{:S(2)}) collective-permute-start(bf16[2,128,512]{2,1,0:T(8,128)(2,1)S(1)} %get-tuple-element.191), channel_id=1, source_target_pairs={{0,3},{1,2},{2,1},{3,0},{4,7},{5,6},{6,5},{7,4},{8,11},{9,10},{10,... | collective-permute-start | bytes 786440 | tf_op jit(solution)/shard_map/ppermute | solution.py:288
  178.2 14.7 %collective-permute-start = (bf16[2,128,512]{2,1,0:T(8,128)(2,1)S(1)}, bf16[2,128,512]{2,1,0:T(8,128)(2,1)S(1)}, u32[]{:S(2)}, u32[]{:S(2)}) collective-permute-start(bf16[2,128,512]{2,1,0:T(8,128)(2,1)S(1)} %get-tuple-element.190), channel_id=1, source_target_pairs={{0,1},{1,0},{2,3},{3,2},{4,5},{5,4},{6,7},{7,6},{8,9},{9,8},{10,11... | collective-permute-start | bytes 786440 | tf_op jit(solution)/shard_map/ppermute | solution.py:288
  195.5 298.2 %copy-start = (f32[256,2048]{1,0:T(8,128)}, f32[256,2048]{1,0:T(8,128)S(1)}, u32[]{:S(2)}) copy-start(f32[256,2048]{1,0:T(8,128)S(1)} %get-tuple-element.203) | copy-start | bytes 6291460
  195.5 298.2 %copy-start.45 = (f32[256]{0:T(256)}, f32[256]{0:T(256)S(1)}, u32[]{:S(2)}) copy-start(f32[256]{0:T(256)S(1)} %add_rsqrt_fusion) | copy-start | bytes 3076
  195.8 26.2 %collective-permute-start.6 = (bf16[2,128,2048]{2,1,0:T(8,128)(2,1)S(1)}, bf16[2,128,2048]{2,1,0:T(8,128)(2,1)S(1)}, u32[]{:S(2)}, u32[]{:S(2)}) collective-permute-start(bf16[2,128,2048]{2,1,0:T(8,128)(2,1)S(1)} %bitcast.226), channel_id=1, source_target_pairs={{0,1},{1,0},{2,3},{3,2},{4,5},{5,4},{6,7},{7,6},{8,9},{9,8},{10,11... | collective-permute-start | bytes 3145736 | tf_op jit(solution)/shard_map/ppermute | solution.py:288
  195.9 26.1 %collective-permute-start.7 = (bf16[2,128,2048]{2,1,0:T(8,128)(2,1)S(1)}, bf16[2,128,2048]{2,1,0:T(8,128)(2,1)S(1)}, u32[]{:S(2)}, u32[]{:S(2)}) collective-permute-start(bf16[2,128,2048]{2,1,0:T(8,128)(2,1)S(1)} %bitcast.227), channel_id=1, source_target_pairs={{0,2},{1,3},{2,0},{3,1},{4,6},{5,7},{6,4},{7,5},{8,10},{9,11},{10,... | collective-permute-start | bytes 3145736 | tf_op jit(solution)/shard_map/ppermute | solution.py:288
  197.1 45.9 %collective-permute-start.8 = (bf16[2,128,2048]{2,1,0:T(8,128)(2,1)S(1)}, bf16[2,128,2048]{2,1,0:T(8,128)(2,1)S(1)}, u32[]{:S(2)}, u32[]{:S(2)}) collective-permute-start(bf16[2,128,2048]{2,1,0:T(8,128)(2,1)S(1)} %bitcast.228), channel_id=1, source_target_pairs={{0,3},{1,2},{2,1},{3,0},{4,7},{5,6},{6,5},{7,4},{8,11},{9,10},{10,... | collective-permute-start | bytes 3145736 | tf_op jit(solution)/shard_map/ppermute | solution.py:288
  440.5 26.3 %collective-permute-start.15 = (bf16[2,128,2048]{2,1,0:T(8,128)(2,1)}, bf16[2,128,2048]{2,1,0:T(8,128)(2,1)}, u32[]{:S(2)}, u32[]{:S(2)}) collective-permute-start(bf16[2,128,2048]{2,1,0:T(8,128)(2,1)} %get-tuple-element.149), channel_id=1, source_target_pairs={{0,1},{1,0},{2,3},{3,2},{4,5},{5,4},{6,7},{7,6},{8,9},{9,8},{10,11... | collective-permute-start | bytes 3145736 | tf_op jit(solution)/shard_map/ppermute | solution.py:288
  442.0 47.8 %collective-permute-start.16 = (bf16[2,128,2048]{2,1,0:T(8,128)(2,1)}, bf16[2,128,2048]{2,1,0:T(8,128)(2,1)}, u32[]{:S(2)}, u32[]{:S(2)}) collective-permute-start(bf16[2,128,2048]{2,1,0:T(8,128)(2,1)} %get-tuple-element.151), channel_id=1, source_target_pairs={{0,2},{1,3},{2,0},{3,1},{4,6},{5,7},{6,4},{7,5},{8,10},{9,11},{10,... | collective-permute-start | bytes 3145736 | tf_op jit(solution)/shard_map/ppermute | solution.py:288
  443.5 46.4 %collective-permute-start.17 = (bf16[2,128,2048]{2,1,0:T(8,128)(2,1)}, bf16[2,128,2048]{2,1,0:T(8,128)(2,1)}, u32[]{:S(2)}, u32[]{:S(2)}) collective-permute-start(bf16[2,128,2048]{2,1,0:T(8,128)(2,1)} %get-tuple-element.150), channel_id=1, source_target_pairs={{0,3},{1,2},{2,1},{3,0},{4,7},{5,6},{6,5},{7,4},{8,11},{9,10},{10,... | collective-permute-start | bytes 3145736 | tf_op jit(solution)/shard_map/ppermute | solution.py:288
  498.1 11.2 collective-permute-start.18
  502.0 13.1 %collective-permute-start.19 = (bf16[2,128,512]{2,1,0:T(8,128)(2,1)S(1)}, bf16[2,128,512]{2,1,0:T(8,128)(2,1)S(1)}, u32[]{:S(2)}, u32[]{:S(2)}) collective-permute-start(bf16[2,128,512]{2,1,0:T(8,128)(2,1)S(1)} %bitcast.263), channel_id=1, source_target_pairs={{0,2},{1,3},{2,0},{3,1},{4,6},{5,7},{6,4},{7,5},{8,10},{9,11},{10,... | collective-permute-start | bytes 786440 | tf_op jit(solution)/shard_map/ppermute | solution.py:288
  505.6 9.5 collective-permute-start.20
  553.4 439.9 %reduce-scatter.7.cloned.1.call-start = ((), (), s32[]{:S(2)}) async-start(), calls=%async_computation.9 | async-start | bytes 6488064 | tf_op jit(solution)/shard_map/reduce_scatter | solution.py:431
  553.7 26.5 %collective-permute-start.30 = (bf16[2,128,2048]{2,1,0:T(8,128)(2,1)}, bf16[2,128,2048]{2,1,0:T(8,128)(2,1)}, u32[]{:S(2)}, u32[]{:S(2)}) collective-permute-start(bf16[2,128,2048]{2,1,0:T(8,128)(2,1)} %bitcast.76), channel_id=1, source_target_pairs={{0,1},{1,0},{2,3},{3,2},{4,5},{5,4},{6,7},{7,6},{8,9},{9,8},{10,11... | collective-permute-start | bytes 3145736 | tf_op jit(solution)/shard_map/ppermute | solution.py:288
  554.5 46.1 %collective-permute-start.31 = (bf16[2,128,2048]{2,1,0:T(8,128)(2,1)}, bf16[2,128,2048]{2,1,0:T(8,128)(2,1)}, u32[]{:S(2)}, u32[]{:S(2)}) collective-permute-start(bf16[2,128,2048]{2,1,0:T(8,128)(2,1)} %bitcast.76), channel_id=1, source_target_pairs={{0,2},{1,3},{2,0},{3,1},{4,6},{5,7},{6,4},{7,5},{8,10},{9,11},{10,... | collective-permute-start | bytes 3145736 | tf_op jit(solution)/shard_map/ppermute | solution.py:288
  555.8 47.2 %collective-permute-start.32 = (bf16[2,128,2048]{2,1,0:T(8,128)(2,1)}, bf16[2,128,2048]{2,1,0:T(8,128)(2,1)}, u32[]{:S(2)}, u32[]{:S(2)}) collective-permute-start(bf16[2,128,2048]{2,1,0:T(8,128)(2,1)} %bitcast.76), channel_id=1, source_target_pairs={{0,3},{1,2},{2,1},{3,0},{4,7},{5,6},{6,5},{7,4},{8,11},{9,10},{10,... | collective-permute-start | bytes 3145736 | tf_op jit(solution)/shard_map/ppermute | solution.py:288
  557.6 112.4 %collective-permute-start.22 = (bf16[2048,768]{1,0:T(8,128)(2,1)}, bf16[2048,768]{1,0:T(8,128)(2,1)S(1)}, u32[]{:S(2)}, u32[]{:S(2)}) collective-permute-start(bf16[2048,768]{1,0:T(8,128)(2,1)} %all-gather.7.cloned.1.call-done.w_ref), channel_id=1, source_target_pairs={{0,1},{1,0},{2,3},{3,2},{4,5},{5,4},{6,7},{7,6},{8,9},{9,8},{10,11... | collective-permute-start | bytes 9437192 | tf_op jit(solution)/shard_map/ppermute | solution.py:288
  558.4 188.3 %collective-permute-start.26 = (bf16[2048,768]{1,0:T(8,128)(2,1)}, bf16[2048,768]{1,0:T(8,128)(2,1)}, u32[]{:S(2)}, u32[]{:S(2)}) collective-permute-start(bf16[2048,768]{1,0:T(8,128)(2,1)} %all-gather.7.cloned.1.call-done.w_ref), channel_id=1, source_target_pairs={{0,3},{1,2},{2,1},{3,0},{4,7},{5,6},{6,5},{7,4},{8,11},{9,10},{10,... | collective-permute-start | bytes 9437192 | tf_op jit(solution)/shard_map/ppermute | solution.py:288
  580.2 173.3 %collective-permute-start.24 = (bf16[2048,768]{1,0:T(8,128)(2,1)}, bf16[2048,768]{1,0:T(8,128)(2,1)}, u32[]{:S(2)}, u32[]{:S(2)}) collective-permute-start(bf16[2048,768]{1,0:T(8,128)(2,1)} %all-gather.7.cloned.1.call-done.w_ref), channel_id=1, source_target_pairs={{0,2},{1,3},{2,0},{3,1},{4,6},{5,7},{6,4},{7,5},{8,10},{9,11},{10,... | collective-permute-start | bytes 9437192 | tf_op jit(solution)/shard_map/ppermute | solution.py:288
  611.9 133.7 %collective-permute-start.21 = (bf16[2,128,768]{2,1,0:T(8,128)(2,1)S(1)}, bf16[2,128,768]{2,1,0:T(8,128)(2,1)S(1)}, u32[]{:S(2)}, u32[]{:S(2)}) collective-permute-start(bf16[2,128,768]{2,1,0:T(8,128)(2,1)S(1)} %get-tuple-element.178), channel_id=1, source_target_pairs={{0,1},{1,0},{2,3},{3,2},{4,5},{5,4},{6,7},{7,6},{8,9},{9,8},{10,11... | collective-permute-start | bytes 1179656 | tf_op jit(solution)/shard_map/ppermute | solution.py:288
  613.2 137.4 %collective-permute-start.25 = (bf16[2,128,768]{2,1,0:T(8,128)(2,1)S(1)}, bf16[2,128,768]{2,1,0:T(8,128)(2,1)S(1)}, u32[]{:S(2)}, u32[]{:S(2)}) collective-permute-start(bf16[2,128,768]{2,1,0:T(8,128)(2,1)S(1)} %get-tuple-element.179), channel_id=1, source_target_pairs={{0,3},{1,2},{2,1},{3,0},{4,7},{5,6},{6,5},{7,4},{8,11},{9,10},{10,... | collective-permute-start | bytes 1179656 | tf_op jit(solution)/shard_map/ppermute | solution.py:288
  670.0 83.4 %collective-permute-start.23 = (bf16[2,128,768]{2,1,0:T(8,128)(2,1)S(1)}, bf16[2,128,768]{2,1,0:T(8,128)(2,1)S(1)}, u32[]{:S(2)}, u32[]{:S(2)}) collective-permute-start(bf16[2,128,768]{2,1,0:T(8,128)(2,1)S(1)} %get-tuple-element.176), channel_id=1, source_target_pairs={{0,2},{1,3},{2,0},{3,1},{4,6},{5,7},{6,4},{7,5},{8,10},{9,11},{10,... | collective-permute-start | bytes 1179656 | tf_op jit(solution)/shard_map/ppermute | solution.py:288
  762.7 250.3 %reduce-scatter.9.cloned.1.call-start = ((), (), s32[]{:S(2)}) async-start(), calls=%async_computation.10 | async-start | bytes 14155776 | tf_op jit(solution)/shard_map/reduce_scatter | solution.py:383
  795.3 289.5 %reduce-scatter.11.cloned.1.call-start = ((), (), s32[]{:S(2)}) async-start(), calls=%async_computation.11 | async-start | bytes 14155776 | tf_op jit(solution)/shard_map/reduce_scatter | solution.py:383
  842.4 44.3 %collective-permute-start.10 = (bf16[2,128,2048]{2,1,0:T(8,128)(2,1)S(1)}, bf16[2,128,2048]{2,1,0:T(8,128)(2,1)S(1)}, u32[]{:S(2)}, u32[]{:S(2)}) collective-permute-start(bf16[2,128,2048]{2,1,0:T(8,128)(2,1)S(1)} %get-tuple-element.162), channel_id=1, source_target_pairs={{0,2},{1,3},{2,0},{3,1},{4,6},{5,7},{6,4},{7,5},{8,10},{9,11},{10,... | collective-permute-start | bytes 3145736 | tf_op jit(solution)/shard_map/ppermute | solution.py:288
  843.2 43.5 %collective-permute-start.11 = (bf16[2,128,2048]{2,1,0:T(8,128)(2,1)S(1)}, bf16[2,128,2048]{2,1,0:T(8,128)(2,1)S(1)}, u32[]{:S(2)}, u32[]{:S(2)}) collective-permute-start(bf16[2,128,2048]{2,1,0:T(8,128)(2,1)S(1)} %get-tuple-element.161), channel_id=1, source_target_pairs={{0,3},{1,2},{2,1},{3,0},{4,7},{5,6},{6,5},{7,4},{8,11},{9,10},{10,... | collective-permute-start | bytes 3145736 | tf_op jit(solution)/shard_map/ppermute | solution.py:288
  844.6 43.3 %collective-permute-start.9 = (bf16[2,128,2048]{2,1,0:T(8,128)(2,1)S(1)}, bf16[2,128,2048]{2,1,0:T(8,128)(2,1)S(1)}, u32[]{:S(2)}, u32[]{:S(2)}) collective-permute-start(bf16[2,128,2048]{2,1,0:T(8,128)(2,1)S(1)} %get-tuple-element.160), channel_id=1, source_target_pairs={{0,1},{1,0},{2,3},{3,2},{4,5},{5,4},{6,7},{7,6},{8,9},{9,8},{10,11... | collective-permute-start | bytes 3145736 | tf_op jit(solution)/shard_map/ppermute | solution.py:288
  891.2 26.4 %collective-permute-start.12 = (bf16[2,128,2048]{2,1,0:T(8,128)(2,1)}, bf16[2,128,2048]{2,1,0:T(8,128)(2,1)}, u32[]{:S(2)}, u32[]{:S(2)}) collective-permute-start(bf16[2,128,2048]{2,1,0:T(8,128)(2,1)} %bitcast.35), channel_id=1, source_target_pairs={{0,1},{1,0},{2,3},{3,2},{4,5},{5,4},{6,7},{7,6},{8,9},{9,8},{10,11... | collective-permute-start | bytes 3145736 | tf_op jit(solution)/shard_map/ppermute | solution.py:288
  891.3 48.9 %collective-permute-start.13 = (bf16[2,128,2048]{2,1,0:T(8,128)(2,1)}, bf16[2,128,2048]{2,1,0:T(8,128)(2,1)}, u32[]{:S(2)}, u32[]{:S(2)}) collective-permute-start(bf16[2,128,2048]{2,1,0:T(8,128)(2,1)} %bitcast.35), channel_id=1, source_target_pairs={{0,2},{1,3},{2,0},{3,1},{4,6},{5,7},{6,4},{7,5},{8,10},{9,11},{10,... | collective-permute-start | bytes 3145736 | tf_op jit(solution)/shard_map/ppermute | solution.py:288
  892.1 48.0 %collective-permute-start.14 = (bf16[2,128,2048]{2,1,0:T(8,128)(2,1)}, bf16[2,128,2048]{2,1,0:T(8,128)(2,1)}, u32[]{:S(2)}, u32[]{:S(2)}) collective-permute-start(bf16[2,128,2048]{2,1,0:T(8,128)(2,1)} %bitcast.35), channel_id=1, source_target_pairs={{0,3},{1,2},{2,1},{3,0},{4,7},{5,6},{6,5},{7,4},{8,11},{9,10},{10,... | collective-permute-start | bytes 3145736 | tf_op jit(solution)/shard_map/ppermute | solution.py:288
  894.7 67.8 %collective-permute-start.27 = (bf16[2,128,2048]{2,1,0:T(8,128)(2,1)}, bf16[2,128,2048]{2,1,0:T(8,128)(2,1)S(1)}, u32[]{:S(2)}, u32[]{:S(2)}) collective-permute-start(bf16[2,128,2048]{2,1,0:T(8,128)(2,1)} %bitcast.68), channel_id=1, source_target_pairs={{0,1},{1,0},{2,3},{3,2},{4,5},{5,4},{6,7},{7,6},{8,9},{9,8},{10,11... | collective-permute-start | bytes 3145736 | tf_op jit(solution)/shard_map/ppermute | solution.py:288
  894.7 87.2 %collective-permute-start.28 = (bf16[2,128,2048]{2,1,0:T(8,128)(2,1)}, bf16[2,128,2048]{2,1,0:T(8,128)(2,1)}, u32[]{:S(2)}, u32[]{:S(2)}) collective-permute-start(bf16[2,128,2048]{2,1,0:T(8,128)(2,1)} %bitcast.68), channel_id=1, source_target_pairs={{0,2},{1,3},{2,0},{3,1},{4,6},{5,7},{6,4},{7,5},{8,10},{9,11},{10,... | collective-permute-start | bytes 3145736 | tf_op jit(solution)/shard_map/ppermute | solution.py:288
  917.7 64.2 %collective-permute-start.29 = (bf16[2,128,2048]{2,1,0:T(8,128)(2,1)}, bf16[2,128,2048]{2,1,0:T(8,128)(2,1)}, u32[]{:S(2)}, u32[]{:S(2)}) collective-permute-start(bf16[2,128,2048]{2,1,0:T(8,128)(2,1)} %bitcast.68), channel_id=1, source_target_pairs={{0,3},{1,2},{2,1},{3,0},{4,7},{5,6},{6,5},{7,4},{8,11},{9,10},{10,... | collective-permute-start | bytes 3145736 | tf_op jit(solution)/shard_map/ppermute | solution.py:288
  995.0 16.7 %collective-permute-start.33 = (bf16[256,128]{0,1:T(8,128)(2,1)}, bf16[256,128]{0,1:T(8,128)(2,1)}, u32[]{:S(2)}, u32[]{:S(2)}) collective-permute-start(bf16[256,128]{0,1:T(8,128)(2,1)} %slice.279), channel_id=1, source_target_pairs={{0,1},{1,0},{2,3},{3,2},{4,5},{5,4},{6,7},{7,6},{8,9},{9,8},{10,11... | collective-permute-start | bytes 196616 | tf_op jit(solution)/shard_map/ppermute | solution.py:288
  996.7 14.9 %collective-permute-start.34 = (bf16[256,128]{0,1:T(8,128)(2,1)}, bf16[256,128]{0,1:T(8,128)(2,1)}, u32[]{:S(2)}, u32[]{:S(2)}) collective-permute-start(bf16[256,128]{0,1:T(8,128)(2,1)} %slice.279), channel_id=1, source_target_pairs={{0,2},{1,3},{2,0},{3,1},{4,6},{5,7},{6,4},{7,5},{8,10},{9,11},{10,... | collective-permute-start | bytes 196616 | tf_op jit(solution)/shard_map/ppermute | solution.py:288
  997.0 14.7 %collective-permute-start.35 = (bf16[256,128]{0,1:T(8,128)(2,1)}, bf16[256,128]{0,1:T(8,128)(2,1)}, u32[]{:S(2)}, u32[]{:S(2)}) collective-permute-start(bf16[256,128]{0,1:T(8,128)(2,1)} %slice.279), channel_id=1, source_target_pairs={{0,3},{1,2},{2,1},{3,0},{4,7},{5,6},{6,5},{7,4},{8,11},{9,10},{10,... | collective-permute-start | bytes 196616 | tf_op jit(solution)/shard_map/ppermute | solution.py:288
  (60 other events, 1126.7 us)
Sparse Core Ops, SparseCore 0:
  10.3 40.9 all-gather.6
  52.9 31.0 all-gather.8
  86.2 44.4 all-gather.14
  132.7 117.5 all-gather.10
  252.3 113.6 all-gather.12
  553.6 47.3 reduce-scatter.4
  762.8 62.1 reduce-scatter.6
  827.3 127.5 reduce-scatter.8
  957.2 127.5 reduce-scatter.10

commit v2 on v1

--- a/solution.py
+++ b/solution.py
@@ -13,6 +13,7 @@
 MICRO = 2
 STEP = 5
 CHUNKS = 2
+SUB = 512
 
 norm_eps = 1e-05
 rope_base = 500000.0
@@ -26,6 +27,13 @@
 F32 = jnp.float32
 BF16 = jnp.bfloat16
 VMEM_LIMIT = 60 * 1024 * 1024
+HINT = 20
+
+
+def hint(flops, bytes_accessed, transcendentals):
+    return pl.CostEstimate(
+        flops=flops // HINT, bytes_accessed=bytes_accessed // HINT, transcendentals=transcendentals
+    )
 
 
 def lane_tables(positions, kinds):
@@ -87,7 +95,7 @@
             jax.ShapeDtypeStruct((rows, width), BF16),
         ],
         compiler_params=pltpu.CompilerParams(vmem_limit_bytes=VMEM_LIMIT),
-        cost_estimate=pl.CostEstimate(
+        cost_estimate=hint(
             flops=2 * rows * depth * width, bytes_accessed=4 * rows * depth, transcendentals=0
         ),
         name="project",
@@ -188,7 +196,7 @@
         out_specs=q_spec,
         out_shape=jax.ShapeDtypeStruct(q.shape, BF16),
         compiler_params=pltpu.CompilerParams(vmem_limit_bytes=VMEM_LIMIT),
-        cost_estimate=pl.CostEstimate(
+        cost_estimate=hint(
             flops=16 * micro * seqs * span_rows * width * n_dp * span_rows,
             bytes_accessed=4 * q.size + 2 * kv.size,
             transcendentals=0,
@@ -212,7 +220,7 @@
             jax.ShapeDtypeStruct(kv.shape, BF16),
         ],
         compiler_params=pltpu.CompilerParams(vmem_limit_bytes=VMEM_LIMIT),
-        cost_estimate=pl.CostEstimate(
+        cost_estimate=hint(
             flops=40 * micro * seqs * span_rows * width * n_dp * span_rows,
             bytes_accessed=6 * q.size + 4 * kv.size,
             transcendentals=0,
@@ -245,6 +253,232 @@
 
 def dot_tn(left, right):
     return lax.dot_general(left, right, (((0,), (0,)), ((), ())), preferred_element_type=F32)
+
+
+def gated_kernel(last, steps, u_ref, g_ref, w_ref, *refs):
+    if last:
+        y_old, du_old, hid_ref, dgu_ref, y_out, du_out, y_sum, du_sum, y_low, du_low, sem = refs
+    else:
+        hid_ref, dgu_ref, y_out, du_out, y_sum, du_sum, y_low, du_low, sem = refs
+    step = pl.program_id(0)
+    depth = w_ref.shape[0]
+    sub = hid_ref.shape[1]
+    cols = min(512, depth)
+
+    @pl.when(step == 0)
+    def _():
+        y_sum[...] = jnp.zeros_like(y_sum)
+        du_sum[...] = jnp.zeros_like(du_sum)
+        if last:
+            pltpu.make_async_copy(y_old, y_low, sem.at[0]).start()
+            pltpu.make_async_copy(du_old, du_low, sem.at[1]).start()
+
+    gate_proj = dot(u_ref[...], w_ref[:, :sub])
+    up_proj = dot(u_ref[...], w_ref[:, sub : 2 * sub])
+    sigmoid_gate = jax.nn.sigmoid(gate_proj)
+    silu_gate = gate_proj * sigmoid_gate
+    hid_ref[...] = (silu_gate * up_proj).astype(BF16)
+    d_hidden = dot(g_ref[...], w_ref[:, 2 * sub :])
+    d_gate = d_hidden * up_proj * sigmoid_gate * (1.0 + gate_proj * (1.0 - sigmoid_gate))
+    dgu_ref[:, :sub] = d_gate.astype(BF16)
+    dgu_ref[:, sub:] = (d_hidden * silu_gate).astype(BF16)
+    for start in range(0, depth, cols):
+        part = slice(start, start + cols)
+        du_sum[:, part] += dot_nt(dgu_ref[...], w_ref[part, : 2 * sub])
+        y_sum[:, part] += dot_nt(hid_ref[...], w_ref[part, 2 * sub :])
+
+    @pl.when(step == steps - 1)
+    def _():
+        copy_y = pltpu.make_async_copy(y_low, y_out, sem.at[0])
+        copy_du = pltpu.make_async_copy(du_low, du_out, sem.at[1])
+        if last:
+            pltpu.make_async_copy(y_old, y_low, sem.at[0]).wait()
+            pltpu.make_async_copy(du_old, du_low, sem.at[1]).wait()
+            du_low[...] = (du_sum[...] + du_low[...].astype(F32)).astype(BF16)
+            copy_du.start()
+            y_low[...] = (y_sum[...] + y_low[...].astype(F32)).astype(BF16)
+        else:
+            du_low[...] = du_sum[...].astype(BF16)
+            copy_du.start()
+            y_low[...] = y_sum[...].astype(BF16)
+        copy_y.start()
+        copy_du.wait()
+        copy_y.wait()
+
+
+def feed_forward(u, g, weights, sub, sums):
+    rows, depth = u.shape
+    steps = weights.shape[1] // (3 * sub)
+    last = sums is not None
+    whole = functools.partial(pl.BlockSpec, pipeline_mode=pl.Buffered(1))
+    anywhere = pl.BlockSpec(memory_space=pl.ANY)
+    return pl.pallas_call(
+        functools.partial(gated_kernel, last, steps),
+        grid=(steps,),
+        in_specs=[
+            whole((rows, depth), lambda j: (0, 0)),
+            whole((rows, depth), lambda j: (0, 0)),
+            pl.BlockSpec((depth, 3 * sub), lambda j: (0, j)),
+        ]
+        + ([anywhere, anywhere] if last else []),
+        out_specs=[
+            pl.BlockSpec((rows, sub), lambda j: (0, j)),
+            pl.BlockSpec((rows, 2 * sub), lambda j: (0, j)),
+            anywhere,
+            anywhere,
+        ],
+        out_shape=[
+            jax.ShapeDtypeStruct((rows, steps * sub), BF16),
+            jax.ShapeDtypeStruct((rows, 2 * steps * sub), BF16),
+            jax.ShapeDtypeStruct((rows, depth), BF16),
+            jax.ShapeDtypeStruct((rows, depth), BF16),
+        ],
+        scratch_shapes=[
+            pltpu.VMEM((rows, depth), F32),
+            pltpu.VMEM((rows, depth), F32),
+            pltpu.VMEM((rows, depth), BF16),
+            pltpu.VMEM((rows, depth), BF16),
+            pltpu.SemaphoreType.DMA((2,)),
+        ],
+        compiler_params=pltpu.CompilerParams(vmem_limit_bytes=VMEM_LIMIT),
+        cost_estimate=hint(
+            flops=12 * rows * depth * steps * sub,
+            bytes_accessed=2 * weights.size + 8 * rows * depth,
+            transcendentals=0,
+        ),
+        name="feed_forward",
+    )(u, g, weights, *(sums if last else ()))
+
+
+def outer_kernel(batches, sub, steps, half, core_ref, *refs):
+    u_refs, g_refs = refs[:batches], refs[batches : 2 * batches]
+    hid_refs, dgu_refs = refs[2 * batches : 3 * batches], refs[3 * batches : 4 * batches]
+    outs = refs[4 * batches :]
+
+    def products(out_ref):
+        for j in range(steps):
+            both = slice(2 * j * sub, 2 * (j + 1) * sub)
+            one = slice(j * sub, (j + 1) * sub)
+            total = dot_tn(u_refs[0][...], dgu_refs[0][:, both])
+            for m in range(1, batches):
+                total += dot_tn(u_refs[m][...], dgu_refs[m][:, both])
+            out_ref[0, :, 3 * j * sub : 3 * j * sub + 2 * sub] = total.astype(BF16)
+            total = dot_tn(g_refs[0][...], hid_refs[0][:, one])
+            for m in range(1, batches):
+                total += dot_tn(g_refs[m][...], hid_refs[m][:, one])
+            out_ref[0, :, 3 * j * sub + 2 * sub : 3 * (j + 1) * sub] = total.astype(BF16)
+
+    if len(outs) == 1:
+        products(outs[0])
+    else:
+
+        @pl.when(pl.program_id(0) < half)
+        def _():
+            products(outs[0])
+
+        @pl.when(pl.program_id(0) >= half)
+        def _():
+            products(outs[1])
+
+
+def outer_products(core, us, gs, hids, dgus, own, sub, split):
+    batches = len(us)
+    rows, depth = us[0].shape
+    n_dp = depth // own
+    half = n_dp // 2
+    width = hids[0].shape[1]
+    steps = width // sub
+    if split:
+
+        def place(i, core_ref):
+            mine = jnp.where(i < half, 1 - core_ref[0], core_ref[0])
+            return (i % half) * 2 + mine
+
+        out_specs = [
+            pl.BlockSpec((1, own, 3 * width), lambda i, r: (jnp.minimum(i, half - 1), 0, 0)),
+            pl.BlockSpec((1, own, 3 * width), lambda i, r: (jnp.maximum(i - half, 0), 0, 0)),
+        ]
+        out_shape = [jax.ShapeDtypeStruct((half, own, 3 * width), BF16)] * 2
+    else:
+
+        def place(i, core_ref):
+            return i
+
+        out_specs = [pl.BlockSpec((1, own, 3 * width), lambda i, r: (i, 0, 0))]
+        out_shape = [jax.ShapeDtypeStruct((n_dp, own, 3 * width), BF16)]
+    whole = functools.partial(pl.BlockSpec, pipeline_mode=pl.Buffered(1))
+    column = pl.BlockSpec((rows, own), lambda i, r: (0, place(i, r)))
+    return pl.pallas_call(
+        functools.partial(outer_kernel, batches, sub, steps, half),
+        grid_spec=pltpu.PrefetchScalarGridSpec(
+            num_scalar_prefetch=1,
+            grid=(n_dp,),
+            in_specs=[column] * (2 * batches)
+            + [whole((rows, width), lambda i, r: (0, 0))] * batches
+            + [whole((rows, 2 * width), lambda i, r: (0, 0))] * batches,
+            out_specs=out_specs,
+        ),
+        out_shape=out_shape,
+        compiler_params=pltpu.CompilerParams(vmem_limit_bytes=VMEM_LIMIT),
+        cost_estimate=hint(
+            flops=6 * rows * batches * depth * width,
+            bytes_accessed=6 * depth * width,
+            transcendentals=0,
+        ),
+        name="outer_products",
+    )(core, *us, *gs, *hids, *dgus)
+
+
+def step_kernel(turned, decay, steps, chunks, *refs):
+    grads = refs[:chunks]
+    mean_ref, square_ref, weight_ref, grad_ref, moment_ref, spread_ref, update_ref = refs[chunks:]
+    place = pl.program_id(1)
+    for c in range(chunks):
+
+        @pl.when(place // steps == c)
+        def _(c=c):
+            gradient = grads[c][...].astype(F32)
+            if turned:
+                gradient = gradient.T
+            gradient = gradient.reshape(grad_ref.shape)
+            moment, spread, change = adam_update(
+                gradient, mean_ref[...], square_ref[...], weight_ref[...].astype(F32), decay
+            )
+            grad_ref[...] = gradient
+            moment_ref[...] = moment
+            spread_ref[...] = spread
+            update_ref[...] = change
+
+
+def step_from_chunks(grads, old_mean, square, weight, sub, offset, turned, decay):
+    chunks, own = len(grads), grads[0].shape[0]
+    steps = grads[0].shape[1] // (3 * sub)
+
+    def grad_spec(c):
+        def index(i, p):
+            j = jnp.clip(p - c * steps, 0, steps - 1)
+            return (0, 3 * j + i + offset)
+
+        return pl.BlockSpec((own, sub), index)
+
+    if turned:
+        lead, spec = 1, pl.BlockSpec((sub, own), lambda i, p: (p, 0))
+    else:
+        lead, spec = old_mean.shape[0], pl.BlockSpec((1, own, sub), lambda i, p: (i, 0, p))
+    return tuple(
+        pl.pallas_call(
+            functools.partial(step_kernel, turned, decay, steps, chunks),
+            grid=(lead, chunks * steps),
+            in_specs=[grad_spec(c) for c in range(chunks)] + [spec] * 3,
+            out_specs=[spec] * 4,
+            out_shape=[jax.ShapeDtypeStruct(old_mean.shape, F32)] * 4,
+            compiler_params=pltpu.CompilerParams(vmem_limit_bytes=VMEM_LIMIT),
+            cost_estimate=hint(
+                flops=20 * old_mean.size, bytes_accessed=28 * old_mean.size, transcendentals=0
+            ),
+            name="weight_step",
+        )(*grads, old_mean, square, weight)
+    )
 
 
 def per_device(
@@ -283,6 +517,8 @@
     group = q_width // HD // (kv_width // (2 * HD))
     device = lax.axis_index("dp")
     rank = lax.axis_index("tp")
+    line = n_dp // 2
+    place, core = device // 2, device % 2
 
     def swap(value, k):
         return lax.ppermute(value, "tp", [(i, i ^ k) for i in range(n_tp)])
@@ -292,18 +528,85 @@
             [lax.dynamic_slice_in_dim(value, rank ^ k, 1, axis=1) for k in range(n_tp)], axis=1
         )
 
-    def gather_rows(own):
-        return jnp.stack([own] + [swap(own, k) for k in range(1, n_tp)], axis=1)
+    def gather_blocks(own):
+        half = own.shape[0] // 2
+        got = [own, swap(own, 1), swap(own, 2)]
+        got.append(jnp.concatenate([swap(got[1][:half], 2), swap(got[2][half:], 1)], axis=0))
+        return got + [swap(own, k) for k in range(4, n_tp)]
 
     def exchange(blocks):
         return [blocks[0]] + [swap(blocks[k], k) for k in range(1, n_tp)]
 
-    def scatter_sum(partial):
-        got = exchange([partial[:, k].astype(BF16) for k in range(n_tp)])
-        total = partial[:, 0].astype(F32)
-        for k in range(1, n_tp):
-            total = total + got[k].astype(F32)
+    def total_of(parts):
+        total = parts[0].astype(F32)
+        for part in parts[1:]:
+            total = total + part.astype(F32)
         return total
+
+    def gather_pair(owns):
+        got = [owns, [swap(own, 1) for own in owns], [swap(own, 2) for own in owns]]
+        got.append([swap(got[1][0], 2)] + [swap(own, 1) for own in got[2][1:]])
+        return got + [[swap(own, k) for own in owns] for k in range(4, n_tp)]
+
+    def scatter_pair(blocks):
+        first = swap(blocks[0][3], 1)
+        seconds = [swap(blocks[m][3], 2) for m in range(1, MICRO)]
+        to_two = total_of([blocks[0][2], first]).astype(BF16)
+        to_one = [total_of([blocks[m][1], seconds[m - 1]]).astype(BF16) for m in range(1, MICRO)]
+        yield [to_two] + to_one
+        totals = []
+        for m in range(MICRO):
+            one = blocks[m][1] if m == 0 else to_one[m - 1]
+            two = to_two if m == 0 else blocks[m][2]
+            far = [swap(blocks[m][k], k) for k in range(4, n_tp)]
+            totals.append(total_of([blocks[m][0], swap(one, 1), swap(two, 2)] + far))
+        yield totals
+
+    def line_sum(other, own):
+        met = lax.ppermute(other, "dp", [(i, i ^ 1) for i in range(n_dp)])
+        yield [met]
+
+        def share(index):
+            index = jnp.clip(index, 0, line - 1)
+            return lax.dynamic_index_in_dim(own, index, 0, False).astype(
+                F32
+            ) + lax.dynamic_index_in_dim(met, index, 0, False).astype(F32)
+
+        sends = []
+        for far in range(1, line):
+            for way in (far, -far):
+                sends.append((way, share(place + way).astype(BF16)))
+        yield [value for _, value in sends]
+        total = share(place)
+        for far in range(1, line):
+            arrived = []
+            for way, value in sends:
+                if abs(way) == far:
+                    pairs = [
+                        (i, i + 2 * way) for i in range(n_dp) if 0 <= i + 2 * way < n_dp
+                    ]
+                    arrived.append(lax.ppermute(value, "dp", pairs))
+            if far <= 3:
+                yield arrived
+            for value in arrived:
+                total = total + value.astype(F32)
+        yield [total]
+
+    def my_half(value):
+        return lax.dynamic_slice_in_dim(value, core * (depth // 2), depth // 2, axis=0)
+
+    def swap_cores(value):
+        return lax.ppermute(value, "dp", [(i, i ^ 1) for i in range(n_dp)])
+
+    def both_halves(near, far):
+        return jnp.where(
+            core == 0,
+            jnp.concatenate([near, far], axis=1),
+            jnp.concatenate([far, near], axis=1),
+        )
+
+    def after(value, *earlier):
+        return lax.optimization_barrier((value,) + earlier)[0]
 
     qkv_full = lax.all_gather(
         jnp.concatenate([w_query, w_keyval], axis=1), "dp", axis=0, tiled=True
@@ -322,114 +625,214 @@
 
     x = reorder(tokens.reshape(MICRO, n_tp, block_rows, depth))
     seed = reorder(cotangent.reshape(MICRO, n_tp, block_rows, depth))
-    rows = MICRO * SEQS * span_rows
+    batch_rows = SEQS * span_rows
+    rows = MICRO * batch_rows
     gain_one, gain_two = gains_full[0:1], gains_full[1:2]
     attn_in, qkv = project(x.reshape(rows, depth), gain_one, qkv_full, cos_t, sin_t)
     qkv = qkv.reshape(MICRO, SEQS, span_rows, q_width + kv_width)
     q, kv = qkv[..., :q_width], qkv[..., q_width:]
     kv_all = lax.all_gather(kv, "dp", axis=0, tiled=False)
 
+    sub = min(SUB, hidden_width // CHUNKS)
     chunk = hidden_width // CHUNKS
     w_down_t = w_down.T
     mlp_full = []
     for c in range(CHUNKS):
-        cols = slice(c * chunk, (c + 1) * chunk)
-        shard = jnp.concatenate(
-            [w_gateup[0][:, cols], w_gateup[1][:, cols], w_down_t[:, cols]], axis=1
-        )
+        pieces = []
+        for start in range(c * chunk, (c + 1) * chunk, sub):
+            cols = slice(start, start + sub)
+            pieces += [w_gateup[0][:, cols], w_gateup[1][:, cols], w_down_t[:, cols]]
+        shard = jnp.concatenate(pieces, axis=1)
         mlp_full.append(lax.all_gather(shard, "dp", axis=0, tiled=True))
 
     attended = attend(qpos, kpos, q, kv_all, group)
-    by_block = (MICRO, n_tp, block_rows, -1)
-
-    out_t_all = [out_t_full] + [swap(out_t_full, k) for k in range(1, n_tp)]
-    attended_blocks = attended.reshape(by_block)
+    attended_blocks = attended.reshape(MICRO, n_tp, block_rows, q_width)
+    out_near = my_half(out_t_full)
+    out_near = jnp.concatenate([out_near] + [swap(out_near, k) for k in range(1, n_tp)], axis=1)
+    out_far = swap_cores(out_near)
     heads_in = exchange([attended_blocks[:, k] for k in range(n_tp)])
     own_rows = MICRO * block_rows
     x_own = x[:, 0].reshape(own_rows, depth).astype(F32)
-    seed_own = seed[:, 0].reshape(own_rows, depth).astype(F32)
-    middle = x_own
-    for k in range(n_tp):
-        middle = middle + dot_nt(heads_in[k].reshape(own_rows, q_width), out_t_all[k])
+    heads_cat = jnp.concatenate([v.reshape(own_rows, q_width) for v in heads_in], axis=1)
+    middle = x_own + both_halves(dot_nt(heads_cat, out_near), dot_nt(heads_cat, out_far))
     scale_two = mean_square_scale(middle)
     normed_two = middle * scale_two
     u_own = (normed_two * gain_two.astype(F32)).astype(BF16)
-    u = gather_rows(u_own.reshape(MICRO, block_rows, depth)).reshape(rows, depth)
-    g = seed.reshape(rows, depth)
-
-    y_part = None
-    du_part = None
-    mlp_grads = []
-    for c in range(CHUNKS):
-        weights = mlp_full[c]
-        gate_proj = dot(u, weights[:, :chunk])
-        up_proj = dot(u, weights[:, chunk : 2 * chunk])
-        d_hidden = dot(g, weights[:, 2 * chunk :])
-        sigmoid_gate = jax.nn.sigmoid(gate_proj)
-        silu_gate = gate_proj * sigmoid_gate
-        hidden = (silu_gate * up_proj).astype(BF16)
-        d_gate = (
-            d_hidden * up_proj * sigmoid_gate * (1.0 + gate_proj * (1.0 - sigmoid_gate))
-        ).astype(BF16)
-        d_up = (d_hidden * silu_gate).astype(BF16)
-        d_both = jnp.concatenate([d_gate, d_up], axis=1)
-        du_term = dot_nt(d_both, weights[:, : 2 * chunk])
-        y_term = dot_nt(hidden, weights[:, 2 * chunk :])
-        du_part = du_term if du_part is None else du_part + du_term
-        y_part = y_term if y_part is None else y_part + y_term
-        grads = jnp.concatenate(
-            [dot_tn(u, d_both).astype(BF16), dot_tn(g, hidden).astype(BF16)], axis=1
-        )
-        mlp_grads.append(lax.psum_scatter(grads, "dp", scatter_dimension=0, tiled=True))
-
-    d_mixed = scatter_sum(du_part.reshape(by_block)).reshape(own_rows, depth)
-    gain_grad_two = jnp.sum(d_mixed * normed_two, axis=0)
-    d_middle = seed_own + norm_back(d_mixed * gain_two.astype(F32), normed_two, scale_two)
-    d_mid_low = d_middle.astype(BF16)
-    do_rows = [
-        dot(d_mid_low, out_t_all[k]).astype(BF16).reshape(MICRO, block_rows, q_width)
-        for k in range(n_tp)
+    batches = range(MICRO)
+    gathered = [g.reshape(MICRO, block_rows, depth) for g in gather_blocks(u_own)]
+    u = [jnp.concatenate([gathered[k][m] for k in range(n_tp)], axis=0) for m in batches]
+    g = [seed[m].reshape(batch_rows, depth) for m in batches]
+
+    qkv_half = after(my_half(qkv_full), u[0])
+    quarter = depth // 4
+    qkv_quarters = [qkv_half[:quarter], qkv_half[quarter:]]
+    qkv_moves = [(k, i) for i in range(2) for k in range(1, min(n_tp, 3))]
+    qkv_moves = [qkv_moves[:2], qkv_moves[2:]] + [
+        [(k, i) for k in range(3, n_tp)] for i in range(2)
     ]
-    d_attend = jnp.stack(exchange(do_rows), axis=1).reshape(q.shape)
+    qkv_got = {}
+
+    def move_qkv():
+        if not qkv_moves:
+            return []
+        now = qkv_moves.pop(0)
+        for k, i in now:
+            qkv_got[k, i] = swap(qkv_quarters[i], k)
+        return [qkv_got[move] for move in now]
+
+    def blocks_of(value):
+        return [value[k * block_rows : (k + 1) * block_rows] for k in range(n_tp)]
+
+    def own_part(value, m):
+        return value[m * block_rows : (m + 1) * block_rows]
+
+    core_index = core.astype(jnp.int32).reshape(1)
+    gain_two_f = gain_two.astype(F32)
+    gain_one_f = gain_one.astype(F32)
     cos_q, sin_q = cos_t[:, : group * HD], sin_t[:, : group * HD]
-    d_query_low, d_kv_part = attend_back(qpos, kpos, cos_q, sin_q, q, d_attend, kv_all, group)
-    own_grad = lax.psum_scatter(d_kv_part, "dp", scatter_dimension=0, tiled=False).astype(F32)
-
-    block_own = middle + scatter_sum(y_part.reshape(by_block)).reshape(own_rows, depth)
-    out_rows = gather_rows(block_own.astype(BF16).reshape(MICRO, block_rows, depth))
-    block_output = reorder(out_rows).reshape(rows, depth)
-    d_mid_rows = gather_rows(d_mid_low.reshape(MICRO, block_rows, depth)).reshape(rows, depth)
+    cos_k, sin_k = cos_t[:, q_width:], sin_t[:, q_width:]
+    gain_grads = [0.0, 0.0]
+    sums = [None] * MICRO
+
+    def expand(c, m, *earlier):
+        hid, dgu, y_low, du_low = feed_forward(
+            after(u[m], *earlier), g[m], mlp_full[c], sub, sums[m]
+        )
+        sums[m] = (y_low, du_low)
+        return hid, dgu
+
+    def close(hids, dgus, *earlier):
+        (grads,) = outer_products(
+            core_index, [after(u[0], *earlier)] + u[1:], g, hids, dgus, own_depth, sub, False
+        )
+        return grads, lax.psum_scatter(grads, "dp", scatter_dimension=0, tiled=False)
+
+    chunk_grads = []
+    earlier = []
+    for c in range(CHUNKS - 1):
+        hids, dgus = [], []
+        for m in batches:
+            hid, dgu = expand(c, m, *earlier)
+            earlier = [hid] + move_qkv()
+            hids.append(hid)
+            dgus.append(dgu)
+        grads, owned = close(hids, dgus, *earlier)
+        earlier = [grads] + move_qkv()
+        chunk_grads.append(owned)
+
+    d_middles, d_mid_lows, d_attends, all_rows = [], [], [], []
+    hids, dgus = [], []
+    for m in batches:
+        hid, dgu = expand(CHUNKS - 1, m, *earlier)
+        earlier = [hid] + move_qkv()
+        hids.append(hid)
+        dgus.append(dgu)
+    qkv_near = [qkv_half] + [
+        jnp.concatenate([qkv_got[k, i] for i in range(2)], axis=0) for k in range(1, n_tp)
+    ]
+    qkv_near = after(jnp.concatenate(qkv_near, axis=1), *earlier)
+    qkv_far = swap_cores(qkv_near)
+    for m in batches:
+        if m == 1:
+            grads, owned = close(hids, dgus, all_rows[0], qkv_near)
+            chunk_grads.append(owned)
+            earlier = [grads, qkv_far]
+        got = exchange(blocks_of(sums[m][1]))
+        d_mixed = total_of([after(got[0], *(earlier if m else []))] + got[1:])
+        normed = own_part(normed_two, m)
+        gain_grads[1] = gain_grads[1] + jnp.sum(d_mixed * normed, axis=0)
+        d_middle = seed[m, 0].astype(F32) + norm_back(
+            d_mixed * gain_two_f, normed, own_part(scale_two, m)
+        )
+        d_mid_low = d_middle.astype(BF16)
+        near, far = (
+            lax.dynamic_slice_in_dim(d_mid_low, side * (depth // 2), depth // 2, axis=1)
+            for side in (core, 1 - core)
+        )
+        do_rows = (dot(near, out_near) + dot(far, out_far)).astype(BF16)
+        all_rows.append(do_rows)
+        do_blocks = [do_rows[:, k * q_width : (k + 1) * q_width] for k in range(n_tp)]
+        d_attends.append(jnp.concatenate(exchange(do_blocks), axis=0).reshape((1,) + q.shape[1:]))
+        d_middles.append(d_middle)
+        d_mid_lows.append(d_mid_low)
+
+    y_stages = scatter_pair([blocks_of(after(sums[m][0], d_attends[-1])) for m in batches])
+    y_sends = next(y_stages)
+    d_queries, kv_stages = [], []
+    for m in batches:
+        waits = [all_rows[-1]] if m == 0 else y_sends
+        d_query_low, d_kv_part = attend_back(
+            qpos,
+            kpos,
+            cos_q,
+            sin_q,
+            q[m : m + 1],
+            after(d_attends[m], *waits),
+            kv_all[:, m : m + 1],
+            group,
+        )
+        d_queries.append(d_query_low[0])
+        by_core = d_kv_part.reshape((line, 2) + d_kv_part.shape[2:])
+        kv_stages.append(
+            line_sum(
+                lax.dynamic_index_in_dim(by_core, 1 - core, 1, False),
+                lax.dynamic_index_in_dim(by_core, core, 1, False),
+            )
+        )
+    blocks_own = [own_part(middle, m) + total for m, total in enumerate(next(y_stages))]
+    d_mid_rows = gather_pair([after(v, d_attends[-1]) for v in d_mid_lows])
+    d_mid_rows = jnp.concatenate(
+        [d_mid_rows[k][m] for m in batches for k in range(n_tp)], axis=0
+    )
+    out_rows = gather_pair([value.astype(BF16) for value in blocks_own])
+
+    block_output = jnp.zeros((MICRO, n_tp, block_rows, depth), BF16)
+    grad_tokens = jnp.zeros((MICRO, n_tp, block_rows, depth), F32)
+
+    def placed(buffer, m, blocks):
+        for k in range(n_tp):
+            piece = blocks[k].astype(buffer.dtype)[None, None]
+            buffer = lax.dynamic_update_slice(buffer, piece, (m, rank ^ k, 0, 0))
+        return buffer
+
+    lane = jnp.arange(kv_width)
+    d_qkvs = []
+    for m in batches:
+        block_output = placed(block_output, m, [out_rows[k][m] for k in range(n_tp)])
+        own_grad = list(kv_stages[m])[-1][0]
+        own_grad = after(own_grad, *(blocks_own if m == 0 else []))
+        scaled = own_grad * sin_k
+        turned = jnp.where(
+            lane % HD < HD // 2,
+            jnp.roll(scaled, -(HD // 2), axis=-1),
+            jnp.roll(scaled, HD // 2, axis=-1),
+        )
+        d_kv_low = (own_grad * cos_k + turned).astype(BF16)
+        d_qkv = jnp.concatenate([d_queries[m], d_kv_low], axis=-1)
+        d_qkv = d_qkv.reshape(batch_rows, q_width + kv_width)
+        d_qkvs.append(d_qkv)
+        d_heads = exchange(blocks_of(d_qkv))
+        heads_cat = jnp.concatenate(d_heads, axis=1)
+        d_act = both_halves(dot_nt(heads_cat, qkv_near), dot_nt(heads_cat, qkv_far))
+        x_part = own_part(x_own, m)
+        scale_one = mean_square_scale(x_part)
+        normed_one = x_part * scale_one
+        gain_grads[0] = gain_grads[0] + jnp.sum(d_act * normed_one, axis=0)
+        tokens_own = d_middles[m] + norm_back(d_act * gain_one_f, normed_one, scale_one)
+        tokens_low = tokens_own.astype(BF16)
+        grad_tokens = placed(
+            grad_tokens, m, [tokens_low] + [swap(tokens_low, k) for k in range(1, n_tp)]
+        )
+    mlp_grads = [v.reshape(own_depth, -1) for v in chunk_grads]
+    block_output = block_output.reshape(rows, depth)
+    grad_tokens = grad_tokens.reshape(rows, depth)
+
     out_grad_t = dot_tn(d_mid_rows, attended.reshape(rows, q_width)).astype(BF16)
-
-    cos_k, sin_k = cos_t[:, q_width:], sin_t[:, q_width:]
-    scaled = own_grad * sin_k
-    lane = jnp.arange(kv_width)
-    turned = jnp.where(
-        lane % HD < HD // 2,
-        jnp.roll(scaled, -(HD // 2), axis=-1),
-        jnp.roll(scaled, HD // 2, axis=-1),
-    )
-    d_kv_low = (own_grad * cos_k + turned).astype(BF16)
-    d_qkv = jnp.concatenate([d_query_low, d_kv_low], axis=-1)
-    qkv_all = [qkv_full] + [swap(qkv_full, k) for k in range(1, n_tp)]
-    d_blocks = d_qkv.reshape(by_block)
-    d_heads = exchange([d_blocks[:, k] for k in range(n_tp)])
-    d_act = None
-    for k in range(n_tp):
-        term = dot_nt(d_heads[k].reshape(own_rows, q_width + kv_width), qkv_all[k])
-        d_act = term if d_act is None else d_act + term
-    scale_one = mean_square_scale(x_own)
-    normed_one = x_own * scale_one
-    gain_grad_one = jnp.sum(d_act * normed_one, axis=0)
-    tokens_own = d_middle + norm_back(d_act * gain_one.astype(F32), normed_one, scale_one)
-    tokens_rows = gather_rows(tokens_own.astype(BF16).reshape(MICRO, block_rows, depth))
-    grad_tokens = reorder(tokens_rows).reshape(rows, depth).astype(F32)
-
-    qkv_grad = dot_tn(attn_in, d_qkv.reshape(rows, q_width + kv_width)).astype(BF16)
-    gain_cols = jnp.stack([gain_grad_one, gain_grad_two], axis=1)
+    qkv_grad = dot_tn(attn_in, jnp.concatenate(d_qkvs, axis=0)).astype(BF16)
+    gain_cols = jnp.stack(gain_grads, axis=1)
     gain_cols = jnp.pad(gain_cols, ((0, 0), (0, 126))).astype(BF16)
     attn_grads = lax.psum_scatter(
-        jnp.concatenate([qkv_grad, out_grad_t, gain_cols], axis=1),
+        after(jnp.concatenate([qkv_grad, out_grad_t, gain_cols], axis=1), *chunk_grads),
         "dp",
         scatter_dimension=0,
         tiled=True,
@@ -443,14 +846,6 @@
     grad_keyval = attn_grads[:, q_width : q_width + kv_width].astype(F32)
     grad_output = attn_grads[:, q_width + kv_width : 2 * q_width + kv_width].astype(F32).T
     grad_gains = gain_sum[:, :2].T
-    grad_gateup = jnp.stack(
-        [
-            jnp.concatenate([part[:, i * chunk : (i + 1) * chunk] for part in mlp_grads], axis=1)
-            for i in range(2)
-        ]
-    ).astype(F32)
-    grad_down = jnp.concatenate([part[:, 2 * chunk :] for part in mlp_grads], axis=1).astype(F32).T
-
     def with_update(gradient, old_mean, square, weight, decay):
         return (gradient,) + adam_update(gradient, old_mean, square, weight.astype(F32), decay)
 
@@ -459,8 +854,10 @@
         + with_update(grad_query, mean_query, square_query, w_query, weight_decay)
         + with_update(grad_keyval, mean_keyval, square_keyval, w_keyval, weight_decay)
         + with_update(grad_output, mean_output, square_output, w_output, weight_decay)
-        + with_update(grad_gateup, mean_gateup, square_gateup, w_gateup, weight_decay)
-        + with_update(grad_down, mean_down, square_down, w_down, weight_decay)
+        + step_from_chunks(
+            mlp_grads, mean_gateup, square_gateup, w_gateup, sub, 0, False, weight_decay
+        )
+        + step_from_chunks(mlp_grads, mean_down, square_down, w_down, sub, 2, True, weight_decay)
         + with_update(grad_gains, mean_gains, square_gains, norm_gains, 0.0)
     )
 

time: 1140 us -> 867 us (0.76)
  waiting for transfers between devices: 633 us -> 277 us
  Pallas kernels: 77.4 us -> 227 us
  matrix products: 176 us -> 50 us
  starting transfers between devices: 40.2 us -> 110 us
    ppermute x36 -> x61, waiting for transfers between devices: 394 us -> 198 us  [swap(): return lax.ppermute(value, 'tp', [(i, i ^ k) for i in range(n_tp)])]
    pallas_call x0 -> x8, Pallas kernels: none -> 148 us  [the longest x4 88.3 us: feed_forward(): pl.pallas_call(functools.partial(gated_kernel, last, steps), grid=(steps,...]
    reduce_scatter x4 -> x3, waiting for transfers between devices: 69.6 us -> 0.02 us  [the longest x1 0.02 us: per_device(): lax.psum_scatter(after(jnp.concatenate([qkv_grad, out_grad_t, gain_cols],...]
    all_gather x2, waiting for transfers between devices: 102 us -> 32.8 us  [per_device(): mlp_full.append(lax.all_gather(shard, 'dp', axis=0, tiled=True))]
    dot_general x10 -> x4, matrix products: 69.5 us -> 14.9 us  [dot(): return jnp.dot(left, right, preferred_element_type=F32)]
    all_gather x1, waiting for transfers between devices: 39.4 us -> 0.01 us  [per_device(): kv_all = lax.all_gather(kv, 'dp', axis=0, tiled=False)]
    dot_general x12 -> x6, matrix products: 60.6 us -> 22.1 us  [dot_nt(): lax.dot_general(left, right, (((1,), (1,)), ((), ())), preferred_element_...]
    ppermute x0 -> x16, starting transfers between devices: none -> 38.3 us  [the longest x12 38.2 us: line_sum(): arrived.append(lax.ppermute(value, 'dp', pairs))]
  transfers between devices with their start and end apart: 45 -> 85, of which waited for: 25 -> 29; matrix products, arithmetic and copies ran while one was open for 19% -> 24% of each run, Pallas kernels for 4% -> 26%
where the time goes in v2:
time: 867 us; the launch traced here: 861 us
  waiting for transfers between devices  277 us (32%)
  Pallas kernels  227 us (26%)
  starting transfers between devices  110 us (13%)
  other arithmetic  87.4 us (10%)
  local copies, waits for them, and re-layouts  80.4 us (9%)
  matrix products  50 us (6%)
  between operations  15.9 us (2%)
  blocking collectives  13.5 us (2%)
    ppermute x61, waiting for transfers between devices, swap(): return lax.ppermute(value, 'tp', [(i, i ^ k) for i in range(n_tp)])  198 us
    pallas_call x4, Pallas kernels, feed_forward(): pl.pallas_call(functools.partial(gated_kernel, last, steps), grid=(steps,...  88.3 us
    ppermute x61, starting transfers between devices, swap(): return lax.ppermute(value, 'tp', [(i, i ^ k) for i in range(n_tp)])  70.4 us
    pallas_call x2, Pallas kernels, attend_back(): pl.pallas_call(functools.partial(attend_back_kernel, group), grid=(micro,...  38.9 us
    pallas_call x2, Pallas kernels, outer_products(): pl.pallas_call(functools.partial(outer_kernel, batches, sub, steps, half)...  38.7 us
    ppermute x12, starting transfers between devices, line_sum(): arrived.append(lax.ppermute(value, 'dp', pairs))  38.2 us
    all_gather x2, waiting for transfers between devices, per_device(): mlp_full.append(lax.all_gather(shard, 'dp', axis=0, tiled=True))  32.8 us
    unnamed x141, local copies, waits for them, and re-layouts  29.6 us
  transfers between devices with their start and end apart: 85, of which 29 were waited for; matrix products, arithmetic and copies ran while one was open for 24% of the time, Pallas kernels for 26%

profile of v2, /device:TPU:0, one launch (start us, length us, event | category | flops | bytes accessed | tf_op | source)
XLA Modules:
  0.0 861.3 jit_solution(17330685246229251178)
XLA Ops:
  13.4 13.5 %all_gather.21 = bf16[2,2048]{1,0:T(2,128)(2,1)S(1)} all-gather(bf16[2,256]{1,0:T(2,128)(2,1)S(1)} %copy-done.43), channel_id=1, replica_groups=mesh['dp'=8,'tp'=4] {'dp'}, dimensions={1}, use_global_device_ids=true | all-gather | bytes 9216 | tf_op jit(solution)/shard_map/all_gather | solution.py:614
  32.7 18.6 %all-gather.7.cloned.1.call-done.w_ref = bf16[2048,768]{1,0:T(8,128)(2,1)} async-done(((bf16[256,768]{1,0:T(8,128)(2,1)}), bf16[2048,768]{1,0:T(8,128)(2,1)}) %all-gather.7.cloned.1.call-update) | async-done | bytes 3145744 | tf_op jit(solution)/shard_map/all_gather | solution.py:611
  51.3 11.0 %project.1 = (bf16[1024,2048]{1,0:T(8,128)(2,1)}, bf16[1024,768]{1,0:T(8,128)(2,1)}) custom-call(bf16[1024,2048]{1,0:T(8,128)(2,1)} %bitcast.265, bf16[1,2048]{1,0:T(2,128)(2,1)} %get-tuple-element.329.gain_ref, bf16[2048,768]{1,0:T(8,128)(2,1)} %all-gather.7.cloned.1.call-done.w_ref, f32[128,768]{1,0:T(8,128)} %concatenate.159.cos_ref, ...), custom_call_target="tpu_custom_call" | custom-call | flops 161061280 | bytes 419430 | tf_op jit(solution)/shard_map/project/pallas_call | solution.py:79
  72.1 11.9 %all-gather.9.cloned.1.call-done = bf16[2048,512]{0,1:T(8,128)(2,1)} async-done(((bf16[256,512]{0,1:T(8,128)(2,1)}), bf16[2048,512]{0,1:T(8,128)(2,1)}) %all-gather.9.cloned.1.call-update) | async-done | bytes 2097168 | tf_op jit(solution)/shard_map/all_gather | solution.py:615
  88.9 22.5 %collective-permute-done.3 = bf16[1024,512]{0,1:T(8,128)(2,1)S(1)} collective-permute-done((bf16[1024,512]{0,1:T(8,128)(2,1)S(1)}, bf16[1024,512]{0,1:T(8,128)(2,1)S(1)}, u32[]{:S(2)}, u32[]{:S(2)}) %collective-permute-start.3) | collective-permute-done | bytes 1048608 | tf_op jit(solution)/shard_map/ppermute | solution.py:524
  111.4 21.9 %collective-permute-done.4 = bf16[1024,512]{0,1:T(8,128)(2,1)S(1)} collective-permute-done((bf16[1024,512]{0,1:T(8,128)(2,1)S(1)}, bf16[1024,512]{0,1:T(8,128)(2,1)S(1)}, u32[]{:S(2)}, u32[]{:S(2)}) %collective-permute-start.4) | collective-permute-done | bytes 1048608 | tf_op jit(solution)/shard_map/ppermute | solution.py:524
  139.4 29.1 %attend.1 = bf16[2,4,128,512]{3,2,1,0:T(8,128)(2,1)} custom-call(s32[128,1]{1,0:T(8,128)} %copy.83.qpos_ref, s32[1,1024]{1,0:T(1,128)} %add.538.kpos_ref, bf16[2,4,128,512]{3,2,1,0:T(8,128)(2,1)} %slice.439.q_ref, bf16[8,2,4,128,256]{4,3,2,1,0:T(8,128)(2,1)} %bitcast.266), custom_call_target="tpu_custom_call" | custom-call | flops 429496736 | bytes 314572 | tf_op jit(solution)/shard_map/attend/pallas_call | solution.py:192
  174.1 11.2 %collective-permute-done.1 = bf16[2,128,512]{2,1,0:T(8,128)(2,1)} collective-permute-done((bf16[2,128,512]{2,1,0:T(8,128)(2,1)}, bf16[2,128,512]{2,1,0:T(8,128)(2,1)}, u32[]{:S(2)}, u32[]{:S(2)}) %collective-permute-start.1) | collective-permute-done | bytes 262176 | tf_op jit(solution)/shard_map/ppermute | solution.py:524
  186.5 3.9 fusion.70
  190.4 3.7 fusion.69
  201.5 20.4 %collective-permute-done.7 = bf16[256,2048]{1,0:T(8,128)(2,1)S(1)} collective-permute-done((bf16[256,2048]{1,0:T(8,128)(2,1)S(1)}, bf16[256,2048]{1,0:T(8,128)(2,1)S(1)}, u32[]{:S(2)}, u32[]{:S(2)}) %collective-permute-start.7) | collective-permute-done | bytes 1048608 | tf_op jit(solution)/shard_map/ppermute | solution.py:524
  225.8 9.7 %collective-permute-done.9 = bf16[128,2048]{1,0:T(8,128)(2,1)S(1)} collective-permute-done((bf16[128,2048]{1,0:T(8,128)(2,1)S(1)}, bf16[128,2048]{1,0:T(8,128)(2,1)S(1)}, u32[]{:S(2)}, u32[]{:S(2)}) %collective-permute-start.9) | collective-permute-done | bytes 524320 | tf_op jit(solution)/shard_map/ppermute | solution.py:524
  248.2 21.9 %feed_forward.4 = (bf16[512,1024]{1,0:T(8,128)(2,1)}, bf16[512,2048]{1,0:T(8,128)(2,1)}, bf16[512,2048]{1,0:T(8,128)(2,1)}, bf16[512,2048]{1,0:T(8,128)(2,1)}) custom-call(bf16[512,2048]{1,0:T(8,128)(2,1)} %pad_maximum_fusion.4.u_ref.refs_0_, bf16[512,2048]{1,0:T(8,128)(2,1)} %bitcast.261, bf16[2048,3072]{1,0:T(8,128)(2,1)} %all-gather.11.cloned.1.call-done.w_ref), custom_call_target="tpu_custom_call" | custom-call | flops 644245120 | bytes 1048576 | tf_op jit(solution)/shard_map/feed_forward/pallas_call | solution.py:315
  270.1 22.3 %feed_forward.5 = (bf16[512,1024]{1,0:T(8,128)(2,1)}, bf16[512,2048]{1,0:T(8,128)(2,1)}, bf16[512,2048]{1,0:T(8,128)(2,1)}, bf16[512,2048]{1,0:T(8,128)(2,1)}) custom-call(bf16[512,2048]{1,0:T(8,128)(2,1)} %pad_maximum_fusion.5.u_ref.refs_1_, bf16[512,2048]{1,0:T(8,128)(2,1)} %bitcast.257, bf16[2048,3072]{1,0:T(8,128)(2,1)} %all-gather.11.cloned.1.call-done.w_ref), custom_call_target="tpu_custom_call" | custom-call | flops 644245120 | bytes 1048576 | tf_op jit(solution)/shard_map/feed_forward/pallas_call | solution.py:315
  292.5 19.5 %outer_products.2 = bf16[8,256,3072]{2,1,0:T(8,128)(2,1)} custom-call(s32[1]{0:T(128)} %bitcast.19.core_ref, bf16[512,2048]{1,0:T(8,128)(2,1)} %pad_maximum_fusion.4.u_ref.refs_0_, bf16[512,2048]{1,0:T(8,128)(2,1)} %pad_maximum_fusion.5.u_ref.refs_1_, bf16[512,2048]{1,0:T(8,128)(2,1)} %bitcast.262, bf16[512,2048]{1,0:T(8,128)(2,1)} %bitcast.258, ...), custom_call_target="tpu_custom_call" | custom-call | flops 644245120 | bytes 629145 | tf_op jit(solution)/shard_map/outer_products/pallas_call | solution.py:411
  315.5 18.0 %collective-permute-done.15 = bf16[512,768]{1,0:T(8,128)(2,1)S(1)} collective-permute-done((bf16[512,768]{1,0:T(8,128)(2,1)}, bf16[512,768]{1,0:T(8,128)(2,1)S(1)}, u32[]{:S(2)}, u32[]{:S(2)}) %collective-permute-start.15) | collective-permute-done | bytes 786464 | tf_op jit(solution)/shard_map/ppermute | solution.py:524
  333.5 31.2 %all-gather.13.cloned.1.call-done.w_ref = bf16[2048,3072]{1,0:T(8,128)(2,1)} async-done(((bf16[256,3072]{1,0:T(8,128)(2,1)}), bf16[2048,3072]{1,0:T(8,128)(2,1)}) %all-gather.13.cloned.1.call-update) | async-done | bytes 12582928 | tf_op jit(solution)/shard_map/all_gather | solution.py:646
  364.7 21.9 %feed_forward.6 = (bf16[512,1024]{1,0:T(8,128)(2,1)}, bf16[512,2048]{1,0:T(8,128)(2,1)}, bf16[512,2048]{1,0:T(8,128)(2,1)}, bf16[512,2048]{1,0:T(8,128)(2,1)}) custom-call(bf16[512,2048]{1,0:T(8,128)(2,1)} %pad_maximum_fusion.4.u_ref.refs_0_, bf16[512,2048]{1,0:T(8,128)(2,1)} %bitcast.263, bf16[2048,3072]{1,0:T(8,128)(2,1)} %all-gather.13.cloned.1.call-done.w_ref, ...), custom_call_target="tpu_custom_call" | custom-call | flops 644245120 | bytes 1048576 | tf_op jit(solution)/shard_map/feed_forward/pallas_call | solution.py:315
  393.0 23.2 %maximum_maximum_fusion = bf16[1024,3072]{1,0:T(8,128)(2,1)} fusion(bf16[512,768]{1,0:T(8,128)(2,1)} %collective-permute-done.16, bf16[512,768]{1,0:T(8,128)(2,1)S(1)} %copy-done.33, bf16[512,768]{1,0:T(8,128)(2,1)} %collective-permute-done.14, bf16[512,768]{1,0:T(8,128)(2,1)} %collective-permute-done.12, bf16[512,768]{1,0:T(8,128)(2,1)} %collective-permute-done.13, ...), kind=kLoop, calls=%fused_computation | loop fusion | flops 44040192 | bytes 12582912 | tf_op jit(solution)/shard_map/concatenate | solution.py:733
  416.2 22.3 %feed_forward.7 = (bf16[512,1024]{1,0:T(8,128)(2,1)}, bf16[512,2048]{1,0:T(8,128)(2,1)}, bf16[512,2048]{1,0:T(8,128)(2,1)}, bf16[512,2048]{1,0:T(8,128)(2,1)}) custom-call(bf16[512,2048]{1,0:T(8,128)(2,1)} %pad_maximum_fusion.5.u_ref.refs_1_, bf16[512,2048]{1,0:T(8,128)(2,1)} %bitcast.259, bf16[2048,3072]{1,0:T(8,128)(2,1)} %all-gather.13.cloned.1.call-done.w_ref, ...), custom_call_target="tpu_custom_call" | custom-call | flops 644245120 | bytes 1048576 | tf_op jit(solution)/shard_map/feed_forward/pallas_call | solution.py:315
  451.9 19.3 %outer_products.3 = bf16[8,256,3072]{2,1,0:T(8,128)(2,1)} custom-call(s32[1]{0:T(128)} %bitcast.19.core_ref, bf16[512,2048]{1,0:T(8,128)(2,1)} %pad_maximum_fusion.4.u_ref.refs_0_, bf16[512,2048]{1,0:T(8,128)(2,1)} %pad_maximum_fusion.5.u_ref.refs_1_, bf16[512,2048]{1,0:T(8,128)(2,1)} %bitcast.264, bf16[512,2048]{1,0:T(8,128)(2,1)} %bitcast.260, ...), custom_call_target="tpu_custom_call" | custom-call | flops 644245120 | bytes 629145 | tf_op jit(solution)/shard_map/outer_products/pallas_call | solution.py:411
  484.3 22.8 %collective-permute-done.40 = bf16[128,512]{1,0:T(8,128)(2,1)S(1)} collective-permute-done((bf16[128,512]{1,0:T(8,128)(2,1)S(1)}, bf16[128,512]{1,0:T(8,128)(2,1)S(1)}, u32[]{:S(2)}, u32[]{:S(2)}) %collective-permute-start.40) | collective-permute-done | bytes 131104 | tf_op jit(solution)/shard_map/ppermute | solution.py:524
  517.0 3.7 fusion.49
  528.7 19.5 %attend_back.2 = (bf16[1,4,128,512]{3,2,1,0:T(8,128)(2,1)}, bf16[8,1,4,128,256]{4,3,2,1,0:T(8,128)(2,1)}) custom-call(s32[128,1]{1,0:T(8,128)} %copy.83.qpos_ref, s32[1,1024]{1,0:T(1,128)} %add.538.kpos_ref, f32[128,256]{1,0:T(8,128)} %concatenate.179.cos_ref, f32[128,256]{1,0:T(8,128)} %concatenate.180.sin_ref, ...), custom_call_target="tpu_custom_call" | custom-call | flops 536870912 | bytes 288358 | tf_op jit(solution)/shard_map/attend_back/pallas_call | solution.py:213
  560.3 9.0 %collective-permute-done.33 = bf16[128,2048]{1,0:T(8,128)(2,1)S(1)} collective-permute-done((bf16[128,2048]{1,0:T(8,128)(2,1)S(1)}, bf16[128,2048]{1,0:T(8,128)(2,1)S(1)}, u32[]{:S(2)}, u32[]{:S(2)}) %collective-permute-start.33) | collective-permute-done | bytes 524320 | tf_op jit(solution)/shard_map/ppermute | solution.py:524
  573.9 19.5 %attend_back.3 = (bf16[1,4,128,512]{3,2,1,0:T(8,128)(2,1)}, bf16[8,1,4,128,256]{4,3,2,1,0:T(8,128)(2,1)}) custom-call(s32[128,1]{1,0:T(8,128)} %copy.83.qpos_ref, s32[1,1024]{1,0:T(1,128)} %add.538.kpos_ref, f32[128,256]{1,0:T(8,128)} %concatenate.179.cos_ref, f32[128,256]{1,0:T(8,128)} %concatenate.180.sin_ref, ...), custom_call_target="tpu_custom_call" | custom-call | flops 536870912 | bytes 288358 | tf_op jit(solution)/shard_map/attend_back/pallas_call | solution.py:213
  613.6 3.9 collective-permute-done.70
  625.0 6.9 collective-permute-start.47
  634.4 3.8 convolution_convert_fusion.1
  638.2 7.1 collective-permute-done.46
  648.0 5.4 collective-permute-start.56
  654.7 5.9 collective-permute-start.58
  662.8 6.9 collective-permute-start.60
  674.1 7.6 collective-permute-done.59
  686.9 7.3 collective-permute-done.35
  702.8 9.3 %convolution_convert_fusion = bf16[2048,768]{0,1:T(8,128)(2,1)} fusion(bf16[1024,2048]{1,0:T(8,128)(2,1)S(1)} %copy-done.54, bf16[512,256]{1,0:T(8,128)(2,1)S(1)} %bitcast.296, bf16[512,512]{1,0:T(8,128)(2,1)S(1)} %bitcast.300, bf16[512,256]{1,0:T(8,128)(2,1)S(1)} %bitcast.295, bf16[512,512]{1,0:T(8,128)(2,1)S(1)} %bitcast.298), kind=kOutput, calls=%fused_computation.5 | convolution fusion | flops 3229089792 | bytes 8912896 | tf_op jit(solution)/shard_map/dot_general | solution.py:255
  714.6 5.0 fusion.71
  722.9 5.0 fusion.73
  731.1 6.0 pad_maximum_fusion
  748.7 4.5 broadcast_in_dim.117
  758.1 4.1 collective-permute-done.37
  765.4 8.5 collective-permute-done.52
  777.9 6.4 collective-permute-done.54
  791.3 5.1 collective-permute-done.38
  797.2 10.4 %collective-permute-done.65 = bf16[128,2048]{1,0:T(8,128)(2,1)S(1)} collective-permute-done((bf16[128,2048]{1,0:T(8,128)(2,1)S(1)}, bf16[128,2048]{1,0:T(8,128)(2,1)S(1)}, u32[]{:S(2)}, u32[]{:S(2)}) %collective-permute-start.65) | collective-permute-done | bytes 524320 | tf_op jit(solution)/shard_map/ppermute | solution.py:524
  809.8 4.2 collective-permute-done.67
  815.0 7.1 weight_step.3
  822.1 14.1 %weight_step.2 = (f32[2,256,2048]{2,1,0:T(8,128)}, f32[2,256,2048]{2,1,0:T(8,128)}, f32[2,256,2048]{2,1,0:T(8,128)}, f32[2,256,2048]{2,1,0:T(8,128)}) custom-call(bf16[256,3072]{1,0:T(8,128)(2,1)} %bitcast.274, bf16[256,3072]{1,0:T(8,128)(2,1)} %bitcast.276, f32[2,256,2048]{2,1,0:T(8,128)} %refs_2_.2, f32[2,256,2048]{2,1,0:T(8,128)} %refs_3_.2, ...), custom_call_target="tpu_custom_call" | custom-call | flops 1048576 | bytes 1468006 | tf_op jit(solution)/shard_map/weight_step/pallas_call | solution.py:469
  (413 shorter events, 249.6 us)
Async XLA Ops:
  7.2 44.1 %all-gather.7.cloned.1.call-start = ((), (), s32[]{:S(2)}) async-start(), calls=%async_computation.3 | async-start | bytes 3538944 | tf_op jit(solution)/shard_map/all_gather | solution.py:611
  9.1 74.9 %all-gather.9.cloned.1.call-start = ((), (), s32[]{:S(2)}) async-start(), calls=%async_computation.4 | async-start | bytes 2359296 | tf_op jit(solution)/shard_map/all_gather | solution.py:615
  9.8 129.5 %all-gather.15.cloned.1.call-start = ((), (), s32[]{:S(2)}) async-start(), calls=%async_computation.10 | async-start | bytes 4718592 | tf_op jit(solution)/shard_map/all_gather | solution.py:634
  64.2 184.0 %all-gather.11.cloned.1.call-start = ((), (), s32[]{:S(2)}) async-start(), calls=%async_computation.5 | async-start | bytes 14155776 | tf_op jit(solution)/shard_map/all_gather | solution.py:646
  70.9 293.8 %all-gather.13.cloned.1.call-start = ((), (), s32[]{:S(2)}) async-start(), calls=%async_computation.6 | async-start | bytes 14155776 | tf_op jit(solution)/shard_map/all_gather | solution.py:646
  71.5 665.6 %reduce-scatter.4.cloned.1.call-start = ((), (), s32[]{:S(2)}) async-start(), calls=%async_computation.7 | async-start | bytes 14155776 | tf_op jit(solution)/shard_map/reduce_scatter | solution.py:708
  85.3 26.1 %collective-permute-start.3 = (bf16[1024,512]{0,1:T(8,128)(2,1)S(1)}, bf16[1024,512]{0,1:T(8,128)(2,1)S(1)}, u32[]{:S(2)}, u32[]{:S(2)}) collective-permute-start(bf16[1024,512]{0,1:T(8,128)(2,1)S(1)} %constant_dynamic-slice_fusion.5), channel_id=1, source_target_pairs={{0,1},{1,0},{2,3},{3,2},{4,5},{5,4},{6,7},{7,6},{8,9},{9,8},{10,11... | collective-permute-start | bytes 3145736 | tf_op jit(solution)/shard_map/ppermute | solution.py:524
  85.4 47.8 %collective-permute-start.4 = (bf16[1024,512]{0,1:T(8,128)(2,1)S(1)}, bf16[1024,512]{0,1:T(8,128)(2,1)S(1)}, u32[]{:S(2)}, u32[]{:S(2)}) collective-permute-start(bf16[1024,512]{0,1:T(8,128)(2,1)S(1)} %constant_dynamic-slice_fusion.5), channel_id=1, source_target_pairs={{0,2},{1,3},{2,0},{3,1},{4,6},{5,7},{6,4},{7,5},{8,10},{9,11},{10,... | collective-permute-start | bytes 3145736 | tf_op jit(solution)/shard_map/ppermute | solution.py:524
  86.7 46.6 %collective-permute-start.5 = (bf16[1024,512]{0,1:T(8,128)(2,1)S(1)}, bf16[1024,512]{0,1:T(8,128)(2,1)S(1)}, u32[]{:S(2)}, u32[]{:S(2)}) collective-permute-start(bf16[1024,512]{0,1:T(8,128)(2,1)S(1)} %constant_dynamic-slice_fusion.5), channel_id=1, source_target_pairs={{0,3},{1,2},{2,1},{3,0},{4,7},{5,6},{6,5},{7,4},{8,11},{9,10},{10,... | collective-permute-start | bytes 3145736 | tf_op jit(solution)/shard_map/ppermute | solution.py:524
  135.5 54.9 %collective-permute-start.6 = (bf16[1024,2048]{0,1:T(8,128)(2,1)}, bf16[1024,2048]{0,1:T(8,128)(2,1)}, u32[]{:S(2)}, u32[]{:S(2)}) collective-permute-start(bf16[1024,2048]{0,1:T(8,128)(2,1)} %pad_maximum_fusion.2), channel_id=1, source_target_pairs={{0,4},{4,0},{8,12},{12,8},{16,20},{20,16},{24,28},{28,24},{1,5},{5... | collective-permute-start | bytes 12582920 | tf_op jit(solution)/shard_map/ppermute | solution.py:599
  197.4 24.5 %collective-permute-start.7 = (bf16[256,2048]{1,0:T(8,128)(2,1)S(1)}, bf16[256,2048]{1,0:T(8,128)(2,1)S(1)}, u32[]{:S(2)}, u32[]{:S(2)}) collective-permute-start(bf16[256,2048]{1,0:T(8,128)(2,1)S(1)} %get-tuple-element.233), channel_id=1, source_target_pairs={{0,1},{1,0},{2,3},{3,2},{4,5},{5,4},{6,7},{7,6},{8,9},{9,8},{10,11... | collective-permute-start | bytes 3145736 | tf_op jit(solution)/shard_map/ppermute | solution.py:524
  200.1 25.2 %collective-permute-start.8 = (bf16[256,2048]{1,0:T(8,128)(2,1)S(1)}, bf16[256,2048]{1,0:T(8,128)(2,1)S(1)}, u32[]{:S(2)}, u32[]{:S(2)}) collective-permute-start(bf16[256,2048]{1,0:T(8,128)(2,1)S(1)} %get-tuple-element.233), channel_id=1, source_target_pairs={{0,2},{1,3},{2,0},{3,1},{4,6},{5,7},{6,4},{7,5},{8,10},{9,11},{10,... | collective-permute-start | bytes 3145736 | tf_op jit(solution)/shard_map/ppermute | solution.py:524
  238.3 31.8 %collective-permute-start.11 = (bf16[512,768]{1,0:T(8,128)(2,1)}, bf16[512,768]{1,0:T(8,128)(2,1)S(1)}, u32[]{:S(2)}, u32[]{:S(2)}) collective-permute-start(bf16[512,768]{1,0:T(8,128)(2,1)} %get-tuple-element.276), channel_id=1, source_target_pairs={{0,1},{1,0},{2,3},{3,2},{4,5},{5,4},{6,7},{7,6},{8,9},{9,8},{10,11... | collective-permute-start | bytes 2359304 | tf_op jit(solution)/shard_map/ppermute | solution.py:524
  239.2 30.9 %collective-permute-start.12 = (bf16[512,768]{1,0:T(8,128)(2,1)}, bf16[512,768]{1,0:T(8,128)(2,1)}, u32[]{:S(2)}, u32[]{:S(2)}) collective-permute-start(bf16[512,768]{1,0:T(8,128)(2,1)} %get-tuple-element.276), channel_id=1, source_target_pairs={{0,2},{1,3},{2,0},{3,1},{4,6},{5,7},{6,4},{7,5},{8,10},{9,11},{10,... | collective-permute-start | bytes 2359304 | tf_op jit(solution)/shard_map/ppermute | solution.py:524
  240.2 52.3 %collective-permute-start.13 = (bf16[512,768]{1,0:T(8,128)(2,1)}, bf16[512,768]{1,0:T(8,128)(2,1)}, u32[]{:S(2)}, u32[]{:S(2)}) collective-permute-start(bf16[512,768]{1,0:T(8,128)(2,1)} %get-tuple-element.275), channel_id=1, source_target_pairs={{0,1},{1,0},{2,3},{3,2},{4,5},{5,4},{6,7},{7,6},{8,9},{9,8},{10,11... | collective-permute-start | bytes 2359304 | tf_op jit(solution)/shard_map/ppermute | solution.py:524
  241.1 51.3 %collective-permute-start.14 = (bf16[512,768]{1,0:T(8,128)(2,1)}, bf16[512,768]{1,0:T(8,128)(2,1)}, u32[]{:S(2)}, u32[]{:S(2)}) collective-permute-start(bf16[512,768]{1,0:T(8,128)(2,1)} %get-tuple-element.275), channel_id=1, source_target_pairs={{0,2},{1,3},{2,0},{3,1},{4,6},{5,7},{6,4},{7,5},{8,10},{9,11},{10,... | collective-permute-start | bytes 2359304 | tf_op jit(solution)/shard_map/ppermute | solution.py:524
  311.9 425.2 %reduce-scatter.6.cloned.1.call-start = ((), (), s32[]{:S(2)}) async-start(), calls=%async_computation.8 | async-start | bytes 14155776 | tf_op jit(solution)/shard_map/reduce_scatter | solution.py:708
  312.0 21.5 %collective-permute-start.15 = (bf16[512,768]{1,0:T(8,128)(2,1)}, bf16[512,768]{1,0:T(8,128)(2,1)S(1)}, u32[]{:S(2)}, u32[]{:S(2)}) collective-permute-start(bf16[512,768]{1,0:T(8,128)(2,1)} %get-tuple-element.276), channel_id=1, source_target_pairs={{0,3},{1,2},{2,1},{3,0},{4,7},{5,6},{6,5},{7,4},{8,11},{9,10},{10,... | collective-permute-start | bytes 2359304 | tf_op jit(solution)/shard_map/ppermute | solution.py:524
  314.4 78.6 %collective-permute-start.16 = (bf16[512,768]{1,0:T(8,128)(2,1)}, bf16[512,768]{1,0:T(8,128)(2,1)}, u32[]{:S(2)}, u32[]{:S(2)}) collective-permute-start(bf16[512,768]{1,0:T(8,128)(2,1)} %get-tuple-element.275), channel_id=1, source_target_pairs={{0,3},{1,2},{2,1},{3,0},{4,7},{5,6},{6,5},{7,4},{8,11},{9,10},{10,... | collective-permute-start | bytes 2359304 | tf_op jit(solution)/shard_map/ppermute | solution.py:524
  389.5 49.0 %collective-permute-start.17 = (bf16[128,2048]{1,0:T(8,128)(2,1)}, bf16[128,2048]{1,0:T(8,128)(2,1)S(1)}, u32[]{:S(2)}, u32[]{:S(2)}) collective-permute-start(bf16[128,2048]{1,0:T(8,128)(2,1)} %get-tuple-element.266), channel_id=1, source_target_pairs={{0,1},{1,0},{2,3},{3,2},{4,5},{5,4},{6,7},{7,6},{8,9},{9,8},{10,11... | collective-permute-start | bytes 1572872 | tf_op jit(solution)/shard_map/ppermute | solution.py:524
  391.0 47.6 %collective-permute-start.18 = (bf16[128,2048]{1,0:T(8,128)(2,1)}, bf16[128,2048]{1,0:T(8,128)(2,1)S(1)}, u32[]{:S(2)}, u32[]{:S(2)}) collective-permute-start(bf16[128,2048]{1,0:T(8,128)(2,1)} %get-tuple-element.265), channel_id=1, source_target_pairs={{0,2},{1,3},{2,0},{3,1},{4,6},{5,7},{6,4},{7,5},{8,10},{9,11},{10,... | collective-permute-start | bytes 1572872 | tf_op jit(solution)/shard_map/ppermute | solution.py:524
  392.4 46.1 %collective-permute-start.19 = (bf16[128,2048]{1,0:T(8,128)(2,1)}, bf16[128,2048]{1,0:T(8,128)(2,1)}, u32[]{:S(2)}, u32[]{:S(2)}) collective-permute-start(bf16[128,2048]{1,0:T(8,128)(2,1)} %get-tuple-element.264), channel_id=1, source_target_pairs={{0,3},{1,2},{2,1},{3,0},{4,7},{5,6},{6,5},{7,4},{8,11},{9,10},{10,... | collective-permute-start | bytes 1572872 | tf_op jit(solution)/shard_map/ppermute | solution.py:524
  471.2 365.1 %reduce-scatter.8.cloned.1.call-start = ((), (), s32[]{:S(2)}) async-start(), calls=%async_computation.9 | async-start | bytes 6488064 | tf_op jit(solution)/shard_map/reduce_scatter | solution.py:834
  471.4 42.4 %collective-permute-start.20 = (bf16[1024,3072]{1,0:T(8,128)(2,1)}, bf16[1024,3072]{1,0:T(8,128)(2,1)}, u32[]{:S(2)}, u32[]{:S(2)}) collective-permute-start(bf16[1024,3072]{1,0:T(8,128)(2,1)} %maximum_maximum_fusion), channel_id=1, source_target_pairs={{0,4},{4,0},{8,12},{12,8},{16,20},{20,16},{24,28},{28,24},{1,5},{5... | collective-permute-start | bytes 18874376 | tf_op jit(solution)/shard_map/ppermute | solution.py:599
  478.3 35.6 %collective-permute-start.21 = (bf16[128,2048]{1,0:T(8,128)(2,1)S(1)}, bf16[128,2048]{1,0:T(8,128)(2,1)S(1)}, u32[]{:S(2)}, u32[]{:S(2)}) collective-permute-start(bf16[128,2048]{1,0:T(8,128)(2,1)S(1)} %get-tuple-element.270), channel_id=1, source_target_pairs={{0,1},{1,0},{2,3},{3,2},{4,5},{5,4},{6,7},{7,6},{8,9},{9,8},{10,11... | collective-permute-start | bytes 1572872 | tf_op jit(solution)/shard_map/ppermute | solution.py:524
  479.2 34.6 %collective-permute-start.22 = (bf16[128,2048]{1,0:T(8,128)(2,1)S(1)}, bf16[128,2048]{1,0:T(8,128)(2,1)S(1)}, u32[]{:S(2)}, u32[]{:S(2)}) collective-permute-start(bf16[128,2048]{1,0:T(8,128)(2,1)S(1)} %get-tuple-element.269), channel_id=1, source_target_pairs={{0,2},{1,3},{2,0},{3,1},{4,6},{5,7},{6,4},{7,5},{8,10},{9,11},{10,... | collective-permute-start | bytes 1572872 | tf_op jit(solution)/shard_map/ppermute | solution.py:524
  480.7 33.2 %collective-permute-start.23 = (bf16[128,2048]{1,0:T(8,128)(2,1)S(1)}, bf16[128,2048]{1,0:T(8,128)(2,1)S(1)}, u32[]{:S(2)}, u32[]{:S(2)}) collective-permute-start(bf16[128,2048]{1,0:T(8,128)(2,1)S(1)} %get-tuple-element.268), channel_id=1, source_target_pairs={{0,3},{1,2},{2,1},{3,0},{4,7},{5,6},{6,5},{7,4},{8,11},{9,10},{10,... | collective-permute-start | bytes 1572872 | tf_op jit(solution)/shard_map/ppermute | solution.py:524
  481.8 25.3 %collective-permute-start.40 = (bf16[128,512]{1,0:T(8,128)(2,1)S(1)}, bf16[128,512]{1,0:T(8,128)(2,1)S(1)}, u32[]{:S(2)}, u32[]{:S(2)}) collective-permute-start(bf16[128,512]{1,0:T(8,128)(2,1)S(1)} %get-tuple-element.313), channel_id=1, source_target_pairs={{0,2},{1,3},{2,0},{3,1},{4,6},{5,7},{6,4},{7,5},{8,10},{9,11},{10,... | collective-permute-start | bytes 393224 | tf_op jit(solution)/shard_map/ppermute | solution.py:524
  525.2 25.4 %collective-permute-start.24 = (bf16[128,512]{1,0:T(8,128)(2,1)}, bf16[128,512]{1,0:T(8,128)(2,1)S(1)}, u32[]{:S(2)}, u32[]{:S(2)}) collective-permute-start(bf16[128,512]{1,0:T(8,128)(2,1)} %get-tuple-element.322), channel_id=1, source_target_pairs={{0,1},{1,0},{2,3},{3,2},{4,5},{5,4},{6,7},{7,6},{8,9},{9,8},{10,11... | collective-permute-start | bytes 393224 | tf_op jit(solution)/shard_map/ppermute | solution.py:524
  526.2 24.5 %collective-permute-start.25 = (bf16[128,512]{1,0:T(8,128)(2,1)S(1)}, bf16[128,512]{1,0:T(8,128)(2,1)S(1)}, u32[]{:S(2)}, u32[]{:S(2)}) collective-permute-start(bf16[128,512]{1,0:T(8,128)(2,1)S(1)} %get-tuple-element.321), channel_id=1, source_target_pairs={{0,2},{1,3},{2,0},{3,1},{4,6},{5,7},{6,4},{7,5},{8,10},{9,11},{10,... | collective-permute-start | bytes 393224 | tf_op jit(solution)/shard_map/ppermute | solution.py:524
  527.7 23.0 %collective-permute-start.26 = (bf16[128,512]{1,0:T(8,128)(2,1)S(1)}, bf16[128,512]{1,0:T(8,128)(2,1)}, u32[]{:S(2)}, u32[]{:S(2)}) collective-permute-start(bf16[128,512]{1,0:T(8,128)(2,1)S(1)} %get-tuple-element.320), channel_id=1, source_target_pairs={{0,3},{1,2},{2,1},{3,0},{4,7},{5,6},{6,5},{7,4},{8,11},{9,10},{10,... | collective-permute-start | bytes 393224 | tf_op jit(solution)/shard_map/ppermute | solution.py:524
  550.6 49.7 %collective-permute-start.42 = (bf16[4,4,128,256]{3,2,1,0:T(8,128)(2,1)}, bf16[4,4,128,256]{3,2,1,0:T(8,128)(2,1)}, u32[]{:S(2)}, u32[]{:S(2)}) collective-permute-start(bf16[4,4,128,256]{3,2,1,0:T(8,128)(2,1)} %dynamic-slice_bitcast_fusion.1), channel_id=1, source_target_pairs={{0,4},{4,0},{8,12},{12,8},{16,20},{20,16},{24,28},{28,24},{1,5},{5... | collective-permute-start | bytes 3145736 | tf_op jit(solution)/shard_map/ppermute | solution.py:566
  558.7 34.7 %collective-permute-start.68 = (bf16[128,2048]{1,0:T(8,128)(2,1)S(1)}, bf16[128,2048]{1,0:T(8,128)(2,1)}, u32[]{:S(2)}, u32[]{:S(2)}) collective-permute-start(bf16[128,2048]{1,0:T(8,128)(2,1)S(1)} %get-tuple-element.107), channel_id=1, source_target_pairs={{0,1},{1,0},{2,3},{3,2},{4,5},{5,4},{6,7},{7,6},{8,9},{9,8},{10,11... | collective-permute-start | bytes 1572872 | tf_op jit(solution)/shard_map/ppermute | solution.py:524
  559.9 37.6 %collective-permute-start.69 = (bf16[128,2048]{1,0:T(8,128)(2,1)S(1)}, bf16[128,2048]{1,0:T(8,128)(2,1)}, u32[]{:S(2)}, u32[]{:S(2)}) collective-permute-start(bf16[128,2048]{1,0:T(8,128)(2,1)S(1)} %get-tuple-element.107), channel_id=1, source_target_pairs={{0,2},{1,3},{2,0},{3,1},{4,6},{5,7},{6,4},{7,5},{8,10},{9,11},{10,... | collective-permute-start | bytes 1572872 | tf_op jit(solution)/shard_map/ppermute | solution.py:524
  569.3 33.2 %collective-permute-start.27 = (bf16[128,2048]{1,0:T(8,128)(2,1)}, bf16[128,2048]{1,0:T(8,128)(2,1)}, u32[]{:S(2)}, u32[]{:S(2)}) collective-permute-start(bf16[128,2048]{1,0:T(8,128)(2,1)} %get-tuple-element.261), channel_id=1, source_target_pairs={{0,1},{1,0},{2,3},{3,2},{4,5},{5,4},{6,7},{7,6},{8,9},{9,8},{10,11... | collective-permute-start | bytes 1572872 | tf_op jit(solution)/shard_map/ppermute | solution.py:524
  571.8 32.2 %collective-permute-start.72 = (bf16[128,2048]{1,0:T(8,128)(2,1)S(1)}, bf16[128,2048]{1,0:T(8,128)(2,1)}, u32[]{:S(2)}, u32[]{:S(2)}) collective-permute-start(bf16[128,2048]{1,0:T(8,128)(2,1)S(1)} %get-tuple-element.108), channel_id=1, source_target_pairs={{0,2},{1,3},{2,0},{3,1},{4,6},{5,7},{6,4},{7,5},{8,10},{9,11},{10,... | collective-permute-start | bytes 1572872 | tf_op jit(solution)/shard_map/ppermute | solution.py:524
  597.5 21.5 %collective-permute-start.71 = (bf16[128,2048]{1,0:T(8,128)(2,1)S(1)}, bf16[128,2048]{1,0:T(8,128)(2,1)S(1)}, u32[]{:S(2)}, u32[]{:S(2)}) collective-permute-start(bf16[128,2048]{1,0:T(8,128)(2,1)S(1)} %get-tuple-element.108), channel_id=1, source_target_pairs={{0,1},{1,0},{2,3},{3,2},{4,5},{5,4},{6,7},{7,6},{8,9},{9,8},{10,11... | collective-permute-start | bytes 1572872 | tf_op jit(solution)/shard_map/ppermute | solution.py:524
  600.4 47.1 %collective-permute-start.55 = (bf16[4,4,128,256]{3,2,1,0:T(8,128)(2,1)S(1)}, bf16[4,4,128,256]{3,2,1,0:T(8,128)(2,1)S(1)}, u32[]{:S(2)}, u32[]{:S(2)}) collective-permute-start(bf16[4,4,128,256]{3,2,1,0:T(8,128)(2,1)S(1)} %dynamic-slice_bitcast_fusion), channel_id=1, source_target_pairs={{0,4},{4,0},{8,12},{12,8},{16,20},{20,16},{24,28},{28,24},{1,5},{5... | collective-permute-start | bytes 3145736 | tf_op jit(solution)/shard_map/ppermute | solution.py:566
  623.6 21.6 %collective-permute-start.46 = (bf16[4,128,256]{2,1,0:T(8,128)(2,1)S(1)}, bf16[4,128,256]{2,1,0:T(8,128)(2,1)S(1)}, u32[]{:S(2)}, u32[]{:S(2)}) collective-permute-start(bf16[4,128,256]{2,1,0:T(8,128)(2,1)S(1)} %get-tuple-element.250), channel_id=1, source_target_pairs={{16,0},{20,4},{24,8},{28,12},{17,1},{21,5},{25,9},{29,13},{18,2},{... | collective-permute-start | bytes 786440 | tf_op jit(solution)/shard_map/ppermute | solution.py:588
  625.0 21.3 %collective-permute-start.47 = (bf16[4,128,256]{2,1,0:T(8,128)(2,1)S(1)}, bf16[4,128,256]{2,1,0:T(8,128)(2,1)S(1)}, u32[]{:S(2)}, u32[]{:S(2)}) collective-permute-start(bf16[4,128,256]{2,1,0:T(8,128)(2,1)S(1)} %get-tuple-element.249), channel_id=1, source_target_pairs={{0,24},{4,28},{1,25},{5,29},{2,26},{6,30},{3,27},{7,31}} | collective-permute-start | bytes 786440 | tf_op jit(solution)/shard_map/ppermute | solution.py:588
  633.3 27.4 %collective-permute-start.30 = (bf16[128,2048]{1,0:T(8,128)(2,1)S(1)}, bf16[128,2048]{1,0:T(8,128)(2,1)S(1)}, u32[]{:S(2)}, u32[]{:S(2)}) collective-permute-start(bf16[128,2048]{1,0:T(8,128)(2,1)S(1)} %get-tuple-element.228), channel_id=1, source_target_pairs={{0,1},{1,0},{2,3},{3,2},{4,5},{5,4},{6,7},{7,6},{8,9},{9,8},{10,11... | collective-permute-start | bytes 1572872 | tf_op jit(solution)/shard_map/ppermute | solution.py:524
  648.0 21.7 %collective-permute-start.56 = (bf16[4,128,256]{2,1,0:T(8,128)(2,1)S(1)}, bf16[4,128,256]{2,1,0:T(8,128)(2,1)S(1)}, u32[]{:S(2)}, u32[]{:S(2)}) collective-permute-start(bf16[4,128,256]{2,1,0:T(8,128)(2,1)S(1)} %get-tuple-element.253), channel_id=1, source_target_pairs={{0,8},{4,12},{8,16},{12,20},{16,24},{20,28},{1,9},{5,13},{9,17},{1... | collective-permute-start | bytes 786440 | tf_op jit(solution)/shard_map/ppermute | solution.py:588
  672.6 21.6 %collective-permute-start.35 = (bf16[128,2048]{1,0:T(8,128)(2,1)S(1)}, bf16[128,2048]{1,0:T(8,128)(2,1)S(1)}, u32[]{:S(2)}, u32[]{:S(2)}) collective-permute-start(bf16[128,2048]{1,0:T(8,128)(2,1)S(1)} %copy-done.39), channel_id=1, source_target_pairs={{0,2},{1,3},{2,0},{3,1},{4,6},{5,7},{6,4},{7,5},{8,10},{9,11},{10,... | collective-permute-start | bytes 1572872 | tf_op jit(solution)/shard_map/ppermute | solution.py:524
  698.0 24.8 %collective-permute-start.49 = (bf16[128,768]{1,0:T(8,128)(2,1)S(1)}, bf16[128,768]{1,0:T(8,128)(2,1)S(1)}, u32[]{:S(2)}, u32[]{:S(2)}) collective-permute-start(bf16[128,768]{1,0:T(8,128)(2,1)S(1)} %get-tuple-element.300), channel_id=1, source_target_pairs={{0,1},{1,0},{2,3},{3,2},{4,5},{5,4},{6,7},{7,6},{8,9},{9,8},{10,11... | collective-permute-start | bytes 589832 | tf_op jit(solution)/shard_map/ppermute | solution.py:524
  698.6 24.2 %collective-permute-start.50 = (bf16[128,768]{1,0:T(8,128)(2,1)S(1)}, bf16[128,768]{1,0:T(8,128)(2,1)S(1)}, u32[]{:S(2)}, u32[]{:S(2)}) collective-permute-start(bf16[128,768]{1,0:T(8,128)(2,1)S(1)} %get-tuple-element.302), channel_id=1, source_target_pairs={{0,2},{1,3},{2,0},{3,1},{4,6},{5,7},{6,4},{7,5},{8,10},{9,11},{10,... | collective-permute-start | bytes 589832 | tf_op jit(solution)/shard_map/ppermute | solution.py:524
  757.5 26.8 %collective-permute-start.54 = (bf16[128,2048]{1,0:T(8,128)(2,1)S(1)}, bf16[128,2048]{1,0:T(8,128)(2,1)S(1)}, u32[]{:S(2)}, u32[]{:S(2)}) collective-permute-start(bf16[128,2048]{1,0:T(8,128)(2,1)S(1)} %get-tuple-element.222), channel_id=1, source_target_pairs={{0,3},{1,2},{2,1},{3,0},{4,7},{5,6},{6,5},{7,4},{8,11},{9,10},{10,... | collective-permute-start | bytes 1572872 | tf_op jit(solution)/shard_map/ppermute | solution.py:524
  762.2 34.2 %collective-permute-start.38 = (bf16[128,2048]{1,0:T(8,128)(2,1)S(1)}, bf16[128,2048]{1,0:T(8,128)(2,1)S(1)}, u32[]{:S(2)}, u32[]{:S(2)}) collective-permute-start(bf16[128,2048]{1,0:T(8,128)(2,1)S(1)} %collective-permute-done.37), channel_id=1, source_target_pairs={{0,1},{1,0},{2,3},{3,2},{4,5},{5,4},{6,7},{7,6},{8,9},{9,8},{10,11... | collective-permute-start | bytes 1572872 | tf_op jit(solution)/shard_map/ppermute | solution.py:524
  789.8 24.1 %collective-permute-start.67 = (bf16[128,2048]{1,0:T(8,128)(2,1)S(1)}, bf16[128,2048]{1,0:T(8,128)(2,1)S(1)}, u32[]{:S(2)}, u32[]{:S(2)}) collective-permute-start(bf16[128,2048]{1,0:T(8,128)(2,1)S(1)} %get-tuple-element.220), channel_id=1, source_target_pairs={{0,3},{1,2},{2,1},{3,0},{4,7},{5,6},{6,5},{7,4},{8,11},{9,10},{10,... | collective-permute-start | bytes 1572872 | tf_op jit(solution)/shard_map/ppermute | solution.py:524
  (94 other events, 1232.2 us)
Sparse Core Ops, SparseCore 0:
  10.3 40.9 all-gather.6
  52.9 31.1 all-gather.8
  86.2 44.4 all-gather.14
  132.7 115.4 all-gather.10
  249.7 114.9 all-gather.12
  366.9 127.4 reduce-scatter.3
  496.6 131.1 reduce-scatter.5
  737.3 64.7 reduce-scatter.7

commit v3 on v2

--- a/solution.py
+++ b/solution.py
@@ -481,6 +481,469 @@
     )
 
 
+def paired(index, k):
+    bit = 1
+    while bit <= k:
+        if k & bit:
+            index = index + bit - 2 * bit * ((index // bit) % 2)
+        bit *= 2
+    return index
+
+
+def tail_kernel(n_dp, n_tp, group, *refs):
+    (
+        du_refs,
+        y_refs,
+        seed_ref,
+        middle_ref,
+        x_ref,
+        gains_ref,
+        out_refs,
+        qkv_refs,
+        q_ref,
+        kv_ref,
+        qpos_ref,
+        kpos_ref,
+        cos_ref,
+        sin_ref,
+        d_qkv_ref,
+        mid_rows,
+        out_rows,
+        tok_rows,
+        gain_ref,
+    ) = (refs[0:2], refs[2:4]) + refs[4:8] + (refs[8:10], refs[10:12]) + refs[12:23]
+    (
+        weights,
+        du_got,
+        y_got,
+        own_mid,
+        mid_low,
+        block_low,
+        tok_low,
+        do_send,
+        do_got,
+        shares,
+        met,
+        z_send,
+        z_got,
+        heads_got,
+        local_sem,
+        du_s,
+        du_r,
+        y_s,
+        y_r,
+        mid_s,
+        mid_r,
+        block_s,
+        block_r,
+        tok_s,
+        tok_r,
+        do_s,
+        do_r,
+        core_s,
+        core_r,
+        z_s,
+        z_r,
+        heads_s,
+        heads_r,
+    ) = refs[23:]
+    line = n_dp // 2
+    batches = range(MICRO)
+    others = range(1, n_tp)
+    dp, tp = lax.axis_index("dp"), lax.axis_index("tp")
+    place, core = dp // 2, dp % 2
+    depth = middle_ref.shape[1]
+    rows = mid_low.shape[1]
+    seq_rows = q_ref.shape[2]
+    q_width = q_ref.shape[3]
+    kv_width = kv_ref.shape[4]
+    width = q_width + kv_width
+    half = depth // 2
+
+    def rank(k):
+        return (dp, paired(tp, k))
+
+    def spot(k):
+        return (paired(place, k) * 2 + core, tp)
+
+    other_core = (place * 2 + 1 - core, tp)
+
+    def remote(src, dst, send, recv, device):
+        return pltpu.make_async_remote_copy(
+            src_ref=src,
+            dst_ref=dst,
+            send_sem=send,
+            recv_sem=recv,
+            device_id=device,
+            device_id_type=pl.DeviceIdType.MESH,
+        )
+
+    def block(k):
+        return pl.ds(k * rows, rows)
+
+    du_moves = [
+        [
+            remote(
+                du_refs[m].at[block(k)], du_got.at[m, k], du_s.at[m, k], du_r.at[m, k], rank(k)
+            )
+            for k in others
+        ]
+        for m in batches
+    ]
+    y_moves = [
+        [
+            remote(y_refs[m].at[block(k)], y_got.at[m, k], y_s.at[m, k], y_r.at[m, k], rank(k))
+            for k in others
+        ]
+        for m in batches
+    ]
+
+    def row_moves(low, got, send, recv):
+        return [
+            [
+                remote(low.at[m], got.at[m, k], send.at[m, k], recv.at[m, k], rank(k))
+                for k in others
+            ]
+            for m in batches
+        ]
+
+    mid_moves = row_moves(mid_low, mid_rows, mid_s, mid_r)
+    block_moves = row_moves(block_low, out_rows, block_s, block_r)
+    tok_moves = row_moves(tok_low, tok_rows, tok_s, tok_r)
+    do_moves = [
+        [
+            remote(
+                do_send.at[m, k], do_got.at[m, block(k)], do_s.at[m, k], do_r.at[m, k], rank(k)
+            )
+            for k in others
+        ]
+        for m in batches
+    ]
+    core_moves = [
+        remote(shares.at[m, 1 - core], met.at[m], core_s.at[m], core_r.at[m], other_core)
+        for m in batches
+    ]
+    z_moves = [
+        [
+            remote(z_send.at[m, k], z_got.at[m, k], z_s.at[m, k], z_r.at[m, k], spot(k))
+            for k in range(1, line)
+        ]
+        for m in batches
+    ]
+    heads_moves = [
+        [
+            remote(
+                d_qkv_ref.at[m, block(k)],
+                heads_got.at[m, k],
+                heads_s.at[m, k],
+                heads_r.at[m, k],
+                rank(k),
+            )
+            for k in others
+        ]
+        for m in batches
+    ]
+
+    def start(moves):
+        for move in moves:
+            move.start()
+
+    def arrive(moves):
+        for move in moves:
+            move.wait_recv()
+
+    def sent(moves):
+        for move in moves:
+            move.wait_send()
+
+    own_copies = [
+        pltpu.make_async_copy(ref.at[pl.ds(0, rows)], got.at[m, 0], local_sem.at[i, m])
+        for i, (pair, got) in enumerate(((du_refs, du_got), (y_refs, y_got)))
+        for m, ref in enumerate(pair)
+    ]
+    load_out = [
+        pltpu.make_async_copy(
+            ref, weights.at[side, :, pl.ds(0, n_tp * q_width)], local_sem.at[6, side]
+        )
+        for side, ref in enumerate(out_refs)
+    ]
+    load_qkv = [
+        pltpu.make_async_copy(ref, weights.at[side], local_sem.at[2, side])
+        for side, ref in enumerate(qkv_refs)
+    ]
+    keep = [
+        [
+            pltpu.make_async_copy(low.at[m], got.at[m, 0], local_sem.at[3 + i, m])
+            for m in batches
+        ]
+        for i, (low, got) in enumerate(
+            ((mid_low, mid_rows), (block_low, out_rows), (tok_low, tok_rows))
+        )
+    ]
+
+    barrier = pltpu.get_barrier_semaphore()
+    peers = [rank(k) for k in others] + [other_core] + [spot(k) for k in range(1, line)]
+    for peer in peers:
+        pl.semaphore_signal(barrier, inc=1, device_id=peer, device_id_type=pl.DeviceIdType.MESH)
+    pl.semaphore_wait(barrier, len(peers))
+
+    for moves in du_moves:
+        start(moves)
+    start(own_copies)
+    start(load_out)
+    gain_one = gains_ref[0:1, :].astype(F32)
+    gain_two = gains_ref[1:2, :].astype(F32)
+    gain_ref[...] = jnp.zeros_like(gain_ref)
+
+    def total_of(got, m):
+        total = got[m, 0].astype(F32)
+        for k in others:
+            total = total + got[m, k].astype(F32)
+        return total
+
+    for copy in own_copies:
+        copy.wait()
+    for m in batches:
+        part = slice(m * rows, (m + 1) * rows)
+        arrive(du_moves[m])
+        d_mixed = total_of(du_got, m)
+        middle = middle_ref[part, :]
+        scale = mean_square_scale(middle)
+        normed = middle * scale
+        gain_ref[1:2, :] += jnp.sum(d_mixed * normed, axis=0, keepdims=True)
+        d_middle = seed_ref[part, :].astype(F32) + norm_back(d_mixed * gain_two, normed, scale)
+        own_mid[m] = d_middle
+        mid_low[m] = d_middle.astype(BF16)
+        if m == 0:
+            for copy in load_out:
+                copy.wait()
+        near_cols = pl.ds(pl.multiple_of(core * half, half), half)
+        far_cols = pl.ds(pl.multiple_of((1 - core) * half, half), half)
+        near, far = mid_low[m, :, near_cols], mid_low[m, :, far_cols]
+        for k in range(n_tp):
+            lanes = slice(k * q_width, (k + 1) * q_width)
+            rows_out = (dot(near, weights[0, :, lanes]) + dot(far, weights[1, :, lanes])).astype(
+                BF16
+            )
+            if k == 0:
+                do_got[m, 0:rows, :] = rows_out
+            else:
+                do_send[m, k] = rows_out
+        start(do_moves[m])
+    start(load_qkv)
+    for m in batches:
+        start(mid_moves[m])
+        keep[0][m].start()
+        start(y_moves[m])
+
+    def attend_back_seq(m, s):
+        seq = pl.ds(s * seq_rows, seq_rows)
+        for h in range(kv_width // (2 * HD)):
+            pair = slice(h * 2 * HD, (h + 1) * 2 * HD)
+            keyvals = kv_ref[:, m, s, :, pair].reshape(-1, 2 * HD)
+            grads = None
+            for part in range(group // 2):
+                lanes = slice((h * group + 2 * part) * HD, (h * group + 2 * part + 2) * HD)
+                q_pad = stack_heads(q_ref[m, s, :, lanes], 2, False)
+                do_pad = stack_heads(do_got[m, seq, lanes], 2, True)
+                probs = scores_and_probs(q_pad, keyvals, qpos_ref[...], kpos_ref[...], 2)
+                d_probs = dot_nt(do_pad, keyvals)
+                d_scores = probs * (d_probs - jnp.sum(d_probs * probs, axis=-1, keepdims=True))
+                ds_low = d_scores.astype(BF16) * HD ** (-0.5)
+                dq = unstack_heads(dot(ds_low, keyvals), 2, False)
+                cos_q, sin_q = cos_ref[:, 0 : 2 * HD], sin_ref[:, 0 : 2 * HD]
+                dq = dq * cos_q + half_turn(dq * sin_q)
+                d_qkv_ref[m, seq, lanes] = dq.astype(BF16)
+                term = dot_tn(ds_low, q_pad) + dot_tn(probs.astype(BF16), do_pad)
+                grads = term if grads is None else grads + term
+            grads = grads.astype(BF16)
+            for i in range(n_dp):
+                shares[m, i % 2, i // 2, seq, pair] = grads[i * seq_rows : (i + 1) * seq_rows]
+
+    def attend_back_range(m, low, high):
+        @pl.loop(low, high)
+        def _(s):
+            attend_back_seq(m, s)
+
+    def send_along(m):
+        arrive([core_moves[m]])
+        for k in range(1, line):
+            there = paired(place, k)
+            z_send[m, k] = (
+                shares[m, core, there].astype(F32) + met[m, there].astype(F32)
+            ).astype(BF16)
+        start(z_moves[m])
+
+    def close_keys(m):
+        arrive(z_moves[m])
+        total = shares[m, core, place].astype(F32) + met[m, place].astype(F32)
+        for k in range(1, line):
+            total = total + z_got[m, k].astype(F32)
+        cos_k, sin_k = cos_ref[:, q_width:], sin_ref[:, q_width:]
+        for s in range(SEQS):
+            seq = slice(s * seq_rows, (s + 1) * seq_rows)
+            grad = total[seq]
+            d_qkv_ref[m, seq, q_width:] = (grad * cos_k + half_turn(grad * sin_k)).astype(BF16)
+        start(heads_moves[m])
+
+    def close_block(m):
+        arrive(y_moves[m])
+        part = slice(m * rows, (m + 1) * rows)
+        block_low[m] = (middle_ref[part, :] + total_of(y_got, m)).astype(BF16)
+        start(block_moves[m])
+        keep[1][m].start()
+
+    def close_tokens(m):
+        arrive(heads_moves[m])
+        part = slice(m * rows, (m + 1) * rows)
+        heads = [d_qkv_ref[m, 0:rows, :]] + [heads_got[m, k] for k in others]
+        sides = []
+        for side in range(2):
+            total = dot_nt(heads[0], weights[side, :, 0:width])
+            for k in others:
+                total = total + dot_nt(heads[k], weights[side, :, k * width : (k + 1) * width])
+            sides.append(total)
+        d_act = jnp.where(
+            core == 0,
+            jnp.concatenate(sides, axis=1),
+            jnp.concatenate(sides[::-1], axis=1),
+        )
+        x_part = x_ref[part, :].astype(F32)
+        scale = mean_square_scale(x_part)
+        normed = x_part * scale
+        gain_ref[0:1, :] += jnp.sum(d_act * normed, axis=0, keepdims=True)
+        tok_low[m] = (own_mid[m] + norm_back(d_act * gain_one, normed, scale)).astype(BF16)
+        start(tok_moves[m])
+        keep[2][m].start()
+
+    arrive(do_moves[0])
+    attend_back_range(0, 0, SEQS)
+    core_moves[0].start()
+    arrive(do_moves[1])
+    attend_back_range(1, 0, SEQS // 2)
+    send_along(0)
+    attend_back_range(1, SEQS // 2, SEQS)
+    core_moves[1].start()
+    for copy in load_qkv:
+        copy.wait()
+    close_keys(0)
+    send_along(1)
+    close_tokens(0)
+    close_block(0)
+    close_keys(1)
+    close_tokens(1)
+    close_block(1)
+    for m in batches:
+        for moves in (mid_moves[m], block_moves[m], tok_moves[m]):
+            arrive(moves)
+            sent(moves)
+        for moves in (du_moves[m], y_moves[m], do_moves[m], [core_moves[m]], z_moves[m]):
+            sent(moves)
+        sent(heads_moves[m])
+        for copies in keep:
+            copies[m].wait()
+
+
+def tail(
+    n_dp, n_tp, group, sums, seed, middle, x, gains, out_w, qkv_w, q, kv, qpos, kpos, cos, sin
+):
+    own_rows, depth = middle.shape
+    rows = own_rows // MICRO
+    batch_rows = n_tp * rows
+    line = n_dp // 2
+    q_width, kv_width = q.shape[3], kv.shape[4]
+    width = q_width + kv_width
+    anywhere = pl.BlockSpec(memory_space=pl.ANY)
+    vmem = pl.BlockSpec(memory_space=pltpu.VMEM)
+    dma = pltpu.SemaphoreType.DMA
+    gathered = jax.ShapeDtypeStruct((MICRO, n_tp, rows, depth), BF16)
+    return pl.pallas_call(
+        functools.partial(tail_kernel, n_dp, n_tp, group),
+        in_specs=[anywhere] * 4 + [vmem] * 4 + [anywhere] * 4 + [vmem] * 6,
+        out_specs=[vmem] + [anywhere] * 3 + [vmem],
+        out_shape=[
+            jax.ShapeDtypeStruct((MICRO, batch_rows, width), BF16),
+            gathered,
+            gathered,
+            gathered,
+            jax.ShapeDtypeStruct((2, depth), F32),
+        ],
+        scratch_shapes=[
+            pltpu.VMEM((2, depth // 2, n_tp * width), BF16),
+            pltpu.VMEM((MICRO, n_tp, rows, depth), BF16),
+            pltpu.VMEM((MICRO, n_tp, rows, depth), BF16),
+            pltpu.VMEM((MICRO, rows, depth), F32),
+            pltpu.VMEM((MICRO, rows, depth), BF16),
+            pltpu.VMEM((MICRO, rows, depth), BF16),
+            pltpu.VMEM((MICRO, rows, depth), BF16),
+            pltpu.VMEM((MICRO, n_tp, rows, q_width), BF16),
+            pltpu.VMEM((MICRO, batch_rows, q_width), BF16),
+            pltpu.VMEM((MICRO, 2, line, batch_rows, kv_width), BF16),
+            pltpu.VMEM((MICRO, line, batch_rows, kv_width), BF16),
+            pltpu.VMEM((MICRO, line, batch_rows, kv_width), BF16),
+            pltpu.VMEM((MICRO, line, batch_rows, kv_width), BF16),
+            pltpu.VMEM((MICRO, n_tp, rows, width), BF16),
+            dma((7, 2)),
+        ]
+        + [dma((MICRO, n_tp))] * 12
+        + [dma((MICRO,))] * 2
+        + [dma((MICRO, line))] * 2
+        + [dma((MICRO, n_tp))] * 2,
+        compiler_params=pltpu.CompilerParams(
+            collective_id=0, has_side_effects=True, vmem_limit_bytes=VMEM_LIMIT
+        ),
+        cost_estimate=hint(
+            flops=10**10,
+            bytes_accessed=10**8,
+            transcendentals=0,
+        ),
+        name="tail",
+    )(
+        sums[0][1],
+        sums[1][1],
+        sums[0][0],
+        sums[1][0],
+        seed,
+        middle,
+        x,
+        gains,
+        *out_w,
+        *qkv_w,
+        q,
+        kv,
+        qpos,
+        kpos,
+        cos,
+        sin,
+    )
+
+
+def spread_kernel(rank_ref, out_ref, tok_ref, block_ref, grad_ref):
+    block_ref[...] = out_ref[...]
+    grad_ref[...] = tok_ref[...].astype(F32)
+
+
+def spread(rank, out_rows, tok_rows):
+    micro, n_tp, rows, depth = out_rows.shape
+    here = pl.BlockSpec((1, 1, rows, depth), lambda m, k, r: (m, k, 0, 0))
+    there = pl.BlockSpec((1, 1, rows, depth), lambda m, k, r: (m, r[0] ^ k, 0, 0))
+    return pl.pallas_call(
+        spread_kernel,
+        grid_spec=pltpu.PrefetchScalarGridSpec(
+            num_scalar_prefetch=1,
+            grid=(micro, n_tp),
+            in_specs=[here, here],
+            out_specs=[there, there],
+        ),
+        out_shape=[
+            jax.ShapeDtypeStruct(out_rows.shape, BF16),
+            jax.ShapeDtypeStruct(out_rows.shape, F32),
+        ],
+        compiler_params=pltpu.CompilerParams(vmem_limit_bytes=VMEM_LIMIT),
+        name="spread",
+    )(rank, out_rows, tok_rows)
+
+
 def per_device(
     n_dp,
     n_tp,
@@ -665,20 +1128,19 @@
 
     qkv_half = after(my_half(qkv_full), u[0])
     quarter = depth // 4
-    qkv_quarters = [qkv_half[:quarter], qkv_half[quarter:]]
+    qkv_width = q_width + kv_width
+    qkv_near = jnp.zeros((depth // 2, n_tp * qkv_width), BF16)
+    qkv_near = lax.dynamic_update_slice(qkv_near, qkv_half, (0, 0))
     qkv_moves = [(k, i) for i in range(2) for k in range(1, min(n_tp, 3))]
     qkv_moves = [qkv_moves[:2], qkv_moves[2:]] + [
         [(k, i) for k in range(3, n_tp)] for i in range(2)
     ]
-    qkv_got = {}
-
-    def move_qkv():
-        if not qkv_moves:
-            return []
-        now = qkv_moves.pop(0)
-        for k, i in now:
-            qkv_got[k, i] = swap(qkv_quarters[i], k)
-        return [qkv_got[move] for move in now]
+
+    def move_qkv(buffer):
+        for k, i in qkv_moves.pop(0) if qkv_moves else []:
+            got = swap(qkv_half[i * quarter : (i + 1) * quarter], k)
+            buffer = lax.dynamic_update_slice(buffer, got, (i * quarter, k * qkv_width))
+        return buffer
 
     def blocks_of(value):
         return [value[k * block_rows : (k + 1) * block_rows] for k in range(n_tp)]
@@ -713,121 +1175,55 @@
         hids, dgus = [], []
         for m in batches:
             hid, dgu = expand(c, m, *earlier)
-            earlier = [hid] + move_qkv()
+            qkv_near = move_qkv(qkv_near)
+            earlier = [hid, qkv_near]
             hids.append(hid)
             dgus.append(dgu)
         grads, owned = close(hids, dgus, *earlier)
-        earlier = [grads] + move_qkv()
+        qkv_near = move_qkv(qkv_near)
+        earlier = [grads, qkv_near]
         chunk_grads.append(owned)
 
     d_middles, d_mid_lows, d_attends, all_rows = [], [], [], []
     hids, dgus = [], []
     for m in batches:
         hid, dgu = expand(CHUNKS - 1, m, *earlier)
-        earlier = [hid] + move_qkv()
+        qkv_near = move_qkv(qkv_near)
+        earlier = [hid, qkv_near]
+        if m == 0:
+            qkv_far = swap_cores(qkv_near)
         hids.append(hid)
         dgus.append(dgu)
-    qkv_near = [qkv_half] + [
-        jnp.concatenate([qkv_got[k, i] for i in range(2)], axis=0) for k in range(1, n_tp)
-    ]
-    qkv_near = after(jnp.concatenate(qkv_near, axis=1), *earlier)
-    qkv_far = swap_cores(qkv_near)
-    for m in batches:
-        if m == 1:
-            grads, owned = close(hids, dgus, all_rows[0], qkv_near)
-            chunk_grads.append(owned)
-            earlier = [grads, qkv_far]
-        got = exchange(blocks_of(sums[m][1]))
-        d_mixed = total_of([after(got[0], *(earlier if m else []))] + got[1:])
-        normed = own_part(normed_two, m)
-        gain_grads[1] = gain_grads[1] + jnp.sum(d_mixed * normed, axis=0)
-        d_middle = seed[m, 0].astype(F32) + norm_back(
-            d_mixed * gain_two_f, normed, own_part(scale_two, m)
-        )
-        d_mid_low = d_middle.astype(BF16)
-        near, far = (
-            lax.dynamic_slice_in_dim(d_mid_low, side * (depth // 2), depth // 2, axis=1)
-            for side in (core, 1 - core)
-        )
-        do_rows = (dot(near, out_near) + dot(far, out_far)).astype(BF16)
-        all_rows.append(do_rows)
-        do_blocks = [do_rows[:, k * q_width : (k + 1) * q_width] for k in range(n_tp)]
-        d_attends.append(jnp.concatenate(exchange(do_blocks), axis=0).reshape((1,) + q.shape[1:]))
-        d_middles.append(d_middle)
-        d_mid_lows.append(d_mid_low)
-
-    y_stages = scatter_pair([blocks_of(after(sums[m][0], d_attends[-1])) for m in batches])
-    y_sends = next(y_stages)
-    d_queries, kv_stages = [], []
-    for m in batches:
-        waits = [all_rows[-1]] if m == 0 else y_sends
-        d_query_low, d_kv_part = attend_back(
-            qpos,
-            kpos,
-            cos_q,
-            sin_q,
-            q[m : m + 1],
-            after(d_attends[m], *waits),
-            kv_all[:, m : m + 1],
-            group,
-        )
-        d_queries.append(d_query_low[0])
-        by_core = d_kv_part.reshape((line, 2) + d_kv_part.shape[2:])
-        kv_stages.append(
-            line_sum(
-                lax.dynamic_index_in_dim(by_core, 1 - core, 1, False),
-                lax.dynamic_index_in_dim(by_core, core, 1, False),
-            )
-        )
-    blocks_own = [own_part(middle, m) + total for m, total in enumerate(next(y_stages))]
-    d_mid_rows = gather_pair([after(v, d_attends[-1]) for v in d_mid_lows])
-    d_mid_rows = jnp.concatenate(
-        [d_mid_rows[k][m] for m in batches for k in range(n_tp)], axis=0
-    )
-    out_rows = gather_pair([value.astype(BF16) for value in blocks_own])
-
-    block_output = jnp.zeros((MICRO, n_tp, block_rows, depth), BF16)
-    grad_tokens = jnp.zeros((MICRO, n_tp, block_rows, depth), F32)
-
-    def placed(buffer, m, blocks):
-        for k in range(n_tp):
-            piece = blocks[k].astype(buffer.dtype)[None, None]
-            buffer = lax.dynamic_update_slice(buffer, piece, (m, rank ^ k, 0, 0))
-        return buffer
-
-    lane = jnp.arange(kv_width)
-    d_qkvs = []
-    for m in batches:
-        block_output = placed(block_output, m, [out_rows[k][m] for k in range(n_tp)])
-        own_grad = list(kv_stages[m])[-1][0]
-        own_grad = after(own_grad, *(blocks_own if m == 0 else []))
-        scaled = own_grad * sin_k
-        turned = jnp.where(
-            lane % HD < HD // 2,
-            jnp.roll(scaled, -(HD // 2), axis=-1),
-            jnp.roll(scaled, HD // 2, axis=-1),
-        )
-        d_kv_low = (own_grad * cos_k + turned).astype(BF16)
-        d_qkv = jnp.concatenate([d_queries[m], d_kv_low], axis=-1)
-        d_qkv = d_qkv.reshape(batch_rows, q_width + kv_width)
-        d_qkvs.append(d_qkv)
-        d_heads = exchange(blocks_of(d_qkv))
-        heads_cat = jnp.concatenate(d_heads, axis=1)
-        d_act = both_halves(dot_nt(heads_cat, qkv_near), dot_nt(heads_cat, qkv_far))
-        x_part = own_part(x_own, m)
-        scale_one = mean_square_scale(x_part)
-        normed_one = x_part * scale_one
-        gain_grads[0] = gain_grads[0] + jnp.sum(d_act * normed_one, axis=0)
-        tokens_own = d_middles[m] + norm_back(d_act * gain_one_f, normed_one, scale_one)
-        tokens_low = tokens_own.astype(BF16)
-        grad_tokens = placed(
-            grad_tokens, m, [tokens_low] + [swap(tokens_low, k) for k in range(1, n_tp)]
-        )
-    mlp_grads = [v.reshape(own_depth, -1) for v in chunk_grads]
+    grads, owned = close(hids, dgus, *earlier, qkv_far)
+    chunk_grads.append(owned)
+    tail_sums = [after(sums[0], grads)] + sums[1:]
+    d_qkv, mid_rows, out_rows, tok_rows, gain_part = tail(
+        n_dp,
+        n_tp,
+        group,
+        tail_sums,
+        seed[:, 0].reshape(own_rows, depth),
+        middle,
+        x[:, 0].reshape(own_rows, depth),
+        gains_full,
+        (out_near, out_far),
+        (qkv_near, qkv_far),
+        q,
+        kv_all,
+        qpos,
+        kpos,
+        cos_t,
+        sin_t,
+    )
+    block_output, grad_tokens = spread(rank.astype(jnp.int32).reshape(1), out_rows, tok_rows)
     block_output = block_output.reshape(rows, depth)
     grad_tokens = grad_tokens.reshape(rows, depth)
+    d_mid_rows = mid_rows.reshape(rows, depth)
+    d_qkvs = [d_qkv.reshape(rows, q_width + kv_width)]
+    gain_grads = [gain_part[0], gain_part[1]]
 
     out_grad_t = dot_tn(d_mid_rows, attended.reshape(rows, q_width)).astype(BF16)
+    mlp_grads = [v.reshape(own_depth, -1) for v in chunk_grads]
     qkv_grad = dot_tn(attn_in, jnp.concatenate(d_qkvs, axis=0)).astype(BF16)
     gain_cols = jnp.stack(gain_grads, axis=1)
     gain_cols = jnp.pad(gain_cols, ((0, 0), (0, 126))).astype(BF16)

time: 867 us -> 823 us (0.949)
  Pallas kernels: 227 us -> 477 us
  starting transfers between devices: 110 us -> 23.3 us
  waiting for transfers between devices: 277 us -> 195 us
  other arithmetic: 87.4 us -> 30.2 us
  matrix products: 50 us -> 17 us
  local copies, waits for them, and re-layouts: 80.4 us -> 47.9 us
    pallas_call x2, Pallas kernels: 38.9 us -> 287 us  [the longest x1 277 us: tail(): pl.pallas_call(functools.partial(tail_kernel, n_dp, n_tp, group), in_spec...]
    ppermute x61 -> x19, waiting for transfers between devices: 198 us -> 127 us  [swap(): return lax.ppermute(value, 'tp', [(i, i ^ k) for i in range(n_tp)])]
    ppermute x61 -> x19, starting transfers between devices: 70.4 us -> 22.5 us  [swap(): return lax.ppermute(value, 'tp', [(i, i ^ k) for i in range(n_tp)])]
    ppermute x14 -> x0, starting transfers between devices: 38.2 us -> none  [the longest x12 38.2 us: line_sum(): arrived.append(lax.ppermute(value, 'dp', pairs))]
    reduce_scatter x1, waiting for transfers between devices: 0.02 us -> 28.8 us  [per_device(): lax.psum_scatter(after(jnp.concatenate([qkv_grad, out_grad_t, gain_cols],...]
    concatenate x3 -> x0, other arithmetic: 25.8 us -> none  [the longest x1 23.2 us: per_device(): qkv_near = after(jnp.concatenate(qkv_near, axis=1), *earlier)]
    all_gather x2, waiting for transfers between devices: 32.8 us -> 10.9 us  [per_device(): mlp_full.append(lax.all_gather(shard, 'dp', axis=0, tiled=True))]
    dot_general x6 -> x2, matrix products: 22.1 us -> 6.99 us  [dot_nt(): lax.dot_general(left, right, (((1,), (1,)), ((), ())), preferred_element_...]
  transfers between devices with their start and end apart: 85 -> 29, of which waited for: 29 -> 15; matrix products, arithmetic and copies ran while one was open for 24% -> 10% of each run, Pallas kernels for 26% -> 58%
where the time goes in v3:
time: 823 us; the launch traced here: 818 us
  Pallas kernels  477 us (58%)
  waiting for transfers between devices  195 us (24%)
  local copies, waits for them, and re-layouts  47.9 us (6%)
  other arithmetic  30.2 us (4%)
  starting transfers between devices  23.3 us (3%)
  matrix products  17 us (2%)
  between operations  14.9 us (2%)
  blocking collectives  13.5 us (2%)
    pallas_call x1, Pallas kernels, tail(): pl.pallas_call(functools.partial(tail_kernel, n_dp, n_tp, group), in_spec...  277 us
    ppermute x19, waiting for transfers between devices, swap(): return lax.ppermute(value, 'tp', [(i, i ^ k) for i in range(n_tp)])  127 us
    pallas_call x4, Pallas kernels, feed_forward(): pl.pallas_call(functools.partial(gated_kernel, last, steps), grid=(steps,...  89.3 us
    pallas_call x2, Pallas kernels, outer_products(): pl.pallas_call(functools.partial(outer_kernel, batches, sub, steps, half)...  39.1 us
    pallas_call x1, Pallas kernels, attend(): pl.pallas_call(functools.partial(attend_kernel, group), grid=(micro, seqs...  29.1 us
    reduce_scatter x1, waiting for transfers between devices, per_device(): lax.psum_scatter(after(jnp.concatenate([qkv_grad, out_grad_t, gain_cols],...  28.8 us
    ppermute x19, starting transfers between devices, swap(): return lax.ppermute(value, 'tp', [(i, i ^ k) for i in range(n_tp)])  22.5 us
    unnamed x69, local copies, waits for them, and re-layouts  22 us
  transfers between devices with their start and end apart: 29, of which 15 were waited for; matrix products, arithmetic and copies ran while one was open for 10% of the time, Pallas kernels for 58%

profile of v3, /device:TPU:0, one launch (start us, length us, event | category | flops | bytes accessed | tf_op | source)
XLA Modules:
  0.0 818.0 jit_solution(2390608826395066952)
XLA Ops:
  7.2 1.8 pad_maximum_fusion.7
  9.1 1.8 copy.162
  14.6 13.5 %all_gather.21.refs_7_ = bf16[2,2048]{1,0:T(2,128)(2,1)S(1)} all-gather(bf16[2,256]{1,0:T(2,128)(2,1)S(1)} %copy-done.19), channel_id=1, replica_groups=mesh['dp'=8,'tp'=4] {'dp'}, dimensions={1}, use_global_device_ids=true | all-gather | bytes 9216 | tf_op jit(solution)/shard_map/all_gather | solution.py:1077
  28.0 2.7 constant_dynamic-slice_fusion.10
  30.8 2.3 pad_maximum_fusion.1
  33.7 17.6 %all-gather.7.cloned.1.call-done.w_ref = bf16[2048,768]{1,0:T(8,128)(2,1)} async-done(((bf16[256,768]{1,0:T(8,128)(2,1)}), bf16[2048,768]{1,0:T(8,128)(2,1)}) %all-gather.7.cloned.1.call-update) | async-done | bytes 3145744 | tf_op jit(solution)/shard_map/all_gather | solution.py:1074
  51.3 11.0 %project.1 = (bf16[1024,2048]{1,0:T(8,128)(2,1)}, bf16[1024,768]{1,0:T(8,128)(2,1)}) custom-call(bf16[1024,2048]{1,0:T(8,128)(2,1)} %bitcast.99, bf16[1,2048]{1,0:T(2,128)(2,1)} %get-tuple-element.268.gain_ref, bf16[2048,768]{1,0:T(8,128)(2,1)} %all-gather.7.cloned.1.call-done.w_ref, f32[128,768]{1,0:T(8,128)} %concatenate.71.cos_ref.refs_16_, ...), custom_call_target="tpu_custom_call" | custom-call | flops 161061280 | bytes 419430 | tf_op jit(solution)/shard_map/project/pallas_call | solution.py:79
  62.3 2.0 slice.182
  64.4 2.3 copy.171
  71.1 10.4 %all-gather.9.cloned.1.call-done = bf16[2048,512]{1,0:T(8,128)(2,1)} async-done(((bf16[256,512]{1,0:T(8,128)(2,1)}), bf16[2048,512]{1,0:T(8,128)(2,1)}) %all-gather.9.cloned.1.call-update) | async-done | bytes 2097168 | tf_op jit(solution)/shard_map/all_gather | solution.py:1078
  82.8 2.4 collective-permute-start.5
  86.3 23.4 %collective-permute-done.5 = bf16[1024,512]{1,0:T(8,128)(2,1)S(1)} collective-permute-done((bf16[1024,512]{1,0:T(8,128)(2,1)S(1)}, bf16[1024,512]{1,0:T(8,128)(2,1)S(1)}, u32[]{:S(2)}, u32[]{:S(2)}) %collective-permute-start.5) | collective-permute-done | bytes 1048608 | tf_op jit(solution)/shard_map/ppermute | solution.py:987
  109.8 21.7 %collective-permute-done.4 = bf16[1024,512]{1,0:T(8,128)(2,1)S(1)} collective-permute-done((bf16[1024,512]{1,0:T(8,128)(2,1)S(1)}, bf16[1024,512]{1,0:T(8,128)(2,1)S(1)}, u32[]{:S(2)}, u32[]{:S(2)}) %collective-permute-start.4) | collective-permute-done | bytes 1048608 | tf_op jit(solution)/shard_map/ppermute | solution.py:987
  131.6 2.3 pad_maximum_fusion.2.refs_8_
  136.4 29.1 %attend.1 = bf16[2,4,128,512]{3,2,1,0:T(8,128)(2,1)} custom-call(s32[128,1]{1,0:T(8,128)} %copy.161.qpos_ref.refs_14_, s32[1,1024]{1,0:T(1,128)} %add.182.kpos_ref.refs_15_, bf16[2,4,128,512]{3,2,1,0:T(8,128)(2,1)} %slice.181.q_ref.refs_12_, bf16[8,2,4,128,256]{4,3,2,1,0:T(8,128)(2,1)} %bitcast.100), custom_call_target="tpu_custom_call" | custom-call | flops 429496736 | bytes 314572 | tf_op jit(solution)/shard_map/attend/pallas_call | solution.py:192
  170.4 6.5 collective-permute-done.2
  176.9 5.2 collective-permute-done.1
  182.1 3.5 fusion.11
  185.7 3.5 fusion.10
  189.7 2.1 multiply_convert_fusion
  196.1 20.8 %collective-permute-done.7 = bf16[256,2048]{1,0:T(8,128)(2,1)S(1)} collective-permute-done((bf16[256,2048]{1,0:T(8,128)(2,1)S(1)}, bf16[256,2048]{1,0:T(8,128)(2,1)S(1)}, u32[]{:S(2)}, u32[]{:S(2)}) %collective-permute-start.7) | collective-permute-done | bytes 1048608 | tf_op jit(solution)/shard_map/ppermute | solution.py:987
  221.1 9.7 %collective-permute-done.9 = bf16[128,2048]{1,0:T(8,128)(2,1)S(1)} collective-permute-done((bf16[128,2048]{1,0:T(8,128)(2,1)S(1)}, bf16[128,2048]{1,0:T(8,128)(2,1)S(1)}, u32[]{:S(2)}, u32[]{:S(2)}) %collective-permute-start.9) | collective-permute-done | bytes 524320 | tf_op jit(solution)/shard_map/ppermute | solution.py:987
  235.7 2.5 fusion.23
  239.2 3.5 dynamic_update_slice.21
  244.1 10.0 %collective-permute-done.11 = bf16[512,768]{1,0:T(8,128)(2,1)S(1)} collective-permute-done((bf16[512,768]{1,0:T(8,128)(2,1)S(1)}, bf16[512,768]{1,0:T(8,128)(2,1)S(1)}, u32[]{:S(2)}, u32[]{:S(2)}) %collective-permute-start.11) | collective-permute-done | bytes 786464 | tf_op jit(solution)/shard_map/ppermute | solution.py:987
  256.1 23.1 %feed_forward.4 = (bf16[512,1024]{1,0:T(8,128)(2,1)}, bf16[512,2048]{1,0:T(8,128)(2,1)}, bf16[512,2048]{1,0:T(8,128)(2,1)}, bf16[512,2048]{1,0:T(8,128)(2,1)}) custom-call(bf16[512,2048]{1,0:T(8,128)(2,1)} %pad_maximum_fusion.4.u_ref.refs_0_, bf16[512,2048]{1,0:T(8,128)(2,1)} %bitcast.94, bf16[2048,3072]{1,0:T(8,128)(2,1)} %all-gather.11.cloned.1.call-done.w_ref), custom_call_target="tpu_custom_call" | custom-call | flops 644245120 | bytes 1048576 | tf_op jit(solution)/shard_map/feed_forward/pallas_call | solution.py:315
  279.1 21.9 %feed_forward.5 = (bf16[512,1024]{1,0:T(8,128)(2,1)}, bf16[512,2048]{1,0:T(8,128)(2,1)}, bf16[512,2048]{1,0:T(8,128)(2,1)}, bf16[512,2048]{1,0:T(8,128)(2,1)}) custom-call(bf16[512,2048]{1,0:T(8,128)(2,1)} %pad_maximum_fusion.5.u_ref.refs_1_, bf16[512,2048]{1,0:T(8,128)(2,1)} %bitcast.90, bf16[2048,3072]{1,0:T(8,128)(2,1)} %all-gather.11.cloned.1.call-done.w_ref), custom_call_target="tpu_custom_call" | custom-call | flops 644245120 | bytes 1048576 | tf_op jit(solution)/shard_map/feed_forward/pallas_call | solution.py:315
  302.9 19.4 %outer_products.2 = bf16[8,256,3072]{2,1,0:T(8,128)(2,1)} custom-call(s32[1]{0:T(128)} %bitcast.24.core_ref, bf16[512,2048]{1,0:T(8,128)(2,1)} %pad_maximum_fusion.4.u_ref.refs_0_, bf16[512,2048]{1,0:T(8,128)(2,1)} %pad_maximum_fusion.5.u_ref.refs_1_, bf16[512,2048]{1,0:T(8,128)(2,1)} %bitcast.95, bf16[512,2048]{1,0:T(8,128)(2,1)} %bitcast.91, ...), custom_call_target="tpu_custom_call" | custom-call | flops 644245120 | bytes 629145 | tf_op jit(solution)/shard_map/outer_products/pallas_call | solution.py:411
  322.4 2.0 collective-permute-start.15
  325.4 18.5 %collective-permute-done.15 = bf16[512,768]{1,0:T(8,128)(2,1)S(1)} collective-permute-done((bf16[512,768]{1,0:T(8,128)(2,1)S(1)}, bf16[512,768]{1,0:T(8,128)(2,1)S(1)}, u32[]{:S(2)}, u32[]{:S(2)}) %collective-permute-start.15) | collective-permute-done | bytes 786464 | tf_op jit(solution)/shard_map/ppermute | solution.py:987
  344.8 9.3 %collective-permute-done.16 = bf16[512,768]{1,0:T(8,128)(2,1)S(1)} collective-permute-done((bf16[512,768]{1,0:T(8,128)(2,1)S(1)}, bf16[512,768]{1,0:T(8,128)(2,1)S(1)}, u32[]{:S(2)}, u32[]{:S(2)}) %collective-permute-start.16) | collective-permute-done | bytes 786464 | tf_op jit(solution)/shard_map/ppermute | solution.py:987
  355.0 10.9 %all-gather.13.cloned.1.call-done.w_ref = bf16[2048,3072]{1,0:T(8,128)(2,1)} async-done(((bf16[256,3072]{1,0:T(8,128)(2,1)}), bf16[2048,3072]{1,0:T(8,128)(2,1)}) %all-gather.13.cloned.1.call-update) | async-done | bytes 12582928 | tf_op jit(solution)/shard_map/all_gather | solution.py:1109
  365.9 22.3 %feed_forward.6 = (bf16[512,1024]{1,0:T(8,128)(2,1)}, bf16[512,2048]{1,0:T(8,128)(2,1)}, bf16[512,2048]{1,0:T(8,128)(2,1)}, bf16[512,2048]{1,0:T(8,128)(2,1)}) custom-call(bf16[512,2048]{1,0:T(8,128)(2,1)} %pad_maximum_fusion.4.u_ref.refs_0_, bf16[512,2048]{1,0:T(8,128)(2,1)} %bitcast.96, bf16[2048,3072]{1,0:T(8,128)(2,1)} %all-gather.13.cloned.1.call-done.w_ref, ...), custom_call_target="tpu_custom_call" | custom-call | flops 644245120 | bytes 1048576 | tf_op jit(solution)/shard_map/feed_forward/pallas_call | solution.py:315
  388.2 22.0 %feed_forward.7 = (bf16[512,1024]{1,0:T(8,128)(2,1)}, bf16[512,2048]{1,0:T(8,128)(2,1)}, bf16[512,2048]{1,0:T(8,128)(2,1)}, bf16[512,2048]{1,0:T(8,128)(2,1)}) custom-call(bf16[512,2048]{1,0:T(8,128)(2,1)} %pad_maximum_fusion.5.u_ref.refs_1_, bf16[512,2048]{1,0:T(8,128)(2,1)} %bitcast.92, bf16[2048,3072]{1,0:T(8,128)(2,1)} %all-gather.13.cloned.1.call-done.w_ref, ...), custom_call_target="tpu_custom_call" | custom-call | flops 644245120 | bytes 1048576 | tf_op jit(solution)/shard_map/feed_forward/pallas_call | solution.py:315
  410.2 19.7 %outer_products.3 = bf16[8,256,3072]{2,1,0:T(8,128)(2,1)} custom-call(s32[1]{0:T(128)} %bitcast.24.core_ref, bf16[512,2048]{1,0:T(8,128)(2,1)} %pad_maximum_fusion.4.u_ref.refs_0_, bf16[512,2048]{1,0:T(8,128)(2,1)} %pad_maximum_fusion.5.u_ref.refs_1_, bf16[512,2048]{1,0:T(8,128)(2,1)} %bitcast.97, bf16[512,2048]{1,0:T(8,128)(2,1)} %bitcast.93, ...), custom_call_target="tpu_custom_call" | custom-call | flops 644245120 | bytes 629145 | tf_op jit(solution)/shard_map/outer_products/pallas_call | solution.py:411
  430.0 277.1 %tail.1 = (bf16[2,512,768]{2,1,0:T(8,128)(2,1)}, bf16[2,4,128,2048]{3,2,1,0:T(8,128)(2,1)}, bf16[2,4,128,2048]{3,2,1,0:T(8,128)(2,1)}, bf16[2,4,128,2048]{3,2,1,0:T(8,128)(2,1)}, f32[2,2048]{1,0:T(2,128)}) custom-call(bf16[512,2048]{1,0:T(8,128)(2,1)} %get-tuple-element.89.refs_0_, bf16[512,2048]{1,0:T(8,128)(2,1)} %get-tuple-element.90.refs_1_, ...), custom_call_target="tpu_custom_call" | custom-call | flops 500000000 | bytes 5000000 | tf_op jit(solution)/shard_map/tail/pallas_call | solution.py:860
  707.9 6.0 bitcast_convert_fusion
  714.0 4.0 convolution_convert_fusion
  718.0 8.9 %pad_maximum_fusion = bf16[2048,1408]{0,1:T(8,128)(2,1)} fusion(bf16[2048,128]{0,1:T(8,128)(2,1)S(1)} %fusion.8, bf16[2048,512]{0,1:T(8,128)(2,1)} %bitcast_convert_fusion, bf16[2048,768]{0,1:T(8,128)(2,1)S(1)} %convolution_convert_fusion), kind=kLoop, calls=%fused_computation | loop fusion | flops 17301504 | bytes 11534336 | tf_op jit(solution)/shard_map/concatenate | solution.py:1231
  730.3 10.0 %spread.1 = (bf16[2,4,128,2048]{3,2,1,0:T(8,128)(2,1)}, f32[2,4,128,2048]{3,2,1,0:T(8,128)}) custom-call(s32[1]{0:T(128)} %bitcast.rank_ref, bf16[2,4,128,2048]{3,2,1,0:T(8,128)(2,1)} %get-tuple-element.93.out_ref, bf16[2,4,128,2048]{3,2,1,0:T(8,128)(2,1)} %get-tuple-element.94.tok_ref), custom_call_target="tpu_custom_call" | custom-call | tf_op jit(solution)/shard_map/spread/pallas_call | solution.py:930
  740.3 7.1 weight_step.3
  747.4 13.9 %weight_step.2 = (f32[2,256,2048]{2,1,0:T(8,128)}, f32[2,256,2048]{2,1,0:T(8,128)}, f32[2,256,2048]{2,1,0:T(8,128)}, f32[2,256,2048]{2,1,0:T(8,128)}) custom-call(bf16[256,3072]{1,0:T(8,128)(2,1)} %bitcast.104, bf16[256,3072]{1,0:T(8,128)(2,1)} %bitcast.106, f32[2,256,2048]{2,1,0:T(8,128)} %refs_2_.2, f32[2,256,2048]{2,1,0:T(8,128)} %refs_3_.2, ...), custom_call_target="tpu_custom_call" | custom-call | flops 1048576 | bytes 1468006 | tf_op jit(solution)/shard_map/weight_step/pallas_call | solution.py:469
  761.3 28.8 %reduce-scatter.8.cloned.1.call-done = bf16[256,1408]{0,1:T(8,128)(2,1)} async-done(((bf16[2048,1408]{0,1:T(8,128)(2,1)}), bf16[256,1408]{0,1:T(8,128)(2,1)}) %reduce-scatter.8.cloned.1.call-update) | async-done | bytes 720912 | tf_op jit(solution)/shard_map/reduce_scatter | solution.py:1230
  790.9 2.4 collective-permute-start.20
  795.4 2.5 add_multiply_fusion
  799.4 1.8 copy.187
  801.2 1.8 copy.186
  803.0 1.8 copy.185
  (162 shorter events, 56.1 us)
Async XLA Ops:
  7.2 44.1 %all-gather.7.cloned.1.call-start = ((), (), s32[]{:S(2)}) async-start(), calls=%async_computation.3 | async-start | bytes 3538944 | tf_op jit(solution)/shard_map/all_gather | solution.py:1074
  9.1 72.4 %all-gather.9.cloned.1.call-start = ((), (), s32[]{:S(2)}) async-start(), calls=%async_computation.4 | async-start | bytes 2359296 | tf_op jit(solution)/shard_map/all_gather | solution.py:1078
  10.9 3.6 copy-start.19
  11.0 125.5 %all-gather.15.cloned.1.call-start = ((), (), s32[]{:S(2)}) async-start(), calls=%async_computation.10 | async-start | bytes 4718592 | tf_op jit(solution)/shard_map/all_gather | solution.py:1097
  28.0 5.1 copy-start.18
  30.8 158.9 %copy-start = (bf16[2,1,128,2048]{3,2,1,0:T(8,128)(2,1)}, bf16[2,1,128,2048]{3,2,1,0:T(8,128)(2,1)S(1)}, u32[]{:S(2)}) copy-start(bf16[2,1,128,2048]{3,2,1,0:T(8,128)(2,1)S(1)} %get-tuple-element.236) | copy-start | bytes 3145732
  62.3 4.4 copy-start.2
  64.3 191.7 %all-gather.11.cloned.1.call-start = ((), (), s32[]{:S(2)}) async-start(), calls=%async_computation.5 | async-start | bytes 14155776 | tf_op jit(solution)/shard_map/all_gather | solution.py:1109
  66.8 1.3 copy-start.5
  69.4 1.1 copy-start.7
  69.4 296.5 %all-gather.13.cloned.1.call-start = ((), (), s32[]{:S(2)}) async-start(), calls=%async_computation.6 | async-start | bytes 14155776 | tf_op jit(solution)/shard_map/all_gather | solution.py:1109
  70.6 656.3 %reduce-scatter.4.cloned.1.call-start = ((), (), s32[]{:S(2)}) async-start(), calls=%async_computation.7 | async-start | bytes 14155776 | tf_op jit(solution)/shard_map/reduce_scatter | solution.py:1170
  82.8 52.6 %copy-start.10 = (bf16[1024,768]{1,0:T(8,128)(2,1)S(1)}, bf16[1024,768]{1,0:T(8,128)(2,1)}, u32[]{:S(2)}) copy-start(bf16[1024,768]{1,0:T(8,128)(2,1)} %get-tuple-element.68) | copy-start | bytes 4718596
  82.8 27.0 %collective-permute-start.5 = (bf16[1024,512]{1,0:T(8,128)(2,1)S(1)}, bf16[1024,512]{1,0:T(8,128)(2,1)S(1)}, u32[]{:S(2)}, u32[]{:S(2)}) collective-permute-start(bf16[1024,512]{1,0:T(8,128)(2,1)S(1)} %constant_dynamic-slice_fusion.5), channel_id=1, source_target_pairs={{0,3},{1,2},{2,1},{3,0},{4,7},{5,6},{6,5},{7,4},{8,11},{9,10},{10,... | collective-permute-start | bytes 3145736 | tf_op jit(solution)/shard_map/ppermute | solution.py:987
  85.2 46.3 %collective-permute-start.4 = (bf16[1024,512]{1,0:T(8,128)(2,1)S(1)}, bf16[1024,512]{1,0:T(8,128)(2,1)S(1)}, u32[]{:S(2)}, u32[]{:S(2)}) collective-permute-start(bf16[1024,512]{1,0:T(8,128)(2,1)S(1)} %constant_dynamic-slice_fusion.5), channel_id=1, source_target_pairs={{0,2},{1,3},{2,0},{3,1},{4,6},{5,7},{6,4},{7,5},{8,10},{9,11},{10,... | collective-permute-start | bytes 3145736 | tf_op jit(solution)/shard_map/ppermute | solution.py:987
  85.8 45.8 %collective-permute-start.3 = (bf16[1024,512]{1,0:T(8,128)(2,1)S(1)}, bf16[1024,512]{1,0:T(8,128)(2,1)S(1)}, u32[]{:S(2)}, u32[]{:S(2)}) collective-permute-start(bf16[1024,512]{1,0:T(8,128)(2,1)S(1)} %constant_dynamic-slice_fusion.5), channel_id=1, source_target_pairs={{0,1},{1,0},{2,3},{3,2},{4,5},{5,4},{6,7},{7,6},{8,9},{9,8},{10,11... | collective-permute-start | bytes 3145736 | tf_op jit(solution)/shard_map/ppermute | solution.py:987
  133.9 51.8 %collective-permute-start.6 = (bf16[1024,2048]{1,0:T(8,128)(2,1)}, bf16[1024,2048]{1,0:T(8,128)(2,1)}, u32[]{:S(2)}, u32[]{:S(2)}) collective-permute-start(bf16[1024,2048]{1,0:T(8,128)(2,1)} %pad_maximum_fusion.2.refs_8_), channel_id=1, source_target_pairs={{0,4},{4,0},{8,12},{12,8},{16,20},{20,16},{24,28},{28,24},{1,5},{5... | collective-permute-start | bytes 12582920 | tf_op jit(solution)/shard_map/ppermute | solution.py:1062
  166.8 10.1 %collective-permute-start.2 = (bf16[2,128,512]{2,1,0:T(8,128)(2,1)S(1)}, bf16[2,128,512]{2,1,0:T(8,128)(2,1)S(1)}, u32[]{:S(2)}, u32[]{:S(2)}) collective-permute-start(bf16[2,128,512]{2,1,0:T(8,128)(2,1)S(1)} %get-tuple-element.263), channel_id=1, source_target_pairs={{0,3},{1,2},{2,1},{3,0},{4,7},{5,6},{6,5},{7,4},{8,11},{9,10},{10,... | collective-permute-start | bytes 786440 | tf_op jit(solution)/shard_map/ppermute | solution.py:987
  168.6 13.6 %collective-permute-start.1 = (bf16[2,128,512]{2,1,0:T(8,128)(2,1)S(1)}, bf16[2,128,512]{2,1,0:T(8,128)(2,1)S(1)}, u32[]{:S(2)}, u32[]{:S(2)}) collective-permute-start(bf16[2,128,512]{2,1,0:T(8,128)(2,1)S(1)} %get-tuple-element.264), channel_id=1, source_target_pairs={{0,2},{1,3},{2,0},{3,1},{4,6},{5,7},{6,4},{7,5},{8,10},{9,11},{10,... | collective-permute-start | bytes 786440 | tf_op jit(solution)/shard_map/ppermute | solution.py:987
  169.8 12.3 %collective-permute-start = (bf16[2,128,512]{2,1,0:T(8,128)(2,1)S(1)}, bf16[2,128,512]{2,1,0:T(8,128)(2,1)S(1)}, u32[]{:S(2)}, u32[]{:S(2)}) collective-permute-start(bf16[2,128,512]{2,1,0:T(8,128)(2,1)S(1)} %get-tuple-element.265), channel_id=1, source_target_pairs={{0,1},{1,0},{2,3},{3,2},{4,5},{5,4},{6,7},{7,6},{8,9},{9,8},{10,11... | collective-permute-start | bytes 786440 | tf_op jit(solution)/shard_map/ppermute | solution.py:987
  189.6 3.5 copy-start.4
  191.7 25.2 %collective-permute-start.7 = (bf16[256,2048]{1,0:T(8,128)(2,1)S(1)}, bf16[256,2048]{1,0:T(8,128)(2,1)S(1)}, u32[]{:S(2)}, u32[]{:S(2)}) collective-permute-start(bf16[256,2048]{1,0:T(8,128)(2,1)S(1)} %get-tuple-element.228), channel_id=1, source_target_pairs={{0,1},{1,0},{2,3},{3,2},{4,5},{5,4},{6,7},{7,6},{8,9},{9,8},{10,11... | collective-permute-start | bytes 3145736 | tf_op jit(solution)/shard_map/ppermute | solution.py:987
  193.7 2.3 copy-start.3
  194.7 25.4 %collective-permute-start.8 = (bf16[256,2048]{1,0:T(8,128)(2,1)S(1)}, bf16[256,2048]{1,0:T(8,128)(2,1)S(1)}, u32[]{:S(2)}, u32[]{:S(2)}) collective-permute-start(bf16[256,2048]{1,0:T(8,128)(2,1)S(1)} %get-tuple-element.228), channel_id=1, source_target_pairs={{0,2},{1,3},{2,0},{3,1},{4,6},{5,7},{6,4},{7,5},{8,10},{9,11},{10,... | collective-permute-start | bytes 3145736 | tf_op jit(solution)/shard_map/ppermute | solution.py:987
  217.0 13.8 %collective-permute-start.9 = (bf16[128,2048]{1,0:T(8,128)(2,1)S(1)}, bf16[128,2048]{1,0:T(8,128)(2,1)S(1)}, u32[]{:S(2)}, u32[]{:S(2)}) collective-permute-start(bf16[128,2048]{1,0:T(8,128)(2,1)S(1)} %get-tuple-element.259), channel_id=1, source_target_pairs={{0,2},{1,3},{2,0},{3,1},{4,6},{5,7},{6,4},{7,5},{8,10},{9,11},{10,... | collective-permute-start | bytes 1572872 | tf_op jit(solution)/shard_map/ppermute | solution.py:987
  220.1 22.5 %collective-permute-start.10 = (bf16[128,2048]{1,0:T(8,128)(2,1)S(1)}, bf16[128,2048]{1,0:T(8,128)(2,1)S(1)}, u32[]{:S(2)}, u32[]{:S(2)}) collective-permute-start(bf16[128,2048]{1,0:T(8,128)(2,1)S(1)} %get-tuple-element.260), channel_id=1, source_target_pairs={{0,1},{1,0},{2,3},{3,2},{4,5},{5,4},{6,7},{7,6},{8,9},{9,8},{10,11... | collective-permute-start | bytes 1572872 | tf_op jit(solution)/shard_map/ppermute | solution.py:987
  232.5 22.6 %collective-permute-start.12 = (bf16[512,768]{1,0:T(8,128)(2,1)S(1)}, bf16[512,768]{1,0:T(8,128)(2,1)S(1)}, u32[]{:S(2)}, u32[]{:S(2)}) collective-permute-start(bf16[512,768]{1,0:T(8,128)(2,1)S(1)} %get-tuple-element.243), channel_id=1, source_target_pairs={{0,2},{1,3},{2,0},{3,1},{4,6},{5,7},{6,4},{7,5},{8,10},{9,11},{10,... | collective-permute-start | bytes 2359304 | tf_op jit(solution)/shard_map/ppermute | solution.py:987
  233.7 20.5 %collective-permute-start.11 = (bf16[512,768]{1,0:T(8,128)(2,1)S(1)}, bf16[512,768]{1,0:T(8,128)(2,1)S(1)}, u32[]{:S(2)}, u32[]{:S(2)}) collective-permute-start(bf16[512,768]{1,0:T(8,128)(2,1)S(1)} %get-tuple-element.243), channel_id=1, source_target_pairs={{0,1},{1,0},{2,3},{3,2},{4,5},{5,4},{6,7},{7,6},{8,9},{9,8},{10,11... | collective-permute-start | bytes 2359304 | tf_op jit(solution)/shard_map/ppermute | solution.py:987
  234.6 66.4 %collective-permute-start.13 = (bf16[512,768]{1,0:T(8,128)(2,1)S(1)}, bf16[512,768]{1,0:T(8,128)(2,1)S(1)}, u32[]{:S(2)}, u32[]{:S(2)}) collective-permute-start(bf16[512,768]{1,0:T(8,128)(2,1)S(1)} %get-tuple-element.242), channel_id=1, source_target_pairs={{0,1},{1,0},{2,3},{3,2},{4,5},{5,4},{6,7},{7,6},{8,9},{9,8},{10,11... | collective-permute-start | bytes 2359304 | tf_op jit(solution)/shard_map/ppermute | solution.py:987
  238.3 63.7 %collective-permute-start.14 = (bf16[512,768]{1,0:T(8,128)(2,1)S(1)}, bf16[512,768]{1,0:T(8,128)(2,1)S(1)}, u32[]{:S(2)}, u32[]{:S(2)}) collective-permute-start(bf16[512,768]{1,0:T(8,128)(2,1)S(1)} %get-tuple-element.242), channel_id=1, source_target_pairs={{0,2},{1,3},{2,0},{3,1},{4,6},{5,7},{6,4},{7,5},{8,10},{9,11},{10,... | collective-permute-start | bytes 2359304 | tf_op jit(solution)/shard_map/ppermute | solution.py:987
  322.4 404.5 %reduce-scatter.6.cloned.1.call-start = ((), (), s32[]{:S(2)}) async-start(), calls=%async_computation.8 | async-start | bytes 14155776 | tf_op jit(solution)/shard_map/reduce_scatter | solution.py:1170
  322.4 21.4 %collective-permute-start.15 = (bf16[512,768]{1,0:T(8,128)(2,1)S(1)}, bf16[512,768]{1,0:T(8,128)(2,1)S(1)}, u32[]{:S(2)}, u32[]{:S(2)}) collective-permute-start(bf16[512,768]{1,0:T(8,128)(2,1)S(1)} %get-tuple-element.243), channel_id=1, source_target_pairs={{0,3},{1,2},{2,1},{3,0},{4,7},{5,6},{6,5},{7,4},{8,11},{9,10},{10,... | collective-permute-start | bytes 2359304 | tf_op jit(solution)/shard_map/ppermute | solution.py:987
  324.4 29.7 %collective-permute-start.16 = (bf16[512,768]{1,0:T(8,128)(2,1)S(1)}, bf16[512,768]{1,0:T(8,128)(2,1)S(1)}, u32[]{:S(2)}, u32[]{:S(2)}) collective-permute-start(bf16[512,768]{1,0:T(8,128)(2,1)S(1)} %get-tuple-element.242), channel_id=1, source_target_pairs={{0,3},{1,2},{2,1},{3,0},{4,7},{5,6},{6,5},{7,4},{8,11},{9,10},{10,... | collective-permute-start | bytes 2359304 | tf_op jit(solution)/shard_map/ppermute | solution.py:987
  355.0 55.2 %collective-permute-start.17 = (bf16[1024,3072]{1,0:T(8,128)(2,1)}, bf16[1024,3072]{1,0:T(8,128)(2,1)}, u32[]{:S(2)}, u32[]{:S(2)}) collective-permute-start(bf16[1024,3072]{1,0:T(8,128)(2,1)} %constant_dynamic-update-slice_fusion.3.refs_10_), channel_id=1, source_target_pairs={{0,4},{4,0},{8,12},{12,8},{16,20},{20,16},{24,28},{28,24},{1,5},{5... | collective-permute-start | bytes 18874376 | tf_op jit(solution)/shard_map/ppermute | solution.py:1062
  429.9 360.2 %reduce-scatter.8.cloned.1.call-start = ((), (), s32[]{:S(2)}) async-start(), calls=%async_computation.9 | async-start | bytes 6488064 | tf_op jit(solution)/shard_map/reduce_scatter | solution.py:1230
  430.0 278.0 %copy-start.6 = (bf16[2,4,128,512]{3,2,1,0:T(8,128)(2,1)S(1)}, bf16[2,4,128,512]{3,2,1,0:T(8,128)(2,1)}, u32[]{:S(2)}) copy-start(bf16[2,4,128,512]{3,2,1,0:T(8,128)(2,1)} %attend.1) | copy-start | bytes 3145732
  707.9 6.1 copy-start.22
  707.9 6.1 copy-start.23
  726.9 1.2 copy-start.16
  726.9 1.3 copy-start.17
  747.4 48.0 %copy-start.11 = (bf16[512,256]{1,0:T(8,128)(2,1)S(1)}, bf16[512,256]{1,0:T(8,128)(2,1)}, u32[]{:S(2)}) copy-start(bf16[512,256]{1,0:T(8,128)(2,1)} %param.26) | copy-start | bytes 786436
  747.4 48.0 %copy-start.13 = (f32[512,256]{1,0:T(8,128)S(1)}, f32[512,256]{1,0:T(8,128)}, u32[]{:S(2)}) copy-start(f32[512,256]{1,0:T(8,128)} %param.35) | copy-start | bytes 1572868
  790.9 7.0 copy-start.9
  790.9 18.7 %collective-permute-start.20 = (bf16[256,128]{0,1:T(8,128)(2,1)S(1)}, bf16[256,128]{0,1:T(8,128)(2,1)S(1)}, u32[]{:S(2)}, u32[]{:S(2)}) collective-permute-start(bf16[256,128]{0,1:T(8,128)(2,1)S(1)} %slice.213), channel_id=1, source_target_pairs={{0,3},{1,2},{2,1},{3,0},{4,7},{5,6},{6,5},{7,4},{8,11},{9,10},{10,... | collective-permute-start | bytes 196616 | tf_op jit(solution)/shard_map/ppermute | solution.py:987
  793.3 16.3 %collective-permute-start.19 = (bf16[256,128]{0,1:T(8,128)(2,1)S(1)}, bf16[256,128]{0,1:T(8,128)(2,1)}, u32[]{:S(2)}, u32[]{:S(2)}) collective-permute-start(bf16[256,128]{0,1:T(8,128)(2,1)S(1)} %slice.213), channel_id=1, source_target_pairs={{0,2},{1,3},{2,0},{3,1},{4,6},{5,7},{6,4},{7,5},{8,10},{9,11},{10,... | collective-permute-start | bytes 196616 | tf_op jit(solution)/shard_map/ppermute | solution.py:987
  793.9 15.7 %collective-permute-start.18 = (bf16[256,128]{0,1:T(8,128)(2,1)S(1)}, bf16[256,128]{0,1:T(8,128)(2,1)}, u32[]{:S(2)}, u32[]{:S(2)}) collective-permute-start(bf16[256,128]{0,1:T(8,128)(2,1)S(1)} %slice.213), channel_id=1, source_target_pairs={{0,1},{1,0},{2,3},{3,2},{4,5},{5,4},{6,7},{7,6},{8,9},{9,8},{10,11... | collective-permute-start | bytes 196616 | tf_op jit(solution)/shard_map/ppermute | solution.py:987
  805.6 4.0 copy-start.20
  805.6 4.0 copy-start.21
  (5 other events, 5.2 us)
Sparse Core Ops, SparseCore 0:
  10.2 40.9 all-gather.6
  53.5 27.9 all-gather.8
  83.6 46.6 all-gather.14
  132.4 115.4 all-gather.10
  249.4 116.4 all-gather.12
  368.0 127.7 reduce-scatter.3
  498.1 161.3 reduce-scatter.5
  727.1 62.9 reduce-scatter.7

commit v4 on v3

--- a/solution.py
+++ b/solution.py
@@ -255,11 +255,119 @@
     return lax.dot_general(left, right, (((0,), (0,)), ((), ())), preferred_element_type=F32)
 
 
-def gated_kernel(last, steps, u_ref, g_ref, w_ref, *refs):
+def paired(index, k):
+    bit = 1
+    while bit <= k:
+        if k & bit:
+            index = index + bit - 2 * bit * ((index // bit) % 2)
+        bit *= 2
+    return index
+
+
+def remote(src, dst, send, recv, device):
+    return pltpu.make_async_remote_copy(
+        src_ref=src,
+        dst_ref=dst,
+        send_sem=send,
+        recv_sem=recv,
+        device_id=device,
+        device_id_type=pl.DeviceIdType.MESH,
+    )
+
+
+def meet(peers):
+    barrier = pltpu.get_barrier_semaphore()
+    for peer in peers:
+        pl.semaphore_signal(barrier, inc=1, device_id=peer, device_id_type=pl.DeviceIdType.MESH)
+    pl.semaphore_wait(barrier, len(peers))
+
+
+def start(moves):
+    for move in moves:
+        move.start()
+
+
+def arrive(moves):
+    for move in moves:
+        move.wait_recv()
+
+
+def sent(moves):
+    for move in moves:
+        move.wait_send()
+
+
+def row_moves(remote, rank, n_tp, low, got, send, recv):
+    first = [
+        [
+            remote(low.at[m], got.at[m, k], send.at[m, k], recv.at[m, k], rank(k))
+            for k in range(1, n_tp)
+            if k != 3
+        ]
+        for m in range(MICRO)
+    ]
+    relay = [
+        remote(got.at[m, 1 + m], got.at[m, 3], send.at[m, 3], recv.at[m, 3], rank(2 - m))
+        for m in range(MICRO)
+    ]
+    return first, relay
+
+
+def relay_rows(first, relay):
+    for m in range(MICRO):
+        first[m][m].wait_recv()
+        relay[m].start()
+
+
+def close_rows(first, relay):
+    for m in range(MICRO):
+        for i, move in enumerate(first[m]):
+            if i != m:
+                move.wait_recv()
+            move.wait_send()
+        relay[m].wait_recv()
+        relay[m].wait_send()
+
+
+def carried(n_tp, src, got, send, recv):
+    dp, tp = lax.axis_index("dp"), lax.axis_index("tp")
+    rows = got.shape[1]
+    return [
+        remote(
+            src.at[pl.ds(k * rows, rows)],
+            got.at[k],
+            send.at[k],
+            recv.at[k],
+            (dp, paired(tp, k)),
+        )
+        for k in range(1, n_tp)
+    ]
+
+
+def carry_start(n_tp, *move):
+    dp, tp = lax.axis_index("dp"), lax.axis_index("tp")
+    meet([(dp, paired(tp, k)) for k in range(1, n_tp)])
+    start(carried(n_tp, *move))
+
+
+def carry_end(n_tp, *move):
+    moves = carried(n_tp, *move)
+    arrive(moves)
+    sent(moves)
+
+
+def gated_kernel(n_tp, last, steps, u_ref, g_ref, w_ref, *refs):
+    refs = list(refs)
+    move = None
+    if n_tp:
+        send, recv = refs[-2:]
+        src, got = refs.pop(2), refs[6]
+        move = (src, got, send, recv)
+        refs = refs[:6] + refs[7:-2]
     if last:
-        y_old, du_old, hid_ref, dgu_ref, y_out, du_out, y_sum, du_sum, y_low, du_low, sem = refs
-    else:
-        hid_ref, dgu_ref, y_out, du_out, y_sum, du_sum, y_low, du_low, sem = refs
+        y_old, du_old = refs[:2]
+        refs = refs[2:]
+    hid_ref, dgu_ref, y_out, du_out, y_sum, du_sum, y_low, du_low, sem = refs
     step = pl.program_id(0)
     depth = w_ref.shape[0]
     sub = hid_ref.shape[1]
@@ -267,6 +375,8 @@
 
     @pl.when(step == 0)
     def _():
+        if move:
+            carry_start(n_tp, *move)
         y_sum[...] = jnp.zeros_like(y_sum)
         du_sum[...] = jnp.zeros_like(du_sum)
         if last:
@@ -304,129 +414,164 @@
         copy_y.start()
         copy_du.wait()
         copy_y.wait()
-
-
-def feed_forward(u, g, weights, sub, sums):
+        if move:
+            carry_end(n_tp, *move)
+
+
+def carrier_params(n_tp, collective_id):
+    if not n_tp:
+        return pltpu.CompilerParams(vmem_limit_bytes=VMEM_LIMIT)
+    return pltpu.CompilerParams(
+        collective_id=collective_id, has_side_effects=True, vmem_limit_bytes=VMEM_LIMIT
+    )
+
+
+def feed_forward(u, g, weights, sub, sums, n_tp=0, carry=None):
     rows, depth = u.shape
     steps = weights.shape[1] // (3 * sub)
     last = sums is not None
     whole = functools.partial(pl.BlockSpec, pipeline_mode=pl.Buffered(1))
     anywhere = pl.BlockSpec(memory_space=pl.ANY)
     return pl.pallas_call(
-        functools.partial(gated_kernel, last, steps),
+        functools.partial(gated_kernel, n_tp, last, steps),
         grid=(steps,),
         in_specs=[
             whole((rows, depth), lambda j: (0, 0)),
             whole((rows, depth), lambda j: (0, 0)),
             pl.BlockSpec((depth, 3 * sub), lambda j: (0, j)),
         ]
-        + ([anywhere, anywhere] if last else []),
+        + ([anywhere, anywhere] if last else [])
+        + ([anywhere] if n_tp else []),
         out_specs=[
             pl.BlockSpec((rows, sub), lambda j: (0, j)),
             pl.BlockSpec((rows, 2 * sub), lambda j: (0, j)),
             anywhere,
             anywhere,
-        ],
+        ]
+        + ([anywhere] if n_tp else []),
         out_shape=[
             jax.ShapeDtypeStruct((rows, steps * sub), BF16),
             jax.ShapeDtypeStruct((rows, 2 * steps * sub), BF16),
             jax.ShapeDtypeStruct((rows, depth), BF16),
             jax.ShapeDtypeStruct((rows, depth), BF16),
-        ],
+        ]
+        + ([jax.ShapeDtypeStruct((n_tp, rows // n_tp, depth), BF16)] if n_tp else []),
         scratch_shapes=[
             pltpu.VMEM((rows, depth), F32),
             pltpu.VMEM((rows, depth), F32),
             pltpu.VMEM((rows, depth), BF16),
             pltpu.VMEM((rows, depth), BF16),
             pltpu.SemaphoreType.DMA((2,)),
-        ],
-        compiler_params=pltpu.CompilerParams(vmem_limit_bytes=VMEM_LIMIT),
+        ]
+        + ([pltpu.SemaphoreType.DMA((n_tp,))] * 2 if n_tp else []),
+        compiler_params=carrier_params(n_tp, 3),
         cost_estimate=hint(
             flops=12 * rows * depth * steps * sub,
             bytes_accessed=2 * weights.size + 8 * rows * depth,
             transcendentals=0,
         ),
         name="feed_forward",
-    )(u, g, weights, *(sums if last else ()))
-
-
-def outer_kernel(batches, sub, steps, half, core_ref, *refs):
+    )(u, g, weights, *(sums if last else ()), *([carry] if n_tp else []))
+
+
+def outer_kernel(n_tp, batches, sub, steps, *refs):
     u_refs, g_refs = refs[:batches], refs[batches : 2 * batches]
     hid_refs, dgu_refs = refs[2 * batches : 3 * batches], refs[3 * batches : 4 * batches]
-    outs = refs[4 * batches :]
-
-    def products(out_ref):
-        for j in range(steps):
-            both = slice(2 * j * sub, 2 * (j + 1) * sub)
-            one = slice(j * sub, (j + 1) * sub)
-            total = dot_tn(u_refs[0][...], dgu_refs[0][:, both])
-            for m in range(1, batches):
-                total += dot_tn(u_refs[m][...], dgu_refs[m][:, both])
-            out_ref[0, :, 3 * j * sub : 3 * j * sub + 2 * sub] = total.astype(BF16)
-            total = dot_tn(g_refs[0][...], hid_refs[0][:, one])
-            for m in range(1, batches):
-                total += dot_tn(g_refs[m][...], hid_refs[m][:, one])
-            out_ref[0, :, 3 * j * sub + 2 * sub : 3 * (j + 1) * sub] = total.astype(BF16)
-
-    if len(outs) == 1:
-        products(outs[0])
+    refs = refs[4 * batches :]
+    move = None
+    if n_tp:
+        src, out_ref, got, send, recv = refs
+        move = (src, got, send, recv)
+
+        @pl.when(pl.program_id(0) == 0)
+        def _():
+            carry_start(n_tp, *move)
+
     else:
-
-        @pl.when(pl.program_id(0) < half)
+        (out_ref,) = refs
+    for j in range(steps):
+        both = slice(2 * j * sub, 2 * (j + 1) * sub)
+        one = slice(j * sub, (j + 1) * sub)
+        total = dot_tn(u_refs[0][...], dgu_refs[0][:, both])
+        for m in range(1, batches):
+            total += dot_tn(u_refs[m][...], dgu_refs[m][:, both])
+        out_ref[0, :, 3 * j * sub : 3 * j * sub + 2 * sub] = total.astype(BF16)
+        total = dot_tn(g_refs[0][...], hid_refs[0][:, one])
+        for m in range(1, batches):
+            total += dot_tn(g_refs[m][...], hid_refs[m][:, one])
+        out_ref[0, :, 3 * j * sub + 2 * sub : 3 * (j + 1) * sub] = total.astype(BF16)
+    if n_tp:
+
+        @pl.when(pl.program_id(0) == pl.num_programs(0) - 1)
         def _():
-            products(outs[0])
-
-        @pl.when(pl.program_id(0) >= half)
-        def _():
-            products(outs[1])
-
-
-def outer_products(core, us, gs, hids, dgus, own, sub, split):
+            carry_end(n_tp, *move)
+
+
+def outer_products(us, gs, hids, dgus, own, sub, n_tp=0, carry=None):
     batches = len(us)
     rows, depth = us[0].shape
     n_dp = depth // own
-    half = n_dp // 2
     width = hids[0].shape[1]
     steps = width // sub
-    if split:
-
-        def place(i, core_ref):
-            mine = jnp.where(i < half, 1 - core_ref[0], core_ref[0])
-            return (i % half) * 2 + mine
-
-        out_specs = [
-            pl.BlockSpec((1, own, 3 * width), lambda i, r: (jnp.minimum(i, half - 1), 0, 0)),
-            pl.BlockSpec((1, own, 3 * width), lambda i, r: (jnp.maximum(i - half, 0), 0, 0)),
-        ]
-        out_shape = [jax.ShapeDtypeStruct((half, own, 3 * width), BF16)] * 2
-    else:
-
-        def place(i, core_ref):
-            return i
-
-        out_specs = [pl.BlockSpec((1, own, 3 * width), lambda i, r: (i, 0, 0))]
-        out_shape = [jax.ShapeDtypeStruct((n_dp, own, 3 * width), BF16)]
     whole = functools.partial(pl.BlockSpec, pipeline_mode=pl.Buffered(1))
-    column = pl.BlockSpec((rows, own), lambda i, r: (0, place(i, r)))
+    column = pl.BlockSpec((rows, own), lambda i: (0, i))
+    anywhere = pl.BlockSpec(memory_space=pl.ANY)
     return pl.pallas_call(
-        functools.partial(outer_kernel, batches, sub, steps, half),
-        grid_spec=pltpu.PrefetchScalarGridSpec(
-            num_scalar_prefetch=1,
-            grid=(n_dp,),
-            in_specs=[column] * (2 * batches)
-            + [whole((rows, width), lambda i, r: (0, 0))] * batches
-            + [whole((rows, 2 * width), lambda i, r: (0, 0))] * batches,
-            out_specs=out_specs,
-        ),
-        out_shape=out_shape,
-        compiler_params=pltpu.CompilerParams(vmem_limit_bytes=VMEM_LIMIT),
+        functools.partial(outer_kernel, n_tp, batches, sub, steps),
+        grid=(n_dp,),
+        in_specs=[column] * (2 * batches)
+        + [whole((rows, width), lambda i: (0, 0))] * batches
+        + [whole((rows, 2 * width), lambda i: (0, 0))] * batches
+        + ([anywhere] if n_tp else []),
+        out_specs=[pl.BlockSpec((1, own, 3 * width), lambda i: (i, 0, 0))]
+        + ([anywhere] if n_tp else []),
+        out_shape=[jax.ShapeDtypeStruct((n_dp, own, 3 * width), BF16)]
+        + ([jax.ShapeDtypeStruct((n_tp, rows // n_tp, depth), BF16)] if n_tp else []),
+        scratch_shapes=[pltpu.SemaphoreType.DMA((n_tp,))] * 2 if n_tp else [],
+        compiler_params=carrier_params(n_tp, 4),
         cost_estimate=hint(
             flops=6 * rows * batches * depth * width,
             bytes_accessed=6 * depth * width,
             transcendentals=0,
         ),
         name="outer_products",
-    )(core, *us, *gs, *hids, *dgus)
+    )(*us, *gs, *hids, *dgus, *([carry] if n_tp else []))
+
+
+def attn_grad_kernel(a_ref, m_ref, qkv_ref, att_ref, gain_ref, out_ref):
+    width = qkv_ref.shape[1]
+    both = width + att_ref.shape[1]
+    out_ref[0, :, :width] = dot_tn(a_ref[...], qkv_ref[...]).astype(BF16)
+    out_ref[0, :, width:both] = dot_tn(m_ref[...], att_ref[...]).astype(BF16)
+    gains = gain_ref[...]
+    filler = jnp.zeros((out_ref.shape[2] - both - gains.shape[0], gains.shape[1]), F32)
+    out_ref[0, :, both:] = jnp.concatenate([gains, filler], axis=0).T.astype(BF16)
+
+
+def attn_weight_grads(attn_in, d_mid, d_qkv, attended, gain_grads, own):
+    rows, depth = attn_in.shape
+    width, q_width = d_qkv.shape[1], attended.shape[1]
+    total = width + q_width + 128
+    column = pl.BlockSpec((rows, own), lambda i: (0, i))
+    whole = functools.partial(pl.BlockSpec, pipeline_mode=pl.Buffered(1))
+    return pl.pallas_call(
+        attn_grad_kernel,
+        grid=(depth // own,),
+        in_specs=[
+            column,
+            column,
+            whole((rows, width), lambda i: (0, 0)),
+            whole((rows, q_width), lambda i: (0, 0)),
+            pl.BlockSpec((2, own), lambda i: (0, i)),
+        ],
+        out_specs=pl.BlockSpec((1, own, total), lambda i: (i, 0, 0)),
+        out_shape=jax.ShapeDtypeStruct((depth // own, own, total), BF16),
+        compiler_params=pltpu.CompilerParams(vmem_limit_bytes=VMEM_LIMIT),
+        cost_estimate=hint(
+            flops=2 * rows * depth * total, bytes_accessed=4 * rows * depth, transcendentals=0
+        ),
+        name="attn_weight_grads",
+    )(attn_in, d_mid, d_qkv, attended, gain_grads)
 
 
 def step_kernel(turned, decay, steps, chunks, *refs):
@@ -481,19 +626,61 @@
     )
 
 
-def paired(index, k):
-    bit = 1
-    while bit <= k:
-        if k & bit:
-            index = index + bit - 2 * bit * ((index // bit) % 2)
-        bit *= 2
-    return index
+def rows_kernel(n_tp, *refs):
+    count = (len(refs) - 1) // 4
+    lows, gots, sems = refs[:count], refs[count : 2 * count], refs[2 * count : -1]
+    local_sem = refs[-1]
+    dp, tp = lax.axis_index("dp"), lax.axis_index("tp")
+
+    def rank(k):
+        return (dp, paired(tp, k))
+
+    meet([rank(k) for k in range(1, n_tp)])
+    plans = [
+        row_moves(remote, rank, n_tp, lows[i], gots[i], sems[2 * i], sems[2 * i + 1])
+        for i in range(count)
+    ]
+    keep = [
+        pltpu.make_async_copy(lows[i].at[m], gots[i].at[m, 0], local_sem.at[i, m])
+        for i in range(count)
+        for m in range(MICRO)
+    ]
+    for first, _ in plans:
+        for moves in first:
+            start(moves)
+    start(keep)
+    for first, relay in plans:
+        relay_rows(first, relay)
+    for first, relay in plans:
+        close_rows(first, relay)
+    for copy in keep:
+        copy.wait()
+
+
+def gather_rows(n_tp, lows):
+    micro, rows, depth = lows[0].shape
+    count = len(lows)
+    anywhere = pl.BlockSpec(memory_space=pl.ANY)
+    return pl.pallas_call(
+        functools.partial(rows_kernel, n_tp),
+        in_specs=[anywhere] * count,
+        out_specs=[anywhere] * count,
+        out_shape=[jax.ShapeDtypeStruct((micro, n_tp, rows, depth), BF16)] * count,
+        scratch_shapes=[pltpu.SemaphoreType.DMA((micro, n_tp))] * (2 * count)
+        + [pltpu.SemaphoreType.DMA((count, micro))],
+        compiler_params=pltpu.CompilerParams(
+            collective_id=1, has_side_effects=True, vmem_limit_bytes=VMEM_LIMIT
+        ),
+        cost_estimate=hint(flops=10**10, bytes_accessed=10**8, transcendentals=0),
+        name="gather_rows",
+    )(*lows)
 
 
 def tail_kernel(n_dp, n_tp, group, *refs):
     (
         du_refs,
         y_refs,
+        du_ins,
         seed_ref,
         middle_ref,
         x_ref,
@@ -509,9 +696,9 @@
         d_qkv_ref,
         mid_rows,
         out_rows,
-        tok_rows,
+        tok_low,
         gain_ref,
-    ) = (refs[0:2], refs[2:4]) + refs[4:8] + (refs[8:10], refs[10:12]) + refs[12:23]
+    ) = (refs[0:2], refs[2:4], refs[4:6]) + refs[6:10] + (refs[10:12], refs[12:14]) + refs[14:25]
     (
         weights,
         du_got,
@@ -519,7 +706,6 @@
         own_mid,
         mid_low,
         block_low,
-        tok_low,
         do_send,
         do_got,
         shares,
@@ -528,16 +714,12 @@
         z_got,
         heads_got,
         local_sem,
-        du_s,
-        du_r,
+        block_s,
+        block_r,
         y_s,
         y_r,
         mid_s,
         mid_r,
-        block_s,
-        block_r,
-        tok_s,
-        tok_r,
         do_s,
         do_r,
         core_s,
@@ -546,7 +728,7 @@
         z_r,
         heads_s,
         heads_r,
-    ) = refs[23:]
+    ) = refs[25:]
     line = n_dp // 2
     batches = range(MICRO)
     others = range(1, n_tp)
@@ -568,28 +750,9 @@
 
     other_core = (place * 2 + 1 - core, tp)
 
-    def remote(src, dst, send, recv, device):
-        return pltpu.make_async_remote_copy(
-            src_ref=src,
-            dst_ref=dst,
-            send_sem=send,
-            recv_sem=recv,
-            device_id=device,
-            device_id_type=pl.DeviceIdType.MESH,
-        )
-
     def block(k):
         return pl.ds(k * rows, rows)
 
-    du_moves = [
-        [
-            remote(
-                du_refs[m].at[block(k)], du_got.at[m, k], du_s.at[m, k], du_r.at[m, k], rank(k)
-            )
-            for k in others
-        ]
-        for m in batches
-    ]
     y_moves = [
         [
             remote(y_refs[m].at[block(k)], y_got.at[m, k], y_s.at[m, k], y_r.at[m, k], rank(k))
@@ -598,18 +761,10 @@
         for m in batches
     ]
 
-    def row_moves(low, got, send, recv):
-        return [
-            [
-                remote(low.at[m], got.at[m, k], send.at[m, k], recv.at[m, k], rank(k))
-                for k in others
-            ]
-            for m in batches
-        ]
-
-    mid_moves = row_moves(mid_low, mid_rows, mid_s, mid_r)
-    block_moves = row_moves(block_low, out_rows, block_s, block_r)
-    tok_moves = row_moves(tok_low, tok_rows, tok_s, tok_r)
+    block_first, block_relay = row_moves(
+        remote, rank, n_tp, block_low, out_rows, block_s, block_r
+    )
+    mid_first, mid_relay = row_moves(remote, rank, n_tp, mid_low, mid_rows, mid_s, mid_r)
     do_moves = [
         [
             remote(
@@ -644,22 +799,20 @@
         for m in batches
     ]
 
-    def start(moves):
-        for move in moves:
-            move.start()
-
-    def arrive(moves):
-        for move in moves:
-            move.wait_recv()
-
-    def sent(moves):
-        for move in moves:
-            move.wait_send()
-
     own_copies = [
         pltpu.make_async_copy(ref.at[pl.ds(0, rows)], got.at[m, 0], local_sem.at[i, m])
         for i, (pair, got) in enumerate(((du_refs, du_got), (y_refs, y_got)))
         for m, ref in enumerate(pair)
+    ]
+    own_copies += [
+        pltpu.make_async_copy(
+            ref.at[pl.ds(1, n_tp - 1)], du_got.at[m, pl.ds(1, n_tp - 1)], local_sem.at[4, m]
+        )
+        for m, ref in enumerate(du_ins)
+    ]
+    keep_block = [
+        pltpu.make_async_copy(block_low.at[m], out_rows.at[m, 0], local_sem.at[5, m])
+        for m in batches
     ]
     load_out = [
         pltpu.make_async_copy(
@@ -672,23 +825,11 @@
         for side, ref in enumerate(qkv_refs)
     ]
     keep = [
-        [
-            pltpu.make_async_copy(low.at[m], got.at[m, 0], local_sem.at[3 + i, m])
-            for m in batches
-        ]
-        for i, (low, got) in enumerate(
-            ((mid_low, mid_rows), (block_low, out_rows), (tok_low, tok_rows))
-        )
-    ]
-
-    barrier = pltpu.get_barrier_semaphore()
-    peers = [rank(k) for k in others] + [other_core] + [spot(k) for k in range(1, line)]
-    for peer in peers:
-        pl.semaphore_signal(barrier, inc=1, device_id=peer, device_id_type=pl.DeviceIdType.MESH)
-    pl.semaphore_wait(barrier, len(peers))
-
-    for moves in du_moves:
-        start(moves)
+        pltpu.make_async_copy(mid_low.at[m], mid_rows.at[m, 0], local_sem.at[3, m])
+        for m in batches
+    ]
+
+    meet([rank(k) for k in others] + [other_core] + [spot(k) for k in range(1, line)])
     start(own_copies)
     start(load_out)
     gain_one = gains_ref[0:1, :].astype(F32)
@@ -705,7 +846,6 @@
         copy.wait()
     for m in batches:
         part = slice(m * rows, (m + 1) * rows)
-        arrive(du_moves[m])
         d_mixed = total_of(du_got, m)
         middle = middle_ref[part, :]
         scale = mean_square_scale(middle)
@@ -732,8 +872,9 @@
         start(do_moves[m])
     start(load_qkv)
     for m in batches:
-        start(mid_moves[m])
-        keep[0][m].start()
+        start(mid_first[m])
+        keep[m].start()
+    for m in batches:
         start(y_moves[m])
 
     def attend_back_seq(m, s):
@@ -790,8 +931,8 @@
         arrive(y_moves[m])
         part = slice(m * rows, (m + 1) * rows)
         block_low[m] = (middle_ref[part, :] + total_of(y_got, m)).astype(BF16)
-        start(block_moves[m])
-        keep[1][m].start()
+        start(block_first[m])
+        keep_block[m].start()
 
     def close_tokens(m):
         arrive(heads_moves[m])
@@ -813,8 +954,6 @@
         normed = x_part * scale
         gain_ref[0:1, :] += jnp.sum(d_act * normed, axis=0, keepdims=True)
         tok_low[m] = (own_mid[m] + norm_back(d_act * gain_one, normed, scale)).astype(BF16)
-        start(tok_moves[m])
-        keep[2][m].start()
 
     arrive(do_moves[0])
     attend_back_range(0, 0, SEQS)
@@ -822,30 +961,30 @@
     arrive(do_moves[1])
     attend_back_range(1, 0, SEQS // 2)
     send_along(0)
+    relay_rows(mid_first, mid_relay)
     attend_back_range(1, SEQS // 2, SEQS)
     core_moves[1].start()
     for copy in load_qkv:
         copy.wait()
+    close_block(0)
     close_keys(0)
     send_along(1)
+    close_block(1)
     close_tokens(0)
-    close_block(0)
     close_keys(1)
+    relay_rows(block_first, block_relay)
     close_tokens(1)
-    close_block(1)
+    close_rows(mid_first, mid_relay)
+    close_rows(block_first, block_relay)
     for m in batches:
-        for moves in (mid_moves[m], block_moves[m], tok_moves[m]):
-            arrive(moves)
+        for moves in (y_moves[m], do_moves[m], [core_moves[m]], z_moves[m], heads_moves[m]):
             sent(moves)
-        for moves in (du_moves[m], y_moves[m], do_moves[m], [core_moves[m]], z_moves[m]):
-            sent(moves)
-        sent(heads_moves[m])
-        for copies in keep:
-            copies[m].wait()
+        keep[m].wait()
+        keep_block[m].wait()
 
 
 def tail(
-    n_dp, n_tp, group, sums, seed, middle, x, gains, out_w, qkv_w, q, kv, qpos, kpos, cos, sin
+    n_dp, n_tp, group, sums, arrived, seed, middle, x, gains, out_w, qkv_w, q, kv, qpos, kpos, cos, sin
 ):
     own_rows, depth = middle.shape
     rows = own_rows // MICRO
@@ -859,13 +998,13 @@
     gathered = jax.ShapeDtypeStruct((MICRO, n_tp, rows, depth), BF16)
     return pl.pallas_call(
         functools.partial(tail_kernel, n_dp, n_tp, group),
-        in_specs=[anywhere] * 4 + [vmem] * 4 + [anywhere] * 4 + [vmem] * 6,
-        out_specs=[vmem] + [anywhere] * 3 + [vmem],
+        in_specs=[anywhere] * 6 + [vmem] * 4 + [anywhere] * 4 + [vmem] * 6,
+        out_specs=[vmem, anywhere, anywhere, vmem, vmem],
         out_shape=[
             jax.ShapeDtypeStruct((MICRO, batch_rows, width), BF16),
             gathered,
             gathered,
-            gathered,
+            jax.ShapeDtypeStruct((MICRO, rows, depth), BF16),
             jax.ShapeDtypeStruct((2, depth), F32),
         ],
         scratch_shapes=[
@@ -873,7 +1012,6 @@
             pltpu.VMEM((MICRO, n_tp, rows, depth), BF16),
             pltpu.VMEM((MICRO, n_tp, rows, depth), BF16),
             pltpu.VMEM((MICRO, rows, depth), F32),
-            pltpu.VMEM((MICRO, rows, depth), BF16),
             pltpu.VMEM((MICRO, rows, depth), BF16),
             pltpu.VMEM((MICRO, rows, depth), BF16),
             pltpu.VMEM((MICRO, n_tp, rows, q_width), BF16),
@@ -885,7 +1023,7 @@
             pltpu.VMEM((MICRO, n_tp, rows, width), BF16),
             dma((7, 2)),
         ]
-        + [dma((MICRO, n_tp))] * 12
+        + [dma((MICRO, n_tp))] * 8
         + [dma((MICRO,))] * 2
         + [dma((MICRO, line))] * 2
         + [dma((MICRO, n_tp))] * 2,
@@ -903,6 +1041,7 @@
         sums[1][1],
         sums[0][0],
         sums[1][0],
+        *arrived,
         seed,
         middle,
         x,
@@ -1156,17 +1295,23 @@
     gain_grads = [0.0, 0.0]
     sums = [None] * MICRO
 
+    arrived = []
+
     def expand(c, m, *earlier):
-        hid, dgu, y_low, du_low = feed_forward(
-            after(u[m], *earlier), g[m], mlp_full[c], sub, sums[m]
+        carry = (n_tp, sums[m - 1][1]) if c == CHUNKS - 1 and m else ()
+        hid, dgu, y_low, du_low, *got = feed_forward(
+            after(u[m], *earlier), g[m], mlp_full[c], sub, sums[m], *carry
         )
         sums[m] = (y_low, du_low)
+        arrived.extend(got)
         return hid, dgu
 
-    def close(hids, dgus, *earlier):
-        (grads,) = outer_products(
-            core_index, [after(u[0], *earlier)] + u[1:], g, hids, dgus, own_depth, sub, False
+    def close(hids, dgus, last, *earlier):
+        carry = (n_tp, sums[-1][1]) if last else ()
+        grads, *got = outer_products(
+            [after(u[0], *earlier)] + u[1:], g, hids, dgus, own_depth, sub, *carry
         )
+        arrived.extend(got)
         return grads, lax.psum_scatter(grads, "dp", scatter_dimension=0, tiled=False)
 
     chunk_grads = []
@@ -1179,7 +1324,7 @@
             earlier = [hid, qkv_near]
             hids.append(hid)
             dgus.append(dgu)
-        grads, owned = close(hids, dgus, *earlier)
+        grads, owned = close(hids, dgus, False, *earlier)
         qkv_near = move_qkv(qkv_near)
         earlier = [grads, qkv_near]
         chunk_grads.append(owned)
@@ -1194,14 +1339,15 @@
             qkv_far = swap_cores(qkv_near)
         hids.append(hid)
         dgus.append(dgu)
-    grads, owned = close(hids, dgus, *earlier, qkv_far)
+    grads, owned = close(hids, dgus, True, *earlier, qkv_far)
     chunk_grads.append(owned)
     tail_sums = [after(sums[0], grads)] + sums[1:]
-    d_qkv, mid_rows, out_rows, tok_rows, gain_part = tail(
+    d_qkv, mid_rows, out_rows, tok_low, gain_part = tail(
         n_dp,
         n_tp,
         group,
         tail_sums,
+        arrived,
         seed[:, 0].reshape(own_rows, depth),
         middle,
         x[:, 0].reshape(own_rows, depth),
@@ -1215,24 +1361,21 @@
         cos_t,
         sin_t,
     )
+    mlp_grads = [v.reshape(own_depth, -1) for v in chunk_grads]
+    attn_part = attn_weight_grads(
+        attn_in,
+        mid_rows.reshape(rows, depth),
+        d_qkv.reshape(rows, q_width + kv_width),
+        attended.reshape(rows, q_width),
+        gain_part,
+        own_depth,
+    )
+    attn_part = after(attn_part, *chunk_grads)
+    attn_grads = lax.psum_scatter(attn_part, "dp", scatter_dimension=0, tiled=False)
+    (tok_rows,) = gather_rows(n_tp, (after(tok_low, attn_part),))
     block_output, grad_tokens = spread(rank.astype(jnp.int32).reshape(1), out_rows, tok_rows)
     block_output = block_output.reshape(rows, depth)
     grad_tokens = grad_tokens.reshape(rows, depth)
-    d_mid_rows = mid_rows.reshape(rows, depth)
-    d_qkvs = [d_qkv.reshape(rows, q_width + kv_width)]
-    gain_grads = [gain_part[0], gain_part[1]]
-
-    out_grad_t = dot_tn(d_mid_rows, attended.reshape(rows, q_width)).astype(BF16)
-    mlp_grads = [v.reshape(own_depth, -1) for v in chunk_grads]
-    qkv_grad = dot_tn(attn_in, jnp.concatenate(d_qkvs, axis=0)).astype(BF16)
-    gain_cols = jnp.stack(gain_grads, axis=1)
-    gain_cols = jnp.pad(gain_cols, ((0, 0), (0, 126))).astype(BF16)
-    attn_grads = lax.psum_scatter(
-        after(jnp.concatenate([qkv_grad, out_grad_t, gain_cols], axis=1), *chunk_grads),
-        "dp",
-        scatter_dimension=0,
-        tiled=True,
-    )
     gain_part = attn_grads[:, 2 * q_width + kv_width :]
     gain_sum = gain_part.astype(F32)
     for k in range(1, n_tp):

time: 823 us -> 760 us (0.923)
  Pallas kernels: 477 us -> 429 us
  other arithmetic: 30.2 us -> 19.3 us
  matrix products: 17 us -> 6.98 us
  waiting for transfers between devices: 195 us -> 204 us
    pallas_call x1, Pallas kernels: 277 us -> 157 us  [tail(): pl.pallas_call(functools.partial(tail_kernel, n_dp, n_tp, group), in_spec...]
    pallas_call x6 -> x8, Pallas kernels: 128 us -> 201 us  [the longest x4 99.2 us: feed_forward(): pl.pallas_call(functools.partial(gated_kernel, n_tp, last, steps), grid=(...]
    reduce_scatter x2, waiting for transfers between devices: 0.01 us -> 33 us  [close(): lax.psum_scatter(grads, 'dp', scatter_dimension=0, tiled=False)]
    reduce_scatter x1, waiting for transfers between devices: 28.8 us -> 5.7 us  [per_device(): lax.psum_scatter(attn_part, 'dp', scatter_dimension=0, tiled=False)]
    dot_general x2 -> x0, matrix products: 10 us -> none  [dot_tn(): lax.dot_general(left, right, (((0,), (0,)), ((), ())), preferred_element_...]
    concatenate x1 -> x0, other arithmetic: 8.88 us -> none  [per_device(): jnp.concatenate([qkv_grad, out_grad_t, gain_cols], axis=1)]
    unnamed x69 -> x67, local copies, waits for them, and re-layouts: 22 us -> 17.3 us
  transfers between devices with their start and end apart: 29 -> 29, of which waited for: 15 -> 16; matrix products, arithmetic and copies ran while one was open for 10% -> 8% of each run, Pallas kernels for 58% -> 57%
where the time goes in v4:
time: 760 us; the launch traced here: 756 us
  Pallas kernels  429 us (56%)
  waiting for transfers between devices  204 us (27%)
  local copies, waits for them, and re-layouts  44.6 us (6%)
  starting transfers between devices  23 us (3%)
  other arithmetic  19.3 us (3%)
  between operations  15 us (2%)
  blocking collectives  13.5 us (2%)
    pallas_call x1, Pallas kernels, tail(): pl.pallas_call(functools.partial(tail_kernel, n_dp, n_tp, group), in_spec...  157 us
    ppermute x19, waiting for transfers between devices, swap(): return lax.ppermute(value, 'tp', [(i, i ^ k) for i in range(n_tp)])  127 us
    pallas_call x4, Pallas kernels, feed_forward(): pl.pallas_call(functools.partial(gated_kernel, n_tp, last, steps), grid=(...  99.2 us
    pallas_call x2, Pallas kernels, outer_products(): pl.pallas_call(functools.partial(outer_kernel, n_tp, batches, sub, steps)...  50.1 us
    pallas_call x1, Pallas kernels, gather_rows(): pl.pallas_call(functools.partial(rows_kernel, n_tp), in_specs=[anywhere]...  39.8 us
    reduce_scatter x2, waiting for transfers between devices, close(): lax.psum_scatter(grads, 'dp', scatter_dimension=0, tiled=False)  33 us
    pallas_call x1, Pallas kernels, attend(): pl.pallas_call(functools.partial(attend_kernel, group), grid=(micro, seqs...  29.1 us
    ppermute x19, starting transfers between devices, swap(): return lax.ppermute(value, 'tp', [(i, i ^ k) for i in range(n_tp)])  22.4 us
  transfers between devices with their start and end apart: 29, of which 16 were waited for; matrix products, arithmetic and copies ran while one was open for 8% of the time, Pallas kernels for 57%

profile of v4, /device:TPU:0, one launch (start us, length us, event | category | flops | bytes accessed | tf_op | source)
XLA Modules:
  0.0 755.5 jit_solution(15447204986228357013)
XLA Ops:
  7.2 1.8 pad_maximum_fusion.6
  9.1 1.8 copy.174
  14.6 13.5 %all_gather.21.refs_9_ = bf16[2,2048]{1,0:T(2,128)(2,1)S(1)} all-gather(bf16[2,256]{1,0:T(2,128)(2,1)S(1)} %copy-done.22), channel_id=1, replica_groups=mesh['dp'=8,'tp'=4] {'dp'}, dimensions={1}, use_global_device_ids=true | all-gather | bytes 9216 | tf_op jit(solution)/shard_map/all_gather | solution.py:1216
  28.0 2.8 constant_dynamic-slice_fusion.10
  30.8 2.3 pad_maximum_fusion
  33.8 17.5 %all-gather.7.cloned.1.call-done.w_ref = bf16[2048,768]{1,0:T(8,128)(2,1)} async-done(((bf16[256,768]{1,0:T(8,128)(2,1)}), bf16[2048,768]{1,0:T(8,128)(2,1)}) %all-gather.7.cloned.1.call-update) | async-done | bytes 3145744 | tf_op jit(solution)/shard_map/all_gather | solution.py:1213
  51.3 11.0 %project.1 = (bf16[1024,2048]{1,0:T(8,128)(2,1)}, bf16[1024,768]{1,0:T(8,128)(2,1)}) custom-call(bf16[1024,2048]{1,0:T(8,128)(2,1)} %bitcast.96, bf16[1,2048]{1,0:T(2,128)(2,1)} %get-tuple-element.276.gain_ref, bf16[2048,768]{1,0:T(8,128)(2,1)} %all-gather.7.cloned.1.call-done.w_ref, f32[128,768]{1,0:T(8,128)} %concatenate.68.cos_ref.refs_18_, ...), custom_call_target="tpu_custom_call" | custom-call | flops 161061280 | bytes 419430 | tf_op jit(solution)/shard_map/project/pallas_call | solution.py:79
  62.3 2.0 slice.172
  64.4 2.3 copy.183
  70.9 10.6 %all-gather.9.cloned.1.call-done = bf16[2048,512]{1,0:T(8,128)(2,1)} async-done(((bf16[256,512]{1,0:T(8,128)(2,1)}), bf16[2048,512]{1,0:T(8,128)(2,1)}) %all-gather.9.cloned.1.call-update) | async-done | bytes 2097168 | tf_op jit(solution)/shard_map/all_gather | solution.py:1217
  82.8 2.4 collective-permute-start.5
  86.3 23.4 %collective-permute-done.5 = bf16[1024,512]{1,0:T(8,128)(2,1)S(1)} collective-permute-done((bf16[1024,512]{1,0:T(8,128)(2,1)S(1)}, bf16[1024,512]{1,0:T(8,128)(2,1)S(1)}, u32[]{:S(2)}, u32[]{:S(2)}) %collective-permute-start.5) | collective-permute-done | bytes 1048608 | tf_op jit(solution)/shard_map/ppermute | solution.py:1126
  109.8 21.7 %collective-permute-done.4 = bf16[1024,512]{1,0:T(8,128)(2,1)S(1)} collective-permute-done((bf16[1024,512]{1,0:T(8,128)(2,1)S(1)}, bf16[1024,512]{1,0:T(8,128)(2,1)S(1)}, u32[]{:S(2)}, u32[]{:S(2)}) %collective-permute-start.4) | collective-permute-done | bytes 1048608 | tf_op jit(solution)/shard_map/ppermute | solution.py:1126
  131.6 2.3 pad_maximum_fusion.1.refs_10_
  136.5 29.1 %attend.1 = bf16[2,4,128,512]{3,2,1,0:T(8,128)(2,1)} custom-call(s32[128,1]{1,0:T(8,128)} %copy.173.qpos_ref.refs_16_, s32[1,1024]{1,0:T(1,128)} %add.180.kpos_ref.refs_17_, bf16[2,4,128,512]{3,2,1,0:T(8,128)(2,1)} %slice.171.q_ref.refs_14_, bf16[8,2,4,128,256]{4,3,2,1,0:T(8,128)(2,1)} %bitcast.94), custom_call_target="tpu_custom_call" | custom-call | flops 429496736 | bytes 314572 | tf_op jit(solution)/shard_map/attend/pallas_call | solution.py:192
  166.9 1.7 collective-permute-start.2
  170.4 6.6 collective-permute-done.2
  177.0 5.2 collective-permute-done.1
  182.2 3.5 fusion.8
  185.7 3.5 fusion.7
  189.7 2.1 multiply_convert_fusion
  196.1 20.8 %collective-permute-done.7 = bf16[256,2048]{1,0:T(8,128)(2,1)S(1)} collective-permute-done((bf16[256,2048]{1,0:T(8,128)(2,1)S(1)}, bf16[256,2048]{1,0:T(8,128)(2,1)S(1)}, u32[]{:S(2)}, u32[]{:S(2)}) %collective-permute-start.7) | collective-permute-done | bytes 1048608 | tf_op jit(solution)/shard_map/ppermute | solution.py:1126
  221.1 9.8 %collective-permute-done.9 = bf16[128,2048]{1,0:T(8,128)(2,1)S(1)} collective-permute-done((bf16[128,2048]{1,0:T(8,128)(2,1)S(1)}, bf16[128,2048]{1,0:T(8,128)(2,1)S(1)}, u32[]{:S(2)}, u32[]{:S(2)}) %collective-permute-start.9) | collective-permute-done | bytes 524320 | tf_op jit(solution)/shard_map/ppermute | solution.py:1126
  230.9 1.5 pad_maximum_fusion.3.u_ref.refs_0_
  235.7 2.5 fusion.20
  239.2 3.5 dynamic_update_slice.21
  242.7 1.5 pad_maximum_fusion.4.u_ref.refs_1_
  244.2 10.0 %collective-permute-done.11 = bf16[512,768]{1,0:T(8,128)(2,1)S(1)} collective-permute-done((bf16[512,768]{1,0:T(8,128)(2,1)S(1)}, bf16[512,768]{1,0:T(8,128)(2,1)S(1)}, u32[]{:S(2)}, u32[]{:S(2)}) %collective-permute-start.11) | collective-permute-done | bytes 786464 | tf_op jit(solution)/shard_map/ppermute | solution.py:1126
  256.0 23.2 %feed_forward.4 = (bf16[512,1024]{1,0:T(8,128)(2,1)}, bf16[512,2048]{1,0:T(8,128)(2,1)}, bf16[512,2048]{1,0:T(8,128)(2,1)}, bf16[512,2048]{1,0:T(8,128)(2,1)}) custom-call(bf16[512,2048]{1,0:T(8,128)(2,1)} %pad_maximum_fusion.3.u_ref.refs_0_, bf16[512,2048]{1,0:T(8,128)(2,1)} %bitcast.85, bf16[2048,3072]{1,0:T(8,128)(2,1)} %all-gather.11.cloned.1.call-done.w_ref), custom_call_target="tpu_custom_call" | custom-call | flops 644245120 | bytes 1048576 | tf_op jit(solution)/shard_map/feed_forward/pallas_call | solution.py:435
  279.3 21.9 %feed_forward.5 = (bf16[512,1024]{1,0:T(8,128)(2,1)}, bf16[512,2048]{1,0:T(8,128)(2,1)}, bf16[512,2048]{1,0:T(8,128)(2,1)}, bf16[512,2048]{1,0:T(8,128)(2,1)}) custom-call(bf16[512,2048]{1,0:T(8,128)(2,1)} %pad_maximum_fusion.4.u_ref.refs_1_, bf16[512,2048]{1,0:T(8,128)(2,1)} %bitcast.89, bf16[2048,3072]{1,0:T(8,128)(2,1)} %all-gather.11.cloned.1.call-done.w_ref), custom_call_target="tpu_custom_call" | custom-call | flops 644245120 | bytes 1048576 | tf_op jit(solution)/shard_map/feed_forward/pallas_call | solution.py:435
  303.1 19.4 %outer_products.2 = bf16[8,256,3072]{2,1,0:T(8,128)(2,1)} custom-call(bf16[512,2048]{1,0:T(8,128)(2,1)} %pad_maximum_fusion.3.u_ref.refs_0_, bf16[512,2048]{1,0:T(8,128)(2,1)} %pad_maximum_fusion.4.u_ref.refs_1_, bf16[512,2048]{1,0:T(8,128)(2,1)} %bitcast.86, bf16[512,2048]{1,0:T(8,128)(2,1)} %bitcast.90, bf16[512,1024]{1,0:T(8,128)(2,1)} %get-tuple-element.73.refs_4_, ...), custom_call_target="tpu_custom_call" | custom-call | flops 644245120 | bytes 629145 | tf_op jit(solution)/shard_map/outer_products/pallas_call | solution.py:519
  323.6 1.9 collective-permute-start.15
  326.6 18.5 %collective-permute-done.15 = bf16[512,768]{1,0:T(8,128)(2,1)S(1)} collective-permute-done((bf16[512,768]{1,0:T(8,128)(2,1)S(1)}, bf16[512,768]{1,0:T(8,128)(2,1)S(1)}, u32[]{:S(2)}, u32[]{:S(2)}) %collective-permute-start.15) | collective-permute-done | bytes 786464 | tf_op jit(solution)/shard_map/ppermute | solution.py:1126
  346.0 9.2 %collective-permute-done.16 = bf16[512,768]{1,0:T(8,128)(2,1)S(1)} collective-permute-done((bf16[512,768]{1,0:T(8,128)(2,1)S(1)}, bf16[512,768]{1,0:T(8,128)(2,1)S(1)}, u32[]{:S(2)}, u32[]{:S(2)}) %collective-permute-start.16) | collective-permute-done | bytes 786464 | tf_op jit(solution)/shard_map/ppermute | solution.py:1126
  356.1 10.7 %all-gather.13.cloned.1.call-done.w_ref = bf16[2048,3072]{1,0:T(8,128)(2,1)} async-done(((bf16[256,3072]{1,0:T(8,128)(2,1)}), bf16[2048,3072]{1,0:T(8,128)(2,1)}) %all-gather.13.cloned.1.call-update) | async-done | bytes 12582928 | tf_op jit(solution)/shard_map/all_gather | solution.py:1248
  366.8 22.1 %feed_forward.6 = (bf16[512,1024]{1,0:T(8,128)(2,1)}, bf16[512,2048]{1,0:T(8,128)(2,1)}, bf16[512,2048]{1,0:T(8,128)(2,1)}, bf16[512,2048]{1,0:T(8,128)(2,1)}) custom-call(bf16[512,2048]{1,0:T(8,128)(2,1)} %pad_maximum_fusion.3.u_ref.refs_0_, bf16[512,2048]{1,0:T(8,128)(2,1)} %bitcast.87, bf16[2048,3072]{1,0:T(8,128)(2,1)} %all-gather.13.cloned.1.call-done.w_ref, ...), custom_call_target="tpu_custom_call" | custom-call | flops 644245120 | bytes 1048576 | tf_op jit(solution)/shard_map/feed_forward/pallas_call | solution.py:435
  388.9 31.9 %feed_forward.7 = (bf16[512,1024]{1,0:T(8,128)(2,1)}, bf16[512,2048]{1,0:T(8,128)(2,1)}, bf16[512,2048]{1,0:T(8,128)(2,1)}, bf16[512,2048]{1,0:T(8,128)(2,1)}, bf16[4,128,2048]{2,1,0:T(8,128)(2,1)}) custom-call(bf16[512,2048]{1,0:T(8,128)(2,1)} %pad_maximum_fusion.4.u_ref.refs_1_, bf16[512,2048]{1,0:T(8,128)(2,1)} %bitcast.91, ...), custom_call_target="tpu_custom_call" | custom-call | flops 644245120 | bytes 1048576 | tf_op jit(solution)/shard_map/feed_forward/pallas_call | solution.py:435
  420.8 30.7 %outer_products.3 = (bf16[8,256,3072]{2,1,0:T(8,128)(2,1)}, bf16[4,128,2048]{2,1,0:T(8,128)(2,1)}) custom-call(bf16[512,2048]{1,0:T(8,128)(2,1)} %pad_maximum_fusion.3.u_ref.refs_0_, bf16[512,2048]{1,0:T(8,128)(2,1)} %pad_maximum_fusion.4.u_ref.refs_1_, bf16[512,2048]{1,0:T(8,128)(2,1)} %bitcast.88, bf16[512,2048]{1,0:T(8,128)(2,1)} %bitcast.92, ...), custom_call_target="tpu_custom_call" | custom-call | flops 644245120 | bytes 629145 | tf_op jit(solution)/shard_map/outer_products/pallas_call | solution.py:519
  451.6 156.5 %tail.1 = (bf16[2,512,768]{2,1,0:T(8,128)(2,1)}, bf16[2,4,128,2048]{3,2,1,0:T(8,128)(2,1)}, bf16[2,4,128,2048]{3,2,1,0:T(8,128)(2,1)}, bf16[2,128,2048]{2,1,0:T(8,128)(2,1)}, f32[2,2048]{1,0:T(2,128)}) custom-call(bf16[512,2048]{1,0:T(8,128)(2,1)} %get-tuple-element.95.refs_2_.refs_0_, bf16[512,2048]{1,0:T(8,128)(2,1)} %get-tuple-element.93.refs_8_.refs_1_, ...), custom_call_target="tpu_custom_call" | custom-call | flops 500000000 | bytes 5000000 | tf_op jit(solution)/shard_map/tail/pallas_call | solution.py:999
  608.2 12.4 %attn_weight_grads.1 = bf16[8,256,1408]{2,1,0:T(8,128)(2,1)} custom-call(bf16[1024,2048]{1,0:T(8,128)(2,1)} %get-tuple-element.102.a_ref, bf16[1024,2048]{1,0:T(8,128)(2,1)} %bitcast.103, bf16[1024,768]{1,0:T(8,128)(2,1)} %bitcast.111, bf16[1024,512]{1,0:T(8,128)(2,1)} %bitcast.97, f32[2,2048]{1,0:T(2,128)} %get-tuple-element.105.gain_ref), custom_call_target="tpu_custom_call" | custom-call | flops 295279008 | bytes 419430 | tf_op jit(solution)/shard_map/attn_weight_grads/pallas_call | solution.py:557
  620.5 33.0 %reduce-scatter.6.cloned.1.call-done = bf16[1,256,3072]{2,1,0:T(8,128)(2,1)} async-done(((bf16[8,256,3072]{2,1,0:T(8,128)(2,1)}), bf16[1,256,3072]{2,1,0:T(8,128)(2,1)}) %reduce-scatter.6.cloned.1.call-update) | async-done | bytes 1572880 | tf_op jit(solution)/shard_map/reduce_scatter | solution.py:1315
  655.0 39.8 %gather_rows.1.tok_ref = bf16[2,4,128,2048]{3,2,1,0:T(8,128)(2,1)} custom-call(bf16[2,128,2048]{2,1,0:T(8,128)(2,1)} %get-tuple-element.107.refs_0_), custom_call_target="tpu_custom_call" | custom-call | flops 500000000 | bytes 5000000 | tf_op jit(solution)/shard_map/gather_rows/pallas_call | solution.py:664
  694.8 9.7 %spread.1 = (bf16[2,4,128,2048]{3,2,1,0:T(8,128)(2,1)}, f32[2,4,128,2048]{3,2,1,0:T(8,128)}) custom-call(s32[1]{0:T(128)} %bitcast.rank_ref, bf16[2,4,128,2048]{3,2,1,0:T(8,128)(2,1)} %get-tuple-element.100.out_ref, bf16[2,4,128,2048]{3,2,1,0:T(8,128)(2,1)} %gather_rows.1.tok_ref), custom_call_target="tpu_custom_call" | custom-call | tf_op jit(solution)/shard_map/spread/pallas_call | solution.py:1069
  704.5 7.1 weight_step.3
  711.6 14.0 %weight_step.2 = (f32[2,256,2048]{2,1,0:T(8,128)}, f32[2,256,2048]{2,1,0:T(8,128)}, f32[2,256,2048]{2,1,0:T(8,128)}, f32[2,256,2048]{2,1,0:T(8,128)}) custom-call(bf16[256,3072]{1,0:T(8,128)(2,1)} %bitcast.100, bf16[256,3072]{1,0:T(8,128)(2,1)} %bitcast.102, f32[2,256,2048]{2,1,0:T(8,128)} %refs_2_.2, f32[2,256,2048]{2,1,0:T(8,128)} %refs_3_.2, ...), custom_call_target="tpu_custom_call" | custom-call | flops 1048576 | bytes 1468006 | tf_op jit(solution)/shard_map/weight_step/pallas_call | solution.py:614
  725.7 5.7 reduce-scatter.8.cloned.1.call-done
  731.4 1.6 slice.201
  732.9 2.4 collective-permute-start.20
  (165 shorter events, 52.0 us)
Async XLA Ops:
  7.2 44.1 %all-gather.7.cloned.1.call-start = ((), (), s32[]{:S(2)}) async-start(), calls=%async_computation.3 | async-start | bytes 3538944 | tf_op jit(solution)/shard_map/all_gather | solution.py:1213
  9.1 72.4 %all-gather.9.cloned.1.call-start = ((), (), s32[]{:S(2)}) async-start(), calls=%async_computation.4 | async-start | bytes 2359296 | tf_op jit(solution)/shard_map/all_gather | solution.py:1217
  10.9 3.6 copy-start.22
  11.0 125.5 %all-gather.15.cloned.1.call-start = ((), (), s32[]{:S(2)}) async-start(), calls=%async_computation.10 | async-start | bytes 4718592 | tf_op jit(solution)/shard_map/all_gather | solution.py:1236
  28.0 5.1 copy-start.21
  30.8 158.8 %copy-start = (bf16[2,1,128,2048]{3,2,1,0:T(8,128)(2,1)}, bf16[2,1,128,2048]{3,2,1,0:T(8,128)(2,1)S(1)}, u32[]{:S(2)}) copy-start(bf16[2,1,128,2048]{3,2,1,0:T(8,128)(2,1)S(1)} %get-tuple-element.246) | copy-start | bytes 3145732
  62.3 4.4 copy-start.2
  64.4 191.7 %all-gather.11.cloned.1.call-start = ((), (), s32[]{:S(2)}) async-start(), calls=%async_computation.5 | async-start | bytes 14155776 | tf_op jit(solution)/shard_map/all_gather | solution.py:1248
  66.8 1.3 copy-start.5
  69.4 1.2 copy-start.7
  69.4 297.3 %all-gather.13.cloned.1.call-start = ((), (), s32[]{:S(2)}) async-start(), calls=%async_computation.6 | async-start | bytes 14155776 | tf_op jit(solution)/shard_map/all_gather | solution.py:1248
  70.6 549.9 %reduce-scatter.4.cloned.1.call-start = ((), (), s32[]{:S(2)}) async-start(), calls=%async_computation.7 | async-start | bytes 14155776 | tf_op jit(solution)/shard_map/reduce_scatter | solution.py:1315
  82.8 52.6 %copy-start.9 = (bf16[1024,768]{1,0:T(8,128)(2,1)S(1)}, bf16[1024,768]{1,0:T(8,128)(2,1)}, u32[]{:S(2)}) copy-start(bf16[1024,768]{1,0:T(8,128)(2,1)} %get-tuple-element.72) | copy-start | bytes 4718596
  82.8 27.0 %collective-permute-start.5 = (bf16[1024,512]{1,0:T(8,128)(2,1)S(1)}, bf16[1024,512]{1,0:T(8,128)(2,1)S(1)}, u32[]{:S(2)}, u32[]{:S(2)}) collective-permute-start(bf16[1024,512]{1,0:T(8,128)(2,1)S(1)} %constant_dynamic-slice_fusion.5), channel_id=1, source_target_pairs={{0,3},{1,2},{2,1},{3,0},{4,7},{5,6},{6,5},{7,4},{8,11},{9,10},{10,... | collective-permute-start | bytes 3145736 | tf_op jit(solution)/shard_map/ppermute | solution.py:1126
  85.2 46.3 %collective-permute-start.4 = (bf16[1024,512]{1,0:T(8,128)(2,1)S(1)}, bf16[1024,512]{1,0:T(8,128)(2,1)S(1)}, u32[]{:S(2)}, u32[]{:S(2)}) collective-permute-start(bf16[1024,512]{1,0:T(8,128)(2,1)S(1)} %constant_dynamic-slice_fusion.5), channel_id=1, source_target_pairs={{0,2},{1,3},{2,0},{3,1},{4,6},{5,7},{6,4},{7,5},{8,10},{9,11},{10,... | collective-permute-start | bytes 3145736 | tf_op jit(solution)/shard_map/ppermute | solution.py:1126
  85.8 45.8 %collective-permute-start.3 = (bf16[1024,512]{1,0:T(8,128)(2,1)S(1)}, bf16[1024,512]{1,0:T(8,128)(2,1)S(1)}, u32[]{:S(2)}, u32[]{:S(2)}) collective-permute-start(bf16[1024,512]{1,0:T(8,128)(2,1)S(1)} %constant_dynamic-slice_fusion.5), channel_id=1, source_target_pairs={{0,1},{1,0},{2,3},{3,2},{4,5},{5,4},{6,7},{7,6},{8,9},{9,8},{10,11... | collective-permute-start | bytes 3145736 | tf_op jit(solution)/shard_map/ppermute | solution.py:1126
  133.9 51.8 %collective-permute-start.6 = (bf16[1024,2048]{1,0:T(8,128)(2,1)}, bf16[1024,2048]{1,0:T(8,128)(2,1)}, u32[]{:S(2)}, u32[]{:S(2)}) collective-permute-start(bf16[1024,2048]{1,0:T(8,128)(2,1)} %pad_maximum_fusion.1.refs_10_), channel_id=1, source_target_pairs={{0,4},{4,0},{8,12},{12,8},{16,20},{20,16},{24,28},{28,24},{1,5},{5... | collective-permute-start | bytes 12582920 | tf_op jit(solution)/shard_map/ppermute | solution.py:1201
  166.9 10.1 %collective-permute-start.2 = (bf16[2,128,512]{2,1,0:T(8,128)(2,1)S(1)}, bf16[2,128,512]{2,1,0:T(8,128)(2,1)S(1)}, u32[]{:S(2)}, u32[]{:S(2)}) collective-permute-start(bf16[2,128,512]{2,1,0:T(8,128)(2,1)S(1)} %get-tuple-element.273), channel_id=1, source_target_pairs={{0,3},{1,2},{2,1},{3,0},{4,7},{5,6},{6,5},{7,4},{8,11},{9,10},{10,... | collective-permute-start | bytes 786440 | tf_op jit(solution)/shard_map/ppermute | solution.py:1126
  168.6 13.6 %collective-permute-start.1 = (bf16[2,128,512]{2,1,0:T(8,128)(2,1)S(1)}, bf16[2,128,512]{2,1,0:T(8,128)(2,1)S(1)}, u32[]{:S(2)}, u32[]{:S(2)}) collective-permute-start(bf16[2,128,512]{2,1,0:T(8,128)(2,1)S(1)} %get-tuple-element.274), channel_id=1, source_target_pairs={{0,2},{1,3},{2,0},{3,1},{4,6},{5,7},{6,4},{7,5},{8,10},{9,11},{10,... | collective-permute-start | bytes 786440 | tf_op jit(solution)/shard_map/ppermute | solution.py:1126
  169.8 12.3 %collective-permute-start = (bf16[2,128,512]{2,1,0:T(8,128)(2,1)S(1)}, bf16[2,128,512]{2,1,0:T(8,128)(2,1)S(1)}, u32[]{:S(2)}, u32[]{:S(2)}) collective-permute-start(bf16[2,128,512]{2,1,0:T(8,128)(2,1)S(1)} %get-tuple-element.275), channel_id=1, source_target_pairs={{0,1},{1,0},{2,3},{3,2},{4,5},{5,4},{6,7},{7,6},{8,9},{9,8},{10,11... | collective-permute-start | bytes 786440 | tf_op jit(solution)/shard_map/ppermute | solution.py:1126
  189.7 3.5 copy-start.4
  191.7 25.2 %collective-permute-start.7 = (bf16[256,2048]{1,0:T(8,128)(2,1)S(1)}, bf16[256,2048]{1,0:T(8,128)(2,1)S(1)}, u32[]{:S(2)}, u32[]{:S(2)}) collective-permute-start(bf16[256,2048]{1,0:T(8,128)(2,1)S(1)} %get-tuple-element.238), channel_id=1, source_target_pairs={{0,1},{1,0},{2,3},{3,2},{4,5},{5,4},{6,7},{7,6},{8,9},{9,8},{10,11... | collective-permute-start | bytes 3145736 | tf_op jit(solution)/shard_map/ppermute | solution.py:1126
  193.7 2.3 copy-start.3
  194.7 25.3 %collective-permute-start.8 = (bf16[256,2048]{1,0:T(8,128)(2,1)S(1)}, bf16[256,2048]{1,0:T(8,128)(2,1)S(1)}, u32[]{:S(2)}, u32[]{:S(2)}) collective-permute-start(bf16[256,2048]{1,0:T(8,128)(2,1)S(1)} %get-tuple-element.238), channel_id=1, source_target_pairs={{0,2},{1,3},{2,0},{3,1},{4,6},{5,7},{6,4},{7,5},{8,10},{9,11},{10,... | collective-permute-start | bytes 3145736 | tf_op jit(solution)/shard_map/ppermute | solution.py:1126
  217.1 13.8 %collective-permute-start.9 = (bf16[128,2048]{1,0:T(8,128)(2,1)S(1)}, bf16[128,2048]{1,0:T(8,128)(2,1)S(1)}, u32[]{:S(2)}, u32[]{:S(2)}) collective-permute-start(bf16[128,2048]{1,0:T(8,128)(2,1)S(1)} %get-tuple-element.269), channel_id=1, source_target_pairs={{0,2},{1,3},{2,0},{3,1},{4,6},{5,7},{6,4},{7,5},{8,10},{9,11},{10,... | collective-permute-start | bytes 1572872 | tf_op jit(solution)/shard_map/ppermute | solution.py:1126
  220.1 22.6 %collective-permute-start.10 = (bf16[128,2048]{1,0:T(8,128)(2,1)S(1)}, bf16[128,2048]{1,0:T(8,128)(2,1)S(1)}, u32[]{:S(2)}, u32[]{:S(2)}) collective-permute-start(bf16[128,2048]{1,0:T(8,128)(2,1)S(1)} %get-tuple-element.270), channel_id=1, source_target_pairs={{0,1},{1,0},{2,3},{3,2},{4,5},{5,4},{6,7},{7,6},{8,9},{9,8},{10,11... | collective-permute-start | bytes 1572872 | tf_op jit(solution)/shard_map/ppermute | solution.py:1126
  232.5 5.8 copy-start.12
  232.5 22.6 %collective-permute-start.12 = (bf16[512,768]{1,0:T(8,128)(2,1)S(1)}, bf16[512,768]{1,0:T(8,128)(2,1)S(1)}, u32[]{:S(2)}, u32[]{:S(2)}) collective-permute-start(bf16[512,768]{1,0:T(8,128)(2,1)S(1)} %get-tuple-element.253), channel_id=1, source_target_pairs={{0,2},{1,3},{2,0},{3,1},{4,6},{5,7},{6,4},{7,5},{8,10},{9,11},{10,... | collective-permute-start | bytes 2359304 | tf_op jit(solution)/shard_map/ppermute | solution.py:1126
  233.7 20.5 %collective-permute-start.11 = (bf16[512,768]{1,0:T(8,128)(2,1)S(1)}, bf16[512,768]{1,0:T(8,128)(2,1)S(1)}, u32[]{:S(2)}, u32[]{:S(2)}) collective-permute-start(bf16[512,768]{1,0:T(8,128)(2,1)S(1)} %get-tuple-element.253), channel_id=1, source_target_pairs={{0,1},{1,0},{2,3},{3,2},{4,5},{5,4},{6,7},{7,6},{8,9},{9,8},{10,11... | collective-permute-start | bytes 2359304 | tf_op jit(solution)/shard_map/ppermute | solution.py:1126
  234.6 66.6 %collective-permute-start.13 = (bf16[512,768]{1,0:T(8,128)(2,1)S(1)}, bf16[512,768]{1,0:T(8,128)(2,1)S(1)}, u32[]{:S(2)}, u32[]{:S(2)}) collective-permute-start(bf16[512,768]{1,0:T(8,128)(2,1)S(1)} %get-tuple-element.252), channel_id=1, source_target_pairs={{0,1},{1,0},{2,3},{3,2},{4,5},{5,4},{6,7},{7,6},{8,9},{9,8},{10,11... | collective-permute-start | bytes 2359304 | tf_op jit(solution)/shard_map/ppermute | solution.py:1126
  238.3 63.9 %collective-permute-start.14 = (bf16[512,768]{1,0:T(8,128)(2,1)S(1)}, bf16[512,768]{1,0:T(8,128)(2,1)S(1)}, u32[]{:S(2)}, u32[]{:S(2)}) collective-permute-start(bf16[512,768]{1,0:T(8,128)(2,1)S(1)} %get-tuple-element.252), channel_id=1, source_target_pairs={{0,2},{1,3},{2,0},{3,1},{4,6},{5,7},{6,4},{7,5},{8,10},{9,11},{10,... | collective-permute-start | bytes 2359304 | tf_op jit(solution)/shard_map/ppermute | solution.py:1126
  322.5 331.0 %reduce-scatter.6.cloned.1.call-start = ((), (), s32[]{:S(2)}) async-start(), calls=%async_computation.8 | async-start | bytes 14155776 | tf_op jit(solution)/shard_map/reduce_scatter | solution.py:1315
  323.6 21.4 %collective-permute-start.15 = (bf16[512,768]{1,0:T(8,128)(2,1)S(1)}, bf16[512,768]{1,0:T(8,128)(2,1)S(1)}, u32[]{:S(2)}, u32[]{:S(2)}) collective-permute-start(bf16[512,768]{1,0:T(8,128)(2,1)S(1)} %copy-done.13), channel_id=1, source_target_pairs={{0,3},{1,2},{2,1},{3,0},{4,7},{5,6},{6,5},{7,4},{8,11},{9,10},{10,... | collective-permute-start | bytes 2359304 | tf_op jit(solution)/shard_map/ppermute | solution.py:1126
  325.5 29.6 %collective-permute-start.16 = (bf16[512,768]{1,0:T(8,128)(2,1)S(1)}, bf16[512,768]{1,0:T(8,128)(2,1)S(1)}, u32[]{:S(2)}, u32[]{:S(2)}) collective-permute-start(bf16[512,768]{1,0:T(8,128)(2,1)S(1)} %get-tuple-element.252), channel_id=1, source_target_pairs={{0,3},{1,2},{2,1},{3,0},{4,7},{5,6},{6,5},{7,4},{8,11},{9,10},{10,... | collective-permute-start | bytes 2359304 | tf_op jit(solution)/shard_map/ppermute | solution.py:1126
  356.1 64.7 %collective-permute-start.17 = (bf16[1024,3072]{1,0:T(8,128)(2,1)}, bf16[1024,3072]{1,0:T(8,128)(2,1)}, u32[]{:S(2)}, u32[]{:S(2)}) collective-permute-start(bf16[1024,3072]{1,0:T(8,128)(2,1)} %constant_dynamic-update-slice_fusion.3.refs_12_), channel_id=1, source_target_pairs={{0,4},{4,0},{8,12},{12,8},{16,20},{20,16},{24,28},{28,24},{1,5},{5... | collective-permute-start | bytes 18874376 | tf_op jit(solution)/shard_map/ppermute | solution.py:1201
  451.6 279.8 %reduce-scatter.8.cloned.1.call-start = ((), (), s32[]{:S(2)}) async-start(), calls=%async_computation.9 | async-start | bytes 6488064 | tf_op jit(solution)/shard_map/reduce_scatter | solution.py:1374
  653.5 1.3 copy-start.18
  711.6 24.8 %copy-start.6 = (bf16[512,256]{0,1:T(8,128)(2,1)S(1)}, bf16[512,256]{0,1:T(8,128)(2,1)}, u32[]{:S(2)}) copy-start(bf16[512,256]{0,1:T(8,128)(2,1)} %copy.174) | copy-start | bytes 786436
  725.6 12.2 %copy-start.14 = (bf16[256,256]{1,0:T(8,128)(2,1)S(1)}, bf16[256,256]{1,0:T(8,128)(2,1)}, u32[]{:S(2)}) copy-start(bf16[256,256]{1,0:T(8,128)(2,1)} %param.25) | copy-start | bytes 393220
  725.7 12.1 %copy-start.19 = (f32[256,256]{1,0:T(8,128)S(1)}, f32[256,256]{1,0:T(8,128)}, u32[]{:S(2)}) copy-start(f32[256,256]{1,0:T(8,128)} %param.33) | copy-start | bytes 786436
  731.4 6.4 copy-start.10
  731.4 6.5 copy-start.20
  732.9 5.9 copy-start.11
  732.9 5.9 copy-start.15
  732.9 5.9 copy-start.16
  732.9 11.5 %collective-permute-start.20 = (bf16[256,128]{1,0:T(8,128)(2,1)}, bf16[256,128]{1,0:T(8,128)(2,1)}, u32[]{:S(2)}, u32[]{:S(2)}) collective-permute-start(bf16[256,128]{1,0:T(8,128)(2,1)} %slice.201), channel_id=1, source_target_pairs={{0,3},{1,2},{2,1},{3,0},{4,7},{5,6},{6,5},{7,4},{8,11},{9,10},{10,... | collective-permute-start | bytes 196616 | tf_op jit(solution)/shard_map/ppermute | solution.py:1126
  735.3 9.1 %collective-permute-start.19 = (bf16[256,128]{1,0:T(8,128)(2,1)}, bf16[256,128]{1,0:T(8,128)(2,1)}, u32[]{:S(2)}, u32[]{:S(2)}) collective-permute-start(bf16[256,128]{1,0:T(8,128)(2,1)} %slice.201), channel_id=1, source_target_pairs={{0,2},{1,3},{2,0},{3,1},{4,6},{5,7},{6,4},{7,5},{8,10},{9,11},{10,... | collective-permute-start | bytes 196616 | tf_op jit(solution)/shard_map/ppermute | solution.py:1126
  735.9 8.5 %collective-permute-start.18 = (bf16[256,128]{1,0:T(8,128)(2,1)}, bf16[256,128]{1,0:T(8,128)(2,1)}, u32[]{:S(2)}, u32[]{:S(2)}) collective-permute-start(bf16[256,128]{1,0:T(8,128)(2,1)} %slice.201), channel_id=1, source_target_pairs={{0,1},{1,0},{2,3},{3,2},{4,5},{5,4},{6,7},{7,6},{8,9},{9,8},{10,11... | collective-permute-start | bytes 196616 | tf_op jit(solution)/shard_map/ppermute | solution.py:1126
  (6 other events, 5.8 us)
Sparse Core Ops, SparseCore 0:
  10.3 40.9 all-gather.6
  53.5 27.9 all-gather.8
  83.6 46.6 all-gather.14
  132.4 115.4 all-gather.10
  249.4 117.3 all-gather.12
  368.9 127.9 reduce-scatter.3
  499.2 154.1 reduce-scatter.5
  655.8 75.5 reduce-scatter.7

commit v5 on v4

--- a/solution.py
+++ b/solution.py
@@ -538,40 +538,63 @@
     )(*us, *gs, *hids, *dgus, *([carry] if n_tp else []))
 
 
-def attn_grad_kernel(a_ref, m_ref, qkv_ref, att_ref, gain_ref, out_ref):
-    width = qkv_ref.shape[1]
-    both = width + att_ref.shape[1]
-    out_ref[0, :, :width] = dot_tn(a_ref[...], qkv_ref[...]).astype(BF16)
-    out_ref[0, :, width:both] = dot_tn(m_ref[...], att_ref[...]).astype(BF16)
-    gains = gain_ref[...]
-    filler = jnp.zeros((out_ref.shape[2] - both - gains.shape[0], gains.shape[1]), F32)
-    out_ref[0, :, both:] = jnp.concatenate([gains, filler], axis=0).T.astype(BF16)
-
-
-def attn_weight_grads(attn_in, d_mid, d_qkv, attended, gain_grads, own):
+def attn_grad_kernel(a_ref, m_ref, qkv_ref, att_ref, out_qkv, out_output):
+    out_qkv[0] = dot_tn(a_ref[...], qkv_ref[...]).astype(BF16)
+    out_output[0] = dot_tn(m_ref[...], att_ref[...]).astype(BF16)
+
+
+def attn_weight_grads(attn_in, d_mid, d_qkv, attended, own):
     rows, depth = attn_in.shape
-    width, q_width = d_qkv.shape[1], attended.shape[1]
-    total = width + q_width + 128
     column = pl.BlockSpec((rows, own), lambda i: (0, i))
     whole = functools.partial(pl.BlockSpec, pipeline_mode=pl.Buffered(1))
+    widths = (d_qkv.shape[1], attended.shape[1])
     return pl.pallas_call(
         attn_grad_kernel,
         grid=(depth // own,),
-        in_specs=[
-            column,
-            column,
-            whole((rows, width), lambda i: (0, 0)),
-            whole((rows, q_width), lambda i: (0, 0)),
-            pl.BlockSpec((2, own), lambda i: (0, i)),
-        ],
-        out_specs=pl.BlockSpec((1, own, total), lambda i: (i, 0, 0)),
-        out_shape=jax.ShapeDtypeStruct((depth // own, own, total), BF16),
+        in_specs=[column, column] + [whole((rows, w), lambda i: (0, 0)) for w in widths],
+        out_specs=[pl.BlockSpec((1, own, w), lambda i: (i, 0, 0)) for w in widths],
+        out_shape=[jax.ShapeDtypeStruct((depth // own, own, w), BF16) for w in widths],
         compiler_params=pltpu.CompilerParams(vmem_limit_bytes=VMEM_LIMIT),
         cost_estimate=hint(
-            flops=2 * rows * depth * total, bytes_accessed=4 * rows * depth, transcendentals=0
+            flops=2 * rows * depth * sum(widths), bytes_accessed=4 * rows * depth, transcendentals=0
         ),
         name="attn_weight_grads",
-    )(attn_in, d_mid, d_qkv, attended, gain_grads)
+    )(attn_in, d_mid, d_qkv, attended)
+
+
+def small_steps_kernel(qkv_ref, out_ref, gain_ref, *refs):
+    states, results = refs[:12], refs[12:]
+    q_width = states[0].shape[1]
+    gradients = (
+        lambda: qkv_ref[0, :, :q_width].astype(F32),
+        lambda: qkv_ref[0, :, q_width:].astype(F32),
+        lambda: out_ref[...].T,
+        lambda: gain_ref[...],
+    )
+    for i, read in enumerate(gradients):
+        gradient = read()
+        mean_ref, square_ref, weight_ref = states[3 * i : 3 * i + 3]
+        decay = weight_decay if i < 3 else 0.0
+        moment, spread, change = adam_update(
+            gradient, mean_ref[...], square_ref[...], weight_ref[...].astype(F32), decay
+        )
+        for ref, value in zip(results[4 * i : 4 * i + 4], (gradient, moment, spread, change)):
+            ref[...] = value
+
+
+def small_steps(qkv_grad, out_grad, gain_grad, *states):
+    vmem = pl.BlockSpec(memory_space=pltpu.VMEM)
+    shapes = [jax.ShapeDtypeStruct(states[3 * i].shape, F32) for i in range(4)]
+    return tuple(
+        pl.pallas_call(
+            small_steps_kernel,
+            in_specs=[vmem] * 15,
+            out_specs=[vmem] * 16,
+            out_shape=[shape for shape in shapes for _ in range(4)],
+            compiler_params=pltpu.CompilerParams(vmem_limit_bytes=VMEM_LIMIT),
+            name="small_steps",
+        )(qkv_grad, out_grad, gain_grad, *states)
+    )
 
 
 def step_kernel(turned, decay, steps, chunks, *refs):
@@ -626,54 +649,157 @@
     )
 
 
-def rows_kernel(n_tp, *refs):
-    count = (len(refs) - 1) // 4
-    lows, gots, sems = refs[:count], refs[count : 2 * count], refs[2 * count : -1]
-    local_sem = refs[-1]
+def finish_kernel(
+    n_dp,
+    n_tp,
+    tok_low,
+    share_ref,
+    gain_ref,
+    tok_rows,
+    grad_ref,
+    gain_own,
+    met,
+    z_send,
+    z_got,
+    ranks_got,
+    gain_sum,
+    gain_got,
+    local_sem,
+    tok_s,
+    tok_r,
+    core_s,
+    core_r,
+    z_s,
+    z_r,
+    rank_s,
+    rank_r,
+    gain_s,
+    gain_r,
+):
+    line = n_dp // 2
+    own = share_ref.shape[1]
     dp, tp = lax.axis_index("dp"), lax.axis_index("tp")
+    place, core = dp // 2, dp % 2
 
     def rank(k):
         return (dp, paired(tp, k))
 
-    meet([rank(k) for k in range(1, n_tp)])
-    plans = [
-        row_moves(remote, rank, n_tp, lows[i], gots[i], sems[2 * i], sems[2 * i + 1])
-        for i in range(count)
-    ]
+    def columns(index):
+        return pl.ds(pl.multiple_of(index * own, own), own)
+
+    first, relay = row_moves(remote, rank, n_tp, tok_low, tok_rows, tok_s, tok_r)
     keep = [
-        pltpu.make_async_copy(lows[i].at[m], gots[i].at[m, 0], local_sem.at[i, m])
-        for i in range(count)
+        pltpu.make_async_copy(tok_low.at[m], tok_rows.at[m, 0], local_sem.at[m])
         for m in range(MICRO)
     ]
-    for first, _ in plans:
-        for moves in first:
-            start(moves)
+    core_moves = [
+        remote(
+            share_ref.at[z * 2 + 1 - core],
+            met.at[z],
+            core_s.at[z],
+            core_r.at[z],
+            (place * 2 + 1 - core, tp),
+        )
+        for z in range(line)
+    ]
+    z_moves = [
+        remote(
+            z_send.at[k], z_got.at[k], z_s.at[k], z_r.at[k], (paired(place, k) * 2 + core, tp)
+        )
+        for k in range(1, line)
+    ]
+    rank_moves = [
+        remote(gain_ref, ranks_got.at[k], rank_s.at[k], rank_r.at[k], rank(k))
+        for k in range(1, n_tp)
+    ]
+    gain_moves = [
+        remote(
+            gain_sum.at[:, columns(paired(dp, j))],
+            gain_got.at[j],
+            gain_s.at[j],
+            gain_r.at[j],
+            (paired(dp, j), tp),
+        )
+        for j in range(1, n_dp)
+    ]
+
+    meet([rank(k) for k in range(1, n_tp)] + [(paired(dp, j), tp) for j in range(1, n_dp)])
+    start(core_moves)
+    start(rank_moves)
+    for moves in first:
+        start(moves)
     start(keep)
-    for first, relay in plans:
-        relay_rows(first, relay)
-    for first, relay in plans:
-        close_rows(first, relay)
+    arrive(core_moves)
+    for k in range(1, line):
+        there = paired(place, k)
+        total = share_ref[there * 2 + core].astype(F32) + met[there].astype(F32)
+        z_send[k] = total.astype(BF16)
+    start(z_moves)
+    arrive(rank_moves)
+    total = gain_ref[...]
+    for k in range(1, n_tp):
+        total = total + ranks_got[k]
+    gain_sum[...] = total
+    start(gain_moves)
+    relay_rows(first, relay)
+    arrive(gain_moves)
+    total = gain_sum[:, columns(dp)]
+    for j in range(1, n_dp):
+        total = total + gain_got[j]
+    gain_own[...] = total
+    arrive(z_moves)
+    total = share_ref[dp].astype(F32) + met[place].astype(F32)
+    for k in range(1, line):
+        total = total + z_got[k].astype(F32)
+    grad_ref[...] = total
+    close_rows(first, relay)
+    for moves in (core_moves, z_moves, rank_moves, gain_moves):
+        sent(moves)
     for copy in keep:
         copy.wait()
 
 
-def gather_rows(n_tp, lows):
-    micro, rows, depth = lows[0].shape
-    count = len(lows)
+def finish(n_dp, n_tp, tok_low, shares, gain_part):
+    micro, rows, depth = tok_low.shape
+    _, own, width = shares.shape
+    line = n_dp // 2
     anywhere = pl.BlockSpec(memory_space=pl.ANY)
+    vmem = pl.BlockSpec(memory_space=pltpu.VMEM)
+    dma = pltpu.SemaphoreType.DMA
     return pl.pallas_call(
-        functools.partial(rows_kernel, n_tp),
-        in_specs=[anywhere] * count,
-        out_specs=[anywhere] * count,
-        out_shape=[jax.ShapeDtypeStruct((micro, n_tp, rows, depth), BF16)] * count,
-        scratch_shapes=[pltpu.SemaphoreType.DMA((micro, n_tp))] * (2 * count)
-        + [pltpu.SemaphoreType.DMA((count, micro))],
+        functools.partial(finish_kernel, n_dp, n_tp),
+        in_specs=[anywhere, vmem, vmem],
+        out_specs=[anywhere, vmem, vmem],
+        out_shape=[
+            jax.ShapeDtypeStruct((micro, n_tp, rows, depth), BF16),
+            jax.ShapeDtypeStruct((own, width), F32),
+            jax.ShapeDtypeStruct((2, own), F32),
+        ],
+        scratch_shapes=[
+            pltpu.VMEM((line, own, width), BF16),
+            pltpu.VMEM((line, own, width), BF16),
+            pltpu.VMEM((line, own, width), BF16),
+            pltpu.VMEM((n_tp, 2, depth), F32),
+            pltpu.VMEM((2, depth), F32),
+            pltpu.VMEM((n_dp, 2, own), F32),
+            dma((micro,)),
+            dma((micro, n_tp)),
+            dma((micro, n_tp)),
+            dma((line,)),
+            dma((line,)),
+            dma((line,)),
+            dma((line,)),
+            dma((n_tp,)),
+            dma((n_tp,)),
+            dma((n_dp,)),
+            dma((n_dp,)),
+        ],
         compiler_params=pltpu.CompilerParams(
             collective_id=1, has_side_effects=True, vmem_limit_bytes=VMEM_LIMIT
         ),
         cost_estimate=hint(flops=10**10, bytes_accessed=10**8, transcendentals=0),
-        name="gather_rows",
-    )(*lows)
+        name="finish",
+    )(tok_low, shares, gain_part)
 
 
 def tail_kernel(n_dp, n_tp, group, *refs):
@@ -1362,42 +1488,44 @@
         sin_t,
     )
     mlp_grads = [v.reshape(own_depth, -1) for v in chunk_grads]
-    attn_part = attn_weight_grads(
+    qkv_shares, out_shares = attn_weight_grads(
         attn_in,
         mid_rows.reshape(rows, depth),
         d_qkv.reshape(rows, q_width + kv_width),
         attended.reshape(rows, q_width),
-        gain_part,
         own_depth,
     )
-    attn_part = after(attn_part, *chunk_grads)
-    attn_grads = lax.psum_scatter(attn_part, "dp", scatter_dimension=0, tiled=False)
-    (tok_rows,) = gather_rows(n_tp, (after(tok_low, attn_part),))
+    tok_rows, out_grad, gain_grad = finish(n_dp, n_tp, tok_low, out_shares, gain_part)
+    qkv_shares = after(qkv_shares, out_grad, *chunk_grads)
+    qkv_grad = lax.psum_scatter(qkv_shares, "dp", scatter_dimension=0, tiled=False)
     block_output, grad_tokens = spread(rank.astype(jnp.int32).reshape(1), out_rows, tok_rows)
     block_output = block_output.reshape(rows, depth)
     grad_tokens = grad_tokens.reshape(rows, depth)
-    gain_part = attn_grads[:, 2 * q_width + kv_width :]
-    gain_sum = gain_part.astype(F32)
-    for k in range(1, n_tp):
-        gain_sum = gain_sum + swap(gain_part, k).astype(F32)
-
-    grad_query = attn_grads[:, :q_width].astype(F32)
-    grad_keyval = attn_grads[:, q_width : q_width + kv_width].astype(F32)
-    grad_output = attn_grads[:, q_width + kv_width : 2 * q_width + kv_width].astype(F32).T
-    grad_gains = gain_sum[:, :2].T
-    def with_update(gradient, old_mean, square, weight, decay):
-        return (gradient,) + adam_update(gradient, old_mean, square, weight.astype(F32), decay)
-
+    small = small_steps(
+        qkv_grad.reshape(1, own_depth, q_width + kv_width),
+        out_grad,
+        gain_grad,
+        mean_query,
+        square_query,
+        w_query,
+        mean_keyval,
+        square_keyval,
+        w_keyval,
+        mean_output,
+        square_output,
+        w_output,
+        mean_gains,
+        square_gains,
+        norm_gains,
+    )
     return (
         (block_output, grad_tokens)
-        + with_update(grad_query, mean_query, square_query, w_query, weight_decay)
-        + with_update(grad_keyval, mean_keyval, square_keyval, w_keyval, weight_decay)
-        + with_update(grad_output, mean_output, square_output, w_output, weight_decay)
+        + small[:12]
         + step_from_chunks(
             mlp_grads, mean_gateup, square_gateup, w_gateup, sub, 0, False, weight_decay
         )
         + step_from_chunks(mlp_grads, mean_down, square_down, w_down, sub, 2, True, weight_decay)
-        + with_update(grad_gains, mean_gains, square_gains, norm_gains, 0.0)
+        + small[12:]
     )
 
 

time: 760 us -> 746 us (0.982)
  Pallas kernels: 429 us -> 444 us
  local copies, waits for them, and re-layouts: 44.6 us -> 33.5 us
  waiting for transfers between devices: 204 us -> 195 us
    reduce_scatter x2, waiting for transfers between devices: 33 us -> 0.43 us  [close(): lax.psum_scatter(grads, 'dp', scatter_dimension=0, tiled=False)]
    reduce_scatter x1, waiting for transfers between devices: 5.7 us -> 28.5 us  [per_device(): lax.psum_scatter(qkv_shares, 'dp', scatter_dimension=0, tiled=False)]
    pallas_call x1 -> x2, Pallas kernels: 39.8 us -> 55.1 us  [the longest x1 50.1 us: finish(): pl.pallas_call(functools.partial(finish_kernel, n_dp, n_tp), in_specs=[an...]
    unnamed x67 -> x29, local copies, waits for them, and re-layouts: 17.3 us -> 8.43 us
    ppermute x19 -> x16, starting transfers between devices: 22.4 us -> 19 us  [swap(): return lax.ppermute(value, 'tp', [(i, i ^ k) for i in range(n_tp)])]
    ppermute x19 -> x16, waiting for transfers between devices: 127 us -> 127 us  [swap(): return lax.ppermute(value, 'tp', [(i, i ^ k) for i in range(n_tp)])]
  transfers between devices with their start and end apart: 29 -> 26, of which waited for: 16 -> 16; matrix products, arithmetic and copies ran while one was open for 8% -> 7% of each run, Pallas kernels for 57% -> 59%
where the time goes in v5:
time: 746 us; the launch traced here: 741 us
  Pallas kernels  444 us (60%)
  waiting for transfers between devices  195 us (26%)
  local copies, waits for them, and re-layouts  33.5 us (4%)
  starting transfers between devices  19.6 us (3%)
  between operations  14.8 us (2%)
  other arithmetic  14.3 us (2%)
  blocking collectives  13.5 us (2%)
    pallas_call x1, Pallas kernels, tail(): pl.pallas_call(functools.partial(tail_kernel, n_dp, n_tp, group), in_spec...  157 us
    ppermute x16, waiting for transfers between devices, swap(): return lax.ppermute(value, 'tp', [(i, i ^ k) for i in range(n_tp)])  127 us
    pallas_call x4, Pallas kernels, feed_forward(): pl.pallas_call(functools.partial(gated_kernel, n_tp, last, steps), grid=(...  99.3 us
    pallas_call x1, Pallas kernels, finish(): pl.pallas_call(functools.partial(finish_kernel, n_dp, n_tp), in_specs=[an...  50.1 us
    pallas_call x2, Pallas kernels, outer_products(): pl.pallas_call(functools.partial(outer_kernel, n_tp, batches, sub, steps)...  50.1 us
    pallas_call x1, Pallas kernels, attend(): pl.pallas_call(functools.partial(attend_kernel, group), grid=(micro, seqs...  29.1 us
    reduce_scatter x1, waiting for transfers between devices, per_device(): lax.psum_scatter(qkv_shares, 'dp', scatter_dimension=0, tiled=False)  28.5 us
    pallas_call x2, Pallas kernels, step_from_chunks(): pl.pallas_call(functools.partial(step_kernel, turned, decay, steps, chunk...  21 us
  transfers between devices with their start and end apart: 26, of which 16 were waited for; matrix products, arithmetic and copies ran while one was open for 7% of the time, Pallas kernels for 59%

profile of v5, /device:TPU:0, one launch (start us, length us, event | category | flops | bytes accessed | tf_op | source)
XLA Modules:
  0.0 740.8 jit_solution(16050047195289511753)
XLA Ops:
  7.2 1.8 pad_maximum_fusion.6
  9.1 1.8 copy.117
  14.6 13.5 %all_gather.21.refs_9_ = bf16[2,2048]{1,0:T(2,128)(2,1)S(1)} all-gather(bf16[2,256]{1,0:T(2,128)(2,1)S(1)} %copy-done.10), channel_id=1, replica_groups=mesh['dp'=8,'tp'=4] {'dp'}, dimensions={1}, use_global_device_ids=true | all-gather | bytes 9216 | tf_op jit(solution)/shard_map/all_gather | solution.py:1342
  28.0 2.7 constant_dynamic-slice_fusion.10
  30.8 2.3 pad_maximum_fusion
  33.7 17.6 %all-gather.7.cloned.1.call-done.w_ref = bf16[2048,768]{1,0:T(8,128)(2,1)} async-done(((bf16[256,768]{1,0:T(8,128)(2,1)}), bf16[2048,768]{1,0:T(8,128)(2,1)}) %all-gather.7.cloned.1.call-update) | async-done | bytes 3145744 | tf_op jit(solution)/shard_map/all_gather | solution.py:1339
  51.3 11.0 %project.1 = (bf16[1024,2048]{1,0:T(8,128)(2,1)}, bf16[1024,768]{1,0:T(8,128)(2,1)}) custom-call(bf16[1024,2048]{1,0:T(8,128)(2,1)} %bitcast.84, bf16[1,2048]{1,0:T(2,128)(2,1)} %get-tuple-element.196.gain_ref, bf16[2048,768]{1,0:T(8,128)(2,1)} %all-gather.7.cloned.1.call-done.w_ref, f32[128,768]{1,0:T(8,128)} %concatenate.68.cos_ref.refs_18_, ...), custom_call_target="tpu_custom_call" | custom-call | flops 161061280 | bytes 419430 | tf_op jit(solution)/shard_map/project/pallas_call | solution.py:79
  62.3 2.0 slice.152
  64.4 2.3 copy.126
  70.9 10.6 %all-gather.9.cloned.1.call-done = bf16[2048,512]{1,0:T(8,128)(2,1)} async-done(((bf16[256,512]{1,0:T(8,128)(2,1)}), bf16[2048,512]{1,0:T(8,128)(2,1)}) %all-gather.9.cloned.1.call-update) | async-done | bytes 2097168 | tf_op jit(solution)/shard_map/all_gather | solution.py:1343
  82.8 2.4 collective-permute-start.5
  86.3 23.4 %collective-permute-done.5 = bf16[1024,512]{1,0:T(8,128)(2,1)S(1)} collective-permute-done((bf16[1024,512]{1,0:T(8,128)(2,1)S(1)}, bf16[1024,512]{1,0:T(8,128)(2,1)S(1)}, u32[]{:S(2)}, u32[]{:S(2)}) %collective-permute-start.5) | collective-permute-done | bytes 1048608 | tf_op jit(solution)/shard_map/ppermute | solution.py:1252
  109.8 21.7 %collective-permute-done.4 = bf16[1024,512]{1,0:T(8,128)(2,1)S(1)} collective-permute-done((bf16[1024,512]{1,0:T(8,128)(2,1)S(1)}, bf16[1024,512]{1,0:T(8,128)(2,1)S(1)}, u32[]{:S(2)}, u32[]{:S(2)}) %collective-permute-start.4) | collective-permute-done | bytes 1048608 | tf_op jit(solution)/shard_map/ppermute | solution.py:1252
  131.6 2.3 pad_maximum_fusion.1.refs_10_
  136.5 29.1 %attend.1 = bf16[2,4,128,512]{3,2,1,0:T(8,128)(2,1)} custom-call(s32[128,1]{1,0:T(8,128)} %copy.116.qpos_ref.refs_16_, s32[1,1024]{1,0:T(1,128)} %add.111.kpos_ref.refs_17_, bf16[2,4,128,512]{3,2,1,0:T(8,128)(2,1)} %slice.151.q_ref.refs_14_, bf16[8,2,4,128,256]{4,3,2,1,0:T(8,128)(2,1)} %bitcast.82), custom_call_target="tpu_custom_call" | custom-call | flops 429496736 | bytes 314572 | tf_op jit(solution)/shard_map/attend/pallas_call | solution.py:192
  166.8 1.7 collective-permute-start.2
  170.4 6.6 collective-permute-done.2
  177.0 5.2 collective-permute-done.1
  182.2 3.5 fusion.5
  185.7 3.5 fusion.4
  189.7 2.1 multiply_convert_fusion
  196.1 20.8 %collective-permute-done.7 = bf16[256,2048]{1,0:T(8,128)(2,1)S(1)} collective-permute-done((bf16[256,2048]{1,0:T(8,128)(2,1)S(1)}, bf16[256,2048]{1,0:T(8,128)(2,1)S(1)}, u32[]{:S(2)}, u32[]{:S(2)}) %collective-permute-start.7) | collective-permute-done | bytes 1048608 | tf_op jit(solution)/shard_map/ppermute | solution.py:1252
  217.0 1.5 collective-permute-start.9
  218.6 1.5 collective-permute-done.8
  221.1 9.7 %collective-permute-done.9 = bf16[128,2048]{1,0:T(8,128)(2,1)S(1)} collective-permute-done((bf16[128,2048]{1,0:T(8,128)(2,1)S(1)}, bf16[128,2048]{1,0:T(8,128)(2,1)S(1)}, u32[]{:S(2)}, u32[]{:S(2)}) %collective-permute-start.9) | collective-permute-done | bytes 524320 | tf_op jit(solution)/shard_map/ppermute | solution.py:1252
  230.8 1.5 pad_maximum_fusion.3.u_ref.refs_0_
  235.7 2.5 fusion.12
  239.1 3.5 dynamic_update_slice.21
  242.7 1.5 pad_maximum_fusion.4.u_ref.refs_1_
  244.1 10.0 %collective-permute-done.11 = bf16[512,768]{1,0:T(8,128)(2,1)S(1)} collective-permute-done((bf16[512,768]{1,0:T(8,128)(2,1)S(1)}, bf16[512,768]{1,0:T(8,128)(2,1)S(1)}, u32[]{:S(2)}, u32[]{:S(2)}) %collective-permute-start.11) | collective-permute-done | bytes 786464 | tf_op jit(solution)/shard_map/ppermute | solution.py:1252
  256.0 23.2 %feed_forward.4 = (bf16[512,1024]{1,0:T(8,128)(2,1)}, bf16[512,2048]{1,0:T(8,128)(2,1)}, bf16[512,2048]{1,0:T(8,128)(2,1)}, bf16[512,2048]{1,0:T(8,128)(2,1)}) custom-call(bf16[512,2048]{1,0:T(8,128)(2,1)} %pad_maximum_fusion.3.u_ref.refs_0_, bf16[512,2048]{1,0:T(8,128)(2,1)} %bitcast.73, bf16[2048,3072]{1,0:T(8,128)(2,1)} %all-gather.11.cloned.1.call-done.w_ref), custom_call_target="tpu_custom_call" | custom-call | flops 644245120 | bytes 1048576 | tf_op jit(solution)/shard_map/feed_forward/pallas_call | solution.py:435
  279.3 22.0 %feed_forward.5 = (bf16[512,1024]{1,0:T(8,128)(2,1)}, bf16[512,2048]{1,0:T(8,128)(2,1)}, bf16[512,2048]{1,0:T(8,128)(2,1)}, bf16[512,2048]{1,0:T(8,128)(2,1)}) custom-call(bf16[512,2048]{1,0:T(8,128)(2,1)} %pad_maximum_fusion.4.u_ref.refs_1_, bf16[512,2048]{1,0:T(8,128)(2,1)} %bitcast.77, bf16[2048,3072]{1,0:T(8,128)(2,1)} %all-gather.11.cloned.1.call-done.w_ref), custom_call_target="tpu_custom_call" | custom-call | flops 644245120 | bytes 1048576 | tf_op jit(solution)/shard_map/feed_forward/pallas_call | solution.py:435
  303.1 19.4 %outer_products.2 = bf16[8,256,3072]{2,1,0:T(8,128)(2,1)} custom-call(bf16[512,2048]{1,0:T(8,128)(2,1)} %pad_maximum_fusion.3.u_ref.refs_0_, bf16[512,2048]{1,0:T(8,128)(2,1)} %pad_maximum_fusion.4.u_ref.refs_1_, bf16[512,2048]{1,0:T(8,128)(2,1)} %bitcast.74, bf16[512,2048]{1,0:T(8,128)(2,1)} %bitcast.78, bf16[512,1024]{1,0:T(8,128)(2,1)} %get-tuple-element.93.refs_4_, ...), custom_call_target="tpu_custom_call" | custom-call | flops 644245120 | bytes 629145 | tf_op jit(solution)/shard_map/outer_products/pallas_call | solution.py:519
  322.6 2.0 collective-permute-start.15
  325.6 18.5 %collective-permute-done.15 = bf16[512,768]{1,0:T(8,128)(2,1)S(1)} collective-permute-done((bf16[512,768]{1,0:T(8,128)(2,1)S(1)}, bf16[512,768]{1,0:T(8,128)(2,1)S(1)}, u32[]{:S(2)}, u32[]{:S(2)}) %collective-permute-start.15) | collective-permute-done | bytes 786464 | tf_op jit(solution)/shard_map/ppermute | solution.py:1252
  345.0 9.2 %collective-permute-done.16 = bf16[512,768]{1,0:T(8,128)(2,1)S(1)} collective-permute-done((bf16[512,768]{1,0:T(8,128)(2,1)S(1)}, bf16[512,768]{1,0:T(8,128)(2,1)S(1)}, u32[]{:S(2)}, u32[]{:S(2)}) %collective-permute-start.16) | collective-permute-done | bytes 786464 | tf_op jit(solution)/shard_map/ppermute | solution.py:1252
  355.2 10.6 %all-gather.13.cloned.1.call-done.w_ref = bf16[2048,3072]{1,0:T(8,128)(2,1)} async-done(((bf16[256,3072]{1,0:T(8,128)(2,1)}), bf16[2048,3072]{1,0:T(8,128)(2,1)}) %all-gather.13.cloned.1.call-update) | async-done | bytes 12582928 | tf_op jit(solution)/shard_map/all_gather | solution.py:1374
  365.8 22.1 %feed_forward.6 = (bf16[512,1024]{1,0:T(8,128)(2,1)}, bf16[512,2048]{1,0:T(8,128)(2,1)}, bf16[512,2048]{1,0:T(8,128)(2,1)}, bf16[512,2048]{1,0:T(8,128)(2,1)}) custom-call(bf16[512,2048]{1,0:T(8,128)(2,1)} %pad_maximum_fusion.3.u_ref.refs_0_, bf16[512,2048]{1,0:T(8,128)(2,1)} %bitcast.75, bf16[2048,3072]{1,0:T(8,128)(2,1)} %all-gather.13.cloned.1.call-done.w_ref, ...), custom_call_target="tpu_custom_call" | custom-call | flops 644245120 | bytes 1048576 | tf_op jit(solution)/shard_map/feed_forward/pallas_call | solution.py:435
  387.9 32.0 %feed_forward.7 = (bf16[512,1024]{1,0:T(8,128)(2,1)}, bf16[512,2048]{1,0:T(8,128)(2,1)}, bf16[512,2048]{1,0:T(8,128)(2,1)}, bf16[512,2048]{1,0:T(8,128)(2,1)}, bf16[4,128,2048]{2,1,0:T(8,128)(2,1)}) custom-call(bf16[512,2048]{1,0:T(8,128)(2,1)} %pad_maximum_fusion.4.u_ref.refs_1_, bf16[512,2048]{1,0:T(8,128)(2,1)} %bitcast.79, ...), custom_call_target="tpu_custom_call" | custom-call | flops 644245120 | bytes 1048576 | tf_op jit(solution)/shard_map/feed_forward/pallas_call | solution.py:435
  419.9 30.7 %outer_products.3 = (bf16[8,256,3072]{2,1,0:T(8,128)(2,1)}, bf16[4,128,2048]{2,1,0:T(8,128)(2,1)}) custom-call(bf16[512,2048]{1,0:T(8,128)(2,1)} %pad_maximum_fusion.3.u_ref.refs_0_, bf16[512,2048]{1,0:T(8,128)(2,1)} %pad_maximum_fusion.4.u_ref.refs_1_, bf16[512,2048]{1,0:T(8,128)(2,1)} %bitcast.76, bf16[512,2048]{1,0:T(8,128)(2,1)} %bitcast.80, ...), custom_call_target="tpu_custom_call" | custom-call | flops 644245120 | bytes 629145 | tf_op jit(solution)/shard_map/outer_products/pallas_call | solution.py:519
  450.7 156.7 %tail.1 = (bf16[2,512,768]{2,1,0:T(8,128)(2,1)}, bf16[2,4,128,2048]{3,2,1,0:T(8,128)(2,1)}, bf16[2,4,128,2048]{3,2,1,0:T(8,128)(2,1)}, bf16[2,128,2048]{2,1,0:T(8,128)(2,1)}, f32[2,2048]{1,0:T(2,128)}) custom-call(bf16[512,2048]{1,0:T(8,128)(2,1)} %get-tuple-element.115.refs_2_.refs_0_, bf16[512,2048]{1,0:T(8,128)(2,1)} %get-tuple-element.113.refs_8_.refs_1_, ...), custom_call_target="tpu_custom_call" | custom-call | flops 500000000 | bytes 5000000 | tf_op jit(solution)/shard_map/tail/pallas_call | solution.py:1125
  607.4 11.6 %attn_weight_grads.1 = (bf16[8,256,768]{2,1,0:T(8,128)(2,1)}, bf16[8,256,512]{2,1,0:T(8,128)(2,1)}) custom-call(bf16[1024,2048]{1,0:T(8,128)(2,1)} %get-tuple-element.122.a_ref, bf16[1024,2048]{1,0:T(8,128)(2,1)} %bitcast.93, bf16[1024,768]{1,0:T(8,128)(2,1)} %bitcast.100, bf16[1024,512]{1,0:T(8,128)(2,1)} %bitcast.86), custom_call_target="tpu_custom_call" | custom-call | flops 268435456 | bytes 419430 | tf_op jit(solution)/shard_map/attn_weight_grads/pallas_call | solution.py:551
  619.0 50.1 %finish.1 = (bf16[2,4,128,2048]{3,2,1,0:T(8,128)(2,1)}, f32[256,512]{1,0:T(8,128)}, f32[2,256]{1,0:T(2,128)}) custom-call(bf16[2,128,2048]{2,1,0:T(8,128)(2,1)} %get-tuple-element.121.tok_low, bf16[8,256,512]{2,1,0:T(8,128)(2,1)} %get-tuple-element.125.share_ref, f32[2,2048]{1,0:T(2,128)} %get-tuple-element.126.gain_ref), custom_call_target="tpu_custom_call" | custom-call | flops 500000000 | bytes 5000000 | tf_op jit(solution)/shard_map/finish/pallas_call | solution.py:769
  669.6 9.6 %spread.1 = (bf16[2,4,128,2048]{3,2,1,0:T(8,128)(2,1)}, f32[2,4,128,2048]{3,2,1,0:T(8,128)}) custom-call(s32[1]{0:T(128)} %bitcast.rank_ref, bf16[2,4,128,2048]{3,2,1,0:T(8,128)(2,1)} %get-tuple-element.120.out_ref, bf16[2,4,128,2048]{3,2,1,0:T(8,128)(2,1)} %get-tuple-element.127.tok_ref), custom_call_target="tpu_custom_call" | custom-call | tf_op jit(solution)/shard_map/spread/pallas_call | solution.py:1195
  679.2 7.1 weight_step.3
  686.3 13.9 %weight_step.2 = (f32[2,256,2048]{2,1,0:T(8,128)}, f32[2,256,2048]{2,1,0:T(8,128)}, f32[2,256,2048]{2,1,0:T(8,128)}, f32[2,256,2048]{2,1,0:T(8,128)}) custom-call(bf16[256,3072]{1,0:T(8,128)(2,1)} %bitcast.88, bf16[256,3072]{1,0:T(8,128)(2,1)} %bitcast.90, f32[2,256,2048]{2,1,0:T(8,128)} %refs_2_.4, f32[2,256,2048]{2,1,0:T(8,128)} %refs_3_.4, ...), custom_call_target="tpu_custom_call" | custom-call | flops 1048576 | bytes 1468006 | tf_op jit(solution)/shard_map/weight_step/pallas_call | solution.py:637
  700.2 28.5 %reduce-scatter.8.cloned.1.call-done.qkv_ref = bf16[1,256,768]{2,1,0:T(8,128)(2,1)} async-done(((bf16[8,256,768]{2,1,0:T(8,128)(2,1)}), bf16[1,256,768]{2,1,0:T(8,128)(2,1)}) %reduce-scatter.8.cloned.1.call-update) | async-done | bytes 393232 | tf_op jit(solution)/shard_map/reduce_scatter | solution.py:1500
  728.7 5.0 small_steps.1
  (106 shorter events, 34.0 us)
Async XLA Ops:
  7.2 44.1 %all-gather.7.cloned.1.call-start = ((), (), s32[]{:S(2)}) async-start(), calls=%async_computation.3 | async-start | bytes 3538944 | tf_op jit(solution)/shard_map/all_gather | solution.py:1339
  9.1 72.4 %all-gather.9.cloned.1.call-start = ((), (), s32[]{:S(2)}) async-start(), calls=%async_computation.4 | async-start | bytes 2359296 | tf_op jit(solution)/shard_map/all_gather | solution.py:1343
  10.9 3.6 copy-start.10
  11.0 125.5 %all-gather.15.cloned.1.call-start = ((), (), s32[]{:S(2)}) async-start(), calls=%async_computation.10 | async-start | bytes 4718592 | tf_op jit(solution)/shard_map/all_gather | solution.py:1362
  28.0 5.1 copy-start.9
  30.8 158.9 %copy-start = (bf16[2,1,128,2048]{3,2,1,0:T(8,128)(2,1)}, bf16[2,1,128,2048]{3,2,1,0:T(8,128)(2,1)S(1)}, u32[]{:S(2)}) copy-start(bf16[2,1,128,2048]{3,2,1,0:T(8,128)(2,1)S(1)} %get-tuple-element.166) | copy-start | bytes 3145732
  62.3 4.4 copy-start.2
  64.3 191.7 %all-gather.11.cloned.1.call-start = ((), (), s32[]{:S(2)}) async-start(), calls=%async_computation.5 | async-start | bytes 14155776 | tf_op jit(solution)/shard_map/all_gather | solution.py:1374
  66.8 1.3 copy-start.5
  68.2 1.1 copy-start.7
  69.4 1.2 copy-start.6
  69.4 296.3 %all-gather.13.cloned.1.call-start = ((), (), s32[]{:S(2)}) async-start(), calls=%async_computation.6 | async-start | bytes 14155776 | tf_op jit(solution)/shard_map/all_gather | solution.py:1374
  70.6 598.6 %reduce-scatter.4.cloned.1.call-start = ((), (), s32[]{:S(2)}) async-start(), calls=%async_computation.7 | async-start | bytes 14155776 | tf_op jit(solution)/shard_map/reduce_scatter | solution.py:1441
  82.8 52.6 %copy-start.8 = (bf16[1024,768]{1,0:T(8,128)(2,1)S(1)}, bf16[1024,768]{1,0:T(8,128)(2,1)}, u32[]{:S(2)}) copy-start(bf16[1024,768]{1,0:T(8,128)(2,1)} %get-tuple-element.92) | copy-start | bytes 4718596
  82.8 27.0 %collective-permute-start.5 = (bf16[1024,512]{1,0:T(8,128)(2,1)S(1)}, bf16[1024,512]{1,0:T(8,128)(2,1)S(1)}, u32[]{:S(2)}, u32[]{:S(2)}) collective-permute-start(bf16[1024,512]{1,0:T(8,128)(2,1)S(1)} %constant_dynamic-slice_fusion.5), channel_id=1, source_target_pairs={{0,3},{1,2},{2,1},{3,0},{4,7},{5,6},{6,5},{7,4},{8,11},{9,10},{10,... | collective-permute-start | bytes 3145736 | tf_op jit(solution)/shard_map/ppermute | solution.py:1252
  85.2 46.3 %collective-permute-start.4 = (bf16[1024,512]{1,0:T(8,128)(2,1)S(1)}, bf16[1024,512]{1,0:T(8,128)(2,1)S(1)}, u32[]{:S(2)}, u32[]{:S(2)}) collective-permute-start(bf16[1024,512]{1,0:T(8,128)(2,1)S(1)} %constant_dynamic-slice_fusion.5), channel_id=1, source_target_pairs={{0,2},{1,3},{2,0},{3,1},{4,6},{5,7},{6,4},{7,5},{8,10},{9,11},{10,... | collective-permute-start | bytes 3145736 | tf_op jit(solution)/shard_map/ppermute | solution.py:1252
  85.8 45.8 %collective-permute-start.3 = (bf16[1024,512]{1,0:T(8,128)(2,1)S(1)}, bf16[1024,512]{1,0:T(8,128)(2,1)S(1)}, u32[]{:S(2)}, u32[]{:S(2)}) collective-permute-start(bf16[1024,512]{1,0:T(8,128)(2,1)S(1)} %constant_dynamic-slice_fusion.5), channel_id=1, source_target_pairs={{0,1},{1,0},{2,3},{3,2},{4,5},{5,4},{6,7},{7,6},{8,9},{9,8},{10,11... | collective-permute-start | bytes 3145736 | tf_op jit(solution)/shard_map/ppermute | solution.py:1252
  133.9 51.8 %collective-permute-start.6 = (bf16[1024,2048]{1,0:T(8,128)(2,1)}, bf16[1024,2048]{1,0:T(8,128)(2,1)}, u32[]{:S(2)}, u32[]{:S(2)}) collective-permute-start(bf16[1024,2048]{1,0:T(8,128)(2,1)} %pad_maximum_fusion.1.refs_10_), channel_id=1, source_target_pairs={{0,4},{4,0},{8,12},{12,8},{16,20},{20,16},{24,28},{28,24},{1,5},{5... | collective-permute-start | bytes 12582920 | tf_op jit(solution)/shard_map/ppermute | solution.py:1327
  166.8 10.1 %collective-permute-start.2 = (bf16[2,128,512]{2,1,0:T(8,128)(2,1)S(1)}, bf16[2,128,512]{2,1,0:T(8,128)(2,1)S(1)}, u32[]{:S(2)}, u32[]{:S(2)}) collective-permute-start(bf16[2,128,512]{2,1,0:T(8,128)(2,1)S(1)} %get-tuple-element.193), channel_id=1, source_target_pairs={{0,3},{1,2},{2,1},{3,0},{4,7},{5,6},{6,5},{7,4},{8,11},{9,10},{10,... | collective-permute-start | bytes 786440 | tf_op jit(solution)/shard_map/ppermute | solution.py:1252
  168.6 13.6 %collective-permute-start.1 = (bf16[2,128,512]{2,1,0:T(8,128)(2,1)S(1)}, bf16[2,128,512]{2,1,0:T(8,128)(2,1)S(1)}, u32[]{:S(2)}, u32[]{:S(2)}) collective-permute-start(bf16[2,128,512]{2,1,0:T(8,128)(2,1)S(1)} %get-tuple-element.194), channel_id=1, source_target_pairs={{0,2},{1,3},{2,0},{3,1},{4,6},{5,7},{6,4},{7,5},{8,10},{9,11},{10,... | collective-permute-start | bytes 786440 | tf_op jit(solution)/shard_map/ppermute | solution.py:1252
  169.8 12.3 %collective-permute-start = (bf16[2,128,512]{2,1,0:T(8,128)(2,1)S(1)}, bf16[2,128,512]{2,1,0:T(8,128)(2,1)S(1)}, u32[]{:S(2)}, u32[]{:S(2)}) collective-permute-start(bf16[2,128,512]{2,1,0:T(8,128)(2,1)S(1)} %get-tuple-element.195), channel_id=1, source_target_pairs={{0,1},{1,0},{2,3},{3,2},{4,5},{5,4},{6,7},{7,6},{8,9},{9,8},{10,11... | collective-permute-start | bytes 786440 | tf_op jit(solution)/shard_map/ppermute | solution.py:1252
  189.6 3.5 copy-start.4
  191.7 25.2 %collective-permute-start.7 = (bf16[256,2048]{1,0:T(8,128)(2,1)S(1)}, bf16[256,2048]{1,0:T(8,128)(2,1)S(1)}, u32[]{:S(2)}, u32[]{:S(2)}) collective-permute-start(bf16[256,2048]{1,0:T(8,128)(2,1)S(1)} %get-tuple-element.158), channel_id=1, source_target_pairs={{0,1},{1,0},{2,3},{3,2},{4,5},{5,4},{6,7},{7,6},{8,9},{9,8},{10,11... | collective-permute-start | bytes 3145736 | tf_op jit(solution)/shard_map/ppermute | solution.py:1252
  193.7 1.0 copy-start.1
  193.7 2.3 copy-start.3
  194.7 25.3 %collective-permute-start.8 = (bf16[256,2048]{1,0:T(8,128)(2,1)S(1)}, bf16[256,2048]{1,0:T(8,128)(2,1)S(1)}, u32[]{:S(2)}, u32[]{:S(2)}) collective-permute-start(bf16[256,2048]{1,0:T(8,128)(2,1)S(1)} %get-tuple-element.158), channel_id=1, source_target_pairs={{0,2},{1,3},{2,0},{3,1},{4,6},{5,7},{6,4},{7,5},{8,10},{9,11},{10,... | collective-permute-start | bytes 3145736 | tf_op jit(solution)/shard_map/ppermute | solution.py:1252
  217.0 13.8 %collective-permute-start.9 = (bf16[128,2048]{1,0:T(8,128)(2,1)S(1)}, bf16[128,2048]{1,0:T(8,128)(2,1)S(1)}, u32[]{:S(2)}, u32[]{:S(2)}) collective-permute-start(bf16[128,2048]{1,0:T(8,128)(2,1)S(1)} %get-tuple-element.189), channel_id=1, source_target_pairs={{0,2},{1,3},{2,0},{3,1},{4,6},{5,7},{6,4},{7,5},{8,10},{9,11},{10,... | collective-permute-start | bytes 1572872 | tf_op jit(solution)/shard_map/ppermute | solution.py:1252
  220.1 22.5 %collective-permute-start.10 = (bf16[128,2048]{1,0:T(8,128)(2,1)S(1)}, bf16[128,2048]{1,0:T(8,128)(2,1)S(1)}, u32[]{:S(2)}, u32[]{:S(2)}) collective-permute-start(bf16[128,2048]{1,0:T(8,128)(2,1)S(1)} %get-tuple-element.190), channel_id=1, source_target_pairs={{0,1},{1,0},{2,3},{3,2},{4,5},{5,4},{6,7},{7,6},{8,9},{9,8},{10,11... | collective-permute-start | bytes 1572872 | tf_op jit(solution)/shard_map/ppermute | solution.py:1252
  232.5 22.6 %collective-permute-start.12 = (bf16[512,768]{1,0:T(8,128)(2,1)S(1)}, bf16[512,768]{1,0:T(8,128)(2,1)S(1)}, u32[]{:S(2)}, u32[]{:S(2)}) collective-permute-start(bf16[512,768]{1,0:T(8,128)(2,1)S(1)} %get-tuple-element.173), channel_id=1, source_target_pairs={{0,2},{1,3},{2,0},{3,1},{4,6},{5,7},{6,4},{7,5},{8,10},{9,11},{10,... | collective-permute-start | bytes 2359304 | tf_op jit(solution)/shard_map/ppermute | solution.py:1252
  233.7 20.5 %collective-permute-start.11 = (bf16[512,768]{1,0:T(8,128)(2,1)S(1)}, bf16[512,768]{1,0:T(8,128)(2,1)S(1)}, u32[]{:S(2)}, u32[]{:S(2)}) collective-permute-start(bf16[512,768]{1,0:T(8,128)(2,1)S(1)} %get-tuple-element.173), channel_id=1, source_target_pairs={{0,1},{1,0},{2,3},{3,2},{4,5},{5,4},{6,7},{7,6},{8,9},{9,8},{10,11... | collective-permute-start | bytes 2359304 | tf_op jit(solution)/shard_map/ppermute | solution.py:1252
  234.6 66.6 %collective-permute-start.13 = (bf16[512,768]{1,0:T(8,128)(2,1)S(1)}, bf16[512,768]{1,0:T(8,128)(2,1)S(1)}, u32[]{:S(2)}, u32[]{:S(2)}) collective-permute-start(bf16[512,768]{1,0:T(8,128)(2,1)S(1)} %get-tuple-element.172), channel_id=1, source_target_pairs={{0,1},{1,0},{2,3},{3,2},{4,5},{5,4},{6,7},{7,6},{8,9},{9,8},{10,11... | collective-permute-start | bytes 2359304 | tf_op jit(solution)/shard_map/ppermute | solution.py:1252
  238.2 64.0 %collective-permute-start.14 = (bf16[512,768]{1,0:T(8,128)(2,1)S(1)}, bf16[512,768]{1,0:T(8,128)(2,1)S(1)}, u32[]{:S(2)}, u32[]{:S(2)}) collective-permute-start(bf16[512,768]{1,0:T(8,128)(2,1)S(1)} %get-tuple-element.172), channel_id=1, source_target_pairs={{0,2},{1,3},{2,0},{3,1},{4,6},{5,7},{6,4},{7,5},{8,10},{9,11},{10,... | collective-permute-start | bytes 2359304 | tf_op jit(solution)/shard_map/ppermute | solution.py:1252
  322.6 347.0 %reduce-scatter.6.cloned.1.call-start = ((), (), s32[]{:S(2)}) async-start(), calls=%async_computation.8 | async-start | bytes 14155776 | tf_op jit(solution)/shard_map/reduce_scatter | solution.py:1441
  322.6 21.4 %collective-permute-start.15 = (bf16[512,768]{1,0:T(8,128)(2,1)S(1)}, bf16[512,768]{1,0:T(8,128)(2,1)S(1)}, u32[]{:S(2)}, u32[]{:S(2)}) collective-permute-start(bf16[512,768]{1,0:T(8,128)(2,1)S(1)} %get-tuple-element.173), channel_id=1, source_target_pairs={{0,3},{1,2},{2,1},{3,0},{4,7},{5,6},{6,5},{7,4},{8,11},{9,10},{10,... | collective-permute-start | bytes 2359304 | tf_op jit(solution)/shard_map/ppermute | solution.py:1252
  324.6 29.7 %collective-permute-start.16 = (bf16[512,768]{1,0:T(8,128)(2,1)S(1)}, bf16[512,768]{1,0:T(8,128)(2,1)S(1)}, u32[]{:S(2)}, u32[]{:S(2)}) collective-permute-start(bf16[512,768]{1,0:T(8,128)(2,1)S(1)} %get-tuple-element.172), channel_id=1, source_target_pairs={{0,3},{1,2},{2,1},{3,0},{4,7},{5,6},{6,5},{7,4},{8,11},{9,10},{10,... | collective-permute-start | bytes 2359304 | tf_op jit(solution)/shard_map/ppermute | solution.py:1252
  355.1 64.8 %collective-permute-start.17 = (bf16[1024,3072]{1,0:T(8,128)(2,1)}, bf16[1024,3072]{1,0:T(8,128)(2,1)}, u32[]{:S(2)}, u32[]{:S(2)}) collective-permute-start(bf16[1024,3072]{1,0:T(8,128)(2,1)} %constant_dynamic-update-slice_fusion.3.refs_12_), channel_id=1, source_target_pairs={{0,4},{4,0},{8,12},{12,8},{16,20},{20,16},{24,28},{28,24},{1,5},{5... | collective-permute-start | bytes 18874376 | tf_op jit(solution)/shard_map/ppermute | solution.py:1327
  450.6 278.1 %reduce-scatter.8.cloned.1.call-start = ((), (), s32[]{:S(2)}) async-start(), calls=%async_computation.9 | async-start | bytes 3538944 | tf_op jit(solution)/shard_map/reduce_scatter | solution.py:1500
Sparse Core Ops, SparseCore 0:
  10.2 40.9 all-gather.6
  53.5 27.9 all-gather.8
  83.6 46.6 all-gather.14
  132.4 115.4 all-gather.10
  249.4 116.3 all-gather.12
  367.9 127.9 reduce-scatter.3
  498.3 171.2 reduce-scatter.5
  671.9 56.8 reduce-scatter.7

commit v6 on v5

--- a/solution.py
+++ b/solution.py
@@ -295,6 +295,47 @@
 def sent(moves):
     for move in moves:
         move.wait_send()
+
+
+class LineSum:
+
+    def __init__(self, line, place, core, tp, value, send, got, send_sem, recv_sem):
+        self.value, self.send, self.got = value, send, got
+        self.slots, self.moves = [], []
+        count, step = 0, 0
+        while (1 << step) < line:
+            size = line >> (step + 1)
+            self.slots.append(list(range(count, count + size)))
+            partner = (paired(place, 1 << step) * 2 + core, tp)
+            self.moves.append(
+                [
+                    remote(send.at[i], got.at[i], send_sem.at[i], recv_sem.at[i], partner)
+                    for i in self.slots[-1]
+                ]
+            )
+            count, step = count + size, step + 1
+        self.steps = step
+
+    def held(self, r, step):
+        total = self.value(r)
+        for s in range(step):
+            total = total + self.got[self.slots[s][r >> (s + 1)]].astype(F32)
+        return total
+
+    def begin(self, step):
+        if step:
+            arrive(self.moves[step - 1])
+        for j, i in enumerate(self.slots[step]):
+            self.send[i] = self.held((1 << step) | (j << (step + 1)), step).astype(BF16)
+        start(self.moves[step])
+
+    def total(self):
+        arrive(self.moves[-1])
+        return self.held(0, self.steps)
+
+    def close(self):
+        for moves in self.moves:
+            sent(moves)
 
 
 def row_moves(remote, rank, n_tp, low, got, send, recv):
@@ -702,12 +743,18 @@
         )
         for z in range(line)
     ]
-    z_moves = [
-        remote(
-            z_send.at[k], z_got.at[k], z_s.at[k], z_r.at[k], (paired(place, k) * 2 + core, tp)
-        )
-        for k in range(1, line)
-    ]
+    sums = LineSum(
+        line,
+        place,
+        core,
+        tp,
+        lambda r: share_ref[paired(place, r) * 2 + core].astype(F32)
+        + met[paired(place, r)].astype(F32),
+        z_send,
+        z_got,
+        z_s,
+        z_r,
+    )
     rank_moves = [
         remote(gain_ref, ranks_got.at[k], rank_s.at[k], rank_r.at[k], rank(k))
         for k in range(1, n_tp)
@@ -730,30 +777,25 @@
         start(moves)
     start(keep)
     arrive(core_moves)
-    for k in range(1, line):
-        there = paired(place, k)
-        total = share_ref[there * 2 + core].astype(F32) + met[there].astype(F32)
-        z_send[k] = total.astype(BF16)
-    start(z_moves)
+    sums.begin(0)
     arrive(rank_moves)
     total = gain_ref[...]
     for k in range(1, n_tp):
         total = total + ranks_got[k]
     gain_sum[...] = total
     start(gain_moves)
+    for step in range(1, sums.steps):
+        sums.begin(step)
     relay_rows(first, relay)
     arrive(gain_moves)
     total = gain_sum[:, columns(dp)]
     for j in range(1, n_dp):
         total = total + gain_got[j]
     gain_own[...] = total
-    arrive(z_moves)
-    total = share_ref[dp].astype(F32) + met[place].astype(F32)
-    for k in range(1, line):
-        total = total + z_got[k].astype(F32)
-    grad_ref[...] = total
+    grad_ref[...] = sums.total()
     close_rows(first, relay)
-    for moves in (core_moves, z_moves, rank_moves, gain_moves):
+    sums.close()
+    for moves in (core_moves, rank_moves, gain_moves):
         sent(moves)
     for copy in keep:
         copy.wait()
@@ -904,11 +946,19 @@
         remote(shares.at[m, 1 - core], met.at[m], core_s.at[m], core_r.at[m], other_core)
         for m in batches
     ]
-    z_moves = [
-        [
-            remote(z_send.at[m, k], z_got.at[m, k], z_s.at[m, k], z_r.at[m, k], spot(k))
-            for k in range(1, line)
-        ]
+    key_sums = [
+        LineSum(
+            line,
+            place,
+            core,
+            tp,
+            lambda r, m=m: shares[m, core, paired(place, r)].astype(F32)
+            + met[m, paired(place, r)].astype(F32),
+            z_send.at[m],
+            z_got.at[m],
+            z_s.at[m],
+            z_r.at[m],
+        )
         for m in batches
     ]
     heads_moves = [
@@ -998,9 +1048,6 @@
         start(do_moves[m])
     start(load_qkv)
     for m in batches:
-        start(mid_first[m])
-        keep[m].start()
-    for m in batches:
         start(y_moves[m])
 
     def attend_back_seq(m, s):
@@ -1034,18 +1081,14 @@
 
     def send_along(m):
         arrive([core_moves[m]])
-        for k in range(1, line):
-            there = paired(place, k)
-            z_send[m, k] = (
-                shares[m, core, there].astype(F32) + met[m, there].astype(F32)
-            ).astype(BF16)
-        start(z_moves[m])
+        key_sums[m].begin(0)
+
+    def advance(m):
+        for step in range(1, key_sums[m].steps):
+            key_sums[m].begin(step)
 
     def close_keys(m):
-        arrive(z_moves[m])
-        total = shares[m, core, place].astype(F32) + met[m, place].astype(F32)
-        for k in range(1, line):
-            total = total + z_got[m, k].astype(F32)
+        total = key_sums[m].total()
         cos_k, sin_k = cos_ref[:, q_width:], sin_ref[:, q_width:]
         for s in range(SEQS):
             seq = slice(s * seq_rows, (s + 1) * seq_rows)
@@ -1084,18 +1127,23 @@
     arrive(do_moves[0])
     attend_back_range(0, 0, SEQS)
     core_moves[0].start()
+    for m in batches:
+        start(mid_first[m])
+        keep[m].start()
     arrive(do_moves[1])
     attend_back_range(1, 0, SEQS // 2)
     send_along(0)
-    relay_rows(mid_first, mid_relay)
     attend_back_range(1, SEQS // 2, SEQS)
     core_moves[1].start()
+    advance(0)
     for copy in load_qkv:
         copy.wait()
+    send_along(1)
     close_block(0)
     close_keys(0)
-    send_along(1)
+    advance(1)
     close_block(1)
+    relay_rows(mid_first, mid_relay)
     close_tokens(0)
     close_keys(1)
     relay_rows(block_first, block_relay)
@@ -1103,7 +1151,8 @@
     close_rows(mid_first, mid_relay)
     close_rows(block_first, block_relay)
     for m in batches:
-        for moves in (y_moves[m], do_moves[m], [core_moves[m]], z_moves[m], heads_moves[m]):
+        key_sums[m].close()
+        for moves in (y_moves[m], do_moves[m], [core_moves[m]], heads_moves[m]):
             sent(moves)
         keep[m].wait()
         keep_block[m].wait()

time: 746 us -> 728 us (0.976)
  waiting for transfers between devices: 195 us -> 175 us
    reduce_scatter x1, waiting for transfers between devices: 28.5 us -> 9.51 us  [per_device(): lax.psum_scatter(qkv_shares, 'dp', scatter_dimension=0, tiled=False)]
  transfers between devices with their start and end apart: 26 -> 26, of which waited for: 16 -> 15; matrix products, arithmetic and copies ran while one was open for 7% -> 7% of each run, Pallas kernels for 59% -> 61%
where the time goes in v6:
time: 728 us; the launch traced here: 723 us
  Pallas kernels  445 us (61%)
  waiting for transfers between devices  175 us (24%)
  local copies, waits for them, and re-layouts  33.5 us (5%)
  starting transfers between devices  19.6 us (3%)
  between operations  14.8 us (2%)
  other arithmetic  14.3 us (2%)
  blocking collectives  13.5 us (2%)
    pallas_call x1, Pallas kernels, tail(): pl.pallas_call(functools.partial(tail_kernel, n_dp, n_tp, group), in_spec...  157 us
    ppermute x16, waiting for transfers between devices, swap(): return lax.ppermute(value, 'tp', [(i, i ^ k) for i in range(n_tp)])  127 us
    pallas_call x4, Pallas kernels, feed_forward(): pl.pallas_call(functools.partial(gated_kernel, n_tp, last, steps), grid=(...  99.3 us
    pallas_call x1, Pallas kernels, finish(): pl.pallas_call(functools.partial(finish_kernel, n_dp, n_tp), in_specs=[an...  51.2 us
    pallas_call x2, Pallas kernels, outer_products(): pl.pallas_call(functools.partial(outer_kernel, n_tp, batches, sub, steps)...  50.1 us
    pallas_call x1, Pallas kernels, attend(): pl.pallas_call(functools.partial(attend_kernel, group), grid=(micro, seqs...  29.1 us
    pallas_call x2, Pallas kernels, step_from_chunks(): pl.pallas_call(functools.partial(step_kernel, turned, decay, steps, chunk...  21.1 us
    ppermute x16, starting transfers between devices, swap(): return lax.ppermute(value, 'tp', [(i, i ^ k) for i in range(n_tp)])  19 us
  transfers between devices with their start and end apart: 26, of which 15 were waited for; matrix products, arithmetic and copies ran while one was open for 7% of the time, Pallas kernels for 61%

profile of v6, /device:TPU:0, one launch (start us, length us, event | category | flops | bytes accessed | tf_op | source)
XLA Modules:
  0.0 722.6 jit_solution(2044518235078323459)
XLA Ops:
  7.2 1.8 pad_maximum_fusion.6
  9.1 1.8 copy.117
  14.6 13.5 %all_gather.21.refs_9_ = bf16[2,2048]{1,0:T(2,128)(2,1)S(1)} all-gather(bf16[2,256]{1,0:T(2,128)(2,1)S(1)} %copy-done.10), channel_id=1, replica_groups=mesh['dp'=8,'tp'=4] {'dp'}, dimensions={1}, use_global_device_ids=true | all-gather | bytes 9216 | tf_op jit(solution)/shard_map/all_gather | solution.py:1391
  28.0 2.7 constant_dynamic-slice_fusion.10
  30.8 2.3 pad_maximum_fusion
  33.7 17.6 %all-gather.7.cloned.1.call-done.w_ref = bf16[2048,768]{1,0:T(8,128)(2,1)} async-done(((bf16[256,768]{1,0:T(8,128)(2,1)}), bf16[2048,768]{1,0:T(8,128)(2,1)}) %all-gather.7.cloned.1.call-update) | async-done | bytes 3145744 | tf_op jit(solution)/shard_map/all_gather | solution.py:1388
  51.3 11.0 %project.1 = (bf16[1024,2048]{1,0:T(8,128)(2,1)}, bf16[1024,768]{1,0:T(8,128)(2,1)}) custom-call(bf16[1024,2048]{1,0:T(8,128)(2,1)} %bitcast.84, bf16[1,2048]{1,0:T(2,128)(2,1)} %get-tuple-element.196.gain_ref, bf16[2048,768]{1,0:T(8,128)(2,1)} %all-gather.7.cloned.1.call-done.w_ref, f32[128,768]{1,0:T(8,128)} %concatenate.68.cos_ref.refs_18_, ...), custom_call_target="tpu_custom_call" | custom-call | flops 161061280 | bytes 419430 | tf_op jit(solution)/shard_map/project/pallas_call | solution.py:79
  62.3 2.0 slice.152
  64.4 2.3 copy.126
  70.9 10.6 %all-gather.9.cloned.1.call-done = bf16[2048,512]{1,0:T(8,128)(2,1)} async-done(((bf16[256,512]{1,0:T(8,128)(2,1)}), bf16[2048,512]{1,0:T(8,128)(2,1)}) %all-gather.9.cloned.1.call-update) | async-done | bytes 2097168 | tf_op jit(solution)/shard_map/all_gather | solution.py:1392
  82.8 2.4 collective-permute-start.5
  86.3 23.4 %collective-permute-done.5 = bf16[1024,512]{1,0:T(8,128)(2,1)S(1)} collective-permute-done((bf16[1024,512]{1,0:T(8,128)(2,1)S(1)}, bf16[1024,512]{1,0:T(8,128)(2,1)S(1)}, u32[]{:S(2)}, u32[]{:S(2)}) %collective-permute-start.5) | collective-permute-done | bytes 1048608 | tf_op jit(solution)/shard_map/ppermute | solution.py:1301
  109.8 21.7 %collective-permute-done.4 = bf16[1024,512]{1,0:T(8,128)(2,1)S(1)} collective-permute-done((bf16[1024,512]{1,0:T(8,128)(2,1)S(1)}, bf16[1024,512]{1,0:T(8,128)(2,1)S(1)}, u32[]{:S(2)}, u32[]{:S(2)}) %collective-permute-start.4) | collective-permute-done | bytes 1048608 | tf_op jit(solution)/shard_map/ppermute | solution.py:1301
  131.6 2.3 pad_maximum_fusion.1.refs_10_
  136.5 29.1 %attend.1 = bf16[2,4,128,512]{3,2,1,0:T(8,128)(2,1)} custom-call(s32[128,1]{1,0:T(8,128)} %copy.116.qpos_ref.refs_16_, s32[1,1024]{1,0:T(1,128)} %add.111.kpos_ref.refs_17_, bf16[2,4,128,512]{3,2,1,0:T(8,128)(2,1)} %slice.151.q_ref.refs_14_, bf16[8,2,4,128,256]{4,3,2,1,0:T(8,128)(2,1)} %bitcast.82), custom_call_target="tpu_custom_call" | custom-call | flops 429496736 | bytes 314572 | tf_op jit(solution)/shard_map/attend/pallas_call | solution.py:192
  166.8 1.7 collective-permute-start.2
  170.4 6.6 collective-permute-done.2
  177.0 5.2 collective-permute-done.1
  182.2 3.5 fusion.5
  185.7 3.5 fusion.4
  189.7 2.1 multiply_convert_fusion
  196.1 20.8 %collective-permute-done.7 = bf16[256,2048]{1,0:T(8,128)(2,1)S(1)} collective-permute-done((bf16[256,2048]{1,0:T(8,128)(2,1)S(1)}, bf16[256,2048]{1,0:T(8,128)(2,1)S(1)}, u32[]{:S(2)}, u32[]{:S(2)}) %collective-permute-start.7) | collective-permute-done | bytes 1048608 | tf_op jit(solution)/shard_map/ppermute | solution.py:1301
  217.0 1.5 collective-permute-start.9
  218.6 1.5 collective-permute-done.8
  221.1 9.7 %collective-permute-done.9 = bf16[128,2048]{1,0:T(8,128)(2,1)S(1)} collective-permute-done((bf16[128,2048]{1,0:T(8,128)(2,1)S(1)}, bf16[128,2048]{1,0:T(8,128)(2,1)S(1)}, u32[]{:S(2)}, u32[]{:S(2)}) %collective-permute-start.9) | collective-permute-done | bytes 524320 | tf_op jit(solution)/shard_map/ppermute | solution.py:1301
  230.8 1.5 pad_maximum_fusion.3.u_ref.refs_0_
  235.7 2.5 fusion.12
  239.1 3.5 dynamic_update_slice.21
  242.7 1.5 pad_maximum_fusion.4.u_ref.refs_1_
  244.1 10.0 %collective-permute-done.11 = bf16[512,768]{1,0:T(8,128)(2,1)S(1)} collective-permute-done((bf16[512,768]{1,0:T(8,128)(2,1)S(1)}, bf16[512,768]{1,0:T(8,128)(2,1)S(1)}, u32[]{:S(2)}, u32[]{:S(2)}) %collective-permute-start.11) | collective-permute-done | bytes 786464 | tf_op jit(solution)/shard_map/ppermute | solution.py:1301
  256.0 23.2 %feed_forward.4 = (bf16[512,1024]{1,0:T(8,128)(2,1)}, bf16[512,2048]{1,0:T(8,128)(2,1)}, bf16[512,2048]{1,0:T(8,128)(2,1)}, bf16[512,2048]{1,0:T(8,128)(2,1)}) custom-call(bf16[512,2048]{1,0:T(8,128)(2,1)} %pad_maximum_fusion.3.u_ref.refs_0_, bf16[512,2048]{1,0:T(8,128)(2,1)} %bitcast.73, bf16[2048,3072]{1,0:T(8,128)(2,1)} %all-gather.11.cloned.1.call-done.w_ref), custom_call_target="tpu_custom_call" | custom-call | flops 644245120 | bytes 1048576 | tf_op jit(solution)/shard_map/feed_forward/pallas_call | solution.py:476
  279.3 22.0 %feed_forward.5 = (bf16[512,1024]{1,0:T(8,128)(2,1)}, bf16[512,2048]{1,0:T(8,128)(2,1)}, bf16[512,2048]{1,0:T(8,128)(2,1)}, bf16[512,2048]{1,0:T(8,128)(2,1)}) custom-call(bf16[512,2048]{1,0:T(8,128)(2,1)} %pad_maximum_fusion.4.u_ref.refs_1_, bf16[512,2048]{1,0:T(8,128)(2,1)} %bitcast.77, bf16[2048,3072]{1,0:T(8,128)(2,1)} %all-gather.11.cloned.1.call-done.w_ref), custom_call_target="tpu_custom_call" | custom-call | flops 644245120 | bytes 1048576 | tf_op jit(solution)/shard_map/feed_forward/pallas_call | solution.py:476
  303.1 19.4 %outer_products.2 = bf16[8,256,3072]{2,1,0:T(8,128)(2,1)} custom-call(bf16[512,2048]{1,0:T(8,128)(2,1)} %pad_maximum_fusion.3.u_ref.refs_0_, bf16[512,2048]{1,0:T(8,128)(2,1)} %pad_maximum_fusion.4.u_ref.refs_1_, bf16[512,2048]{1,0:T(8,128)(2,1)} %bitcast.74, bf16[512,2048]{1,0:T(8,128)(2,1)} %bitcast.78, bf16[512,1024]{1,0:T(8,128)(2,1)} %get-tuple-element.93.refs_4_, ...), custom_call_target="tpu_custom_call" | custom-call | flops 644245120 | bytes 629145 | tf_op jit(solution)/shard_map/outer_products/pallas_call | solution.py:560
  322.6 2.0 collective-permute-start.15
  325.6 18.5 %collective-permute-done.15 = bf16[512,768]{1,0:T(8,128)(2,1)S(1)} collective-permute-done((bf16[512,768]{1,0:T(8,128)(2,1)S(1)}, bf16[512,768]{1,0:T(8,128)(2,1)S(1)}, u32[]{:S(2)}, u32[]{:S(2)}) %collective-permute-start.15) | collective-permute-done | bytes 786464 | tf_op jit(solution)/shard_map/ppermute | solution.py:1301
  345.0 9.2 %collective-permute-done.16 = bf16[512,768]{1,0:T(8,128)(2,1)S(1)} collective-permute-done((bf16[512,768]{1,0:T(8,128)(2,1)S(1)}, bf16[512,768]{1,0:T(8,128)(2,1)S(1)}, u32[]{:S(2)}, u32[]{:S(2)}) %collective-permute-start.16) | collective-permute-done | bytes 786464 | tf_op jit(solution)/shard_map/ppermute | solution.py:1301
  355.2 10.6 %all-gather.13.cloned.1.call-done.w_ref = bf16[2048,3072]{1,0:T(8,128)(2,1)} async-done(((bf16[256,3072]{1,0:T(8,128)(2,1)}), bf16[2048,3072]{1,0:T(8,128)(2,1)}) %all-gather.13.cloned.1.call-update) | async-done | bytes 12582928 | tf_op jit(solution)/shard_map/all_gather | solution.py:1423
  365.8 22.1 %feed_forward.6 = (bf16[512,1024]{1,0:T(8,128)(2,1)}, bf16[512,2048]{1,0:T(8,128)(2,1)}, bf16[512,2048]{1,0:T(8,128)(2,1)}, bf16[512,2048]{1,0:T(8,128)(2,1)}) custom-call(bf16[512,2048]{1,0:T(8,128)(2,1)} %pad_maximum_fusion.3.u_ref.refs_0_, bf16[512,2048]{1,0:T(8,128)(2,1)} %bitcast.75, bf16[2048,3072]{1,0:T(8,128)(2,1)} %all-gather.13.cloned.1.call-done.w_ref, ...), custom_call_target="tpu_custom_call" | custom-call | flops 644245120 | bytes 1048576 | tf_op jit(solution)/shard_map/feed_forward/pallas_call | solution.py:476
  387.9 32.0 %feed_forward.7 = (bf16[512,1024]{1,0:T(8,128)(2,1)}, bf16[512,2048]{1,0:T(8,128)(2,1)}, bf16[512,2048]{1,0:T(8,128)(2,1)}, bf16[512,2048]{1,0:T(8,128)(2,1)}, bf16[4,128,2048]{2,1,0:T(8,128)(2,1)}) custom-call(bf16[512,2048]{1,0:T(8,128)(2,1)} %pad_maximum_fusion.4.u_ref.refs_1_, bf16[512,2048]{1,0:T(8,128)(2,1)} %bitcast.79, ...), custom_call_target="tpu_custom_call" | custom-call | flops 644245120 | bytes 1048576 | tf_op jit(solution)/shard_map/feed_forward/pallas_call | solution.py:476
  419.9 30.7 %outer_products.3 = (bf16[8,256,3072]{2,1,0:T(8,128)(2,1)}, bf16[4,128,2048]{2,1,0:T(8,128)(2,1)}) custom-call(bf16[512,2048]{1,0:T(8,128)(2,1)} %pad_maximum_fusion.3.u_ref.refs_0_, bf16[512,2048]{1,0:T(8,128)(2,1)} %pad_maximum_fusion.4.u_ref.refs_1_, bf16[512,2048]{1,0:T(8,128)(2,1)} %bitcast.76, bf16[512,2048]{1,0:T(8,128)(2,1)} %bitcast.80, ...), custom_call_target="tpu_custom_call" | custom-call | flops 644245120 | bytes 629145 | tf_op jit(solution)/shard_map/outer_products/pallas_call | solution.py:560
  450.7 156.7 %tail.1 = (bf16[2,512,768]{2,1,0:T(8,128)(2,1)}, bf16[2,4,128,2048]{3,2,1,0:T(8,128)(2,1)}, bf16[2,4,128,2048]{3,2,1,0:T(8,128)(2,1)}, bf16[2,128,2048]{2,1,0:T(8,128)(2,1)}, f32[2,2048]{1,0:T(2,128)}) custom-call(bf16[512,2048]{1,0:T(8,128)(2,1)} %get-tuple-element.115.refs_2_.refs_0_, bf16[512,2048]{1,0:T(8,128)(2,1)} %get-tuple-element.113.refs_8_.refs_1_, ...), custom_call_target="tpu_custom_call" | custom-call | flops 500000000 | bytes 5000000 | tf_op jit(solution)/shard_map/tail/pallas_call | solution.py:1174
  607.4 11.6 %attn_weight_grads.1 = (bf16[8,256,768]{2,1,0:T(8,128)(2,1)}, bf16[8,256,512]{2,1,0:T(8,128)(2,1)}) custom-call(bf16[1024,2048]{1,0:T(8,128)(2,1)} %get-tuple-element.122.a_ref, bf16[1024,2048]{1,0:T(8,128)(2,1)} %bitcast.93, bf16[1024,768]{1,0:T(8,128)(2,1)} %bitcast.100, bf16[1024,512]{1,0:T(8,128)(2,1)} %bitcast.86), custom_call_target="tpu_custom_call" | custom-call | flops 268435456 | bytes 419430 | tf_op jit(solution)/shard_map/attn_weight_grads/pallas_call | solution.py:592
  619.0 51.2 %finish.1 = (bf16[2,4,128,2048]{3,2,1,0:T(8,128)(2,1)}, f32[256,512]{1,0:T(8,128)}, f32[2,256]{1,0:T(2,128)}) custom-call(bf16[2,128,2048]{2,1,0:T(8,128)(2,1)} %get-tuple-element.121.tok_low, bf16[8,256,512]{2,1,0:T(8,128)(2,1)} %get-tuple-element.125.share_ref, f32[2,2048]{1,0:T(2,128)} %get-tuple-element.126.gain_ref), custom_call_target="tpu_custom_call" | custom-call | flops 500000000 | bytes 5000000 | tf_op jit(solution)/shard_map/finish/pallas_call | solution.py:811
  670.3 9.6 %spread.1 = (bf16[2,4,128,2048]{3,2,1,0:T(8,128)(2,1)}, f32[2,4,128,2048]{3,2,1,0:T(8,128)}) custom-call(s32[1]{0:T(128)} %bitcast.rank_ref, bf16[2,4,128,2048]{3,2,1,0:T(8,128)(2,1)} %get-tuple-element.120.out_ref, bf16[2,4,128,2048]{3,2,1,0:T(8,128)(2,1)} %get-tuple-element.127.tok_ref), custom_call_target="tpu_custom_call" | custom-call | tf_op jit(solution)/shard_map/spread/pallas_call | solution.py:1244
  679.9 7.1 weight_step.3
  687.0 14.0 %weight_step.2 = (f32[2,256,2048]{2,1,0:T(8,128)}, f32[2,256,2048]{2,1,0:T(8,128)}, f32[2,256,2048]{2,1,0:T(8,128)}, f32[2,256,2048]{2,1,0:T(8,128)}) custom-call(bf16[256,3072]{1,0:T(8,128)(2,1)} %bitcast.88, bf16[256,3072]{1,0:T(8,128)(2,1)} %bitcast.90, f32[2,256,2048]{2,1,0:T(8,128)} %refs_2_.4, f32[2,256,2048]{2,1,0:T(8,128)} %refs_3_.4, ...), custom_call_target="tpu_custom_call" | custom-call | flops 1048576 | bytes 1468006 | tf_op jit(solution)/shard_map/weight_step/pallas_call | solution.py:678
  701.0 9.5 %reduce-scatter.8.cloned.1.call-done.qkv_ref = bf16[1,256,768]{2,1,0:T(8,128)(2,1)} async-done(((bf16[8,256,768]{2,1,0:T(8,128)(2,1)}), bf16[1,256,768]{2,1,0:T(8,128)(2,1)}) %reduce-scatter.8.cloned.1.call-update) | async-done | bytes 393232 | tf_op jit(solution)/shard_map/reduce_scatter | solution.py:1549
  710.5 5.0 small_steps.1
  (106 shorter events, 33.6 us)
Async XLA Ops:
  7.2 44.1 %all-gather.7.cloned.1.call-start = ((), (), s32[]{:S(2)}) async-start(), calls=%async_computation.3 | async-start | bytes 3538944 | tf_op jit(solution)/shard_map/all_gather | solution.py:1388
  9.1 72.4 %all-gather.9.cloned.1.call-start = ((), (), s32[]{:S(2)}) async-start(), calls=%async_computation.4 | async-start | bytes 2359296 | tf_op jit(solution)/shard_map/all_gather | solution.py:1392
  10.9 3.6 copy-start.10
  11.0 125.5 %all-gather.15.cloned.1.call-start = ((), (), s32[]{:S(2)}) async-start(), calls=%async_computation.10 | async-start | bytes 4718592 | tf_op jit(solution)/shard_map/all_gather | solution.py:1411
  28.0 5.1 copy-start.9
  30.8 158.9 %copy-start = (bf16[2,1,128,2048]{3,2,1,0:T(8,128)(2,1)}, bf16[2,1,128,2048]{3,2,1,0:T(8,128)(2,1)S(1)}, u32[]{:S(2)}) copy-start(bf16[2,1,128,2048]{3,2,1,0:T(8,128)(2,1)S(1)} %get-tuple-element.166) | copy-start | bytes 3145732
  62.3 4.4 copy-start.2
  64.3 191.7 %all-gather.11.cloned.1.call-start = ((), (), s32[]{:S(2)}) async-start(), calls=%async_computation.5 | async-start | bytes 14155776 | tf_op jit(solution)/shard_map/all_gather | solution.py:1423
  66.8 1.3 copy-start.5
  68.2 1.1 copy-start.7
  69.4 1.2 copy-start.6
  69.4 296.3 %all-gather.13.cloned.1.call-start = ((), (), s32[]{:S(2)}) async-start(), calls=%async_computation.6 | async-start | bytes 14155776 | tf_op jit(solution)/shard_map/all_gather | solution.py:1423
  70.6 599.7 %reduce-scatter.4.cloned.1.call-start = ((), (), s32[]{:S(2)}) async-start(), calls=%async_computation.7 | async-start | bytes 14155776 | tf_op jit(solution)/shard_map/reduce_scatter | solution.py:1490
  82.8 52.6 %copy-start.8 = (bf16[1024,768]{1,0:T(8,128)(2,1)S(1)}, bf16[1024,768]{1,0:T(8,128)(2,1)}, u32[]{:S(2)}) copy-start(bf16[1024,768]{1,0:T(8,128)(2,1)} %get-tuple-element.92) | copy-start | bytes 4718596
  82.8 27.0 %collective-permute-start.5 = (bf16[1024,512]{1,0:T(8,128)(2,1)S(1)}, bf16[1024,512]{1,0:T(8,128)(2,1)S(1)}, u32[]{:S(2)}, u32[]{:S(2)}) collective-permute-start(bf16[1024,512]{1,0:T(8,128)(2,1)S(1)} %constant_dynamic-slice_fusion.5), channel_id=1, source_target_pairs={{0,3},{1,2},{2,1},{3,0},{4,7},{5,6},{6,5},{7,4},{8,11},{9,10},{10,... | collective-permute-start | bytes 3145736 | tf_op jit(solution)/shard_map/ppermute | solution.py:1301
  85.2 46.3 %collective-permute-start.4 = (bf16[1024,512]{1,0:T(8,128)(2,1)S(1)}, bf16[1024,512]{1,0:T(8,128)(2,1)S(1)}, u32[]{:S(2)}, u32[]{:S(2)}) collective-permute-start(bf16[1024,512]{1,0:T(8,128)(2,1)S(1)} %constant_dynamic-slice_fusion.5), channel_id=1, source_target_pairs={{0,2},{1,3},{2,0},{3,1},{4,6},{5,7},{6,4},{7,5},{8,10},{9,11},{10,... | collective-permute-start | bytes 3145736 | tf_op jit(solution)/shard_map/ppermute | solution.py:1301
  85.8 45.8 %collective-permute-start.3 = (bf16[1024,512]{1,0:T(8,128)(2,1)S(1)}, bf16[1024,512]{1,0:T(8,128)(2,1)S(1)}, u32[]{:S(2)}, u32[]{:S(2)}) collective-permute-start(bf16[1024,512]{1,0:T(8,128)(2,1)S(1)} %constant_dynamic-slice_fusion.5), channel_id=1, source_target_pairs={{0,1},{1,0},{2,3},{3,2},{4,5},{5,4},{6,7},{7,6},{8,9},{9,8},{10,11... | collective-permute-start | bytes 3145736 | tf_op jit(solution)/shard_map/ppermute | solution.py:1301
  133.9 51.8 %collective-permute-start.6 = (bf16[1024,2048]{1,0:T(8,128)(2,1)}, bf16[1024,2048]{1,0:T(8,128)(2,1)}, u32[]{:S(2)}, u32[]{:S(2)}) collective-permute-start(bf16[1024,2048]{1,0:T(8,128)(2,1)} %pad_maximum_fusion.1.refs_10_), channel_id=1, source_target_pairs={{0,4},{4,0},{8,12},{12,8},{16,20},{20,16},{24,28},{28,24},{1,5},{5... | collective-permute-start | bytes 12582920 | tf_op jit(solution)/shard_map/ppermute | solution.py:1376
  166.8 10.1 %collective-permute-start.2 = (bf16[2,128,512]{2,1,0:T(8,128)(2,1)S(1)}, bf16[2,128,512]{2,1,0:T(8,128)(2,1)S(1)}, u32[]{:S(2)}, u32[]{:S(2)}) collective-permute-start(bf16[2,128,512]{2,1,0:T(8,128)(2,1)S(1)} %get-tuple-element.193), channel_id=1, source_target_pairs={{0,3},{1,2},{2,1},{3,0},{4,7},{5,6},{6,5},{7,4},{8,11},{9,10},{10,... | collective-permute-start | bytes 786440 | tf_op jit(solution)/shard_map/ppermute | solution.py:1301
  168.6 13.6 %collective-permute-start.1 = (bf16[2,128,512]{2,1,0:T(8,128)(2,1)S(1)}, bf16[2,128,512]{2,1,0:T(8,128)(2,1)S(1)}, u32[]{:S(2)}, u32[]{:S(2)}) collective-permute-start(bf16[2,128,512]{2,1,0:T(8,128)(2,1)S(1)} %get-tuple-element.194), channel_id=1, source_target_pairs={{0,2},{1,3},{2,0},{3,1},{4,6},{5,7},{6,4},{7,5},{8,10},{9,11},{10,... | collective-permute-start | bytes 786440 | tf_op jit(solution)/shard_map/ppermute | solution.py:1301
  169.8 12.3 %collective-permute-start = (bf16[2,128,512]{2,1,0:T(8,128)(2,1)S(1)}, bf16[2,128,512]{2,1,0:T(8,128)(2,1)S(1)}, u32[]{:S(2)}, u32[]{:S(2)}) collective-permute-start(bf16[2,128,512]{2,1,0:T(8,128)(2,1)S(1)} %get-tuple-element.195), channel_id=1, source_target_pairs={{0,1},{1,0},{2,3},{3,2},{4,5},{5,4},{6,7},{7,6},{8,9},{9,8},{10,11... | collective-permute-start | bytes 786440 | tf_op jit(solution)/shard_map/ppermute | solution.py:1301
  189.6 3.5 copy-start.4
  191.7 25.2 %collective-permute-start.7 = (bf16[256,2048]{1,0:T(8,128)(2,1)S(1)}, bf16[256,2048]{1,0:T(8,128)(2,1)S(1)}, u32[]{:S(2)}, u32[]{:S(2)}) collective-permute-start(bf16[256,2048]{1,0:T(8,128)(2,1)S(1)} %get-tuple-element.158), channel_id=1, source_target_pairs={{0,1},{1,0},{2,3},{3,2},{4,5},{5,4},{6,7},{7,6},{8,9},{9,8},{10,11... | collective-permute-start | bytes 3145736 | tf_op jit(solution)/shard_map/ppermute | solution.py:1301
  193.7 1.0 copy-start.1
  193.7 2.3 copy-start.3
  194.7 25.3 %collective-permute-start.8 = (bf16[256,2048]{1,0:T(8,128)(2,1)S(1)}, bf16[256,2048]{1,0:T(8,128)(2,1)S(1)}, u32[]{:S(2)}, u32[]{:S(2)}) collective-permute-start(bf16[256,2048]{1,0:T(8,128)(2,1)S(1)} %get-tuple-element.158), channel_id=1, source_target_pairs={{0,2},{1,3},{2,0},{3,1},{4,6},{5,7},{6,4},{7,5},{8,10},{9,11},{10,... | collective-permute-start | bytes 3145736 | tf_op jit(solution)/shard_map/ppermute | solution.py:1301
  217.0 13.8 %collective-permute-start.9 = (bf16[128,2048]{1,0:T(8,128)(2,1)S(1)}, bf16[128,2048]{1,0:T(8,128)(2,1)S(1)}, u32[]{:S(2)}, u32[]{:S(2)}) collective-permute-start(bf16[128,2048]{1,0:T(8,128)(2,1)S(1)} %get-tuple-element.189), channel_id=1, source_target_pairs={{0,2},{1,3},{2,0},{3,1},{4,6},{5,7},{6,4},{7,5},{8,10},{9,11},{10,... | collective-permute-start | bytes 1572872 | tf_op jit(solution)/shard_map/ppermute | solution.py:1301
  220.1 22.5 %collective-permute-start.10 = (bf16[128,2048]{1,0:T(8,128)(2,1)S(1)}, bf16[128,2048]{1,0:T(8,128)(2,1)S(1)}, u32[]{:S(2)}, u32[]{:S(2)}) collective-permute-start(bf16[128,2048]{1,0:T(8,128)(2,1)S(1)} %get-tuple-element.190), channel_id=1, source_target_pairs={{0,1},{1,0},{2,3},{3,2},{4,5},{5,4},{6,7},{7,6},{8,9},{9,8},{10,11... | collective-permute-start | bytes 1572872 | tf_op jit(solution)/shard_map/ppermute | solution.py:1301
  232.5 22.6 %collective-permute-start.12 = (bf16[512,768]{1,0:T(8,128)(2,1)S(1)}, bf16[512,768]{1,0:T(8,128)(2,1)S(1)}, u32[]{:S(2)}, u32[]{:S(2)}) collective-permute-start(bf16[512,768]{1,0:T(8,128)(2,1)S(1)} %get-tuple-element.173), channel_id=1, source_target_pairs={{0,2},{1,3},{2,0},{3,1},{4,6},{5,7},{6,4},{7,5},{8,10},{9,11},{10,... | collective-permute-start | bytes 2359304 | tf_op jit(solution)/shard_map/ppermute | solution.py:1301
  233.7 20.5 %collective-permute-start.11 = (bf16[512,768]{1,0:T(8,128)(2,1)S(1)}, bf16[512,768]{1,0:T(8,128)(2,1)S(1)}, u32[]{:S(2)}, u32[]{:S(2)}) collective-permute-start(bf16[512,768]{1,0:T(8,128)(2,1)S(1)} %get-tuple-element.173), channel_id=1, source_target_pairs={{0,1},{1,0},{2,3},{3,2},{4,5},{5,4},{6,7},{7,6},{8,9},{9,8},{10,11... | collective-permute-start | bytes 2359304 | tf_op jit(solution)/shard_map/ppermute | solution.py:1301
  234.6 66.6 %collective-permute-start.13 = (bf16[512,768]{1,0:T(8,128)(2,1)S(1)}, bf16[512,768]{1,0:T(8,128)(2,1)S(1)}, u32[]{:S(2)}, u32[]{:S(2)}) collective-permute-start(bf16[512,768]{1,0:T(8,128)(2,1)S(1)} %get-tuple-element.172), channel_id=1, source_target_pairs={{0,1},{1,0},{2,3},{3,2},{4,5},{5,4},{6,7},{7,6},{8,9},{9,8},{10,11... | collective-permute-start | bytes 2359304 | tf_op jit(solution)/shard_map/ppermute | solution.py:1301
  238.2 64.0 %collective-permute-start.14 = (bf16[512,768]{1,0:T(8,128)(2,1)S(1)}, bf16[512,768]{1,0:T(8,128)(2,1)S(1)}, u32[]{:S(2)}, u32[]{:S(2)}) collective-permute-start(bf16[512,768]{1,0:T(8,128)(2,1)S(1)} %get-tuple-element.172), channel_id=1, source_target_pairs={{0,2},{1,3},{2,0},{3,1},{4,6},{5,7},{6,4},{7,5},{8,10},{9,11},{10,... | collective-permute-start | bytes 2359304 | tf_op jit(solution)/shard_map/ppermute | solution.py:1301
  322.6 347.7 %reduce-scatter.6.cloned.1.call-start = ((), (), s32[]{:S(2)}) async-start(), calls=%async_computation.8 | async-start | bytes 14155776 | tf_op jit(solution)/shard_map/reduce_scatter | solution.py:1490
  322.6 21.4 %collective-permute-start.15 = (bf16[512,768]{1,0:T(8,128)(2,1)S(1)}, bf16[512,768]{1,0:T(8,128)(2,1)S(1)}, u32[]{:S(2)}, u32[]{:S(2)}) collective-permute-start(bf16[512,768]{1,0:T(8,128)(2,1)S(1)} %get-tuple-element.173), channel_id=1, source_target_pairs={{0,3},{1,2},{2,1},{3,0},{4,7},{5,6},{6,5},{7,4},{8,11},{9,10},{10,... | collective-permute-start | bytes 2359304 | tf_op jit(solution)/shard_map/ppermute | solution.py:1301
  324.6 29.7 %collective-permute-start.16 = (bf16[512,768]{1,0:T(8,128)(2,1)S(1)}, bf16[512,768]{1,0:T(8,128)(2,1)S(1)}, u32[]{:S(2)}, u32[]{:S(2)}) collective-permute-start(bf16[512,768]{1,0:T(8,128)(2,1)S(1)} %get-tuple-element.172), channel_id=1, source_target_pairs={{0,3},{1,2},{2,1},{3,0},{4,7},{5,6},{6,5},{7,4},{8,11},{9,10},{10,... | collective-permute-start | bytes 2359304 | tf_op jit(solution)/shard_map/ppermute | solution.py:1301
  355.1 64.8 %collective-permute-start.17 = (bf16[1024,3072]{1,0:T(8,128)(2,1)}, bf16[1024,3072]{1,0:T(8,128)(2,1)}, u32[]{:S(2)}, u32[]{:S(2)}) collective-permute-start(bf16[1024,3072]{1,0:T(8,128)(2,1)} %constant_dynamic-update-slice_fusion.3.refs_12_), channel_id=1, source_target_pairs={{0,4},{4,0},{8,12},{12,8},{16,20},{20,16},{24,28},{28,24},{1,5},{5... | collective-permute-start | bytes 18874376 | tf_op jit(solution)/shard_map/ppermute | solution.py:1376
  450.6 259.9 %reduce-scatter.8.cloned.1.call-start = ((), (), s32[]{:S(2)}) async-start(), calls=%async_computation.9 | async-start | bytes 3538944 | tf_op jit(solution)/shard_map/reduce_scatter | solution.py:1549
Sparse Core Ops, SparseCore 0:
  10.2 40.9 all-gather.6
  53.5 27.9 all-gather.8
  83.6 46.6 all-gather.14
  132.4 115.4 all-gather.10
  249.4 116.3 all-gather.12
  367.9 127.9 reduce-scatter.3
  498.3 171.3 reduce-scatter.5
  672.0 38.5 reduce-scatter.7

commit v7 on v6

--- a/solution.py
+++ b/solution.py
@@ -64,42 +64,39 @@
     return lax.rsqrt(jnp.mean(values * values, axis=-1, keepdims=True) + norm_eps)
 
 
-def project_kernel(x_ref, gain_ref, w_ref, cos_ref, sin_ref, a_ref, qkv_ref):
+def project_kernel(x_ref, gain_ref, w_ref, cos_ref, sin_ref, out_ref, *a_ref):
     x = x_ref[...].astype(F32)
     a = (x * mean_square_scale(x) * gain_ref[...].astype(F32)).astype(BF16)
-    a_ref[...] = a
+    for ref in a_ref:
+        ref[...] = a
     t = jnp.dot(a, w_ref[...], preferred_element_type=F32)
-    qkv_ref[...] = (t * cos_ref[...] + half_turn(t) * sin_ref[...]).astype(BF16)
-
-
-def project(x, gain, weight, cos_t, sin_t):
+    out_ref[...] = (t * cos_ref[...] + half_turn(t) * sin_ref[...]).astype(BF16)
+
+
+def project(x, gain, weights, place, cos_t, sin_t, keep):
     rows, depth = x.shape
-    width = weight.shape[1]
-    block = cos_t.shape[0]
+    block, width = cos_t.shape
+    whole = functools.partial(pl.BlockSpec, pipeline_mode=pl.Buffered(1))
     return pl.pallas_call(
         project_kernel,
         grid=(rows // block,),
         in_specs=[
             pl.BlockSpec((block, depth), lambda i: (i, 0)),
             pl.BlockSpec((1, depth), lambda i: (0, 0)),
-            pl.BlockSpec((depth, width), lambda i: (0, 0)),
+            whole((depth, width), lambda i: (0, place)),
             pl.BlockSpec((block, width), lambda i: (0, 0)),
             pl.BlockSpec((block, width), lambda i: (0, 0)),
         ],
-        out_specs=[
-            pl.BlockSpec((block, depth), lambda i: (i, 0)),
-            pl.BlockSpec((block, width), lambda i: (i, 0)),
-        ],
-        out_shape=[
-            jax.ShapeDtypeStruct((rows, depth), BF16),
-            jax.ShapeDtypeStruct((rows, width), BF16),
-        ],
+        out_specs=[pl.BlockSpec((block, width), lambda i: (i, 0))]
+        + [pl.BlockSpec((block, depth), lambda i: (i, 0))] * keep,
+        out_shape=[jax.ShapeDtypeStruct((rows, width), BF16)]
+        + [jax.ShapeDtypeStruct((rows, depth), BF16)] * keep,
         compiler_params=pltpu.CompilerParams(vmem_limit_bytes=VMEM_LIMIT),
         cost_estimate=hint(
             flops=2 * rows * depth * width, bytes_accessed=4 * rows * depth, transcendentals=0
         ),
         name="project",
-    )(x, gain, weight, cos_t, sin_t)
+    )(x, gain, weights, cos_t, sin_t)
 
 
 def stack_heads(block, group, upper):
@@ -1385,11 +1382,12 @@
     def after(value, *earlier):
         return lax.optimization_barrier((value,) + earlier)[0]
 
-    qkv_full = lax.all_gather(
-        jnp.concatenate([w_query, w_keyval], axis=1), "dp", axis=0, tiled=True
-    )
+    attn_full = lax.all_gather(
+        jnp.concatenate([w_query, w_keyval, w_output.T], axis=1), "dp", axis=0, tiled=True
+    )
+    qkv_full = attn_full[:, : q_width + kv_width]
+    out_t_full = attn_full[:, q_width + kv_width :]
     gains_full = lax.all_gather(norm_gains, "dp", axis=1, tiled=True)
-    out_t_full = lax.all_gather(w_output.T, "dp", axis=0, tiled=True)
 
     offsets = jnp.arange(CH, dtype=jnp.int32)
     all_pos = (span_order[:, None] * CH + offsets[None, :]).reshape(n_dp, parts, -1)
@@ -1405,9 +1403,15 @@
     batch_rows = SEQS * span_rows
     rows = MICRO * batch_rows
     gain_one, gain_two = gains_full[0:1], gains_full[1:2]
-    attn_in, qkv = project(x.reshape(rows, depth), gain_one, qkv_full, cos_t, sin_t)
-    qkv = qkv.reshape(MICRO, SEQS, span_rows, q_width + kv_width)
-    q, kv = qkv[..., :q_width], qkv[..., q_width:]
+    x_rows = x.reshape(rows, depth)
+    cos_k, sin_k = cos_t[:, q_width:], sin_t[:, q_width:]
+    (kv,) = project(x_rows, gain_one, attn_full, q_width // kv_width, cos_k, sin_k, 0)
+    kv = kv.reshape(MICRO, SEQS, span_rows, kv_width)
+    q, attn_in = project(
+        after(x_rows, kv), gain_one, attn_full, 0, cos_t[:, :q_width], sin_t[:, :q_width], 1
+    )
+    q = q.reshape(MICRO, SEQS, span_rows, q_width)
+    out_t_full = after(out_t_full, q)
     kv_all = lax.all_gather(kv, "dp", axis=0, tiled=False)
 
     sub = min(SUB, hidden_width // CHUNKS)

time: 728 us -> 729 us (level)
    all_gather x2, waiting for transfers between devices: 10.6 us -> 0.01 us  [per_device(): mlp_full.append(lax.all_gather(shard, 'dp', axis=0, tiled=True))]
    all_gather x2 -> x1, waiting for transfers between devices: 28.2 us -> 37.4 us  [per_device(): lax.all_gather(jnp.concatenate([w_query, w_keyval, w_output.T], axis=1),...]
    pallas_call x1 -> x2, Pallas kernels: 11 us -> 18.2 us  [project(): pl.pallas_call(project_kernel, grid=(rows // block,), in_specs=[pl.BlockS...]
  transfers between devices with their start and end apart: 26 -> 25, of which waited for: 15 -> 13; matrix products, arithmetic and copies ran while one was open for 7% -> 7% of each run, Pallas kernels for 61% -> 60%
where the time goes in v7:
time: 729 us; the launch traced here: 724 us
  Pallas kernels  446 us (61%)
  waiting for transfers between devices  172 us (24%)
  local copies, waits for them, and re-layouts  36.6 us (5%)
  starting transfers between devices  19.9 us (3%)
  between operations  14.8 us (2%)
  other arithmetic  13.6 us (2%)
  blocking collectives  13.5 us (2%)
  matrix products  7.46 us (1%)
    pallas_call x1, Pallas kernels, tail(): pl.pallas_call(functools.partial(tail_kernel, n_dp, n_tp, group), in_spec...  157 us
    ppermute x16, waiting for transfers between devices, swap(): return lax.ppermute(value, 'tp', [(i, i ^ k) for i in range(n_tp)])  126 us
    pallas_call x4, Pallas kernels, feed_forward(): pl.pallas_call(functools.partial(gated_kernel, n_tp, last, steps), grid=(...  98.3 us
    pallas_call x2, Pallas kernels, outer_products(): pl.pallas_call(functools.partial(outer_kernel, n_tp, batches, sub, steps)...  50.4 us
    pallas_call x1, Pallas kernels, finish(): pl.pallas_call(functools.partial(finish_kernel, n_dp, n_tp), in_specs=[an...  46 us
    all_gather x1, waiting for transfers between devices, per_device(): lax.all_gather(jnp.concatenate([w_query, w_keyval, w_output.T], axis=1),...  37.4 us
    pallas_call x1, Pallas kernels, attend(): pl.pallas_call(functools.partial(attend_kernel, group), grid=(micro, seqs...  29.1 us
    pallas_call x2, Pallas kernels, step_from_chunks(): pl.pallas_call(functools.partial(step_kernel, turned, decay, steps, chunk...  21.2 us
  transfers between devices with their start and end apart: 25, of which 13 were waited for; matrix products, arithmetic and copies ran while one was open for 7% of the time, Pallas kernels for 60%

profile of v7, /device:TPU:0, one launch (start us, length us, event | category | flops | bytes accessed | tf_op | source)
XLA Modules:
  0.0 724.3 jit_solution(14941707116138381672)
XLA Ops:
  8.4 1.9 pad_maximum_fusion.6
  12.7 13.5 %all_gather.15.refs_9_ = bf16[2,2048]{1,0:T(2,128)(2,1)S(1)} all-gather(bf16[2,256]{1,0:T(2,128)(2,1)S(1)} %copy-done.11), channel_id=1, replica_groups=mesh['dp'=8,'tp'=4] {'dp'}, dimensions={1}, use_global_device_ids=true | all-gather | bytes 9216 | tf_op jit(solution)/shard_map/all_gather | solution.py:1390
  26.2 2.6 constant_dynamic-slice_fusion.10
  28.9 2.3 pad_maximum_fusion
  31.8 37.4 %all-gather.5.cloned.1.call-done.w_ref = bf16[2048,1280]{1,0:T(8,128)(2,1)} async-done(((bf16[256,1280]{1,0:T(8,128)(2,1)}), bf16[2048,1280]{1,0:T(8,128)(2,1)}) %all-gather.5.cloned.1.call-update) | async-done | bytes 5242896 | tf_op jit(solution)/shard_map/all_gather | solution.py:1385
  69.2 8.3 %project.3 = bf16[1024,256]{1,0:T(8,128)(2,1)} custom-call(bf16[1024,2048]{1,0:T(8,128)(2,1)} %bitcast.81, bf16[1,2048]{1,0:T(2,128)(2,1)} %get-tuple-element.198.gain_ref, bf16[2048,1280]{1,0:T(8,128)(2,1)} %all-gather.5.cloned.1.call-done.w_ref, f32[128,256]{1,0:T(8,128)} %concatenate.82.cos_ref, f32[128,256]{1,0:T(8,128)} %concatenate.83.sin_ref), custom_call_target="tpu_custom_call" | custom-call | flops 53687092 | bytes 419430 | tf_op jit(solution)/shard_map/project/pallas_call | solution.py:80
  77.5 2.4 copy.105
  86.6 9.9 %project.2 = (bf16[1024,512]{1,0:T(8,128)(2,1)}, bf16[1024,2048]{1,0:T(8,128)(2,1)}) custom-call(bf16[1024,2048]{1,0:T(8,128)(2,1)} %bitcast.82, bf16[1,2048]{1,0:T(2,128)(2,1)} %get-tuple-element.198.gain_ref, bf16[2048,1280]{1,0:T(8,128)(2,1)} %all-gather.5.cloned.1.call-done.w_ref, f32[128,512]{1,0:T(8,128)} %concatenate.80.cos_ref, ...), custom_call_target="tpu_custom_call" | custom-call | flops 107374184 | bytes 419430 | tf_op jit(solution)/shard_map/project/pallas_call | solution.py:80
  96.6 2.5 collective-permute-start.5
  100.2 23.4 %collective-permute-done.5 = bf16[1024,512]{1,0:T(8,128)(2,1)S(1)} collective-permute-done((bf16[1024,512]{1,0:T(8,128)(2,1)S(1)}, bf16[1024,512]{1,0:T(8,128)(2,1)S(1)}, u32[]{:S(2)}, u32[]{:S(2)}) %collective-permute-start.5) | collective-permute-done | bytes 1048608 | tf_op jit(solution)/shard_map/ppermute | solution.py:1298
  123.6 21.7 %collective-permute-done.4 = bf16[1024,512]{1,0:T(8,128)(2,1)S(1)} collective-permute-done((bf16[1024,512]{1,0:T(8,128)(2,1)S(1)}, bf16[1024,512]{1,0:T(8,128)(2,1)S(1)}, u32[]{:S(2)}, u32[]{:S(2)}) %collective-permute-start.4) | collective-permute-done | bytes 1048608 | tf_op jit(solution)/shard_map/ppermute | solution.py:1298
  145.4 2.3 pad_maximum_fusion.1.refs_10_
  149.3 29.1 %attend.1 = bf16[2,4,128,512]{3,2,1,0:T(8,128)(2,1)} custom-call(s32[128,1]{1,0:T(8,128)} %copy.96.qpos_ref.refs_16_, s32[1,1024]{1,0:T(1,128)} %add.111.kpos_ref.refs_17_, bf16[2,4,128,512]{3,2,1,0:T(8,128)(2,1)} %bitcast.93, bf16[8,2,4,128,256]{4,3,2,1,0:T(8,128)(2,1)} %all-gather.7.cloned.1.call-done.kv_ref.refs_15_), custom_call_target="tpu_custom_call" | custom-call | flops 429496736 | bytes 314572 | tf_op jit(solution)/shard_map/attend/pallas_call | solution.py:189
  179.7 1.7 collective-permute-start.2
  181.4 1.3 collective-permute-start.1
  183.2 6.6 collective-permute-done.2
  189.8 5.1 collective-permute-done.1
  195.7 3.8 fusion.5
  199.5 3.7 fusion.4
  203.7 2.0 multiply_convert_fusion
  205.7 1.5 collective-permute-start.7
  210.6 20.3 %collective-permute-done.7 = bf16[256,2048]{1,0:T(8,128)(2,1)S(1)} collective-permute-done((bf16[256,2048]{1,0:T(8,128)(2,1)S(1)}, bf16[256,2048]{1,0:T(8,128)(2,1)S(1)}, u32[]{:S(2)}, u32[]{:S(2)}) %collective-permute-start.7) | collective-permute-done | bytes 1048608 | tf_op jit(solution)/shard_map/ppermute | solution.py:1298
  231.0 1.5 collective-permute-start.9
  234.9 9.8 %collective-permute-done.9 = bf16[128,2048]{1,0:T(8,128)(2,1)S(1)} collective-permute-done((bf16[128,2048]{1,0:T(8,128)(2,1)S(1)}, bf16[128,2048]{1,0:T(8,128)(2,1)S(1)}, u32[]{:S(2)}, u32[]{:S(2)}) %collective-permute-start.9) | collective-permute-done | bytes 524320 | tf_op jit(solution)/shard_map/ppermute | solution.py:1298
  244.7 1.5 pad_maximum_fusion.3.u_ref.refs_0_
  250.4 2.5 fusion.12
  254.2 3.5 dynamic_update_slice.21
  257.7 1.5 pad_maximum_fusion.4.u_ref.refs_1_
  259.2 9.7 %collective-permute-done.11 = bf16[512,768]{1,0:T(8,128)(2,1)S(1)} collective-permute-done((bf16[512,768]{1,0:T(8,128)(2,1)S(1)}, bf16[512,768]{1,0:T(8,128)(2,1)S(1)}, u32[]{:S(2)}, u32[]{:S(2)}) %collective-permute-start.11) | collective-permute-done | bytes 786464 | tf_op jit(solution)/shard_map/ppermute | solution.py:1298
  270.7 22.3 %feed_forward.4 = (bf16[512,1024]{1,0:T(8,128)(2,1)}, bf16[512,2048]{1,0:T(8,128)(2,1)}, bf16[512,2048]{1,0:T(8,128)(2,1)}, bf16[512,2048]{1,0:T(8,128)(2,1)}) custom-call(bf16[512,2048]{1,0:T(8,128)(2,1)} %pad_maximum_fusion.3.u_ref.refs_0_, bf16[512,2048]{1,0:T(8,128)(2,1)} %bitcast.73, bf16[2048,3072]{1,0:T(8,128)(2,1)} %all-gather.9.cloned.1.call-done.w_ref), custom_call_target="tpu_custom_call" | custom-call | flops 644245120 | bytes 1048576 | tf_op jit(solution)/shard_map/feed_forward/pallas_call | solution.py:473
  293.0 21.8 %feed_forward.5 = (bf16[512,1024]{1,0:T(8,128)(2,1)}, bf16[512,2048]{1,0:T(8,128)(2,1)}, bf16[512,2048]{1,0:T(8,128)(2,1)}, bf16[512,2048]{1,0:T(8,128)(2,1)}) custom-call(bf16[512,2048]{1,0:T(8,128)(2,1)} %pad_maximum_fusion.4.u_ref.refs_1_, bf16[512,2048]{1,0:T(8,128)(2,1)} %bitcast.77, bf16[2048,3072]{1,0:T(8,128)(2,1)} %all-gather.9.cloned.1.call-done.w_ref), custom_call_target="tpu_custom_call" | custom-call | flops 644245120 | bytes 1048576 | tf_op jit(solution)/shard_map/feed_forward/pallas_call | solution.py:473
  315.8 2.1 constant_dynamic-update-slice_fusion.4
  317.8 19.3 %outer_products.2 = bf16[8,256,3072]{2,1,0:T(8,128)(2,1)} custom-call(bf16[512,2048]{1,0:T(8,128)(2,1)} %pad_maximum_fusion.3.u_ref.refs_0_, bf16[512,2048]{1,0:T(8,128)(2,1)} %pad_maximum_fusion.4.u_ref.refs_1_, bf16[512,2048]{1,0:T(8,128)(2,1)} %bitcast.74, bf16[512,2048]{1,0:T(8,128)(2,1)} %bitcast.78, bf16[512,1024]{1,0:T(8,128)(2,1)} %get-tuple-element.95.refs_4_, ...), custom_call_target="tpu_custom_call" | custom-call | flops 644245120 | bytes 629145 | tf_op jit(solution)/shard_map/outer_products/pallas_call | solution.py:557
  338.3 1.5 collective-permute-start.15
  339.8 1.4 collective-permute-start.16
  341.2 18.5 %collective-permute-done.15 = bf16[512,768]{1,0:T(8,128)(2,1)S(1)} collective-permute-done((bf16[512,768]{1,0:T(8,128)(2,1)S(1)}, bf16[512,768]{1,0:T(8,128)(2,1)S(1)}, u32[]{:S(2)}, u32[]{:S(2)}) %collective-permute-start.15) | collective-permute-done | bytes 786464 | tf_op jit(solution)/shard_map/ppermute | solution.py:1298
  360.6 9.9 %collective-permute-done.16 = bf16[512,768]{1,0:T(8,128)(2,1)S(1)} collective-permute-done((bf16[512,768]{1,0:T(8,128)(2,1)}, bf16[512,768]{1,0:T(8,128)(2,1)S(1)}, u32[]{:S(2)}, u32[]{:S(2)}) %collective-permute-start.16) | collective-permute-done | bytes 786464 | tf_op jit(solution)/shard_map/ppermute | solution.py:1298
  371.5 22.1 %feed_forward.6 = (bf16[512,1024]{1,0:T(8,128)(2,1)}, bf16[512,2048]{1,0:T(8,128)(2,1)}, bf16[512,2048]{1,0:T(8,128)(2,1)}, bf16[512,2048]{1,0:T(8,128)(2,1)}) custom-call(bf16[512,2048]{1,0:T(8,128)(2,1)} %pad_maximum_fusion.3.u_ref.refs_0_, bf16[512,2048]{1,0:T(8,128)(2,1)} %bitcast.75, bf16[2048,3072]{1,0:T(8,128)(2,1)} %all-gather.11.cloned.1.call-done.w_ref, ...), custom_call_target="tpu_custom_call" | custom-call | flops 644245120 | bytes 1048576 | tf_op jit(solution)/shard_map/feed_forward/pallas_call | solution.py:473
  393.6 32.1 %feed_forward.7 = (bf16[512,1024]{1,0:T(8,128)(2,1)}, bf16[512,2048]{1,0:T(8,128)(2,1)}, bf16[512,2048]{1,0:T(8,128)(2,1)}, bf16[512,2048]{1,0:T(8,128)(2,1)}, bf16[4,128,2048]{2,1,0:T(8,128)(2,1)}) custom-call(bf16[512,2048]{1,0:T(8,128)(2,1)} %pad_maximum_fusion.4.u_ref.refs_1_, bf16[512,2048]{1,0:T(8,128)(2,1)} %bitcast.79, ...), custom_call_target="tpu_custom_call" | custom-call | flops 644245120 | bytes 1048576 | tf_op jit(solution)/shard_map/feed_forward/pallas_call | solution.py:473
  425.8 31.0 %outer_products.3 = (bf16[8,256,3072]{2,1,0:T(8,128)(2,1)}, bf16[4,128,2048]{2,1,0:T(8,128)(2,1)}) custom-call(bf16[512,2048]{1,0:T(8,128)(2,1)} %pad_maximum_fusion.3.u_ref.refs_0_, bf16[512,2048]{1,0:T(8,128)(2,1)} %pad_maximum_fusion.4.u_ref.refs_1_, bf16[512,2048]{1,0:T(8,128)(2,1)} %bitcast.76, bf16[512,2048]{1,0:T(8,128)(2,1)} %bitcast.80, ...), custom_call_target="tpu_custom_call" | custom-call | flops 644245120 | bytes 629145 | tf_op jit(solution)/shard_map/outer_products/pallas_call | solution.py:557
  459.0 156.6 %tail.1 = (bf16[2,512,768]{2,1,0:T(8,128)(2,1)}, bf16[2,4,128,2048]{3,2,1,0:T(8,128)(2,1)}, bf16[2,4,128,2048]{3,2,1,0:T(8,128)(2,1)}, bf16[2,128,2048]{2,1,0:T(8,128)(2,1)}, f32[2,2048]{1,0:T(2,128)}) custom-call(bf16[512,2048]{1,0:T(8,128)(2,1)} %get-tuple-element.117.refs_2_.refs_0_, bf16[512,2048]{1,0:T(8,128)(2,1)} %get-tuple-element.115.refs_8_.refs_1_, ...), custom_call_target="tpu_custom_call" | custom-call | flops 500000000 | bytes 5000000 | tf_op jit(solution)/shard_map/tail/pallas_call | solution.py:1171
  615.6 11.6 %attn_weight_grads.1 = (bf16[8,256,768]{2,1,0:T(8,128)(2,1)}, bf16[8,256,512]{2,1,0:T(8,128)(2,1)}) custom-call(bf16[1024,2048]{1,0:T(8,128)(2,1)} %get-tuple-element.124.a_ref, bf16[1024,2048]{1,0:T(8,128)(2,1)} %bitcast.92, bf16[1024,768]{1,0:T(8,128)(2,1)} %bitcast.100, bf16[1024,512]{1,0:T(8,128)(2,1)} %bitcast.85), custom_call_target="tpu_custom_call" | custom-call | flops 268435456 | bytes 419430 | tf_op jit(solution)/shard_map/attn_weight_grads/pallas_call | solution.py:589
  627.2 46.0 %finish.1 = (bf16[2,4,128,2048]{3,2,1,0:T(8,128)(2,1)}, f32[256,512]{1,0:T(8,128)}, f32[2,256]{1,0:T(2,128)}) custom-call(bf16[2,128,2048]{2,1,0:T(8,128)(2,1)} %get-tuple-element.123.tok_low, bf16[8,256,512]{2,1,0:T(8,128)(2,1)} %get-tuple-element.127.share_ref, f32[2,2048]{1,0:T(2,128)} %get-tuple-element.128.gain_ref), custom_call_target="tpu_custom_call" | custom-call | flops 500000000 | bytes 5000000 | tf_op jit(solution)/shard_map/finish/pallas_call | solution.py:808
  673.3 9.7 %spread.1 = (bf16[2,4,128,2048]{3,2,1,0:T(8,128)(2,1)}, f32[2,4,128,2048]{3,2,1,0:T(8,128)}) custom-call(s32[1]{0:T(128)} %bitcast.rank_ref, bf16[2,4,128,2048]{3,2,1,0:T(8,128)(2,1)} %get-tuple-element.122.out_ref, bf16[2,4,128,2048]{3,2,1,0:T(8,128)(2,1)} %get-tuple-element.129.tok_ref), custom_call_target="tpu_custom_call" | custom-call | tf_op jit(solution)/shard_map/spread/pallas_call | solution.py:1241
  683.0 7.1 weight_step.3
  690.1 14.0 %weight_step.2 = (f32[2,256,2048]{2,1,0:T(8,128)}, f32[2,256,2048]{2,1,0:T(8,128)}, f32[2,256,2048]{2,1,0:T(8,128)}, f32[2,256,2048]{2,1,0:T(8,128)}) custom-call(bf16[256,3072]{1,0:T(8,128)(2,1)} %bitcast.87, bf16[256,3072]{1,0:T(8,128)(2,1)} %bitcast.89, f32[2,256,2048]{2,1,0:T(8,128)} %refs_2_.4, f32[2,256,2048]{2,1,0:T(8,128)} %refs_3_.4, ...), custom_call_target="tpu_custom_call" | custom-call | flops 1048576 | bytes 1468006 | tf_op jit(solution)/shard_map/weight_step/pallas_call | solution.py:675
  704.2 8.1 %reduce-scatter.8.cloned.1.call-done.qkv_ref = bf16[1,256,768]{2,1,0:T(8,128)(2,1)} async-done(((bf16[8,256,768]{2,1,0:T(8,128)(2,1)}), bf16[1,256,768]{2,1,0:T(8,128)(2,1)}) %reduce-scatter.8.cloned.1.call-update) | async-done | bytes 393232 | tf_op jit(solution)/shard_map/reduce_scatter | solution.py:1553
  712.3 5.0 small_steps.1
  (126 shorter events, 35.9 us)
Async XLA Ops:
  7.2 3.3 copy-start.18
  7.2 5.5 copy-start.11
  7.2 62.0 %all-gather.5.cloned.1.call-start = ((), (), s32[]{:S(2)}) async-start(), calls=%async_computation.3 | async-start | bytes 5898240 | tf_op jit(solution)/shard_map/all_gather | solution.py:1385
  10.3 139.0 %all-gather.7.cloned.1.call-start = ((), (), s32[]{:S(2)}) async-start(), calls=%async_computation.4 | async-start | bytes 4718592 | tf_op jit(solution)/shard_map/all_gather | solution.py:1415
  26.2 5.0 copy-start.10
  28.8 174.8 %copy-start = (bf16[2,1,128,2048]{3,2,1,0:T(8,128)(2,1)}, bf16[2,1,128,2048]{3,2,1,0:T(8,128)(2,1)S(1)}, u32[]{:S(2)}) copy-start(bf16[2,1,128,2048]{3,2,1,0:T(8,128)(2,1)S(1)} %get-tuple-element.168) | copy-start | bytes 3145732
  77.5 2.5 copy-start.2
  77.5 193.3 %all-gather.9.cloned.1.call-start = ((), (), s32[]{:S(2)}) async-start(), calls=%async_computation.5 | async-start | bytes 14155776 | tf_op jit(solution)/shard_map/all_gather | solution.py:1427
  80.1 1.2 copy-start.4
  81.5 1.1 copy-start.5
  82.6 1.1 copy-start.6
  83.8 287.7 %all-gather.11.cloned.1.call-start = ((), (), s32[]{:S(2)}) async-start(), calls=%async_computation.6 | async-start | bytes 14155776 | tf_op jit(solution)/shard_map/all_gather | solution.py:1427
  84.4 588.9 %reduce-scatter.4.cloned.1.call-start = ((), (), s32[]{:S(2)}) async-start(), calls=%async_computation.7 | async-start | bytes 14155776 | tf_op jit(solution)/shard_map/reduce_scatter | solution.py:1494
  86.6 9.9 %slice-start = ((bf16[2048,1280]{1,0:T(8,128)(2,1)}), bf16[2048,512]{1,0:T(8,128)(2,1)S(1)}, s32[]{:S(2)}) async-start(bf16[2048,1280]{1,0:T(8,128)(2,1)} %all-gather.5.cloned.1.call-done.w_ref), calls=%async_computation.10 | async-start | bytes 4194304 | tf_op jit(solution)/shard_map/slice | solution.py:1389
  96.6 27.0 %collective-permute-start.5 = (bf16[1024,512]{1,0:T(8,128)(2,1)S(1)}, bf16[1024,512]{1,0:T(8,128)(2,1)S(1)}, u32[]{:S(2)}, u32[]{:S(2)}) collective-permute-start(bf16[1024,512]{1,0:T(8,128)(2,1)S(1)} %constant_dynamic-slice_fusion.5), channel_id=1, source_target_pairs={{0,3},{1,2},{2,1},{3,0},{4,7},{5,6},{6,5},{7,4},{8,11},{9,10},{10,... | collective-permute-start | bytes 3145736 | tf_op jit(solution)/shard_map/ppermute | solution.py:1298
  99.1 46.3 %collective-permute-start.4 = (bf16[1024,512]{1,0:T(8,128)(2,1)S(1)}, bf16[1024,512]{1,0:T(8,128)(2,1)S(1)}, u32[]{:S(2)}, u32[]{:S(2)}) collective-permute-start(bf16[1024,512]{1,0:T(8,128)(2,1)S(1)} %constant_dynamic-slice_fusion.5), channel_id=1, source_target_pairs={{0,2},{1,3},{2,0},{3,1},{4,6},{5,7},{6,4},{7,5},{8,10},{9,11},{10,... | collective-permute-start | bytes 3145736 | tf_op jit(solution)/shard_map/ppermute | solution.py:1298
  99.6 45.8 %collective-permute-start.3 = (bf16[1024,512]{1,0:T(8,128)(2,1)S(1)}, bf16[1024,512]{1,0:T(8,128)(2,1)S(1)}, u32[]{:S(2)}, u32[]{:S(2)}) collective-permute-start(bf16[1024,512]{1,0:T(8,128)(2,1)S(1)} %constant_dynamic-slice_fusion.5), channel_id=1, source_target_pairs={{0,1},{1,0},{2,3},{3,2},{4,5},{5,4},{6,7},{7,6},{8,9},{9,8},{10,11... | collective-permute-start | bytes 3145736 | tf_op jit(solution)/shard_map/ppermute | solution.py:1298
  147.7 51.8 %collective-permute-start.6 = (bf16[1024,2048]{1,0:T(8,128)(2,1)}, bf16[1024,2048]{1,0:T(8,128)(2,1)}, u32[]{:S(2)}, u32[]{:S(2)}) collective-permute-start(bf16[1024,2048]{1,0:T(8,128)(2,1)} %pad_maximum_fusion.1.refs_10_), channel_id=1, source_target_pairs={{0,4},{4,0},{8,12},{12,8},{16,20},{20,16},{24,28},{28,24},{1,5},{5... | collective-permute-start | bytes 12582920 | tf_op jit(solution)/shard_map/ppermute | solution.py:1373
  179.7 19.8 %copy-start.9 = (bf16[2,1,128,512]{3,2,1,0:T(8,128)(2,1)}, bf16[2,1,128,512]{3,2,1,0:T(8,128)(2,1)S(1)}, u32[]{:S(2)}) copy-start(bf16[2,1,128,512]{3,2,1,0:T(8,128)(2,1)S(1)} %get-tuple-element.194) | copy-start | bytes 786436
  179.7 10.1 %collective-permute-start.2 = (bf16[2,128,512]{2,1,0:T(8,128)(2,1)S(1)}, bf16[2,128,512]{2,1,0:T(8,128)(2,1)S(1)}, u32[]{:S(2)}, u32[]{:S(2)}) collective-permute-start(bf16[2,128,512]{2,1,0:T(8,128)(2,1)S(1)} %get-tuple-element.195), channel_id=1, source_target_pairs={{0,3},{1,2},{2,1},{3,0},{4,7},{5,6},{6,5},{7,4},{8,11},{9,10},{10,... | collective-permute-start | bytes 786440 | tf_op jit(solution)/shard_map/ppermute | solution.py:1298
  181.4 13.5 %collective-permute-start.1 = (bf16[2,128,512]{2,1,0:T(8,128)(2,1)S(1)}, bf16[2,128,512]{2,1,0:T(8,128)(2,1)S(1)}, u32[]{:S(2)}, u32[]{:S(2)}) collective-permute-start(bf16[2,128,512]{2,1,0:T(8,128)(2,1)S(1)} %get-tuple-element.196), channel_id=1, source_target_pairs={{0,2},{1,3},{2,0},{3,1},{4,6},{5,7},{6,4},{7,5},{8,10},{9,11},{10,... | collective-permute-start | bytes 786440 | tf_op jit(solution)/shard_map/ppermute | solution.py:1298
  182.7 12.2 %collective-permute-start = (bf16[2,128,512]{2,1,0:T(8,128)(2,1)S(1)}, bf16[2,128,512]{2,1,0:T(8,128)(2,1)S(1)}, u32[]{:S(2)}, u32[]{:S(2)}) collective-permute-start(bf16[2,128,512]{2,1,0:T(8,128)(2,1)S(1)} %get-tuple-element.197), channel_id=1, source_target_pairs={{0,1},{1,0},{2,3},{3,2},{4,5},{5,4},{6,7},{7,6},{8,9},{9,8},{10,11... | collective-permute-start | bytes 786440 | tf_op jit(solution)/shard_map/ppermute | solution.py:1298
  189.8 5.1 copy-start.12
  194.9 0.7 copy-start.14
  194.9 0.8 copy-start.16
  195.7 3.8 copy-start.13
  195.7 3.8 copy-start.15
  195.7 3.8 copy-start.17
  203.7 3.5 copy-start.3
  205.7 25.2 %collective-permute-start.7 = (bf16[256,2048]{1,0:T(8,128)(2,1)S(1)}, bf16[256,2048]{1,0:T(8,128)(2,1)S(1)}, u32[]{:S(2)}, u32[]{:S(2)}) collective-permute-start(bf16[256,2048]{1,0:T(8,128)(2,1)S(1)} %get-tuple-element.160), channel_id=1, source_target_pairs={{0,1},{1,0},{2,3},{3,2},{4,5},{5,4},{6,7},{7,6},{8,9},{9,8},{10,11... | collective-permute-start | bytes 3145736 | tf_op jit(solution)/shard_map/ppermute | solution.py:1298
  207.6 1.0 copy-start.1
  208.6 1.9 slice-start.1
  208.6 25.2 %collective-permute-start.8 = (bf16[256,2048]{1,0:T(8,128)(2,1)S(1)}, bf16[256,2048]{1,0:T(8,128)(2,1)S(1)}, u32[]{:S(2)}, u32[]{:S(2)}) collective-permute-start(bf16[256,2048]{1,0:T(8,128)(2,1)S(1)} %get-tuple-element.160), channel_id=1, source_target_pairs={{0,2},{1,3},{2,0},{3,1},{4,6},{5,7},{6,4},{7,5},{8,10},{9,11},{10,... | collective-permute-start | bytes 3145736 | tf_op jit(solution)/shard_map/ppermute | solution.py:1298
  231.0 13.7 %collective-permute-start.9 = (bf16[128,2048]{1,0:T(8,128)(2,1)S(1)}, bf16[128,2048]{1,0:T(8,128)(2,1)S(1)}, u32[]{:S(2)}, u32[]{:S(2)}) collective-permute-start(bf16[128,2048]{1,0:T(8,128)(2,1)S(1)} %get-tuple-element.191), channel_id=1, source_target_pairs={{0,2},{1,3},{2,0},{3,1},{4,6},{5,7},{6,4},{7,5},{8,10},{9,11},{10,... | collective-permute-start | bytes 1572872 | tf_op jit(solution)/shard_map/ppermute | solution.py:1298
  233.9 23.8 %collective-permute-start.10 = (bf16[128,2048]{1,0:T(8,128)(2,1)S(1)}, bf16[128,2048]{1,0:T(8,128)(2,1)S(1)}, u32[]{:S(2)}, u32[]{:S(2)}) collective-permute-start(bf16[128,2048]{1,0:T(8,128)(2,1)S(1)} %get-tuple-element.192), channel_id=1, source_target_pairs={{0,1},{1,0},{2,3},{3,2},{4,5},{5,4},{6,7},{7,6},{8,9},{9,8},{10,11... | collective-permute-start | bytes 1572872 | tf_op jit(solution)/shard_map/ppermute | solution.py:1298
  247.2 5.7 copy-start.7
  247.2 22.6 %collective-permute-start.12 = (bf16[512,768]{1,0:T(8,128)(2,1)S(1)}, bf16[512,768]{1,0:T(8,128)(2,1)S(1)}, u32[]{:S(2)}, u32[]{:S(2)}) collective-permute-start(bf16[512,768]{1,0:T(8,128)(2,1)S(1)} %get-tuple-element.175), channel_id=1, source_target_pairs={{0,2},{1,3},{2,0},{3,1},{4,6},{5,7},{6,4},{7,5},{8,10},{9,11},{10,... | collective-permute-start | bytes 2359304 | tf_op jit(solution)/shard_map/ppermute | solution.py:1298
  248.4 20.5 %collective-permute-start.11 = (bf16[512,768]{1,0:T(8,128)(2,1)S(1)}, bf16[512,768]{1,0:T(8,128)(2,1)S(1)}, u32[]{:S(2)}, u32[]{:S(2)}) collective-permute-start(bf16[512,768]{1,0:T(8,128)(2,1)S(1)} %get-tuple-element.175), channel_id=1, source_target_pairs={{0,1},{1,0},{2,3},{3,2},{4,5},{5,4},{6,7},{7,6},{8,9},{9,8},{10,11... | collective-permute-start | bytes 2359304 | tf_op jit(solution)/shard_map/ppermute | solution.py:1298
  249.3 65.5 %collective-permute-start.13 = (bf16[512,768]{1,0:T(8,128)(2,1)}, bf16[512,768]{1,0:T(8,128)(2,1)S(1)}, u32[]{:S(2)}, u32[]{:S(2)}) collective-permute-start(bf16[512,768]{1,0:T(8,128)(2,1)} %get-tuple-element.174), channel_id=1, source_target_pairs={{0,1},{1,0},{2,3},{3,2},{4,5},{5,4},{6,7},{7,6},{8,9},{9,8},{10,11... | collective-permute-start | bytes 2359304 | tf_op jit(solution)/shard_map/ppermute | solution.py:1298
  253.0 62.8 %collective-permute-start.14 = (bf16[512,768]{1,0:T(8,128)(2,1)}, bf16[512,768]{1,0:T(8,128)(2,1)}, u32[]{:S(2)}, u32[]{:S(2)}) collective-permute-start(bf16[512,768]{1,0:T(8,128)(2,1)} %get-tuple-element.174), channel_id=1, source_target_pairs={{0,2},{1,3},{2,0},{3,1},{4,6},{5,7},{6,4},{7,5},{8,10},{9,11},{10,... | collective-permute-start | bytes 2359304 | tf_op jit(solution)/shard_map/ppermute | solution.py:1298
  337.2 1.1 copy-start.8
  337.2 336.1 %reduce-scatter.6.cloned.1.call-start = ((), (), s32[]{:S(2)}) async-start(), calls=%async_computation.8 | async-start | bytes 14155776 | tf_op jit(solution)/shard_map/reduce_scatter | solution.py:1494
  338.3 21.4 %collective-permute-start.15 = (bf16[512,768]{1,0:T(8,128)(2,1)S(1)}, bf16[512,768]{1,0:T(8,128)(2,1)S(1)}, u32[]{:S(2)}, u32[]{:S(2)}) collective-permute-start(bf16[512,768]{1,0:T(8,128)(2,1)S(1)} %copy-done.8), channel_id=1, source_target_pairs={{0,3},{1,2},{2,1},{3,0},{4,7},{5,6},{6,5},{7,4},{8,11},{9,10},{10,... | collective-permute-start | bytes 2359304 | tf_op jit(solution)/shard_map/ppermute | solution.py:1298
  339.8 30.7 %collective-permute-start.16 = (bf16[512,768]{1,0:T(8,128)(2,1)}, bf16[512,768]{1,0:T(8,128)(2,1)S(1)}, u32[]{:S(2)}, u32[]{:S(2)}) collective-permute-start(bf16[512,768]{1,0:T(8,128)(2,1)} %get-tuple-element.174), channel_id=1, source_target_pairs={{0,3},{1,2},{2,1},{3,0},{4,7},{5,6},{6,5},{7,4},{8,11},{9,10},{10,... | collective-permute-start | bytes 2359304 | tf_op jit(solution)/shard_map/ppermute | solution.py:1298
  371.5 54.3 %collective-permute-start.17 = (bf16[1024,3072]{1,0:T(8,128)(2,1)}, bf16[1024,3072]{1,0:T(8,128)(2,1)}, u32[]{:S(2)}, u32[]{:S(2)}) collective-permute-start(bf16[1024,3072]{1,0:T(8,128)(2,1)} %constant_dynamic-update-slice_fusion.3.refs_12_), channel_id=1, source_target_pairs={{0,4},{4,0},{8,12},{12,8},{16,20},{20,16},{24,28},{28,24},{1,5},{5... | collective-permute-start | bytes 18874376 | tf_op jit(solution)/shard_map/ppermute | solution.py:1373
  456.8 255.5 %reduce-scatter.8.cloned.1.call-start = ((), (), s32[]{:S(2)}) async-start(), calls=%async_computation.9 | async-start | bytes 3538944 | tf_op jit(solution)/shard_map/reduce_scatter | solution.py:1553
Sparse Core Ops, SparseCore 0:
  10.4 58.7 all-gather.4
  77.6 45.8 all-gather.6
  125.7 115.4 all-gather.8
  242.7 114.9 all-gather.10
  359.9 127.4 reduce-scatter.3
  489.5 172.7 reduce-scatter.5
  673.5 38.7 reduce-scatter.7
